TPU v7x, 32 devices: a whole 2x2x4 slice. The times are simulated.
32 devices in a mesh: fsdp: 4 (over z), seq: 8 (over y, x, core).
Axes of the slice: x: 2, y: 2, z: 4, core: 2. Of those that a mesh axis runs over, the one named last changes fastest.
Arguments:
- tokens: bfloat16 [12288, 1024], P(('fsdp', 'seq')), may hold values from -6 to 6
- cotangent: bfloat16 [12288, 1024], P(('fsdp', 'seq')), may hold values from -6 to 6
- doc_starts: int32 [4, 4], P('fsdp'), may hold values from 0 to 3071, as said below
- gain_one: bfloat16 [1024], P(('fsdp', 'seq')), may hold values from 0.5 to 1.5
- w_query: bfloat16 [1024, 1024], P(('fsdp', 'seq')), may hold values from -1 to 1
- w_key: bfloat16 [1024, 1024], P(('fsdp', 'seq')), may hold values from -1 to 1
- w_value: bfloat16 [1024, 1024], P(('fsdp', 'seq')), may hold values from -0.1875 to 0.1875
- w_swish: bfloat16 [1024, 1024], P(('fsdp', 'seq')), may hold values from -0.1875 to 0.1875
- w_rank_in: bfloat16 [1024, 16], P(('fsdp', 'seq')), may hold values from -0.1875 to 0.1875
- w_rank_out: bfloat16 [16, 1024], P(None, ('fsdp', 'seq')), may hold values from -1.5 to 1.5
- gate_bias: bfloat16 [1024], P(('fsdp', 'seq')), may hold values from -1 to 9
- head_gain: bfloat16 [256], P(('fsdp', 'seq')), may hold values from 0.5 to 1.5
- w_output: bfloat16 [1024, 1024], P(('fsdp', 'seq')), may hold values from -0.375 to 0.375
- gain_two: bfloat16 [1024], P(('fsdp', 'seq')), may hold values from 0.5 to 1.5
- w_gate: bfloat16 [1024, 2816], P(('fsdp', 'seq')), may hold values from -0.1875 to 0.1875
- w_up: bfloat16 [1024, 2816], P(('fsdp', 'seq')), may hold values from -0.1875 to 0.1875
- w_down: bfloat16 [2816, 1024], P(('fsdp', 'seq')), may hold values from -0.21875 to 0.21875
Outputs:
- output: bfloat16 [12288, 1024], P(('fsdp', 'seq'))
- input_grad: float32 [12288, 1024], P(('fsdp', 'seq'))
- grad_gain_one: float32 [1024], P(('fsdp', 'seq'))
- grad_w_query: float32 [1024, 1024], P(('fsdp', 'seq'))
- grad_w_key: float32 [1024, 1024], P(('fsdp', 'seq'))
- grad_w_value: float32 [1024, 1024], P(('fsdp', 'seq'))
- grad_w_swish: float32 [1024, 1024], P(('fsdp', 'seq'))
- grad_w_rank_in: float32 [1024, 16], P(('fsdp', 'seq'))
- grad_w_rank_out: float32 [16, 1024], P(None, ('fsdp', 'seq'))
- grad_gate_bias: float32 [1024], P(('fsdp', 'seq'))
- grad_head_gain: float32 [256], P(('fsdp', 'seq'))
- grad_w_output: float32 [1024, 1024], P(('fsdp', 'seq'))
- grad_gain_two: float32 [1024], P(('fsdp', 'seq'))
- grad_w_gate: float32 [1024, 2816], P(('fsdp', 'seq'))
- grad_w_up: float32 [1024, 2816], P(('fsdp', 'seq'))
- grad_w_down: float32 [2816, 1024], P(('fsdp', 'seq'))
Inputs may be any that keep to these rules, and one draw needn't show every extreme that they name: `doc_starts`: each row holds 4 increasing positions: the first is 0, the second lies among the first 384 positions, the third and fourth among the last 384 positions of the sequence; in some row the fourth is the sequence's last position.
All inputs are finite; a program needn't handle non-finite values.
Results may differ from a plain program's by a relative error of at most 0.029.
Values may be sent and summed in bfloat16 or wider, within the bound.
No kernel may reach another device: no remote copies, remote signals or barrier semaphores. Data moves between devices by JAX's collectives and lax.ppermute only.
A program may use at most 256 MiB of HBM per device.

v0:
```python
from functools import partial

import jax
import jax.numpy as jnp
from jax import lax
from jax.sharding import PartitionSpec as P

HEAD_K = 256
HEAD_V = 256
GROUP = 64


MAXIMUM_ACCURACY = lax.Precision.HIGHEST


def prefix(value, axis, combine, identity):
    length, place = (lax.axis_size(axis), lax.axis_index(axis))
    everything = jax.tree.map(
        lambda part, kind: lax.all_gather(part.astype(kind), axis),
        value,
        (jnp.bfloat16, jnp.bfloat16),
    )
    start = jax.tree.map(
        lambda part, zero: jnp.broadcast_to(jnp.asarray(zero, part.dtype), part.shape),
        value,
        identity,
    )

    def prefix_lap(k, before):
        reached = k < place
        new = combine(
            before, jax.tree.map(lambda part, own: part[k].astype(own.dtype), everything, value)
        )
        return jax.tree.map(lambda a, b: jnp.where(reached, a, b), new, before)

    return lax.fori_loop(0, length, prefix_lap, start)


def entering_2(value, axis, combine, identity):
    length, place = (lax.axis_size(axis), lax.axis_index(axis))
    everything = jax.tree.map(
        lambda part, kind: lax.all_gather(part.astype(kind), axis),
        value,
        jax.tree.map(lambda a: jnp.bfloat16 if a.dtype == jnp.float32 else a.dtype, value),
    )
    start = jax.tree.map(
        lambda part, zero: jnp.broadcast_to(jnp.asarray(zero, part.dtype), part.shape),
        value,
        identity,
    )

    def entering_lap(k, before):
        at = length - 1 - k
        reached = at > place
        new = combine(
            before, jax.tree.map(lambda part, own: part[at].astype(own.dtype), everything, value)
        )
        return jax.tree.map(lambda a, b: jnp.where(reached, a, b), new, before)

    return lax.fori_loop(0, length, entering_lap, start)


def matmul(left, right):
    return jnp.dot(left, right, preferred_element_type=jnp.float32)


def matmul_t(left, right):
    return lax.dot_general(
        left, right, (((0,), (0,)), ((), ())), preferred_element_type=jnp.float32
    )


def matmul_nt(left, right):
    return lax.dot_general(
        left, right, (((1,), (1,)), ((), ())), preferred_element_type=jnp.float32
    )


def norm_rows(values, scales, epsilon):
    return values * lax.rsqrt(jnp.mean(values * values, axis=-1, keepdims=True) + epsilon) * scales


def norm_model(values, scales):
    return norm_rows(values, scales, 1e-06)


def heads_of(tensor, head_width):
    return tensor.reshape(tensor.shape[0], -1, head_width)


def head_gate(mixed_heads, scales, swish_pre):
    headed = norm_rows(mixed_heads, scales, 1e-05) * jax.nn.silu(heads_of(swish_pre, HEAD_V))
    return headed.reshape(headed.shape[0], -1)


def decay_of(gate_pre):
    return heads_of(jax.nn.log_sigmoid(gate_pre) / 16.0, HEAD_K)


def swiglu(gate_proj, up_proj):
    return jax.nn.silu(gate_proj) * up_proj


def document_of(positions, starts):
    return jnp.sum((starts[None, :] <= positions[:, None]).astype(jnp.int32), axis=1) - 1


def combine_states(earlier_part, later_part):
    return (
        earlier_part[0] * later_part[0],
        later_part[0][:, :, None] * earlier_part[1] + later_part[1],
    )


def group_step(passed_state, pieces):
    queries, key_rows, value_matrix, decays, doc_ids, prev_doc = pieces
    running_total = jnp.cumsum(decays, axis=0)
    query_entering = queries * jnp.exp(running_total)
    key_in = key_rows * jnp.exp(-running_total)
    scores = jnp.einsum("thk,shk->hts", query_entering, key_in, precision=MAXIMUM_ACCURACY)
    indices = jnp.arange(doc_ids.shape[0], dtype=jnp.int32)
    allowed = (doc_ids[:, None] == doc_ids[None, :]) & (indices[:, None] >= indices[None, :])
    scores = jnp.where(allowed[None], scores, 0.0)
    within = jnp.einsum("hts,shv->thv", scores, value_matrix, precision=MAXIMUM_ACCURACY)
    entering = (doc_ids == prev_doc).astype(queries.dtype)
    carried_over = jnp.einsum(
        "wiu,iug->wig", query_entering, passed_state, precision=MAXIMUM_ACCURACY
    )
    outputs = within + entering[:, None, None] * carried_over
    closing_sum = running_total[-1]
    tail_rows = (doc_ids == doc_ids[-1]).astype(queries.dtype)
    key_finish = key_rows * jnp.exp(closing_sum[None] - running_total) * tail_rows[:, None, None]
    retained_state = (doc_ids[-1] == prev_doc).astype(queries.dtype)
    updated_state = retained_state * jnp.exp(closing_sum)[:, :, None] * passed_state + jnp.einsum(
        "yaq,yap->aqp", key_finish, value_matrix, precision=MAXIMUM_ACCURACY
    )
    return (updated_state, outputs)


def local_mixer(queries, key_rows, value_matrix, decays, doc_ids, prev_ids, device_keep):
    blocks = queries.shape[0] // GROUP
    rescaled_rows = queries * queries.shape[-1] ** (-0.5)

    def split_blocks(tensor):
        return tensor.reshape((blocks, GROUP) + tensor.shape[1:])

    start_state = jnp.zeros(
        (queries.shape[1], queries.shape[2], value_matrix.shape[2]), jnp.float32
    )
    final_state, outputs = lax.scan(
        group_step,
        start_state,
        (
            split_blocks(rescaled_rows),
            split_blocks(key_rows),
            split_blocks(value_matrix),
            split_blocks(decays),
            split_blocks(doc_ids),
            split_blocks(prev_ids)[:, 0],
        ),
    )
    transfer_scale = device_keep * jnp.exp(jnp.sum(decays, axis=0))
    return (outputs.reshape(value_matrix.shape), final_state, transfer_scale)


def incoming(queries, decays, incoming_state, entry_rows):
    rescaled_rows = queries * queries.shape[-1] ** (-0.5)
    running_total = jnp.cumsum(decays, axis=0)
    return entry_rows[:, None, None] * jnp.einsum(
        "wiu,iug->wig",
        rescaled_rows * jnp.exp(running_total),
        incoming_state,
        precision=MAXIMUM_ACCURACY,
    )


def gather_attention(pieces):
    return (
        lax.all_gather(pieces[0], ("fsdp", "seq"), axis=0, tiled=True),
        lax.all_gather(pieces[1], ("fsdp", "seq"), axis=0, tiled=True),
        lax.all_gather(pieces[2], ("fsdp", "seq"), axis=0, tiled=True),
        lax.all_gather(pieces[3], ("fsdp", "seq"), axis=0, tiled=True),
        lax.all_gather(pieces[4], ("fsdp", "seq"), axis=0, tiled=True),
        lax.all_gather(pieces[5], ("fsdp", "seq"), axis=0, tiled=True),
        lax.all_gather(pieces[6], ("fsdp", "seq"), axis=1, tiled=True),
        lax.all_gather(pieces[7], ("fsdp", "seq"), axis=0, tiled=True),
        lax.all_gather(pieces[8], ("fsdp", "seq"), axis=0, tiled=True),
        lax.all_gather(pieces[9], ("fsdp", "seq"), axis=0, tiled=True),
    )


def gather_feedforward(pieces):
    return (
        lax.all_gather(pieces[0], ("fsdp", "seq"), axis=0, tiled=True),
        lax.all_gather(pieces[1], ("fsdp", "seq"), axis=0, tiled=True),
        lax.all_gather(pieces[2], ("fsdp", "seq"), axis=0, tiled=True),
        lax.all_gather(pieces[3], ("fsdp", "seq"), axis=0, tiled=True),
    )


def forward(inputs, attention, feedforward, context):
    doc_ids, prev_ids, entry_rows, device_keep = context
    (
        gain_one,
        w_query,
        w_key,
        w_value,
        w_swish,
        w_rank_in,
        w_rank_out,
        gate_bias,
        head_gain,
        w_output,
    ) = attention
    gain_two, w_gate, w_up, w_down = feedforward
    normed = norm_model(inputs, gain_one.astype(jnp.float32)).astype(jnp.bfloat16)
    queries = matmul(normed, w_query).astype(jnp.bfloat16)
    key_rows = matmul(normed, w_key).astype(jnp.bfloat16)
    value_matrix = matmul(normed, w_value).astype(jnp.bfloat16)
    low_rank = matmul(normed, w_rank_in).astype(jnp.bfloat16)
    gate_pre = matmul(low_rank, w_rank_out) + gate_bias.astype(jnp.float32)
    swish_pre = matmul(normed, w_swish)
    decays = decay_of(gate_pre)
    query_heads = heads_of(queries.astype(jnp.float32), HEAD_K)
    mixed_zero, final_state, transfer_scale = local_mixer(
        query_heads,
        heads_of(key_rows.astype(jnp.float32), HEAD_K),
        heads_of(value_matrix.astype(jnp.float32), HEAD_V),
        decays,
        doc_ids,
        prev_ids,
        device_keep,
    )
    identity = (jnp.ones_like(transfer_scale), jnp.zeros_like(final_state))
    prefix_scale, incoming_state = prefix(
        (transfer_scale, final_state), "seq", combine_states, identity
    )
    mixed_heads = mixed_zero + incoming(query_heads, decays, incoming_state, entry_rows)
    gated_rows = head_gate(mixed_heads, head_gain.astype(jnp.float32), swish_pre).astype(
        jnp.bfloat16
    )
    hidden_state = inputs + matmul(gated_rows, w_output)
    normed_two = norm_model(hidden_state, gain_two.astype(jnp.float32)).astype(jnp.bfloat16)
    gate_proj = matmul(normed_two, w_gate)
    up_proj = matmul(normed_two, w_up)
    inner_rows = swiglu(gate_proj, up_proj).astype(jnp.bfloat16)
    result = hidden_state + matmul(inner_rows, w_down)
    return (
        result,
        normed,
        queries,
        key_rows,
        value_matrix,
        low_rank,
        gate_pre,
        swish_pre,
        mixed_heads,
        incoming_state,
        transfer_scale,
        gated_rows,
        hidden_state,
        normed_two,
        gate_proj,
        up_proj,
        inner_rows,
    )


def backward(upstream, inputs, attention, feedforward, kept_values, context):
    doc_ids, prev_ids, entry_rows, device_keep = context
    (
        gain_one,
        w_query,
        w_key,
        w_value,
        w_swish,
        w_rank_in,
        w_rank_out,
        gate_bias,
        head_gain,
        w_output,
    ) = attention
    gain_two, w_gate, w_up, w_down = feedforward
    (
        result,
        normed,
        queries,
        key_rows,
        value_matrix,
        low_rank,
        gate_pre,
        swish_pre,
        mixed_heads,
        incoming_state,
        transfer_scale,
        gated_rows,
        hidden_state,
        normed_two,
        gate_proj,
        up_proj,
        inner_rows,
    ) = kept_values
    down_grad = upstream.astype(jnp.bfloat16)
    grad_w_down = matmul_t(inner_rows, down_grad)
    grad_inner = matmul_nt(down_grad, w_down)
    _, pull_mlp = jax.vjp(swiglu, gate_proj, up_proj)
    grad_gate, grad_up = pull_mlp(grad_inner)
    grad_gate = grad_gate.astype(jnp.bfloat16)
    grad_up = grad_up.astype(jnp.bfloat16)
    grad_w_gate = matmul_t(normed_two, grad_gate)
    grad_w_up = matmul_t(normed_two, grad_up)
    grad_normed_two = matmul_nt(grad_gate, w_gate) + matmul_nt(grad_up, w_up)
    _, pull_second = jax.vjp(norm_model, hidden_state, gain_two.astype(jnp.float32))
    hidden_extra, grad_gain_two = pull_second(grad_normed_two)
    grad_hidden = upstream + hidden_extra
    branch_grad = grad_hidden.astype(jnp.bfloat16)
    grad_w_output = matmul_t(gated_rows, branch_grad)
    grad_gated = matmul_nt(branch_grad, w_output)
    _, pull_head = jax.vjp(head_gate, mixed_heads, head_gain.astype(jnp.float32), swish_pre)
    grad_mixed, grad_head_gain, grad_swish = pull_head(grad_gated)
    query_heads = heads_of(queries.astype(jnp.float32), HEAD_K)
    key_heads = heads_of(key_rows.astype(jnp.float32), HEAD_K)
    value_heads = heads_of(value_matrix.astype(jnp.float32), HEAD_V)
    decays, pull_decay = jax.vjp(decay_of, gate_pre)
    _, pull_enter = jax.vjp(
        partial(incoming, entry_rows=entry_rows), query_heads, decays, incoming_state
    )
    grad_q_enter, grad_decay_enter, grad_entry = pull_enter(grad_mixed)
    identity = (jnp.ones_like(transfer_scale), jnp.zeros_like(grad_entry))
    suffix_scale, exit_grad = entering_2(
        (transfer_scale, grad_entry), "seq", combine_states, identity
    )
    grad_scale = jnp.sum(exit_grad * incoming_state, axis=2)
    _, pull_local = jax.vjp(
        partial(local_mixer, doc_ids=doc_ids, prev_ids=prev_ids, device_keep=device_keep),
        query_heads,
        key_heads,
        value_heads,
        decays,
    )
    grad_q_local, grad_key, grad_value, grad_decay_local = pull_local(
        (grad_mixed, exit_grad, grad_scale)
    )
    (grad_gate_pre,) = pull_decay(grad_decay_local + grad_decay_enter)
    gate_grad_low = grad_gate_pre.astype(jnp.bfloat16)
    grad_gate_bias = jnp.sum(gate_grad_low.astype(jnp.float32), axis=0)
    grad_w_rank_out = matmul_t(low_rank, gate_grad_low)
    grad_low_rank = matmul_nt(gate_grad_low, w_rank_out).astype(jnp.bfloat16)
    grad_w_rank_in = matmul_t(normed, grad_low_rank)
    row_count = normed.shape[0]
    swish_grad_low = grad_swish.astype(jnp.bfloat16)
    query_grad_low = (grad_q_local + grad_q_enter).reshape(row_count, -1).astype(jnp.bfloat16)
    key_grad_low = grad_key.reshape(row_count, -1).astype(jnp.bfloat16)
    value_grad_low = grad_value.reshape(row_count, -1).astype(jnp.bfloat16)
    grad_w_swish = matmul_t(normed, swish_grad_low)
    grad_w_query = matmul_t(normed, query_grad_low)
    grad_w_key = matmul_t(normed, key_grad_low)
    grad_w_value = matmul_t(normed, value_grad_low)
    grad_normed = (
        matmul_nt(query_grad_low, w_query)
        + matmul_nt(key_grad_low, w_key)
        + matmul_nt(value_grad_low, w_value)
        + matmul_nt(swish_grad_low, w_swish)
        + matmul_nt(grad_low_rank, w_rank_in)
    )
    _, pull_first = jax.vjp(norm_model, inputs, gain_one.astype(jnp.float32))
    input_extra, grad_gain_one = pull_first(grad_normed)
    input_grad = grad_hidden + input_extra
    attention_grads = (
        lax.psum_scatter(grad_gain_one, ("fsdp", "seq"), scatter_dimension=0, tiled=True),
        lax.psum_scatter(grad_w_query, ("fsdp", "seq"), scatter_dimension=0, tiled=True),
        lax.psum_scatter(grad_w_key, ("fsdp", "seq"), scatter_dimension=0, tiled=True),
        lax.psum_scatter(grad_w_value, ("fsdp", "seq"), scatter_dimension=0, tiled=True),
        lax.psum_scatter(grad_w_swish, ("fsdp", "seq"), scatter_dimension=0, tiled=True),
        lax.psum_scatter(grad_w_rank_in, ("fsdp", "seq"), scatter_dimension=0, tiled=True),
        lax.psum_scatter(grad_w_rank_out, ("fsdp", "seq"), scatter_dimension=1, tiled=True),
        lax.psum_scatter(grad_gate_bias, ("fsdp", "seq"), scatter_dimension=0, tiled=True),
        lax.psum_scatter(grad_head_gain, ("fsdp", "seq"), scatter_dimension=0, tiled=True),
        lax.psum_scatter(grad_w_output, ("fsdp", "seq"), scatter_dimension=0, tiled=True),
    )
    feedforward_grads = (
        lax.psum_scatter(grad_gain_two, ("fsdp", "seq"), scatter_dimension=0, tiled=True),
        lax.psum_scatter(grad_w_gate, ("fsdp", "seq"), scatter_dimension=0, tiled=True),
        lax.psum_scatter(grad_w_up, ("fsdp", "seq"), scatter_dimension=0, tiled=True),
        lax.psum_scatter(grad_w_down, ("fsdp", "seq"), scatter_dimension=0, tiled=True),
    )
    return (input_grad, attention_grads, feedforward_grads)


def shards(
    tokens,
    cotangent,
    doc_starts,
    gain_one,
    w_query,
    w_key,
    w_value,
    w_swish,
    w_rank_in,
    w_rank_out,
    gate_bias,
    head_gain,
    w_output,
    gain_two,
    w_gate,
    w_up,
    w_down,
):
    row_count = tokens.shape[0]
    first_row = lax.axis_index("seq") * row_count
    positions = first_row + jnp.arange(row_count, dtype=jnp.int32)
    starts = doc_starts[0]
    doc_ids = document_of(positions, starts)
    prev_ids = document_of(positions - 1, starts)
    entry_rows = (doc_ids == prev_ids[0]).astype(jnp.float32)
    device_keep = entry_rows[-1]
    context = (doc_ids, prev_ids, entry_rows, device_keep)
    attention_local = (
        gain_one,
        w_query,
        w_key,
        w_value,
        w_swish,
        w_rank_in,
        w_rank_out,
        gate_bias,
        head_gain,
        w_output,
    )
    feedforward_local = (gain_two, w_gate, w_up, w_down)
    inputs = tokens.astype(jnp.float32)
    attention = gather_attention(attention_local)
    feedforward = gather_feedforward(feedforward_local)
    kept_values = forward(inputs, attention, feedforward, context)
    output = kept_values[0].astype(jnp.bfloat16)
    attention = gather_attention(attention_local)
    feedforward = gather_feedforward(feedforward_local)
    kept_values = forward(inputs, attention, feedforward, context)
    upstream = cotangent.astype(jnp.float32)
    input_grad, attention_grads, feedforward_grads = backward(
        upstream, inputs, attention, feedforward, kept_values, context
    )
    return (
        output,
        input_grad,
        attention_grads[0],
        attention_grads[1],
        attention_grads[2],
        attention_grads[3],
        attention_grads[4],
        attention_grads[5],
        attention_grads[6],
        attention_grads[7],
        attention_grads[8],
        attention_grads[9],
        feedforward_grads[0],
        feedforward_grads[1],
        feedforward_grads[2],
        feedforward_grads[3],
    )


def solution(mesh):
    in_specs = (
        P(("fsdp", "seq"), None),
        P(("fsdp", "seq"), None),
        P("fsdp", None),
        P(("fsdp", "seq")),
        P(("fsdp", "seq"), None),
        P(("fsdp", "seq"), None),
        P(("fsdp", "seq"), None),
        P(("fsdp", "seq"), None),
        P(("fsdp", "seq"), None),
        P(None, ("fsdp", "seq")),
        P(("fsdp", "seq")),
        P(("fsdp", "seq")),
        P(("fsdp", "seq"), None),
        P(("fsdp", "seq")),
        P(("fsdp", "seq"), None),
        P(("fsdp", "seq"), None),
        P(("fsdp", "seq"), None),
    )
    out_specs = (
        P(("fsdp", "seq"), None),
        P(("fsdp", "seq"), None),
        P(("fsdp", "seq")),
        P(("fsdp", "seq"), None),
        P(("fsdp", "seq"), None),
        P(("fsdp", "seq"), None),
        P(("fsdp", "seq"), None),
        P(("fsdp", "seq"), None),
        P(None, ("fsdp", "seq")),
        P(("fsdp", "seq")),
        P(("fsdp", "seq")),
        P(("fsdp", "seq"), None),
        P(("fsdp", "seq")),
        P(("fsdp", "seq"), None),
        P(("fsdp", "seq"), None),
        P(("fsdp", "seq"), None),
    )
    return jax.shard_map(shards, mesh=mesh, in_specs=in_specs, out_specs=out_specs, check_vma=False)
```

profile of v0, /device:TPU:0, one launch (start us, length us, event | category | flops | bytes accessed | tf_op | source)
XLA Modules:
  0.0 2343.6 jit_solution(17753718223744197085)
XLA Ops:
  13.7 42.1 %all-reduce.10 = (bf16[1024]{0:T(1024)(128)(2,1)S(1)}, bf16[1024]{0:T(1024)(128)(2,1)S(1)}, bf16[256]{0:T(256)(128)(2,1)S(1)}, bf16[1024]{0:T(1024)(128)(2,1)S(1)}) all-reduce(bf16[1024]{0:T(1024)(128)(2,1)S(1)} %dynamic-update-slice, bf16[1024]{0:T(1024)(128)(2,1)S(1)} %dynamic-update-slice.1, ...), channel_id=1, replica_groups=mesh['fsdp'=4,'seq'=8] {'fsdp','seq'}, use_global_device_ids=true, to_apply=%add.1 | all-reduce | flops 3328 | bytes 13312
  55.9 41.1 %all-gather.2 = bf16[32,32,16]{1,2,0:T(8,128)(2,1)S(1)} all-gather(bf16[1,32,16]{1,2,0:T(8,128)(2,1)} %bitcast.571), channel_id=1, replica_groups=mesh['fsdp'=4,'seq'=8] {'fsdp','seq'}, dimensions={0}, use_global_device_ids=true | all-gather | bytes 33792 | tf_op jit(solution)/shard_map/all_gather | solution.py:184
  97.2 37.6 %all-gather.3 = bf16[32,32,16]{1,2,0:T(8,128)(2,1)S(1)} all-gather(bf16[1,32,16]{1,2,0:T(8,128)(2,1)} %bitcast.572), channel_id=1, replica_groups=mesh['fsdp'=4,'seq'=8] {'fsdp','seq'}, dimensions={0}, use_global_device_ids=true | all-gather | bytes 33792 | tf_op jit(solution)/shard_map/all_gather | solution.py:185
  145.2 3.8 fusion.128
  152.4 34.2 %all-gather.19.cloned.1.call-done = bf16[1024,1024]{1,0:T(8,128)(2,1)} async-done(((bf16[32,1024]{1,0:T(8,128)(2,1)}), bf16[1024,1024]{1,0:T(8,128)(2,1)}) %all-gather.19.cloned.1.call-update) | async-done | bytes 2097168 | tf_op jit(solution)/shard_map/all_gather | solution.py:180
  192.5 70.0 %while.116 = (s32[]{:T(128)}, f32[4,256,256]{2,1,0:T(8,128)S(1)}, f32[6,64,4,256]{3,1,0,2:T(8,128)}, s32[6,64]{1,0:T(8,128)S(1)}, s32[6]{0:T(128)S(1)}, /*index=...) while((s32[]{:T(128)}, f32[4,256,256]{2,1,0:T(8,128)S(1)}, ...), condition=%wide.region_5.6_spmd.clone, body=%wide.region_3.5_spmd.clone.sunk | while | flops 509048064 | bytes 7769278 | solution.py:150
  278.0 8.9 all_gather.85
  289.9 3.2 bitcast_multiply_fusion.9
  293.1 5.9 all-gather.31.cloned.1.call-done
  299.1 20.9 while.117
  319.9 6.8 multiply_reduce_fusion.5
  326.8 31.4 %all-gather.21.cloned.1.call-done = bf16[1024,1024]{1,0:T(8,128)(2,1)} async-done(((bf16[32,1024]{1,0:T(8,128)(2,1)}), bf16[1024,1024]{1,0:T(8,128)(2,1)}) %all-gather.21.cloned.1.call-update) | async-done | bytes 2097168 | tf_op jit(solution)/shard_map/all_gather | solution.py:183
  358.2 4.9 multiply_convert_fusion.3
  363.1 53.0 %all-gather.23.cloned.1.call-done = bf16[1024,1024]{1,0:T(8,128)(2,1)} async-done(((bf16[32,1024]{1,0:T(8,128)(2,1)}), bf16[1024,1024]{1,0:T(8,128)(2,1)}) %all-gather.23.cloned.1.call-update) | async-done | bytes 2097168 | tf_op jit(solution)/shard_map/all_gather | solution.py:188
  421.3 63.8 %all-gather.25.cloned.1.call-done = bf16[1024,2816]{1,0:T(8,128)(2,1)} async-done(((bf16[32,2816]{1,0:T(8,128)(2,1)}), bf16[1024,2816]{1,0:T(8,128)(2,1)}) %all-gather.25.cloned.1.call-update) | async-done | bytes 5767184 | tf_op jit(solution)/shard_map/all_gather | solution.py:195
  485.1 7.3 fusion.162
  492.5 61.8 %all-gather.27.cloned.1.call-done = bf16[1024,2816]{1,0:T(8,128)(2,1)} async-done(((bf16[32,2816]{1,0:T(8,128)(2,1)}), bf16[1024,2816]{1,0:T(8,128)(2,1)}) %all-gather.27.cloned.1.call-update) | async-done | bytes 5767184 | tf_op jit(solution)/shard_map/all_gather | solution.py:196
  554.2 7.3 fusion.163
  561.6 61.8 %all-gather.29.cloned.1.call-done = bf16[2816,1024]{1,0:T(8,128)(2,1)} async-done(((bf16[88,1024]{1,0:T(8,128)(2,1)}), bf16[2816,1024]{1,0:T(8,128)(2,1)}) %all-gather.29.cloned.1.call-update) | async-done | bytes 5767184 | tf_op jit(solution)/shard_map/all_gather | solution.py:197
  623.4 10.8 multiply_convert_fusion
  634.1 6.7 fusion.164
  651.9 3.6 fusion.130
  655.6 83.6 %while.119 = (s32[]{:T(128)}, f32[4,256,256]{2,1,0:T(8,128)S(1)}, f32[6,64,4,256]{3,2,1,0:T(4,128)}, f32[6,64,4,256]{3,2,1,0:T(4,128)}, f32[6,64,4,256]{3,2,1,0:...) while((s32[]{:T(128)}, f32[4,256,256]{2,1,0:T(8,128)S(1)}, ...), condition=%wide.region_19.20_spmd.clone, body=%wide.region_17.19_spmd.clone.sunk | while | flops 257653120 | bytes 9924694 | solution.py:150
  739.2 3.1 copy.244
  742.3 12.0 while.118
  759.0 126.1 %while.115 = (s32[]{:T(128)}, f32[4,256,256]{2,1,0:T(8,128)S(1)}, f32[6,64,4,256]{3,1,0,2:T(8,128)}, bf16[6,64,4,256]{3,1,2,0:T(8,128)(2,1)}, bf16[6,64,4,256]{3...) while((s32[]{:T(128)}, f32[4,256,256]{2,1,0:T(8,128)S(1)}, ...), condition=%wide.region_24.25_spmd, body=%wide.region_20.24_spmd.sunk | while | flops 1013335040 | bytes 28473944 | solution.py:150
  885.1 6.5 fusion.115
  891.6 14.2 fusion.95
  914.1 3.4 fusion.145
  919.2 3.3 fusion.135
  924.0 3.4 fusion.151
  930.2 3.4 fusion.149
  936.3 3.4 fusion.147
  940.8 7.6 fusion.169
  948.5 7.5 fusion.170
  957.2 7.5 fusion.171
  968.7 6.1 add_convert_fusion
  981.6 40.0 %all-reduce.9 = (f32[1024]{0:T(1024)S(1)}, f32[1024]{0:T(1024)S(1)}, f32[256]{0:T(256)S(1)}, f32[1024]{0:T(1024)S(1)}) all-reduce(f32[1024]{0:T(1024)S(1)} %get-tuple-element.1427, f32[1024]{0:T(1024)S(1)} %get-tuple-element.1575, f32[256]{0:T(256)S(1)} %get-tuple-element.1429, ...), channel_id=4, replica_groups=mesh['fsdp'=4,'seq'=8] {'fsdp','seq'}, use_global_device_ids=true, to_apply=%region_30.31.clone | all-reduce | flops 3328 | bytes 26624
  1027.0 18.7 reduce-scatter.33.cloned.1.call-done
  1047.0 130.8 %reduce-scatter.31.cloned.1.call-done = f32[32,16]{1,0:T(8,128)} async-done(((f32[1024,16]{1,0:T(8,128)}), f32[32,16]{1,0:T(8,128)}) %reduce-scatter.31.cloned.1.call-update) | async-done | bytes 2064
  1179.2 138.4 %reduce-scatter.21.cloned.1.call-done = f32[32,1024]{1,0:T(8,128)} async-done(((f32[1024,1024]{1,0:T(8,128)}), f32[32,1024]{1,0:T(8,128)}) %reduce-scatter.21.cloned.1.call-update) | async-done | bytes 131088 | tf_op jit(solution)/shard_map/reduce_scatter | solution.py:374
  1317.6 139.6 %reduce-scatter.23.cloned.1.call-done = f32[32,1024]{1,0:T(8,128)} async-done(((f32[1024,1024]{1,0:T(8,128)}), f32[32,1024]{1,0:T(8,128)}) %reduce-scatter.23.cloned.1.call-update) | async-done | bytes 131088 | tf_op jit(solution)/shard_map/reduce_scatter | solution.py:379
  1457.1 139.3 %reduce-scatter.15.cloned.1.call-done = f32[32,1024]{1,0:T(8,128)} async-done(((f32[1024,1024]{1,0:T(8,128)}), f32[32,1024]{1,0:T(8,128)}) %reduce-scatter.15.cloned.1.call-update) | async-done | bytes 131088 | tf_op jit(solution)/shard_map/reduce_scatter | solution.py:371
  1596.4 139.5 %reduce-scatter.17.cloned.1.call-done = f32[32,1024]{1,0:T(8,128)} async-done(((f32[1024,1024]{1,0:T(8,128)}), f32[32,1024]{1,0:T(8,128)}) %reduce-scatter.17.cloned.1.call-update) | async-done | bytes 131088 | tf_op jit(solution)/shard_map/reduce_scatter | solution.py:372
  1736.0 139.6 %reduce-scatter.19.cloned.1.call-done = f32[32,1024]{1,0:T(8,128)} async-done(((f32[1024,1024]{1,0:T(8,128)}), f32[32,1024]{1,0:T(8,128)}) %reduce-scatter.19.cloned.1.call-update) | async-done | bytes 131088 | tf_op jit(solution)/shard_map/reduce_scatter | solution.py:373
  1875.6 153.5 %reduce-scatter.25.cloned.1.call-done = f32[32,2816]{1,0:T(8,128)} async-done(((f32[1024,2816]{1,0:T(8,128)}), f32[32,2816]{1,0:T(8,128)}) %reduce-scatter.25.cloned.1.call-update) | async-done | bytes 360464 | tf_op jit(solution)/shard_map/reduce_scatter | solution.py:383
  2029.1 153.8 %reduce-scatter.27.cloned.1.call-done = f32[32,2816]{1,0:T(8,128)} async-done(((f32[1024,2816]{1,0:T(8,128)}), f32[32,2816]{1,0:T(8,128)}) %reduce-scatter.27.cloned.1.call-update) | async-done | bytes 360464 | tf_op jit(solution)/shard_map/reduce_scatter | solution.py:384
  2183.0 153.6 %reduce-scatter.29.cloned.1.call-done = f32[88,1024]{1,0:T(8,128)} async-done(((f32[2816,1024]{1,0:T(8,128)}), f32[88,1024]{1,0:T(8,128)}) %reduce-scatter.29.cloned.1.call-update) | async-done | bytes 360464 | tf_op jit(solution)/shard_map/reduce_scatter | solution.py:385
  (596 shorter events, 398.5 us)
Async XLA Ops:
  7.2 127.8 %copy-start = (bf16[384,1024]{1,0:T(8,128)(2,1)S(1)}, bf16[384,1024]{1,0:T(8,128)(2,1)}, u32[]{:S(2)}) copy-start(bf16[384,1024]{1,0:T(8,128)(2,1)} %param.27) | copy-start | bytes 2359300
  7.2 133.5 %all-gather.15.cloned.1.call-start = ((), (), s32[]{:S(2)}) async-start(), calls=%async_computation.10 | async-start | bytes 2162688 | tf_op jit(solution)/shard_map/all_gather | solution.py:181
  7.9 137.2 %all-gather.17.cloned.1.call-start = ((), (), s32[]{:S(2)}) async-start(), calls=%async_computation.11 | async-start | bytes 2162688 | tf_op jit(solution)/shard_map/all_gather | solution.py:182
  8.7 177.9 %all-gather.19.cloned.1.call-start = ((), (), s32[]{:S(2)}) async-start(), calls=%async_computation.12 | async-start | bytes 2162688 | tf_op jit(solution)/shard_map/all_gather | solution.py:180
  9.4 289.7 %all-gather.31.cloned.1.call-start = ((), (), s32[]{:S(2)}) async-start(), calls=%async_computation.26 | async-start | bytes 4718592 | tf_op jit(solution)/shard_map/all_gather | solution.py:19
  97.2 38.1 %copy-start.35 = (bf16[1024,16]{0,1:T(8,128)(2,1)}, bf16[1024,16]{0,1:T(8,128)(2,1)S(1)}, u32[]{:S(2)}) copy-start(bf16[1024,16]{0,1:T(8,128)(2,1)S(1)} %reshape.532) | copy-start | bytes 98308
  138.7 1.9 copy-start.17
  189.2 1.9 copy-start.12
  263.3 94.8 %all-gather.21.cloned.1.call-start = ((), (), s32[]{:S(2)}) async-start(), calls=%async_computation.13 | async-start | bytes 2162688 | tf_op jit(solution)/shard_map/all_gather | solution.py:183
  263.9 152.2 %all-gather.23.cloned.1.call-start = ((), (), s32[]{:S(2)}) async-start(), calls=%async_computation.14 | async-start | bytes 2162688 | tf_op jit(solution)/shard_map/all_gather | solution.py:188
  264.5 220.6 %all-gather.25.cloned.1.call-start = ((), (), s32[]{:S(2)}) async-start(), calls=%async_computation.15 | async-start | bytes 5947392 | tf_op jit(solution)/shard_map/all_gather | solution.py:195
  265.2 289.0 %all-gather.27.cloned.1.call-start = ((), (), s32[]{:S(2)}) async-start(), calls=%async_computation.16 | async-start | bytes 5947392 | tf_op jit(solution)/shard_map/all_gather | solution.py:196
  266.0 357.4 %all-gather.29.cloned.1.call-start = ((), (), s32[]{:S(2)}) async-start(), calls=%async_computation.17 | async-start | bytes 5947392 | tf_op jit(solution)/shard_map/all_gather | solution.py:197
  266.7 475.5 %all-gather.33.cloned.1.call-start = ((), (), s32[]{:S(2)}) async-start(), calls=%async_computation.27 | async-start | bytes 4718592 | tf_op jit(solution)/shard_map/all_gather | solution.py:42
  634.1 6.7 copy-start.33
  634.1 6.7 copy-start.32
  634.1 6.7 copy-start.10
  634.1 6.7 copy-start.39
  640.9 2.7 copy-start.19
  645.2 2.0 copy-start.6
  645.2 2.4 copy-start.7
  648.7 3.2 copy-start.8
  655.5 390.1 %reduce-scatter.33.cloned.1.call-start = ((), (), s32[]{:S(2)}) async-start(), calls=%async_computation.29 | async-start | bytes 540672
  742.3 12.0 copy-start.1
  764.5 3.4 copy-start.2
  785.5 3.4 copy-start.2
  806.4 3.4 copy-start.2
  827.4 3.4 copy-start.2
  848.4 3.4 copy-start.2
  869.3 3.4 copy-start.2
  912.6 265.2 %reduce-scatter.31.cloned.1.call-start = ((), (), s32[]{:S(2)}) async-start(), calls=%async_computation.28 | async-start | bytes 540672
  914.1 403.5 %reduce-scatter.21.cloned.1.call-start = ((), (), s32[]{:S(2)}) async-start(), calls=%async_computation.21 | async-start | bytes 4325376 | tf_op jit(solution)/shard_map/reduce_scatter | solution.py:374
  917.5 1.6 copy-start.13
  917.6 539.6 %reduce-scatter.23.cloned.1.call-start = ((), (), s32[]{:S(2)}) async-start(), calls=%async_computation.22 | async-start | bytes 4325376 | tf_op jit(solution)/shard_map/reduce_scatter | solution.py:379
  922.4 674.0 %reduce-scatter.15.cloned.1.call-start = ((), (), s32[]{:S(2)}) async-start(), calls=%async_computation.18 | async-start | bytes 4325376 | tf_op jit(solution)/shard_map/reduce_scatter | solution.py:371
  924.0 3.4 copy-start.21
  927.4 808.6 %reduce-scatter.17.cloned.1.call-start = ((), (), s32[]{:S(2)}) async-start(), calls=%async_computation.19 | async-start | bytes 4325376 | tf_op jit(solution)/shard_map/reduce_scatter | solution.py:372
  933.6 942.0 %reduce-scatter.19.cloned.1.call-start = ((), (), s32[]{:S(2)}) async-start(), calls=%async_computation.20 | async-start | bytes 4325376 | tf_op jit(solution)/shard_map/reduce_scatter | solution.py:373
  939.7 1089.4 %reduce-scatter.25.cloned.1.call-start = ((), (), s32[]{:S(2)}) async-start(), calls=%async_computation.23 | async-start | bytes 11894784 | tf_op jit(solution)/shard_map/reduce_scatter | solution.py:383
  948.5 1234.5 %reduce-scatter.27.cloned.1.call-start = ((), (), s32[]{:S(2)}) async-start(), calls=%async_computation.24 | async-start | bytes 11894784 | tf_op jit(solution)/shard_map/reduce_scatter | solution.py:384
  956.1 1380.5 %reduce-scatter.29.cloned.1.call-start = ((), (), s32[]{:S(2)}) async-start(), calls=%async_computation.25 | async-start | bytes 11894784 | tf_op jit(solution)/shard_map/reduce_scatter | solution.py:385
  965.9 2.8 copy-start.11
  965.9 2.8 copy-start.31
  968.7 6.2 copy-start.26
  968.7 6.1 copy-start.41
  974.8 1.8 copy-start.42
  976.7 1.8 copy-start.40
  979.5 44.4 %copy-start.38 = (f32[384]{0:T(512)S(1)}, f32[384]{0:T(512)}, u32[]{:S(2)}) copy-start(f32[384]{0:T(512)} %copy-done.37) | copy-start | bytes 4612
  (20 other events, 23.8 us)
Sparse Core Ops, SparseCore 0:
  10.9 59.1 all-gather.14
  72.9 55.6 all-gather.16
  131.4 55.1 all-gather.18
  263.4 35.5 all-gather.30
  301.8 56.3 all-gather.20
  360.9 55.2 all-gather.22
  419.0 66.1 all-gather.24
  488.0 66.2 all-gather.26
  557.1 66.2 all-gather.28
  655.7 35.7 all-gather.32
  912.8 132.8 reduce-scatter.32
  1047.8 129.9 reduce-scatter.30
  1180.7 136.8 reduce-scatter.20
  1320.3 136.8 reduce-scatter.22
  1459.8 136.5 reduce-scatter.14
  1599.1 136.7 reduce-scatter.16
  1738.7 136.8 reduce-scatter.18
  1878.3 150.7 reduce-scatter.24
  2032.0 150.9 reduce-scatter.26
  2185.7 150.7 reduce-scatter.28
where the time goes:
time: 2350 us; the launch traced here: 2340 us
  waiting for transfers between devices  1620 us (69%)
  matrix products  255 us (11%)
  blocking collectives  170 us (7%)
  other arithmetic  155 us (7%)
  local copies, waits for them, and re-layouts  106 us (5%)
    unnamed x22, waiting for transfers between devices  155 us
    reduce_scatter x1, waiting for transfers between devices, backward(): lax.psum_scatter(grad_w_up, ('fsdp', 'seq'), scatter_dimension=0, tiled=T...  154 us
    reduce_scatter x1, waiting for transfers between devices, backward(): lax.psum_scatter(grad_w_down, ('fsdp', 'seq'), scatter_dimension=0, tiled...  154 us
    reduce_scatter x1, waiting for transfers between devices, backward(): lax.psum_scatter(grad_w_gate, ('fsdp', 'seq'), scatter_dimension=0, tiled...  154 us
    reduce_scatter x1, waiting for transfers between devices, backward(): lax.psum_scatter(grad_w_value, ('fsdp', 'seq'), scatter_dimension=0, tile...  140 us
    reduce_scatter x1, waiting for transfers between devices, backward(): lax.psum_scatter(grad_w_output, ('fsdp', 'seq'), scatter_dimension=0, til...  140 us
    reduce_scatter x1, waiting for transfers between devices, backward(): lax.psum_scatter(grad_w_key, ('fsdp', 'seq'), scatter_dimension=0, tiled=...  140 us
    reduce_scatter x1, waiting for transfers between devices, backward(): lax.psum_scatter(grad_w_query, ('fsdp', 'seq'), scatter_dimension=0, tile...  139 us
  transfers between devices with their start and end apart: 20, of which 17 were waited for; matrix products, arithmetic and copies ran while one was open for 10% of the time, Pallas kernels for 0%

commit v1 on v0

--- a/solution.py
+++ b/solution.py
@@ -3,11 +3,242 @@
 import jax
 import jax.numpy as jnp
 from jax import lax
+from jax.experimental import pallas as pl
+from jax.experimental.pallas import tpu as pltpu
+from jax.sharding import Mesh
 from jax.sharding import PartitionSpec as P
 
 HEAD_K = 256
 HEAD_V = 256
 GROUP = 64
+AXES = ("z", "y", "x", "c")
+VMEM = 56 * 1024 * 1024
+F32 = jnp.float32
+BF16 = jnp.bfloat16
+
+
+def shift(value, axis, step):
+    size = lax.axis_size(axis)
+    return lax.ppermute(value, axis, [(i, (i + step) % size) for i in range(size)])
+
+
+def flip(value, axis):
+    return shift(value, axis, 1)
+
+
+def place():
+    return tuple(lax.axis_index(a) for a in AXES)
+
+
+def spread(shard):
+    depth, height = lax.axis_size("z"), lax.axis_size("y")
+    half = depth // 2
+    own = jnp.stack([shard] + [shift(shard, "z", k) for k in range(1, depth)])
+    across = flip(own, "x")
+    pieces = [(own, 0, 0, 0, depth), (across, 0, 1, 0, depth)]
+    for j in range(1, height):
+        along = shift(own, "y", j)
+        pieces.append((along, j, 0, 0, depth))
+        pieces.append((shift(across[:half], "y", j), j, 1, 0, half))
+        pieces.append((flip(along[half:], "x"), j, 1, half, depth))
+    return pieces
+
+
+def gathered(shard):
+    pieces = spread(shard)
+    return [(a, j, i, 0, f, l) for a, j, i, f, l in pieces] + [
+        (flip(a, "c"), j, i, 1, f, l) for a, j, i, f, l in pieces
+    ]
+
+
+def sources(pieces):
+    z, y, x, c = place()
+    depth, height = lax.axis_size("z"), lax.axis_size("y")
+    chips, cores = [], []
+    for _, j, i, other, first, last in pieces:
+        for k in range(first, last):
+            chip = (((z - k) % depth) * height + (y - j) % height) * 2 + (x + i) % 2
+            chips.append(chip)
+            cores.append((c + other) % 2)
+    return jnp.stack(chips + cores).astype(jnp.int32)
+
+
+def assemble(shard, parts):
+    pieces = gathered(shard)
+    where = sources(pieces)
+    arrays = [p[0] for p in pieces]
+    blocks = [(n, k) for n, p in enumerate(pieces) for k in range(p[5] - p[4])]
+    total = len(blocks)
+
+    if any(rows % 16 for _, rows, _, _ in parts):
+        chips, cores = where[:total], where[total:]
+        back = jnp.zeros((total,), jnp.int32).at[chips * 2 + cores].set(jnp.arange(total, dtype=jnp.int32))
+        ordered = jnp.take(jnp.concatenate(arrays), back, axis=0)
+        whole = []
+        for first, rows, by_columns, shape in parts:
+            part = lax.optimization_barrier(ordered[:, first : first + rows])
+            if by_columns:
+                part = part.reshape(total // 2, 2, rows, -1).transpose(0, 2, 1, 3)
+            whole.append(lax.optimization_barrier(part.reshape(shape)))
+        return whole
+
+    def body(where_ref, *refs):
+        ins, outs, sems = refs[: len(arrays)], refs[len(arrays) : -1], refs[-1]
+        for at, (n, k) in enumerate(blocks):
+            chip, core = where_ref[at], where_ref[total + at]
+            for w, (first, rows, by_columns, shape) in enumerate(parts):
+                source = ins[n].at[k, pl.ds(first, rows), :]
+                if by_columns:
+                    width = shape[1] // 2
+                    goal = outs[w].at[
+                        pl.ds(pl.multiple_of(chip * rows, rows), rows),
+                        pl.ds(pl.multiple_of(core * width, width), width),
+                    ]
+                else:
+                    device = chip * 2 + core
+                    goal = outs[w].at[pl.ds(pl.multiple_of(device * rows, rows), rows), :]
+                pltpu.make_async_copy(source, goal, sems.at[w]).start()
+        for w in range(len(parts)):
+            pltpu.make_async_copy(outs[w], outs[w], sems.at[w]).wait()
+
+    hbm = pl.BlockSpec(memory_space=pl.ANY)
+    return pl.pallas_call(
+        body,
+        grid_spec=pltpu.PrefetchScalarGridSpec(
+            num_scalar_prefetch=1,
+            grid=(1,),
+            in_specs=[hbm] * len(arrays),
+            out_specs=[pl.BlockSpec(p[3], lambda n, s: (0, 0)) for p in parts],
+            scratch_shapes=[pltpu.SemaphoreType.DMA((len(parts),))],
+        ),
+        out_shape=[jax.ShapeDtypeStruct(p[3], shard.dtype) for p in parts],
+        compiler_params=pltpu.CompilerParams(vmem_limit_bytes=VMEM),
+    )(where, *arrays)
+
+
+def routes():
+    depth, height = lax.axis_size("z"), lax.axis_size("y")
+    half = depth // 2
+    order = []
+    for j in range(1, height):
+        order += [(j, 1, 0, half), (j, 1, half, depth)]
+    for j in range(1, height):
+        order.append((j, 0, 0, depth))
+    return order + [(0, 1, 0, depth), (0, 0, 0, depth)]
+
+
+def targets():
+    z, y, x, _ = place()
+    depth, height = lax.axis_size("z"), lax.axis_size("y")
+    chips = []
+    for j, i, first, last in routes():
+        for k in range(first, last):
+            chips.append((((z + k) % depth) * height + (y + j) % height) * 2 + (x + i) % 2)
+    return jnp.stack(chips).astype(jnp.int32)
+
+
+def collect(blocks):
+    depth, height = lax.axis_size("z"), lax.axis_size("y")
+    half = depth // 2
+    held = dict(zip(routes(), blocks))
+
+    def wide(a):
+        return a.astype(F32)
+
+    by_x = [flip(held[j, 1, 0, half], "x") for j in range(1, height)]
+    by_y = [shift(held[j, 1, half, depth], "y", j) for j in range(1, height)]
+    straight = held[0, 0, 0, depth]
+    across = held[0, 1, 0, depth]
+    across_late = wide(across[half:])
+    for a in by_y:
+        across_late = across_late + wide(a)
+    across = jnp.concatenate([across[:half], across_late.astype(BF16)])
+    arrived = [flip(across, "x")]
+    for j in range(1, height):
+        along = held[j, 0, 0, depth]
+        early = (wide(along[:half]) + wide(by_x[j - 1])).astype(BF16)
+        arrived.append(shift(jnp.concatenate([early, along[half:]]), "y", j))
+    sums = []
+    for k in range(depth):
+        total = wide(straight[k])
+        for a in arrived:
+            total = total + wide(a[k])
+        sums.append(total)
+    result = sums[0]
+    for k in range(1, depth):
+        result = result + wide(shift(sums[k].astype(BF16), "z", k))
+    return result
+
+
+def weight_grads(left, right, tile, halves=False):
+    order = routes()
+    _, _, _, c = place()
+    chips = targets()
+    count = chips.shape[0]
+    tokens, height = left[0].shape
+    width = right[0].shape[1] // (2 if halves else 1)
+    rows = height // (count if halves else 2 * count)
+    starts = chips * rows if halves else (chips * 2 + c) * rows
+
+    if rows % 16:
+        full = jnp.concatenate(left)
+        product = matmul_t(full, jnp.concatenate(right)).astype(BF16)
+        if halves:
+            product = lax.dynamic_slice_in_dim(product, c * width, width, 1).reshape(count, rows, width)
+        else:
+            product = lax.dynamic_index_in_dim(product.reshape(count, 2, rows, width), c, 1, False)
+        product = jnp.take(product, chips, axis=0)
+        blocks, at = [], 0
+        for _, _, first, last in order:
+            blocks.append(product[at : at + last - first])
+            at += last - first
+        return blocks
+
+    first_tile = c * (width // tile) if halves else jnp.int32(0)
+    numbers = jnp.concatenate([starts, first_tile[None]]).astype(jnp.int32)
+
+    def body(numbers_ref, lo_ref, ls_ref, ro_ref, rs_ref, *refs):
+        outs, (turned, chosen) = refs[:-2], refs[-2:]
+
+        @pl.when(pl.program_id(0) == 0)
+        def _():
+            turned[:, :tokens] = lo_ref[...].T
+            turned[:, tokens:] = ls_ref[...].T
+            for at in range(count):
+                start = pl.multiple_of(numbers_ref[at], 16)
+                chosen[at * rows : (at + 1) * rows, :] = turned[pl.ds(start, rows), :]
+
+        both = jnp.concatenate([ro_ref[...], rs_ref[...]], axis=0)
+        product = jnp.dot(chosen[...], both, preferred_element_type=F32).astype(BF16)
+        at = 0
+        for out, (_, _, first, last) in zip(outs, order):
+            span = (last - first) * rows
+            out[...] = product[at : at + span].reshape(last - first, rows, tile)
+            at += span
+
+    whole = pl.BlockSpec((tokens, height), lambda n, s: (0, 0))
+    strip = pl.BlockSpec((tokens, tile), lambda n, s: (0, n + s[count]))
+    outs = [(last - first, rows, width) for _, _, first, last in order]
+    return pl.pallas_call(
+        body,
+        grid_spec=pltpu.PrefetchScalarGridSpec(
+            num_scalar_prefetch=1,
+            grid=(width // tile,),
+            in_specs=[whole, whole, strip, strip],
+            out_specs=[pl.BlockSpec((n, rows, tile), lambda n, s: (0, 0, n)) for n, _, _ in outs],
+            scratch_shapes=[
+                pltpu.VMEM((height, 2 * tokens), BF16),
+                pltpu.VMEM((count * rows, 2 * tokens), BF16),
+            ],
+        ),
+        out_shape=[jax.ShapeDtypeStruct(o, BF16) for o in outs],
+        compiler_params=pltpu.CompilerParams(vmem_limit_bytes=VMEM),
+        cost_estimate=pl.CostEstimate(
+            flops=4 * tokens * count * rows * width,
+            bytes_accessed=2 * (count * rows * width + 2 * tokens * (height + width)),
+            transcendentals=0,
+        ),
+    )(numbers, left[0], left[1], right[0], right[1])
 
 
 MAXIMUM_ACCURACY = lax.Precision.HIGHEST
@@ -171,30 +402,6 @@
         rescaled_rows * jnp.exp(running_total),
         incoming_state,
         precision=MAXIMUM_ACCURACY,
-    )
-
-
-def gather_attention(pieces):
-    return (
-        lax.all_gather(pieces[0], ("fsdp", "seq"), axis=0, tiled=True),
-        lax.all_gather(pieces[1], ("fsdp", "seq"), axis=0, tiled=True),
-        lax.all_gather(pieces[2], ("fsdp", "seq"), axis=0, tiled=True),
-        lax.all_gather(pieces[3], ("fsdp", "seq"), axis=0, tiled=True),
-        lax.all_gather(pieces[4], ("fsdp", "seq"), axis=0, tiled=True),
-        lax.all_gather(pieces[5], ("fsdp", "seq"), axis=0, tiled=True),
-        lax.all_gather(pieces[6], ("fsdp", "seq"), axis=1, tiled=True),
-        lax.all_gather(pieces[7], ("fsdp", "seq"), axis=0, tiled=True),
-        lax.all_gather(pieces[8], ("fsdp", "seq"), axis=0, tiled=True),
-        lax.all_gather(pieces[9], ("fsdp", "seq"), axis=0, tiled=True),
-    )
-
-
-def gather_feedforward(pieces):
-    return (
-        lax.all_gather(pieces[0], ("fsdp", "seq"), axis=0, tiled=True),
-        lax.all_gather(pieces[1], ("fsdp", "seq"), axis=0, tiled=True),
-        lax.all_gather(pieces[2], ("fsdp", "seq"), axis=0, tiled=True),
-        lax.all_gather(pieces[3], ("fsdp", "seq"), axis=0, tiled=True),
     )
 
 
@@ -233,7 +440,7 @@
     )
     identity = (jnp.ones_like(transfer_scale), jnp.zeros_like(final_state))
     prefix_scale, incoming_state = prefix(
-        (transfer_scale, final_state), "seq", combine_states, identity
+        (transfer_scale, final_state), ("y", "x", "c"), combine_states, identity
     )
     mixed_heads = mixed_zero + incoming(query_heads, decays, incoming_state, entry_rows)
     gated_rows = head_gate(mixed_heads, head_gain.astype(jnp.float32), swish_pre).astype(
@@ -301,20 +508,16 @@
         inner_rows,
     ) = kept_values
     down_grad = upstream.astype(jnp.bfloat16)
-    grad_w_down = matmul_t(inner_rows, down_grad)
     grad_inner = matmul_nt(down_grad, w_down)
     _, pull_mlp = jax.vjp(swiglu, gate_proj, up_proj)
     grad_gate, grad_up = pull_mlp(grad_inner)
     grad_gate = grad_gate.astype(jnp.bfloat16)
     grad_up = grad_up.astype(jnp.bfloat16)
-    grad_w_gate = matmul_t(normed_two, grad_gate)
-    grad_w_up = matmul_t(normed_two, grad_up)
     grad_normed_two = matmul_nt(grad_gate, w_gate) + matmul_nt(grad_up, w_up)
     _, pull_second = jax.vjp(norm_model, hidden_state, gain_two.astype(jnp.float32))
     hidden_extra, grad_gain_two = pull_second(grad_normed_two)
     grad_hidden = upstream + hidden_extra
     branch_grad = grad_hidden.astype(jnp.bfloat16)
-    grad_w_output = matmul_t(gated_rows, branch_grad)
     grad_gated = matmul_nt(branch_grad, w_output)
     _, pull_head = jax.vjp(head_gate, mixed_heads, head_gain.astype(jnp.float32), swish_pre)
     grad_mixed, grad_head_gain, grad_swish = pull_head(grad_gated)
@@ -328,7 +531,7 @@
     grad_q_enter, grad_decay_enter, grad_entry = pull_enter(grad_mixed)
     identity = (jnp.ones_like(transfer_scale), jnp.zeros_like(grad_entry))
     suffix_scale, exit_grad = entering_2(
-        (transfer_scale, grad_entry), "seq", combine_states, identity
+        (transfer_scale, grad_entry), ("y", "x", "c"), combine_states, identity
     )
     grad_scale = jnp.sum(exit_grad * incoming_state, axis=2)
     _, pull_local = jax.vjp(
@@ -344,18 +547,12 @@
     (grad_gate_pre,) = pull_decay(grad_decay_local + grad_decay_enter)
     gate_grad_low = grad_gate_pre.astype(jnp.bfloat16)
     grad_gate_bias = jnp.sum(gate_grad_low.astype(jnp.float32), axis=0)
-    grad_w_rank_out = matmul_t(low_rank, gate_grad_low)
     grad_low_rank = matmul_nt(gate_grad_low, w_rank_out).astype(jnp.bfloat16)
-    grad_w_rank_in = matmul_t(normed, grad_low_rank)
     row_count = normed.shape[0]
     swish_grad_low = grad_swish.astype(jnp.bfloat16)
     query_grad_low = (grad_q_local + grad_q_enter).reshape(row_count, -1).astype(jnp.bfloat16)
     key_grad_low = grad_key.reshape(row_count, -1).astype(jnp.bfloat16)
     value_grad_low = grad_value.reshape(row_count, -1).astype(jnp.bfloat16)
-    grad_w_swish = matmul_t(normed, swish_grad_low)
-    grad_w_query = matmul_t(normed, query_grad_low)
-    grad_w_key = matmul_t(normed, key_grad_low)
-    grad_w_value = matmul_t(normed, value_grad_low)
     grad_normed = (
         matmul_nt(query_grad_low, w_query)
         + matmul_nt(key_grad_low, w_key)
@@ -366,48 +563,93 @@
     _, pull_first = jax.vjp(norm_model, inputs, gain_one.astype(jnp.float32))
     input_extra, grad_gain_one = pull_first(grad_normed)
     input_grad = grad_hidden + input_extra
-    attention_grads = (
-        lax.psum_scatter(grad_gain_one, ("fsdp", "seq"), scatter_dimension=0, tiled=True),
-        lax.psum_scatter(grad_w_query, ("fsdp", "seq"), scatter_dimension=0, tiled=True),
-        lax.psum_scatter(grad_w_key, ("fsdp", "seq"), scatter_dimension=0, tiled=True),
-        lax.psum_scatter(grad_w_value, ("fsdp", "seq"), scatter_dimension=0, tiled=True),
-        lax.psum_scatter(grad_w_swish, ("fsdp", "seq"), scatter_dimension=0, tiled=True),
-        lax.psum_scatter(grad_w_rank_in, ("fsdp", "seq"), scatter_dimension=0, tiled=True),
-        lax.psum_scatter(grad_w_rank_out, ("fsdp", "seq"), scatter_dimension=1, tiled=True),
-        lax.psum_scatter(grad_gate_bias, ("fsdp", "seq"), scatter_dimension=0, tiled=True),
-        lax.psum_scatter(grad_head_gain, ("fsdp", "seq"), scatter_dimension=0, tiled=True),
-        lax.psum_scatter(grad_w_output, ("fsdp", "seq"), scatter_dimension=0, tiled=True),
-    )
-    feedforward_grads = (
-        lax.psum_scatter(grad_gain_two, ("fsdp", "seq"), scatter_dimension=0, tiled=True),
-        lax.psum_scatter(grad_w_gate, ("fsdp", "seq"), scatter_dimension=0, tiled=True),
-        lax.psum_scatter(grad_w_up, ("fsdp", "seq"), scatter_dimension=0, tiled=True),
-        lax.psum_scatter(grad_w_down, ("fsdp", "seq"), scatter_dimension=0, tiled=True),
-    )
-    return (input_grad, attention_grads, feedforward_grads)
-
-
-def shards(
-    tokens,
-    cotangent,
-    doc_starts,
-    gain_one,
-    w_query,
-    w_key,
-    w_value,
-    w_swish,
-    w_rank_in,
-    w_rank_out,
-    gate_bias,
-    head_gain,
-    w_output,
-    gain_two,
-    w_gate,
-    w_up,
-    w_down,
+    return (
+        input_grad,
+        (grad_gain_one, grad_gate_bias, grad_head_gain, grad_gain_two),
+        (gate_grad_low, low_rank, grad_low_rank, normed),
+        jnp.concatenate([query_grad_low, key_grad_low, value_grad_low], axis=1),
+        (gated_rows, branch_grad, swish_grad_low),
+        (normed_two, jnp.concatenate([grad_gate, grad_up], axis=1)),
+        (inner_rows, down_grad),
+    )
+
+
+def pair(value):
+    return (value, flip(value, "c"))
+
+
+def gather_weights(
+    gain_one, w_query, w_key, w_value, w_swish, w_rank_in, w_rank_out, gate_bias, head_gain, w_output, gain_two,
+    w_gate, w_up, w_down,
 ):
+    c = lax.axis_index("c")
+    rows, wide = w_query.shape
+    rank = w_rank_in.shape[1]
+    devices = wide // rows
+    piece = jnp.zeros((rank, wide), BF16)
+    piece = piece.at[:, :rows].set(w_rank_out)
+    piece = piece.at[:, rows : 2 * rows].set(w_rank_in.T)
+    piece = piece.at[0, 2 * rows : 3 * rows].set(gain_one)
+    piece = piece.at[1, 2 * rows : 3 * rows].set(gate_bias)
+    piece = piece.at[2, 2 * rows : 3 * rows].set(gain_two)
+    piece = piece.at[3, 2 * rows : 2 * rows + head_gain.shape[0]].set(head_gain)
+    square = (wide, wide)
+    query, key, value, small = assemble(
+        jnp.concatenate([w_query, w_key, w_value, piece]),
+        [(n * rows, rows, False, square) for n in range(3)] + [(3 * rows, rank, False, (devices * rank, wide))],
+    )
+    swish, output = assemble(
+        jnp.concatenate([w_swish, w_output]), [(n * rows, rows, False, square) for n in range(2)]
+    )
+    ff = w_gate.shape[1]
+    gate, up = assemble(
+        jnp.concatenate([w_gate, w_up]), [(n * rows, rows, False, (wide, ff)) for n in range(2)]
+    )
+    half = wide // 2
+    keep = lax.dynamic_slice_in_dim(w_down, c * half, half, 1)
+    other = flip(lax.dynamic_slice_in_dim(w_down, (1 - c) * half, half, 1), "c")
+    both = jnp.where(c == 0, jnp.concatenate([keep, other]), jnp.concatenate([other, keep]))
+    (down,) = assemble(both, [(0, both.shape[0], True, (ff, wide))])
+    small = small.reshape(devices, rank, wide)
+    rank_out = small[:, :, :rows].transpose(1, 0, 2).reshape(rank, wide)
+    rank_in = small[:, :, rows : 2 * rows].transpose(0, 2, 1).reshape(wide, rank)
+    vectors = small[:, :4, 2 * rows : 3 * rows]
+    attention = (
+        vectors[:, 0].reshape(-1), query, key, value, swish, rank_in, rank_out, vectors[:, 1].reshape(-1),
+        vectors[:, 3, : head_gain.shape[0]].reshape(-1), output,
+    )
+    return attention, (vectors[:, 2].reshape(-1), gate, up, down)
+
+
+def small_grads(vectors, factors):
+    gain_one, gate_bias, head_gain, gain_two = vectors
+    gate_grad, low_rank, low_grad, normed = factors
+    c = lax.axis_index("c")
+    wide = gain_one.shape[0]
+    devices = lax.axis_size("z") * lax.axis_size("y") * 4
+    rows = wide // devices
+    heads = jnp.zeros((devices, rows), F32).at[:, : head_gain.shape[0] // devices].set(head_gain.reshape(devices, -1))
+    table = jnp.concatenate(
+        [matmul_t(normed, low_grad), matmul_t(gate_grad, low_rank)]
+        + [v.reshape(wide, 1) for v in (gain_one, gate_bias, gain_two, heads)],
+        axis=1,
+    )
+    table = jnp.pad(table, ((0, 0), (0, 128 - table.shape[1])))
+    table = table.reshape(devices // 2, 2, rows, 128)
+    mine = lax.dynamic_index_in_dim(table, c, 1, False)
+    theirs = flip(lax.dynamic_index_in_dim(table, 1 - c, 1, False), "c")
+    table = jnp.take((mine + theirs).astype(BF16), targets(), axis=0)
+    blocks, at = [], 0
+    for _, _, first, last in routes():
+        blocks.append(table[at : at + last - first])
+        at += last - first
+    return blocks
+
+
+def shards(tokens, cotangent, doc_starts, *weights):
     row_count = tokens.shape[0]
-    first_row = lax.axis_index("seq") * row_count
+    z, y, x, c = place()
+    first_row = ((y * 2 + x) * 2 + c) * row_count
     positions = first_row + jnp.arange(row_count, dtype=jnp.int32)
     starts = doc_starts[0]
     doc_ids = document_of(positions, starts)
@@ -415,87 +657,53 @@
     entry_rows = (doc_ids == prev_ids[0]).astype(jnp.float32)
     device_keep = entry_rows[-1]
     context = (doc_ids, prev_ids, entry_rows, device_keep)
-    attention_local = (
-        gain_one,
-        w_query,
-        w_key,
-        w_value,
-        w_swish,
-        w_rank_in,
-        w_rank_out,
-        gate_bias,
-        head_gain,
-        w_output,
-    )
-    feedforward_local = (gain_two, w_gate, w_up, w_down)
     inputs = tokens.astype(jnp.float32)
-    attention = gather_attention(attention_local)
-    feedforward = gather_feedforward(feedforward_local)
+    attention, feedforward = gather_weights(*weights)
     kept_values = forward(inputs, attention, feedforward, context)
     output = kept_values[0].astype(jnp.bfloat16)
-    attention = gather_attention(attention_local)
-    feedforward = gather_feedforward(feedforward_local)
-    kept_values = forward(inputs, attention, feedforward, context)
     upstream = cotangent.astype(jnp.float32)
-    input_grad, attention_grads, feedforward_grads = backward(
+    input_grad, vectors, factors, qkv_grad, middle, first, second = backward(
         upstream, inputs, attention, feedforward, kept_values, context
     )
+    gates = collect(weight_grads(pair(first[0]), pair(first[1]), 512))
+    down = collect(weight_grads(pair(second[0]), pair(second[1]), 256, True))
+    gated_rows, branch_grad, swish_grad = middle
+    normed = pair(factors[3])
+    grad_output = collect(weight_grads(pair(gated_rows), pair(branch_grad), 512))
+    grad_swish = collect(weight_grads(normed, pair(swish_grad), 512))
+    qkv = collect(weight_grads(normed, pair(qkv_grad), 512))
+    small = collect(small_grads(vectors, factors))
+    rows, wide = weights[1].shape
+    ff = weights[11].shape[1]
+    own_rows = weights[13].shape[0]
+    keep = lax.dynamic_slice_in_dim(down, c * own_rows, own_rows, 0)
+    other = flip(lax.dynamic_slice_in_dim(down, (1 - c) * own_rows, own_rows, 0), "c")
+    down = jnp.where(c == 0, jnp.concatenate([keep, other], 1), jnp.concatenate([other, keep], 1))
+    rank = weights[5].shape[1]
     return (
         output,
         input_grad,
-        attention_grads[0],
-        attention_grads[1],
-        attention_grads[2],
-        attention_grads[3],
-        attention_grads[4],
-        attention_grads[5],
-        attention_grads[6],
-        attention_grads[7],
-        attention_grads[8],
-        attention_grads[9],
-        feedforward_grads[0],
-        feedforward_grads[1],
-        feedforward_grads[2],
-        feedforward_grads[3],
+        small[:, 2 * rank],
+        qkv[:, :wide],
+        qkv[:, wide : 2 * wide],
+        qkv[:, 2 * wide :],
+        grad_swish,
+        small[:, :rank],
+        small[:, rank : 2 * rank].T,
+        small[:, 2 * rank + 1],
+        small[: weights[8].shape[0], 2 * rank + 3],
+        grad_output,
+        small[:, 2 * rank + 2],
+        gates[:, :ff],
+        gates[:, ff:],
+        down,
     )
 
 
 def solution(mesh):
-    in_specs = (
-        P(("fsdp", "seq"), None),
-        P(("fsdp", "seq"), None),
-        P("fsdp", None),
-        P(("fsdp", "seq")),
-        P(("fsdp", "seq"), None),
-        P(("fsdp", "seq"), None),
-        P(("fsdp", "seq"), None),
-        P(("fsdp", "seq"), None),
-        P(("fsdp", "seq"), None),
-        P(None, ("fsdp", "seq")),
-        P(("fsdp", "seq")),
-        P(("fsdp", "seq")),
-        P(("fsdp", "seq"), None),
-        P(("fsdp", "seq")),
-        P(("fsdp", "seq"), None),
-        P(("fsdp", "seq"), None),
-        P(("fsdp", "seq"), None),
-    )
-    out_specs = (
-        P(("fsdp", "seq"), None),
-        P(("fsdp", "seq"), None),
-        P(("fsdp", "seq")),
-        P(("fsdp", "seq"), None),
-        P(("fsdp", "seq"), None),
-        P(("fsdp", "seq"), None),
-        P(("fsdp", "seq"), None),
-        P(("fsdp", "seq"), None),
-        P(None, ("fsdp", "seq")),
-        P(("fsdp", "seq")),
-        P(("fsdp", "seq")),
-        P(("fsdp", "seq"), None),
-        P(("fsdp", "seq")),
-        P(("fsdp", "seq"), None),
-        P(("fsdp", "seq"), None),
-        P(("fsdp", "seq"), None),
-    )
-    return jax.shard_map(shards, mesh=mesh, in_specs=in_specs, out_specs=out_specs, check_vma=False)
+    fsdp, seq = mesh.shape["fsdp"], mesh.shape["seq"]
+    inner = Mesh(mesh.devices.reshape(fsdp, seq // 4, 2, 2), AXES)
+    rows, vector, columns = P(AXES, None), P(AXES), P(None, AXES)
+    in_specs = (rows, rows, P("z", None), vector, rows, rows, rows, rows, rows, columns, vector, vector, rows, vector) + (rows,) * 3
+    out_specs = (rows, rows, vector) + (rows,) * 5 + (columns, vector, vector, rows, vector) + (rows,) * 3
+    return jax.shard_map(shards, mesh=inner, in_specs=in_specs, out_specs=out_specs, check_vma=False)

time: 2350 us -> 997 us (0.42)
  waiting for transfers between devices: 1620 us -> 208 us
  blocking collectives: 170 us -> 8.94 us
  starting transfers between devices: 1.67 us -> 99.2 us
  Pallas kernels: 0 us -> 66.1 us
  local copies, waits for them, and re-layouts: 106 us -> 163 us
  matrix products: 255 us -> 206 us
  other arithmetic: 155 us -> 199 us
    reduce_scatter x8 -> x0, waiting for transfers between devices: 1160 us -> none  [the longest x1 154 us: backward(): lax.psum_scatter(grad_w_up, ('fsdp', 'seq'), scatter_dimension=0, tiled=T...]
    all_gather x8 -> x0, waiting for transfers between devices: 306 us -> none  [the longest x1 63.8 us: gather_feedforward(): lax.all_gather(pieces[1], ('fsdp', 'seq'), axis=0, tiled=True)]
    ppermute x0 -> x102, waiting for transfers between devices: none -> 208 us  [shift(): lax.ppermute(value, axis, [(i, (i + step) % size) for i in range(size)])]
    unnamed x22 -> x2, waiting for transfers between devices: 155 us -> 0.03 us
    ppermute x0 -> x102, starting transfers between devices: none -> 99.1 us  [shift(): lax.ppermute(value, axis, [(i, (i + step) % size) for i in range(size)])]
    unnamed x2 -> x0, blocking collectives: 82.1 us -> none
    all_gather x2 -> x0, blocking collectives: 78.7 us -> none  [the longest x1 41.1 us: gather_attention(): lax.all_gather(pieces[5], ('fsdp', 'seq'), axis=0, tiled=True)]
    pallas_call x0 -> x9, Pallas kernels: none -> 66.1 us  [the longest x5 39 us: weight_grads(): pl.pallas_call(body, grid_spec=pltpu.PrefetchScalarGridSpec(num_scalar_pr...]
  transfers between devices with their start and end apart: 20 -> 104, of which waited for: 17 -> 32; matrix products, arithmetic and copies ran while one was open for 10% -> 56% of each run, Pallas kernels for 0% -> 7%
where the time goes in v1:
time: 997 us; the launch traced here: 985 us
  waiting for transfers between devices  208 us (21%)
  matrix products  206 us (21%)
  other arithmetic  199 us (20%)
  local copies, waits for them, and re-layouts  163 us (16%)
  starting transfers between devices  99.2 us (10%)
  Pallas kernels  66.1 us (7%)
  loops' own time  18.5 us (2%)
  between operations  16.2 us (2%)
    ppermute x102, waiting for transfers between devices, shift(): lax.ppermute(value, axis, [(i, (i + step) % size) for i in range(size)])  208 us
    ppermute x102, starting transfers between devices, shift(): lax.ppermute(value, axis, [(i, (i + step) % size) for i in range(size)])  99.1 us
    dot_general x24, matrix products, group_step(): jnp.einsum('yaq,yap->aqp', key_finish, value_matrix, precision=MAXIMUM_AC...  44.4 us
    dot_general x10, matrix products, matmul(): return jnp.dot(left, right, preferred_element_type=jnp.float32)  43.2 us
    dynamic_slice x48, local copies, waits for them, and re-layouts, local_mixer(): lax.scan(group_step, start_state, (split_blocks(rescaled_rows), split_blo...  41 us
    dynamic_update_slice x30, other arithmetic, local_mixer(): lax.scan(group_step, start_state, (split_blocks(rescaled_rows), split_blo...  39.5 us
    pallas_call x5, Pallas kernels, weight_grads(): pl.pallas_call(body, grid_spec=pltpu.PrefetchScalarGridSpec(num_scalar_pr...  39 us
    dot_general x18, matrix products, group_step(): jnp.einsum('hts,shv->thv', scores, value_matrix, precision=MAXIMUM_ACCURACY)  32.1 us
  transfers between devices with their start and end apart: 104, of which 32 were waited for; matrix products, arithmetic and copies ran while one was open for 56% of the time, Pallas kernels for 7%

profile of v1, /device:TPU:0, one launch (start us, length us, event | category | flops | bytes accessed | tf_op | source)
XLA Modules:
  0.0 984.8 jit_solution(17058492415685060474)
XLA Ops:
  41.2 8.0 collective-permute-done.1
  49.3 9.5 collective-permute-start.24
  62.0 18.2 %collective-permute-done.38 = bf16[176,512]{1,0:T(8,128)(2,1)S(1)} collective-permute-done((bf16[176,512]{1,0:T(8,128)(2,1)S(1)}, bf16[176,512]{1,0:T(8,128)(2,1)S(1)}, u32[]{:S(2)}, u32[]{:S(2)}) %collective-permute-start.38) | collective-permute-done | bytes 180256 | tf_op jit(solution)/shard_map/ppermute | solution.py:22
  81.6 11.0 %collective-permute-done.25 = bf16[64,2816]{1,0:T(8,128)(2,1)} collective-permute-done((bf16[64,2816]{1,0:T(8,128)(2,1)S(1)}, bf16[64,2816]{1,0:T(8,128)(2,1)}, u32[]{:S(2)}, u32[]{:S(2)}) %collective-permute-start.25) | collective-permute-done | bytes 360480 | tf_op jit(solution)/shard_map/ppermute | solution.py:22
  94.1 5.5 collective-permute-done.26
  106.6 36.5 %collective-permute-done.17.refs_3_ = bf16[2,64,1024]{2,1,0:T(8,128)(2,1)} collective-permute-done((bf16[2,64,1024]{2,1,0:T(8,128)(2,1)S(1)}, bf16[2,64,1024]{2,1,0:T(8,128)(2,1)}, u32[]{:S(2)}, u32[]{:S(2)}) %collective-permute-start.17) | collective-permute-done | bytes 262176 | tf_op jit(solution)/shard_map/ppermute | solution.py:22
  162.5 3.4 collective-permute-done.42.refs_3_
  169.3 6.4 collective-permute-done.5.refs_3_
  183.8 4.9 shard_map.289
  188.7 6.1 shard_map.291
  194.8 12.6 %collective-permute-done.27.refs_1_ = bf16[4,64,2816]{2,1,0:T(8,128)(2,1)} collective-permute-done((bf16[4,64,2816]{2,1,0:T(8,128)(2,1)}, bf16[4,64,2816]{2,1,0:T(8,128)(2,1)}, u32[]{:S(2)}, u32[]{:S(2)}) %collective-permute-start.27) | collective-permute-done | bytes 1441824 | tf_op jit(solution)/shard_map/ppermute | solution.py:22
  208.0 7.2 convolution_bitcast_fusion.4
  221.9 6.9 shard_map.288
  236.9 3.3 convert_multiply_fusion.4
  243.2 4.0 fusion.128
  259.2 3.5 fusion.177
  266.8 83.1 %while.113 = (s32[]{:T(128)}, f32[4,256,256]{2,1,0:T(8,128)S(1)}, f32[6,64,4,256]{3,1,0,2:T(8,128)}, s32[6,64]{1,0:T(8,128)S(1)}, s32[6]{0:T(128)S(1)}, /*index=...) while((s32[]{:T(128)}, f32[4,256,256]{2,1,0:T(8,128)S(1)}, ...), condition=%wide.region_8.9_spmd.clone, body=%wide.region_6.8_spmd.clone.sunk | while | flops 509048064 | bytes 8819022 | solution.py:381
  350.9 100.4 %while.116 = (s32[]{:T(128)}, f32[4,256,256]{2,1,0:T(8,128)S(1)}, f32[6,64,4,256]{3,2,1,0:T(4,128)}, f32[6,64,4,256]{3,2,1,0:T(4,128)}, f32[6,64,4,256]{3,2,1,0:...) while((s32[]{:T(128)}, f32[4,256,256]{2,1,0:T(8,128)S(1)}, ...), condition=%wide.region_22.23_spmd.clone, body=%wide.region_20.22_spmd.clone.sunk | while | flops 257653120 | bytes 9926426 | solution.py:381
  460.9 8.9 all_gather.18
  473.9 9.2 shard_map.290
  483.1 12.2 %while.114 = (s32[]{:T(128)}, f32[4,256,256]{2,1,0:T(8,128)S(1)}, s32[]{:T(128)}, bf16[8,4,256]{2,1,0:T(4,128)(2,1)S(1)}, bf16[8,4,256,256]{3,2,1,0:T(8,128)(2,1)}, /*index=5*/s32[]{:T(128)}, s32[]{:T(128)}) while((s32[]{:T(128)}, f32[4,256,256]{2,1,0:T(8,128)S(1)}, s32[]{:T(128)}, bf16[8,4,256]{2,1,0:T(4,128)(2,1)S(1)}, ...), condition=%wide.region_11.12_spmd.clone, body=%wide.region_10.11_spmd.clone.sunk | while | flops 1311748 | bytes 2631785 | solution.py:267
  495.3 5.5 multiply_reduce_fusion.5
  500.9 4.5 multiply_convert_fusion.3
  511.0 6.0 fusion.184
  517.1 7.2 fusion.93
  543.3 7.1 add_convert_fusion
  550.7 3.8 fusion.130
  557.6 4.7 shard_map.294
  567.3 4.7 shard_map.293
  576.2 3.5 collective-permute-done.67
  580.5 13.4 %collective-permute-done.77 = bf16[4,32,1024]{2,1,0:T(8,128)(2,1)S(1)} collective-permute-done((bf16[4,32,1024]{2,1,0:T(8,128)(2,1)S(1)}, bf16[4,32,1024]{2,1,0:T(8,128)(2,1)S(1)}, u32[]{:S(2)}, u32[]{:S(2)}) %collective-permute-start.77) | collective-permute-done | bytes 262176 | tf_op jit(solution)/shard_map/ppermute | solution.py:22
  594.0 6.5 collective-permute-done.79
  603.3 8.0 shard_map.296
  615.5 13.1 %shard_map.295 = (bf16[2,32,5632]{2,1,0:T(8,128)(2,1)}, bf16[2,32,5632]{2,1,0:T(8,128)(2,1)}, bf16[4,32,5632]{2,1,0:T(8,128)(2,1)}, bf16[4,32,5632]{2,1,0:T(8,128)(2,1)}, bf16[4,32,5632]{2,1,0:T(8,128)(2,1)}) custom-call(s32[17]{0:T(128)} %pad_add_fusion.numbers_ref, bf16[384,1024]{1,0:T(8,128)(2,1)} %copy-done.40, ...), custom_call_target="tpu_custom_call" | custom-call | flops 4429185024 | bytes 15990784 | tf_op jit(solution)/shard_map/pallas_call | solution.py:222
  632.5 10.9 %collective-permute-done.85 = bf16[2,32,5632]{2,1,0:T(8,128)(2,1)S(1)} collective-permute-done((bf16[2,32,5632]{2,1,0:T(8,128)(2,1)}, bf16[2,32,5632]{2,1,0:T(8,128)(2,1)S(1)}, u32[]{:S(2)}, u32[]{:S(2)}) %collective-permute-start.85) | collective-permute-done | bytes 720928 | tf_op jit(solution)/shard_map/ppermute | solution.py:22
  644.9 14.9 %collective-permute-done.87 = bf16[2,32,5632]{2,1,0:T(8,128)(2,1)S(1)} collective-permute-done((bf16[2,32,5632]{2,1,0:T(8,128)(2,1)S(1)}, bf16[2,32,5632]{2,1,0:T(8,128)(2,1)S(1)}, u32[]{:S(2)}, u32[]{:S(2)}) %collective-permute-start.87) | collective-permute-done | bytes 720928 | tf_op jit(solution)/shard_map/ppermute | solution.py:22
  665.6 13.3 %collective-permute-done.97 = bf16[4,176,512]{2,1,0:T(8,128)(2,1)S(1)} collective-permute-done((bf16[4,176,512]{2,1,0:T(8,128)(2,1)S(1)}, bf16[4,176,512]{2,1,0:T(8,128)(2,1)S(1)}, u32[]{:S(2)}, u32[]{:S(2)}) %collective-permute-start.97) | collective-permute-done | bytes 720928 | tf_op jit(solution)/shard_map/ppermute | solution.py:22
  686.6 4.9 collective-permute-done.100
  702.0 4.1 collective-permute-done.88
  711.4 12.3 %while.115 = (s32[]{:T(128)}, f32[4,256,256]{2,1,0:T(8,128)S(1)}, s32[]{:T(128)}, bf16[8,4,256]{2,1,0:T(4,128)(2,1)S(1)}, bf16[8,4,256,256]{3,2,1,0:T(8,128)(2,1...) while((s32[]{:T(128)}, f32[4,256,256]{2,1,0:T(8,128)S(1)}, s32[]{:T(128)}, ...), condition=%wide.region_19.20_spmd.clone, body=%wide.region_18.19_spmd.clone.sunk | while | flops 1311752 | bytes 2631847 | solution.py:291
  728.6 137.6 %while.112 = (s32[]{:T(128)}, f32[4,256,256]{2,1,0:T(8,128)S(1)}, f32[6,64,4,256]{3,1,0,2:T(8,128)}, bf16[6,64,4,256]{3,1,2,0:T(8,128)(2,1)}, bf16[6,64,4,256]{3...) while((s32[]{:T(128)}, f32[4,256,256]{2,1,0:T(8,128)S(1)}, ...), condition=%wide.region_27.28_spmd, body=%wide.region_23.27_spmd.sunk | while | flops 1013335040 | bytes 28473936 | solution.py:381
  866.2 6.5 fusion.120
  872.7 14.2 %fusion.95 = f32[256,4,3,128]{0,2,1,3:T(4,128)S(1)} fusion(f32[256,4,3,128]{0,3,2,1:T(8,128)S(1)} %bitcast.716), kind=kOutput, calls=%fused_computation.188 | output fusion | flops 49938432 | bytes 3145728 | tf_op jit(solution)/shard_map/reduce-window.2
  918.7 8.4 shard_map.292
  939.3 7.6 collective-permute-done.61
  951.9 8.3 collective-permute-done.60
  967.6 3.8 collective-permute-done.63
  971.4 4.2 collective-permute-done.64
  (983 shorter events, 595.5 us)
Async XLA Ops:
  7.2 475.9 %all-gather.5.cloned.1.call-start = ((), (), s32[]{:S(2)}) async-start(), calls=%async_computation | async-start | bytes 4718592 | tf_op jit(solution)/shard_map/all_gather | solution.py:250
  9.0 24.4 %collective-permute-start.12 = (bf16[64,1024]{1,0:T(8,128)(2,1)S(1)}, bf16[64,1024]{1,0:T(8,128)(2,1)S(1)}, u32[]{:S(2)}, u32[]{:S(2)}) collective-permute-start(bf16[64,1024]{1,0:T(8,128)(2,1)S(1)} %constant_dynamic-update-slice_fusion.4), channel_id=1, source_target_pairs={{0,8},{8,16},{16,24},{24,0},{1,9},{9,17},{17,25},{25,1},{2,10},{10... | collective-permute-start | bytes 393224 | tf_op jit(solution)/shard_map/ppermute | solution.py:22
  12.0 24.3 %collective-permute-start.13 = (bf16[64,1024]{1,0:T(8,128)(2,1)S(1)}, bf16[64,1024]{1,0:T(8,128)(2,1)S(1)}, u32[]{:S(2)}, u32[]{:S(2)}) collective-permute-start(bf16[64,1024]{1,0:T(8,128)(2,1)S(1)} %constant_dynamic-update-slice_fusion.4), channel_id=1, source_target_pairs={{0,16},{8,24},{16,0},{24,8},{1,17},{9,25},{17,1},{25,9},{2,18},{10... | collective-permute-start | bytes 393224 | tf_op jit(solution)/shard_map/ppermute | solution.py:22
  14.6 22.3 %collective-permute-start.14 = (bf16[64,1024]{1,0:T(8,128)(2,1)S(1)}, bf16[64,1024]{1,0:T(8,128)(2,1)S(1)}, u32[]{:S(2)}, u32[]{:S(2)}) collective-permute-start(bf16[64,1024]{1,0:T(8,128)(2,1)S(1)} %constant_dynamic-update-slice_fusion.4), channel_id=1, source_target_pairs={{0,24},{8,0},{16,8},{24,16},{1,25},{9,1},{17,9},{25,17},{2,26},{10... | collective-permute-start | bytes 393224 | tf_op jit(solution)/shard_map/ppermute | solution.py:22
  33.4 25.5 %collective-permute-start.2 = (bf16[112,1024]{1,0:T(8,128)(2,1)S(1)}, bf16[112,1024]{1,0:T(8,128)(2,1)S(1)}, u32[]{:S(2)}, u32[]{:S(2)}) collective-permute-start(bf16[112,1024]{1,0:T(8,128)(2,1)S(1)} %get-tuple-element.1824), channel_id=1, source_target_pairs={{0,24},{8,0},{16,8},{24,16},{1,25},{9,1},{17,9},{25,17},{2,26},{10... | collective-permute-start | bytes 688136 | tf_op jit(solution)/shard_map/ppermute | solution.py:22
  36.2 24.2 %collective-permute-start.37 = (bf16[176,512]{1,0:T(8,128)(2,1)S(1)}, bf16[176,512]{1,0:T(8,128)(2,1)S(1)}, u32[]{:S(2)}, u32[]{:S(2)}) collective-permute-start(bf16[176,512]{1,0:T(8,128)(2,1)S(1)} %maximum_select_fusion.2), channel_id=1, source_target_pairs={{0,8},{8,16},{16,24},{24,0},{1,9},{9,17},{17,25},{25,1},{2,10},{10... | collective-permute-start | bytes 540680 | tf_op jit(solution)/shard_map/ppermute | solution.py:22
  36.9 43.3 %collective-permute-start.38 = (bf16[176,512]{1,0:T(8,128)(2,1)S(1)}, bf16[176,512]{1,0:T(8,128)(2,1)S(1)}, u32[]{:S(2)}, u32[]{:S(2)}) collective-permute-start(bf16[176,512]{1,0:T(8,128)(2,1)S(1)} %maximum_select_fusion.2), channel_id=1, source_target_pairs={{0,16},{8,24},{16,0},{24,8},{1,17},{9,25},{17,1},{25,9},{2,18},{10... | collective-permute-start | bytes 540680 | tf_op jit(solution)/shard_map/ppermute | solution.py:22
  39.4 40.8 %collective-permute-start.39 = (bf16[176,512]{1,0:T(8,128)(2,1)S(1)}, bf16[176,512]{1,0:T(8,128)(2,1)S(1)}, u32[]{:S(2)}, u32[]{:S(2)}) collective-permute-start(bf16[176,512]{1,0:T(8,128)(2,1)S(1)} %maximum_select_fusion.2), channel_id=1, source_target_pairs={{0,24},{8,0},{16,8},{24,16},{1,25},{9,1},{17,9},{25,17},{2,26},{10... | collective-permute-start | bytes 540680 | tf_op jit(solution)/shard_map/ppermute | solution.py:22
  49.3 31.5 %collective-permute-start.24 = (bf16[64,2816]{1,0:T(8,128)(2,1)S(1)}, bf16[64,2816]{1,0:T(8,128)(2,1)S(1)}, u32[]{:S(2)}, u32[]{:S(2)}) collective-permute-start(bf16[64,2816]{1,0:T(8,128)(2,1)S(1)} %constant_dynamic-update-slice_fusion.6), channel_id=1, source_target_pairs={{0,8},{8,16},{16,24},{24,0},{1,9},{9,17},{17,25},{25,1},{2,10},{10... | collective-permute-start | bytes 1081352 | tf_op jit(solution)/shard_map/ppermute | solution.py:22
  58.9 43.2 %collective-permute-start.15 = (bf16[4,64,1024]{2,1,0:T(8,128)(2,1)S(1)}, bf16[4,64,1024]{2,1,0:T(8,128)(2,1)S(1)}, u32[]{:S(2)}, u32[]{:S(2)}) collective-permute-start(bf16[4,64,1024]{2,1,0:T(8,128)(2,1)S(1)} %pad_maximum_fusion.10.refs_0_), channel_id=1, source_target_pairs={{0,2},{2,0},{1,3},{3,1},{4,6},{6,4},{5,7},{7,5},{8,10},{10,8},{9,1... | collective-permute-start | bytes 1572872 | tf_op jit(solution)/shard_map/ppermute | solution.py:22
  60.4 43.3 %collective-permute-start.16 = (bf16[4,64,1024]{2,1,0:T(8,128)(2,1)S(1)}, bf16[4,64,1024]{2,1,0:T(8,128)(2,1)}, u32[]{:S(2)}, u32[]{:S(2)}) collective-permute-start(bf16[4,64,1024]{2,1,0:T(8,128)(2,1)S(1)} %pad_maximum_fusion.10.refs_0_), channel_id=1, source_target_pairs={{0,4},{4,0},{1,5},{5,1},{2,6},{6,2},{3,7},{7,3},{8,12},{12,8},{9,1... | collective-permute-start | bytes 1572872 | tf_op jit(solution)/shard_map/ppermute | solution.py:22
  80.8 23.4 %collective-permute-start.19 = (bf16[4,64,1024]{2,1,0:T(8,128)(2,1)S(1)}, bf16[4,64,1024]{2,1,0:T(8,128)(2,1)S(1)}, u32[]{:S(2)}, u32[]{:S(2)}) collective-permute-start(bf16[4,64,1024]{2,1,0:T(8,128)(2,1)S(1)} %pad_maximum_fusion.10.refs_0_), channel_id=1, source_target_pairs={{0,1},{1,0},{2,3},{3,2},{4,5},{5,4},{6,7},{7,6},{8,9},{9,8},{10,11... | collective-permute-start | bytes 1572872 | tf_op jit(solution)/shard_map/ppermute | solution.py:22
  92.6 50.5 %collective-permute-start.40 = (bf16[4,176,512]{2,1,0:T(8,128)(2,1)S(1)}, bf16[4,176,512]{2,1,0:T(8,128)(2,1)S(1)}, u32[]{:S(2)}, u32[]{:S(2)}) collective-permute-start(bf16[4,176,512]{2,1,0:T(8,128)(2,1)S(1)} %pad_maximum_fusion.7.refs_0_), channel_id=1, source_target_pairs={{0,2},{2,0},{1,3},{3,1},{4,6},{6,4},{5,7},{7,5},{8,10},{10,8},{9,1... | collective-permute-start | bytes 2162696 | tf_op jit(solution)/shard_map/ppermute | solution.py:22
  99.5 44.2 %collective-permute-start.41 = (bf16[4,176,512]{2,1,0:T(8,128)(2,1)S(1)}, bf16[4,176,512]{2,1,0:T(8,128)(2,1)S(1)}, u32[]{:S(2)}, u32[]{:S(2)}) collective-permute-start(bf16[4,176,512]{2,1,0:T(8,128)(2,1)S(1)} %pad_maximum_fusion.7.refs_0_), channel_id=1, source_target_pairs={{0,4},{4,0},{1,5},{5,1},{2,6},{6,2},{3,7},{7,3},{8,12},{12,8},{9,1... | collective-permute-start | bytes 2162696 | tf_op jit(solution)/shard_map/ppermute | solution.py:22
  102.1 43.5 %collective-permute-start.3 = (bf16[4,112,1024]{2,1,0:T(8,128)(2,1)}, bf16[4,112,1024]{2,1,0:T(8,128)(2,1)}, u32[]{:S(2)}, u32[]{:S(2)}) collective-permute-start(bf16[4,112,1024]{2,1,0:T(8,128)(2,1)} %pad_maximum_fusion.4.refs_0_), channel_id=1, source_target_pairs={{0,2},{2,0},{1,3},{3,1},{4,6},{6,4},{5,7},{7,5},{8,10},{10,8},{9,1... | collective-permute-start | bytes 2752520 | tf_op jit(solution)/shard_map/ppermute | solution.py:22
  103.7 43.5 %collective-permute-start.4 = (bf16[4,112,1024]{2,1,0:T(8,128)(2,1)}, bf16[4,112,1024]{2,1,0:T(8,128)(2,1)}, u32[]{:S(2)}, u32[]{:S(2)}) collective-permute-start(bf16[4,112,1024]{2,1,0:T(8,128)(2,1)} %pad_maximum_fusion.4.refs_0_), channel_id=1, source_target_pairs={{0,4},{4,0},{1,5},{5,1},{2,6},{6,2},{3,7},{7,3},{8,12},{12,8},{9,1... | collective-permute-start | bytes 2752520 | tf_op jit(solution)/shard_map/ppermute | solution.py:22
  105.0 38.0 %collective-permute-start.17 = (bf16[2,64,1024]{2,1,0:T(8,128)(2,1)S(1)}, bf16[2,64,1024]{2,1,0:T(8,128)(2,1)}, u32[]{:S(2)}, u32[]{:S(2)}) collective-permute-start(bf16[2,64,1024]{2,1,0:T(8,128)(2,1)S(1)} %slice.704), channel_id=1, source_target_pairs={{0,4},{4,0},{1,5},{5,1},{2,6},{6,2},{3,7},{7,3},{8,12},{12,8},{9,1... | collective-permute-start | bytes 786440 | tf_op jit(solution)/shard_map/ppermute | solution.py:22
  161.0 46.4 %collective-permute-start.27 = (bf16[4,64,2816]{2,1,0:T(8,128)(2,1)}, bf16[4,64,2816]{2,1,0:T(8,128)(2,1)}, u32[]{:S(2)}, u32[]{:S(2)}) collective-permute-start(bf16[4,64,2816]{2,1,0:T(8,128)(2,1)} %pad_maximum_fusion.1.refs_0_), channel_id=1, source_target_pairs={{0,2},{2,0},{1,3},{3,1},{4,6},{6,4},{5,7},{7,5},{8,10},{10,8},{9,1... | collective-permute-start | bytes 4325384 | tf_op jit(solution)/shard_map/ppermute | solution.py:22
  165.9 41.6 %collective-permute-start.28 = (bf16[4,64,2816]{2,1,0:T(8,128)(2,1)}, bf16[4,64,2816]{2,1,0:T(8,128)(2,1)}, u32[]{:S(2)}, u32[]{:S(2)}) collective-permute-start(bf16[4,64,2816]{2,1,0:T(8,128)(2,1)} %pad_maximum_fusion.1.refs_0_), channel_id=1, source_target_pairs={{0,4},{4,0},{1,5},{5,1},{2,6},{6,2},{3,7},{7,3},{8,12},{12,8},{9,1... | collective-permute-start | bytes 4325384 | tf_op jit(solution)/shard_map/ppermute | solution.py:22
  180.1 39.2 %collective-permute-start.7 = (bf16[4,112,1024]{2,1,0:T(8,128)(2,1)}, bf16[4,112,1024]{2,1,0:T(8,128)(2,1)}, u32[]{:S(2)}, u32[]{:S(2)}) collective-permute-start(bf16[4,112,1024]{2,1,0:T(8,128)(2,1)} %pad_maximum_fusion.4.refs_0_), channel_id=1, source_target_pairs={{0,1},{1,0},{2,3},{3,2},{4,5},{5,4},{6,7},{7,6},{8,9},{9,8},{10,11... | collective-permute-start | bytes 2752520 | tf_op jit(solution)/shard_map/ppermute | solution.py:22
  180.2 41.1 %collective-permute-start.8 = (bf16[4,112,1024]{2,1,0:T(8,128)(2,1)}, bf16[4,112,1024]{2,1,0:T(8,128)(2,1)}, u32[]{:S(2)}, u32[]{:S(2)}) collective-permute-start(bf16[4,112,1024]{2,1,0:T(8,128)(2,1)} %collective-permute-done.3.refs_1_), channel_id=1, source_target_pairs={{0,1},{1,0},{2,3},{3,2},{4,5},{5,4},{6,7},{7,6},{8,9},{9,8},{10,11... | collective-permute-start | bytes 2752520 | tf_op jit(solution)/shard_map/ppermute | solution.py:22
  181.5 39.9 %collective-permute-start.9 = (bf16[4,112,1024]{2,1,0:T(8,128)(2,1)}, bf16[4,112,1024]{2,1,0:T(8,128)(2,1)}, u32[]{:S(2)}, u32[]{:S(2)}) collective-permute-start(bf16[4,112,1024]{2,1,0:T(8,128)(2,1)} %collective-permute-done.4.refs_2_), channel_id=1, source_target_pairs={{0,1},{1,0},{2,3},{3,2},{4,5},{5,4},{6,7},{7,6},{8,9},{9,8},{10,11... | collective-permute-start | bytes 2752520 | tf_op jit(solution)/shard_map/ppermute | solution.py:22
  219.2 253.4 %collective-permute-start.31 = (bf16[4,64,2816]{2,1,0:T(8,128)(2,1)}, bf16[4,64,2816]{2,1,0:T(8,128)(2,1)}, u32[]{:S(2)}, u32[]{:S(2)}) collective-permute-start(bf16[4,64,2816]{2,1,0:T(8,128)(2,1)} %pad_maximum_fusion.1.refs_0_), channel_id=1, source_target_pairs={{0,1},{1,0},{2,3},{3,2},{4,5},{5,4},{6,7},{7,6},{8,9},{9,8},{10,11... | collective-permute-start | bytes 4325384 | tf_op jit(solution)/shard_map/ppermute | solution.py:22
  219.3 237.1 %collective-permute-start.29 = (bf16[2,64,2816]{2,1,0:T(8,128)(2,1)}, bf16[2,64,2816]{2,1,0:T(8,128)(2,1)}, u32[]{:S(2)}, u32[]{:S(2)}) collective-permute-start(bf16[2,64,2816]{2,1,0:T(8,128)(2,1)} %slice.707), channel_id=1, source_target_pairs={{0,4},{4,0},{1,5},{5,1},{2,6},{6,2},{3,7},{7,3},{8,12},{12,8},{9,1... | collective-permute-start | bytes 2162696 | tf_op jit(solution)/shard_map/ppermute | solution.py:22
  219.8 236.7 %collective-permute-start.30 = (bf16[2,64,2816]{2,1,0:T(8,128)(2,1)}, bf16[2,64,2816]{2,1,0:T(8,128)(2,1)}, u32[]{:S(2)}, u32[]{:S(2)}) collective-permute-start(bf16[2,64,2816]{2,1,0:T(8,128)(2,1)} %slice.708), channel_id=1, source_target_pairs={{0,2},{2,0},{1,3},{3,1},{4,6},{6,4},{5,7},{7,5},{8,10},{10,8},{9,1... | collective-permute-start | bytes 2162696 | tf_op jit(solution)/shard_map/ppermute | solution.py:22
  221.3 251.7 %collective-permute-start.32 = (bf16[4,64,2816]{2,1,0:T(8,128)(2,1)}, bf16[4,64,2816]{2,1,0:T(8,128)(2,1)}, u32[]{:S(2)}, u32[]{:S(2)}) collective-permute-start(bf16[4,64,2816]{2,1,0:T(8,128)(2,1)} %collective-permute-done.27.refs_1_), channel_id=1, source_target_pairs={{0,1},{1,0},{2,3},{3,2},{4,5},{5,4},{6,7},{7,6},{8,9},{9,8},{10,11... | collective-permute-start | bytes 4325384 | tf_op jit(solution)/shard_map/ppermute | solution.py:22
  221.3 251.7 %collective-permute-start.33 = (bf16[4,64,2816]{2,1,0:T(8,128)(2,1)}, bf16[4,64,2816]{2,1,0:T(8,128)(2,1)}, u32[]{:S(2)}, u32[]{:S(2)}) collective-permute-start(bf16[4,64,2816]{2,1,0:T(8,128)(2,1)} %collective-permute-done.28.refs_2_), channel_id=1, source_target_pairs={{0,1},{1,0},{2,3},{3,2},{4,5},{5,4},{6,7},{7,6},{8,9},{9,8},{10,11... | collective-permute-start | bytes 4325384 | tf_op jit(solution)/shard_map/ppermute | solution.py:22
  350.9 360.6 %all-gather.7.cloned.1.call-start = ((), (), s32[]{:S(2)}) async-start(), calls=%async_computation.1 | async-start | bytes 4718592 | tf_op jit(solution)/shard_map/all_gather | solution.py:273
  472.7 92.9 %collective-permute-start.57 = (bf16[384,1024]{1,0:T(8,128)(2,1)}, bf16[384,1024]{1,0:T(8,128)(2,1)}, u32[]{:S(2)}, u32[]{:S(2)}) collective-permute-start(bf16[384,1024]{1,0:T(8,128)(2,1)} %fusion.101.lo_ref), channel_id=1, source_target_pairs={{0,1},{1,0},{2,3},{3,2},{4,5},{5,4},{6,7},{7,6},{8,9},{9,8},{10,11... | collective-permute-start | bytes 2359304 | tf_op jit(solution)/shard_map/ppermute | solution.py:22
  536.6 77.7 %collective-permute-start.84 = (bf16[384,5632]{1,0:T(8,128)(2,1)}, bf16[384,5632]{1,0:T(8,128)(2,1)}, u32[]{:S(2)}, u32[]{:S(2)}) collective-permute-start(bf16[384,5632]{1,0:T(8,128)(2,1)} %pad_maximum_fusion.ro_ref), channel_id=1, source_target_pairs={{0,1},{1,0},{2,3},{3,2},{4,5},{5,4},{6,7},{7,6},{8,9},{9,8},{10,11... | collective-permute-start | bytes 12976136 | tf_op jit(solution)/shard_map/ppermute | solution.py:22
  536.8 20.8 %collective-permute-start.74 = (bf16[384,1024]{1,0:T(8,128)(2,1)}, bf16[384,1024]{1,0:T(8,128)(2,1)}, u32[]{:S(2)}, u32[]{:S(2)}) collective-permute-start(bf16[384,1024]{1,0:T(8,128)(2,1)} %copy.311.lo_ref), channel_id=1, source_target_pairs={{0,1},{1,0},{2,3},{3,2},{4,5},{5,4},{6,7},{7,6},{8,9},{9,8},{10,11... | collective-permute-start | bytes 2359304 | tf_op jit(solution)/shard_map/ppermute | solution.py:22
  543.1 22.6 %collective-permute-start.66 = (bf16[384,1024]{1,0:T(8,128)(2,1)}, bf16[384,1024]{1,0:T(8,128)(2,1)}, u32[]{:S(2)}, u32[]{:S(2)}) collective-permute-start(bf16[384,1024]{1,0:T(8,128)(2,1)} %copy.312.ro_ref), channel_id=1, source_target_pairs={{0,1},{1,0},{2,3},{3,2},{4,5},{5,4},{6,7},{7,6},{8,9},{9,8},{10,11... | collective-permute-start | bytes 2359304 | tf_op jit(solution)/shard_map/ppermute | solution.py:22
  550.4 52.9 %collective-permute-start.92 = (bf16[384,2816]{1,0:T(8,128)(2,1)}, bf16[384,2816]{1,0:T(8,128)(2,1)}, u32[]{:S(2)}, u32[]{:S(2)}) collective-permute-start(bf16[384,2816]{1,0:T(8,128)(2,1)} %get-tuple-element.1794.lo_ref), channel_id=1, source_target_pairs={{0,1},{1,0},{2,3},{3,2},{4,5},{5,4},{6,7},{7,6},{8,9},{9,8},{10,11... | collective-permute-start | bytes 6488072 | tf_op jit(solution)/shard_map/ppermute | solution.py:22
  565.6 35.9 %collective-permute-start.93 = (bf16[384,1024]{1,0:T(8,128)(2,1)}, bf16[384,1024]{1,0:T(8,128)(2,1)S(1)}, u32[]{:S(2)}, u32[]{:S(2)}) collective-permute-start(bf16[384,1024]{1,0:T(8,128)(2,1)} %ro_ref), channel_id=1, source_target_pairs={{0,1},{1,0},{2,3},{3,2},{4,5},{5,4},{6,7},{7,6},{8,9},{9,8},{10,11... | collective-permute-start | bytes 2359304 | tf_op jit(solution)/shard_map/ppermute | solution.py:22
  580.4 33.0 %collective-permute-start.83 = (bf16[384,1024]{1,0:T(8,128)(2,1)S(1)}, bf16[384,1024]{1,0:T(8,128)(2,1)}, u32[]{:S(2)}, u32[]{:S(2)}) collective-permute-start(bf16[384,1024]{1,0:T(8,128)(2,1)S(1)} %copy-done.41), channel_id=1, source_target_pairs={{0,1},{1,0},{2,3},{3,2},{4,5},{5,4},{6,7},{7,6},{8,9},{9,8},{10,11... | collective-permute-start | bytes 2359304 | tf_op jit(solution)/shard_map/ppermute | solution.py:22
  600.5 60.5 %collective-permute-start.68 = (bf16[4,32,1024]{2,1,0:T(8,128)(2,1)S(1)}, bf16[4,32,1024]{2,1,0:T(8,128)(2,1)}, u32[]{:S(2)}, u32[]{:S(2)}) collective-permute-start(bf16[4,32,1024]{2,1,0:T(8,128)(2,1)S(1)} %pad_maximum_fusion.11), channel_id=1, source_target_pairs={{0,2},{2,0},{1,3},{3,1},{4,6},{6,4},{5,7},{7,5},{8,10},{10,8},{9,1... | collective-permute-start | bytes 786440 | tf_op jit(solution)/shard_map/ppermute | solution.py:22
  601.5 60.7 %collective-permute-start.70 = (bf16[4,32,1024]{2,1,0:T(8,128)(2,1)S(1)}, bf16[4,32,1024]{2,1,0:T(8,128)(2,1)}, u32[]{:S(2)}, u32[]{:S(2)}) collective-permute-start(bf16[4,32,1024]{2,1,0:T(8,128)(2,1)S(1)} %pad_maximum_fusion.12), channel_id=1, source_target_pairs={{0,4},{4,0},{1,5},{5,1},{2,6},{6,2},{3,7},{7,3},{8,12},{12,8},{9,1... | collective-permute-start | bytes 786440 | tf_op jit(solution)/shard_map/ppermute | solution.py:22
  603.3 78.7 %collective-permute-start.80 = (bf16[32,1024]{1,0:T(8,128)(2,1)}, bf16[32,1024]{1,0:T(8,128)(2,1)}, u32[]{:S(2)}, u32[]{:S(2)}) collective-permute-start(bf16[32,1024]{1,0:T(8,128)(2,1)} %get-tuple-element.1810), channel_id=1, source_target_pairs={{0,8},{8,16},{16,24},{24,0},{1,9},{9,17},{17,25},{25,1},{2,10},{10... | collective-permute-start | bytes 196616 | tf_op jit(solution)/shard_map/ppermute | solution.py:22
  629.7 34.5 %collective-permute-start.95 = (bf16[4,176,512]{2,1,0:T(8,128)(2,1)S(1)}, bf16[4,176,512]{2,1,0:T(8,128)(2,1)S(1)}, u32[]{:S(2)}, u32[]{:S(2)}) collective-permute-start(bf16[4,176,512]{2,1,0:T(8,128)(2,1)S(1)} %pad_maximum_fusion.8), channel_id=1, source_target_pairs={{0,2},{2,0},{1,3},{3,1},{4,6},{6,4},{5,7},{7,5},{8,10},{10,8},{9,1... | collective-permute-start | bytes 2162696 | tf_op jit(solution)/shard_map/ppermute | solution.py:22
  661.0 41.0 %collective-permute-start.86 = (bf16[4,32,5632]{2,1,0:T(8,128)(2,1)S(1)}, bf16[4,32,5632]{2,1,0:T(8,128)(2,1)S(1)}, u32[]{:S(2)}, u32[]{:S(2)}) collective-permute-start(bf16[4,32,5632]{2,1,0:T(8,128)(2,1)S(1)} %pad_maximum_fusion.2), channel_id=1, source_target_pairs={{0,2},{2,0},{1,3},{3,1},{4,6},{6,4},{5,7},{7,5},{8,10},{10,8},{9,1... | collective-permute-start | bytes 4325384 | tf_op jit(solution)/shard_map/ppermute | solution.py:22
  662.2 43.9 %collective-permute-start.88 = (bf16[4,32,5632]{2,1,0:T(8,128)(2,1)S(1)}, bf16[4,32,5632]{2,1,0:T(8,128)(2,1)S(1)}, u32[]{:S(2)}, u32[]{:S(2)}) collective-permute-start(bf16[4,32,5632]{2,1,0:T(8,128)(2,1)S(1)} %pad_maximum_fusion.3), channel_id=1, source_target_pairs={{0,4},{4,0},{1,5},{5,1},{2,6},{6,2},{3,7},{7,3},{8,12},{12,8},{9,1... | collective-permute-start | bytes 4325384 | tf_op jit(solution)/shard_map/ppermute | solution.py:22
  707.6 200.9 %collective-permute-start.89 = (bf16[32,5632]{1,0:T(8,128)(2,1)}, bf16[32,5632]{1,0:T(8,128)(2,1)}, u32[]{:S(2)}, u32[]{:S(2)}) collective-permute-start(bf16[32,5632]{1,0:T(8,128)(2,1)} %get-tuple-element.1797), channel_id=1, source_target_pairs={{0,8},{8,16},{16,24},{24,0},{1,9},{9,17},{17,25},{25,1},{2,10},{10... | collective-permute-start | bytes 1081352 | tf_op jit(solution)/shard_map/ppermute | solution.py:22
  707.6 200.9 %collective-permute-start.90 = (bf16[32,5632]{1,0:T(8,128)(2,1)}, bf16[32,5632]{1,0:T(8,128)(2,1)}, u32[]{:S(2)}, u32[]{:S(2)}) collective-permute-start(bf16[32,5632]{1,0:T(8,128)(2,1)} %get-tuple-element.1799), channel_id=1, source_target_pairs={{0,16},{8,24},{16,0},{24,8},{1,17},{9,25},{17,1},{25,9},{2,18},{10... | collective-permute-start | bytes 1081352 | tf_op jit(solution)/shard_map/ppermute | solution.py:22
  710.4 198.1 %collective-permute-start.91 = (bf16[32,5632]{1,0:T(8,128)(2,1)}, bf16[32,5632]{1,0:T(8,128)(2,1)}, u32[]{:S(2)}, u32[]{:S(2)}) collective-permute-start(bf16[32,5632]{1,0:T(8,128)(2,1)} %get-tuple-element.1798), channel_id=1, source_target_pairs={{0,24},{8,0},{16,8},{24,16},{1,25},{9,1},{17,9},{25,17},{2,26},{10... | collective-permute-start | bytes 1081352 | tf_op jit(solution)/shard_map/ppermute | solution.py:22
  928.6 21.9 %collective-permute-start.54 = (bf16[32,128]{1,0:T(8,128)(2,1)S(1)}, bf16[32,128]{1,0:T(8,128)(2,1)S(1)}, u32[]{:S(2)}, u32[]{:S(2)}) collective-permute-start(bf16[32,128]{1,0:T(8,128)(2,1)S(1)} %get-tuple-element.1825), channel_id=1, source_target_pairs={{0,8},{8,16},{16,24},{24,0},{1,9},{9,17},{17,25},{25,1},{2,10},{10... | collective-permute-start | bytes 24584 | tf_op jit(solution)/shard_map/ppermute | solution.py:22
  929.7 20.8 %collective-permute-start.55 = (bf16[32,128]{1,0:T(8,128)(2,1)S(1)}, bf16[32,128]{1,0:T(8,128)(2,1)S(1)}, u32[]{:S(2)}, u32[]{:S(2)}) collective-permute-start(bf16[32,128]{1,0:T(8,128)(2,1)S(1)} %get-tuple-element.1827), channel_id=1, source_target_pairs={{0,16},{8,24},{16,0},{24,8},{1,17},{9,25},{17,1},{25,9},{2,18},{10... | collective-permute-start | bytes 24584 | tf_op jit(solution)/shard_map/ppermute | solution.py:22
  930.7 19.8 %collective-permute-start.56 = (bf16[32,128]{1,0:T(8,128)(2,1)S(1)}, bf16[32,128]{1,0:T(8,128)(2,1)S(1)}, u32[]{:S(2)}, u32[]{:S(2)}) collective-permute-start(bf16[32,128]{1,0:T(8,128)(2,1)S(1)} %get-tuple-element.1826), channel_id=1, source_target_pairs={{0,24},{8,0},{16,8},{24,16},{1,25},{9,1},{17,9},{25,17},{2,26},{10... | collective-permute-start | bytes 24584 | tf_op jit(solution)/shard_map/ppermute | solution.py:22
  938.4 21.8 %collective-permute-start.60 = (bf16[4,32,3072]{2,1,0:T(8,128)(2,1)}, bf16[4,32,3072]{2,1,0:T(8,128)(2,1)}, u32[]{:S(2)}, u32[]{:S(2)}) collective-permute-start(bf16[4,32,3072]{2,1,0:T(8,128)(2,1)} %pad_maximum_fusion.5), channel_id=1, source_target_pairs={{0,2},{2,0},{1,3},{3,1},{4,6},{6,4},{5,7},{7,5},{8,10},{10,8},{9,1... | collective-permute-start | bytes 2359304 | tf_op jit(solution)/shard_map/ppermute | solution.py:22
  (170 other events, 1751.3 us)
Sparse Core Ops, SparseCore 0:
  351.0 34.0 all-gather.4
  557.7 41.9 all-gather.6

commit v2 on v0

v2 whole, which is shorter than its diff:
```python
from functools import partial

import jax
import jax.numpy as jnp
from jax import lax
from jax.experimental import pallas as pl
from jax.experimental.pallas import tpu as pltpu
from jax.sharding import Mesh
from jax.sharding import PartitionSpec as P

HEAD_K = 256
HEAD_V = 256
GROUP = 64
LANES = 128
AXES = ("z", "y", "x", "c")
VMEM = 56 * 1024 * 1024
QUICK = pl.CostEstimate(flops=0, bytes_accessed=0, transcendentals=0)
F32 = jnp.float32
BF16 = jnp.bfloat16


def shift(value, axis, step):
    size = lax.axis_size(axis)
    return lax.ppermute(value, axis, [(i, (i + step) % size) for i in range(size)])


def flip(value, axis):
    return shift(value, axis, 1)


def place():
    return tuple(lax.axis_index(a) for a in AXES)


def after(done, *values):
    out = lax.optimization_barrier((values, done))[0]
    return out[0] if len(values) == 1 else out


def square_plane():
    return lax.axis_size("y") == 2


def cross(value, late):
    perm = [(i, i ^ (2 if (i % 2 == 0) != late else 4)) for i in range(8)]
    return lax.ppermute(value, ("y", "x", "c"), perm)


def neighbour(early, late, core):
    _, y, x, _ = place()
    by_x = jnp.where(core == 0, early, late)
    by_y = jnp.where(core == 0, late, early)
    return (y + by_y) % 2, (x + by_x) % 2


def gathered(own, early, late, corner):
    pieces = [(own, 0, 0, 0), (early, 1, 0, 0), (late, 0, 1, 0), (corner, 1, 1, 0)]
    return pieces + [(flip(a, "c"), i, j, 1) for a, i, j, _ in pieces]


def sources(pieces):
    z, _, _, c = place()
    depth = lax.axis_size("z")
    chips, cores = [], []
    for _, early, late, other in pieces:
        core = (c + other) % 2
        y, x = neighbour(early, late, core)
        for k in range(depth):
            chips.append((((z - k) % depth) * 2 + y) * 2 + x)
            cores.append(core)
    return jnp.stack(chips + cores).astype(jnp.int32)


def assemble(pieces, rows, shape, by_columns=False):
    where = sources(pieces)
    arrays = [p[0] for p in pieces]
    depth = arrays[0].shape[0]
    blocks = [(n, k) for n in range(len(pieces)) for k in range(depth)]
    total = len(blocks)

    def body(where_ref, *refs):
        ins, out, sem = refs[: len(arrays)], refs[-2], refs[-1]
        for at, (n, k) in enumerate(blocks):
            chip, core = where_ref[at], where_ref[total + at]
            if by_columns:
                width = shape[1] // 2
                goal = out.at[
                    pl.ds(pl.multiple_of(chip * rows, rows), rows),
                    pl.ds(pl.multiple_of(core * width, width), width),
                ]
            else:
                goal = out.at[pl.ds(pl.multiple_of((chip * 2 + core) * rows, rows), rows), :]
            pltpu.make_async_copy(ins[n].at[k], goal, sem).start()
        pltpu.make_async_copy(out, out, sem).wait()

    return pl.pallas_call(
        body,
        grid_spec=pltpu.PrefetchScalarGridSpec(
            num_scalar_prefetch=1,
            grid=(1,),
            in_specs=[pl.BlockSpec(memory_space=pl.ANY)] * len(arrays),
            out_specs=pl.BlockSpec(shape, lambda n, s: (0, 0)),
            scratch_shapes=[pltpu.SemaphoreType.DMA],
        ),
        out_shape=jax.ShapeDtypeStruct(shape, BF16),
        compiler_params=pltpu.CompilerParams(vmem_limit_bytes=VMEM),
        cost_estimate=QUICK,
    )(where, *arrays)


def layout():
    _, _, _, c = place()
    depth, height = lax.axis_size("z"), lax.axis_size("y")
    if not square_plane():
        return [jnp.arange(depth * height * 2, dtype=jnp.int32)]

    def column(early, late):
        y, x = neighbour(early, late, c)
        return (jnp.arange(depth, dtype=jnp.int32) * 2 + y) * 2 + x

    return [jnp.concatenate([column(1, 0), column(1, 1)]), column(0, 1), column(0, 0)]


def wide(a):
    return a.astype(F32)


class Sum:
    def __init__(self, blocks):
        self.blocks = blocks

    def first(self, done=()):
        self.arrived = cross(after(done, self.blocks[0]), False) if square_plane() else ()
        return self.arrived

    def second(self, done=()):
        if not square_plane():
            self.through = ()
            return ()
        depth = lax.axis_size("z")
        arrived, kept = after(done, self.arrived, self.blocks[1])
        self.through = cross((wide(kept) + wide(arrived[depth:])).astype(BF16), True)
        return self.through

    def third(self, done=()):
        width = self.blocks[-1].shape[-1]
        if not square_plane():
            total = self.blocks[0].reshape(-1, width)
            return wide(lax.psum_scatter(total, ("z", "y", "x"), scatter_dimension=0, tiled=True))
        depth = lax.axis_size("z")
        arrived, through = after(done, self.arrived, self.through)
        total = wide(self.blocks[2]) + wide(arrived[:depth]) + wide(through)
        total = total.astype(BF16).reshape(-1, width)
        return wide(lax.psum_scatter(total, "z", scatter_dimension=0, tiled=True))


def weight_grads(groups, tile, halves=False, table=None):
    _, _, _, c = place()
    chips = layout()
    spans = [a.shape[0] for a in chips]
    chips = jnp.concatenate(chips)
    count = chips.shape[0]
    lefts = [left for left, _ in groups]
    rights = [right for _, group in groups for right in group]
    owner = [n for n, (_, group) in enumerate(groups) for _ in group]
    tokens, height = lefts[0][0].shape
    each = rights[0][0].shape[1] // (2 if halves else 1)
    width = each * len(rights)
    rows = height // (count if halves else 2 * count)
    starts = chips * rows if halves else (chips * 2 + c) * rows

    if rows % 16:
        products = []
        for n, right in zip(owner, rights):
            product = tn(jnp.concatenate(lefts[n]), jnp.concatenate(right)).astype(BF16)
            if halves:
                product = lax.dynamic_slice_in_dim(product, c * each, each, 1).reshape(count, rows, each)
            else:
                product = lax.dynamic_index_in_dim(product.reshape(count, 2, rows, each), c, 1, False)
            products.append(product)
        if table is not None:
            product = wide(table[1])
            for left, right in table[0]:
                product = product + tn(jnp.concatenate(left), jnp.concatenate(right))
            product = product.astype(BF16).reshape(count, 2, rows, LANES)
            products.append(lax.dynamic_index_in_dim(product, c, 1, False))
        product = jnp.take(jnp.concatenate(products, axis=2), chips, axis=0)
        blocks, at = [], 0
        for span in spans:
            blocks.append(product[at : at + span])
            at += span
        return Sum(blocks)

    strips = each // tile
    first_tile = c * strips if halves else jnp.int32(0)
    numbers = jnp.concatenate([starts, first_tile[None]]).astype(jnp.int32)

    steps = width // tile
    terms, base = table if table is not None else ((), None)
    flat = [a for left in lefts for a in left] + [a for right in rights for a in right]
    narrow = [a for left, right in terms for a in (*left, *right)]
    if table is not None:
        narrow.append(base)

    def body(numbers_ref, *refs):
        left_refs, right_refs = refs[: 2 * len(lefts)], refs[2 * len(lefts) : len(flat)]
        narrow_refs = refs[len(flat) : len(flat) + len(narrow)]
        outs, (turned, chosen, total, based) = refs[len(flat) + len(narrow) : -4], refs[-4:]
        step = pl.program_id(0)

        def start(at):
            return pl.ds(pl.multiple_of(numbers_ref[at], 16), rows)

        def turn(lo_ref, ls_ref):
            turned[:, :tokens] = lo_ref[...].T
            turned[:, tokens:] = ls_ref[...].T
            for at in range(count):
                chosen[at * rows : (at + 1) * rows, :] = turned[start(at), :]

        def put(product, columns):
            at = 0
            for out, span in zip(outs, spans):
                out[:, :, :columns] = product[at : at + span * rows].reshape(span, rows, columns)
                at += span * rows

        def strip(ro_ref, rs_ref):
            both = jnp.concatenate([ro_ref[...], rs_ref[...]], axis=0)
            put(nn(chosen[...], both).astype(BF16), tile)

        def term(n):
            lo_ref, ls_ref, ro_ref, rs_ref = narrow_refs[4 * n : 4 * n + 4]
            turn(lo_ref, ls_ref)
            both = jnp.concatenate([ro_ref[...], rs_ref[...]], axis=0)
            product = nn(chosen[...], both)
            if n == 0:
                total[...] = product
            else:
                total[...] += product
            if n == len(terms) - 1:
                for at in range(count):
                    based[at * rows : (at + 1) * rows, :] = narrow_refs[-1][start(at), :]
                put((total[...] + wide(based[...])).astype(BF16), LANES)

        for n in range(len(lefts)):
            pl.when(step == owner.index(n) * strips)(partial(turn, *left_refs[2 * n : 2 * n + 2]))
        if len(rights) == 1:
            strip(*right_refs)
        else:
            for n in range(len(rights)):
                pl.when(step // strips == n)(partial(strip, *right_refs[2 * n : 2 * n + 2]))
        for n in range(len(terms)):
            pl.when(step == steps + n)(partial(term, n))

    def column(n):
        return lambda step, s: (0, jnp.clip(step - n * strips, 0, strips - 1) + s[count])

    def full(a):
        return pl.BlockSpec(a.shape, lambda n, s: (0,) * a.ndim)

    right_specs = [pl.BlockSpec((tokens, tile), column(n)) for n in range(len(rights)) for _ in range(2)]
    columns = width + (LANES if table is not None else 0)
    last = steps - (table is None)
    outs = [(span, rows, columns) for span in spans]
    blocks = pl.pallas_call(
        body,
        grid_spec=pltpu.PrefetchScalarGridSpec(
            num_scalar_prefetch=1,
            grid=(steps + len(terms),),
            in_specs=[full(a) for left in lefts for a in left] + right_specs + [full(a) for a in narrow],
            out_specs=[pl.BlockSpec((n, rows, tile), lambda n, s: (0, 0, jnp.minimum(n, last))) for n, _, _ in outs],
            scratch_shapes=[
                pltpu.VMEM((height, 2 * tokens), BF16),
                pltpu.VMEM((count * rows, 2 * tokens), BF16),
                pltpu.VMEM((count * rows, LANES), F32),
                pltpu.VMEM((count * rows, LANES), BF16),
            ],
        ),
        out_shape=[jax.ShapeDtypeStruct(o, BF16) for o in outs],
        compiler_params=pltpu.CompilerParams(vmem_limit_bytes=VMEM),
        cost_estimate=QUICK,
    )(numbers, *flat, *narrow)
    return Sum(blocks)


def nn(left, right):
    return jnp.dot(left, right, preferred_element_type=F32)


def nt(left, right):
    return lax.dot_general(left, right, (((1,), (1,)), ((), ())), preferred_element_type=F32)


def tn(left, right):
    return lax.dot_general(left, right, (((0,), (0,)), ((), ())), preferred_element_type=F32)


def summed(ones, values):
    high = values.astype(BF16)
    low = (values - high.astype(F32)).astype(BF16)
    return nn(ones, high) + nn(ones, low)


def triangle(size, relation, block=None):
    row = lax.broadcasted_iota(jnp.int32, (size, size), 0)
    column = lax.broadcasted_iota(jnp.int32, (size, size), 1)
    chosen = relation(row, column)
    if block is not None:
        chosen = chosen & (row // block == column // block)
    return jnp.where(chosen, 1.0, 0.0).astype(BF16)


def log_decay(gate_pre):
    return (jnp.minimum(gate_pre, 0.0) - jnp.log1p(jnp.exp(-jnp.abs(gate_pre)))) * (1.0 / 16.0)


def sigmoid(v):
    return 1.0 / (1.0 + jnp.exp(-v))


def spec(shape, index=None):
    index = index or (lambda *_: (0,) * len(shape))
    return pl.BlockSpec(shape, index)


def by_head(rows):
    return spec((rows, HEAD_K), lambda h: (0, h))


def kernel_call(body, grid, ins, outs, scratch=()):
    return pl.pallas_call(
        body,
        grid=grid,
        in_specs=[s for _, s in ins],
        out_specs=[s for _, _, s in outs],
        out_shape=[jax.ShapeDtypeStruct(shape, dtype) for shape, dtype, _ in outs],
        scratch_shapes=list(scratch),
        compiler_params=pltpu.CompilerParams(vmem_limit_bytes=VMEM),
        cost_estimate=QUICK,
    )(*[a for a, _ in ins])


MESSAGE = HEAD_V + 16


def unit_columns(rows, columns, start):
    row = lax.broadcasted_iota(jnp.int32, (rows, columns), 0)
    column = lax.broadcasted_iota(jnp.int32, (rows, columns), 1)
    return jnp.where(column == row + start, 1.0, 0.0).astype(BF16)


def first_weights(w_key, w_value, rank_in, rank_out, vectors):
    rows, width = w_key.shape
    rank = rank_in.shape[1]

    def body(wk, wv, ri, ro, *refs):
        vector_refs, out = refs[:-1], refs[-1]
        out[:, :width] = wk[...]
        out[:, width : 2 * width] = wv[...]
        table = nn(ri[...], unit_columns(rank, LANES, 0)) + tn(ro[...], unit_columns(rank, LANES, rank))
        for n, v in enumerate(vector_refs):
            mine = unit_columns(v.shape[1], rows, 0)
            table = table + tn(nn(v[...], mine).astype(BF16), unit_columns(1, LANES, 2 * rank + n))
        out[:, 2 * width :] = table.astype(BF16)

    ins = [w_key, w_value, rank_in, rank_out, *[v.reshape(1, -1) for v in vectors]]
    shape = (rows, 2 * width + LANES)
    return kernel_call(body, (1,), [(a, spec(a.shape)) for a in ins], [(shape, BF16, spec(shape))])[0]


def project(tokens, weights, marks, rank):
    rows, width = tokens.shape
    heads = width // HEAD_K
    at_table = 2 * width // LANES

    def body(x_ref, wk, wv, table, part_ref, marks_ref, n_out, low_out, k_out, v_out, g_out, m_out, vectors_out):
        @pl.when(pl.program_id(0) == 0)
        def _():
            vectors = nt(unit_columns(8, LANES, 2 * rank), table[...])
            vectors_out[...] = vectors
            x = x_ref[...].astype(F32)
            scale = lax.rsqrt(jnp.mean(x * x, axis=1, keepdims=True) + 1e-06)
            n_out[...] = (x * scale * vectors[1:2]).astype(BF16)
            low = nn(n_out[...], table[...]).astype(BF16)
            lane = lax.broadcasted_iota(jnp.int32, (LANES, LANES), 1)
            row = lax.broadcasted_iota(jnp.int32, (LANES, LANES), 0)
            move = jnp.where((lane == row + rank) & (row < rank), 1.0, 0.0).astype(BF16)
            one = jnp.where(lax.broadcasted_iota(jnp.int32, (rows, LANES), 1) == 2 * rank, 1.0, 0.0)
            low_out[...] = (nn(low, move) + one).astype(BF16)

        normed = n_out[...]
        key = nn(normed, wk[...]).astype(BF16)
        value = nn(normed, wv[...]).astype(BF16)
        k_out[...] = key
        v_out[...] = value
        gate = nt(low_out[...], part_ref[...])
        g_out[...] = gate
        decay = log_decay(gate)
        later = summed(triangle(rows, lambda i, j: j > i), decay)
        last = marks_ref[:, 4:5]
        finish = (key.astype(F32) * jnp.exp(later) * last).astype(BF16)
        m_out[0, :HEAD_V] = tn(value, finish).astype(BF16)
        total = jnp.exp(jnp.sum(decay, axis=0, keepdims=True)) * marks_ref[rows - 1 :, 3:4]
        m_out[0, HEAD_V:] = jnp.broadcast_to(total, (MESSAGE - HEAD_V, HEAD_K)).astype(BF16)

    return kernel_call(
        body,
        (heads,),
        [
            (tokens, spec((rows, width))),
            (weights, by_head(width)),
            (weights, spec((width, HEAD_K), lambda h: (0, heads + h))),
            (weights, spec((width, LANES), lambda h: (0, at_table))),
            (weights, spec((HEAD_K, LANES), lambda h: (h, at_table))),
            (marks, spec(marks.shape)),
        ],
        [
            ((rows, width), BF16, spec((rows, width))),
            ((rows, LANES), BF16, spec((rows, LANES))),
            ((rows, width), BF16, by_head(rows)),
            ((rows, width), BF16, by_head(rows)),
            ((rows, width), F32, by_head(rows)),
            ((heads, MESSAGE, HEAD_K), BF16, spec((1, MESSAGE, HEAD_K), lambda h: (h, 0, 0))),
            ((8, width), F32, spec((8, width))),
        ],
    )


def scaled(queries):
    return queries.astype(F32) * HEAD_K ** (-0.5)


def mixer(normed, keys, values, gate_pre, entered, weights, head_gain, tokens, gain, marks, doc_row):
    rows, wide = tokens.shape
    heads = wide // HEAD_K
    blocks = rows // GROUP

    def body(
        n_ref, k_ref, v_ref, g_ref, s_ref, wq, ws, hg_ref, wo, x_ref, gain_ref, marks_ref, doc_ref,
        q_ref, mixed_out, swish_out, gated_out, hidden_out, two_out, states_out, state, total,
    ):
        h = pl.program_id(0)
        q_ref[...] = nn(n_ref[...], wq[...]).astype(BF16)
        swish = nn(n_ref[...], ws[...])
        swish_out[...] = swish
        along = summed(triangle(rows, lambda i, j: j <= i, GROUP), log_decay(g_ref[...]))
        state[...] = s_ref[0].astype(F32)
        causal = triangle(GROUP, lambda i, j: j <= i) > 0
        for n in range(blocks):
            at = slice(n * GROUP, (n + 1) * GROUP)
            marks_n = marks_ref[at]
            run = along[at]
            end = run[GROUP - 1 :]
            key = k_ref[at].astype(F32)
            value = v_ref[at]
            query_in = (scaled(q_ref[at]) * jnp.exp(run)).astype(BF16)
            key_in = (key * jnp.exp(-run)).astype(BF16)
            key_out = (key * jnp.exp(end - run) * marks_n[:, 2:3]).astype(BF16)
            allowed = causal & (marks_n[:, 0:1] == doc_ref[:, at])
            scores = jnp.where(allowed, nt(query_in, key_in), 0.0).astype(BF16)
            before = state[...].astype(BF16)
            states_out[0, n] = before
            mixed_out[at] = nn(scores, value) + marks_n[:, 1:2] * nt(query_in, before)
            kept = marks_n[GROUP - 1 :, 1:2] * jnp.exp(end)
            state[...] = kept * state[...] + tn(value, key_out)
        states_out[0, blocks] = state[...].astype(BF16)
        mixed = mixed_out[...]
        norm = lax.rsqrt(jnp.mean(mixed * mixed, axis=1, keepdims=True) + 1e-05)
        gated = (mixed * norm * hg_ref[...] * (swish * sigmoid(swish))).astype(BF16)
        gated_out[...] = gated
        part = nn(gated, wo[...])

        @pl.when(h == 0)
        def _():
            total[...] = x_ref[...].astype(F32) + part

        @pl.when(h > 0)
        def _():
            total[...] += part

        @pl.when(h == heads - 1)
        def _():
            hidden = total[...]
            hidden_out[...] = hidden
            scale = lax.rsqrt(jnp.mean(hidden * hidden, axis=1, keepdims=True) + 1e-06)
            two_out[...] = (hidden * scale * gain_ref[...]).astype(BF16)

    return kernel_call(
        body,
        (heads,),
        [
            (normed, spec((rows, wide))),
            (keys, by_head(rows)),
            (values, by_head(rows)),
            (gate_pre, by_head(rows)),
            (entered, spec((1, HEAD_V, HEAD_K), lambda h: (h, 0, 0))),
            (weights, by_head(wide)),
            (weights, spec((wide, HEAD_V), lambda h: (0, heads + h))),
            (head_gain, spec((1, HEAD_V))),
            (weights, spec((HEAD_V, wide), lambda h: (h, 2))),
            (tokens, spec((rows, wide))),
            (gain, spec((1, wide))),
            (marks, spec(marks.shape)),
            (doc_row, spec(doc_row.shape)),
        ],
        [
            ((rows, wide), BF16, by_head(rows)),
            ((rows, wide), F32, by_head(rows)),
            ((rows, wide), F32, by_head(rows)),
            ((rows, wide), BF16, by_head(rows)),
            ((rows, wide), F32, spec((rows, wide))),
            ((rows, wide), BF16, spec((rows, wide))),
            ((heads, blocks + 1, HEAD_V, HEAD_K), BF16, spec((1, blocks + 1, HEAD_V, HEAD_K), lambda h: (h, 0, 0, 0))),
        ],
        [pltpu.VMEM((HEAD_V, HEAD_K), F32), pltpu.VMEM((rows, wide), F32)],
    )


def feed(normed_two, cotangent, w_both, w_down, hidden, gain):
    rows, wide = hidden.shape
    inner = w_both.shape[1] // 2
    tile = 256
    steps = inner // tile

    def body(
        n_ref, c_ref, wg, wu, wd, hidden_ref, gain_ref,
        out_ref, inner_out, gate_out, up_out, grad_out, low_out, forward_sum, back_sum,
    ):
        step = pl.program_id(0)
        normed = n_ref[...]
        gate = nn(normed, wg[...])
        up = nn(normed, wu[...])
        soft = sigmoid(gate)
        silu = gate * soft
        product = (silu * up).astype(BF16)
        inner_out[...] = product
        grad = nt(c_ref[...], wd[...])
        grad_up = (grad * silu).astype(BF16)
        grad_gate = (grad * up * (soft * (1.0 + gate * (1.0 - soft)))).astype(BF16)
        up_out[...] = grad_up
        gate_out[...] = grad_gate
        ahead = nn(product, wd[...])
        back = nt(grad_gate, wg[...]) + nt(grad_up, wu[...])

        @pl.when(step == 0)
        def _():
            forward_sum[...] = hidden_ref[...] + ahead
            back_sum[...] = back

        @pl.when(step > 0)
        def _():
            forward_sum[...] += ahead
            back_sum[...] += back

        @pl.when(step == steps - 1)
        def _():
            out_ref[...] = forward_sum[...].astype(BF16)
            hidden = hidden_ref[...]
            scale = lax.rsqrt(jnp.mean(hidden * hidden, axis=1, keepdims=True) + 1e-06)
            unit = hidden * scale
            grad = back_sum[...] * gain_ref[...]
            grad = scale * (grad - unit * jnp.mean(grad * unit, axis=1, keepdims=True))
            grad = c_ref[...].astype(F32) + grad
            grad_out[...] = grad
            low_out[...] = grad.astype(BF16)

    strip = spec((wide, tile), lambda n: (0, n))
    column = spec((rows, tile), lambda n: (0, n))
    whole = spec((rows, wide))
    return kernel_call(
        body,
        (steps,),
        [
            (normed_two, whole),
            (cotangent, whole),
            (w_both, strip),
            (w_both, spec((wide, tile), lambda n: (0, n + steps))),
            (w_down, spec((tile, wide), lambda n: (n, 0))),
            (hidden, whole),
            (gain, spec((1, wide))),
        ],
        [
            ((rows, wide), BF16, whole),
            ((rows, inner), BF16, column),
            ((rows, inner), BF16, column),
            ((rows, inner), BF16, column),
            ((rows, wide), F32, whole),
            ((rows, wide), BF16, whole),
        ],
        [pltpu.VMEM((rows, wide), F32), pltpu.VMEM((rows, wide), F32)],
    )


def head_back(grad_low, weights, mixed, swish, head_gain, queries, gate_pre, decays, marks):
    rows, wide = mixed.shape
    heads = wide // HEAD_K

    def body(gh_ref, wo, mixed_ref, swish_ref, hg_ref, q_ref, g_ref, d_ref, marks_ref, gm_out, gs_out, hg_out, m_out):
        grad = nt(gh_ref[...], wo[...])
        mixed = mixed_ref[...]
        swish = swish_ref[...]
        soft = sigmoid(swish)
        silu = swish * soft
        norm = lax.rsqrt(jnp.mean(mixed * mixed, axis=1, keepdims=True) + 1e-05)
        unit = mixed * norm
        gain = hg_ref[...]
        gs_out[...] = (grad * unit * gain * (soft * (1.0 + swish * (1.0 - soft)))).astype(BF16)
        by_gain = jnp.sum(grad * unit * silu, axis=0, keepdims=True)

        @pl.when(pl.program_id(0) == 0)
        def _():
            hg_out[...] = by_gain

        @pl.when(pl.program_id(0) > 0)
        def _():
            hg_out[...] += by_gain

        inner = grad * gain * silu
        grad_mixed = norm * (inner - unit * jnp.mean(inner * unit, axis=1, keepdims=True))
        gm_out[...] = grad_mixed.astype(BF16)
        along = summed(triangle(rows, lambda i, j: j <= i), log_decay(g_ref[...]))
        query_in = (scaled(q_ref[...]) * jnp.exp(along)).astype(BF16)
        m_out[0, :HEAD_V] = tn((grad_mixed * marks_ref[:, 3:4]).astype(BF16), query_in).astype(BF16)
        m_out[0, HEAD_V:] = d_ref[0]

    return kernel_call(
        body,
        (heads,),
        [
            (grad_low, spec((rows, wide))),
            (weights, spec((HEAD_V, wide), lambda h: (h, 2))),
            (mixed, by_head(rows)),
            (swish, by_head(rows)),
            (head_gain, spec((1, HEAD_V))),
            (queries, by_head(rows)),
            (gate_pre, by_head(rows)),
            (decays, spec((1, MESSAGE - HEAD_V, HEAD_K), lambda h: (h, 0, 0))),
            (marks, spec(marks.shape)),
        ],
        [
            ((rows, wide), BF16, by_head(rows)),
            ((rows, wide), BF16, by_head(rows)),
            ((1, HEAD_V), F32, spec((1, HEAD_V))),
            ((heads, MESSAGE, HEAD_K), BF16, spec((1, MESSAGE, HEAD_K), lambda h: (h, 0, 0))),
        ],
    )


def mixer_back(queries, keys, values, gate_pre, grad_mixed, states, leaving, first, marks, doc_row, rank):
    rows, wide = queries.shape
    heads = wide // HEAD_K
    blocks = rows // GROUP

    def body(
        q_ref, k_ref, v_ref, g_ref, gm_ref, s_ref, l_ref, ro, marks_ref, doc_ref,
        gq_out, gk_out, gv_out, gg_out, low_out, state_grad, slope, low,
    ):
        h = pl.program_id(0)
        gate = g_ref[...]
        along = summed(triangle(rows, lambda i, j: j <= i, GROUP), log_decay(gate))
        state_grad[...] = l_ref[0].astype(F32)
        causal = triangle(GROUP, lambda i, j: j <= i) > 0
        onward = triangle(GROUP, lambda i, j: j >= i)
        for n in reversed(range(blocks)):
            at = slice(n * GROUP, (n + 1) * GROUP)
            marks_n = marks_ref[at]
            run = along[at]
            end = run[GROUP - 1 :]
            key = k_ref[at].astype(F32)
            value = v_ref[at]
            grad = gm_ref[at]
            entering = marks_n[:, 1:2]
            up, down = jnp.exp(run), jnp.exp(-run)
            out = jnp.exp(end - run) * marks_n[:, 2:3]
            query_in = (scaled(q_ref[at]) * up).astype(BF16)
            key_in = (key * down).astype(BF16)
            key_out = (key * out).astype(BF16)
            allowed = causal & (marks_n[:, 0:1] == doc_ref[:, at])
            scores = jnp.where(allowed, nt(query_in, key_in), 0.0).astype(BF16)
            grad_scores = jnp.where(allowed, nt(grad, value), 0.0).astype(BF16)
            leaving = state_grad[...].astype(BF16)
            grad_query = nn(grad_scores, key_in) + entering * nn(grad, s_ref[0, n])
            grad_key_in = tn(grad_scores, query_in)
            grad_key_out = nn(value, leaving)
            gv_out[at] = (tn(scores, grad) + nt(key_out, leaving)).astype(BF16)
            gq_out[at] = (grad_query * up * HEAD_K ** (-0.5)).astype(BF16)
            gk_out[at] = (grad_key_in * down + grad_key_out * out).astype(BF16)
            change = (
                query_in.astype(F32) * grad_query
                - key_in.astype(F32) * grad_key_in
                - key_out.astype(F32) * grad_key_out
            )
            closing = jnp.sum(s_ref[0, n + 1].astype(F32) * leaving.astype(F32), axis=0, keepdims=True)
            slope[at] = summed(onward, change) + closing
            kept = marks_n[GROUP - 1 :, 1:2] * jnp.exp(end)
            state_grad[...] = kept * state_grad[...] + tn(grad, (query_in.astype(F32) * entering).astype(BF16))
        grad_gate = (slope[...] * sigmoid(-gate) * (1.0 / 16.0)).astype(BF16)
        gg_out[...] = grad_gate
        part = nn(grad_gate, ro[...])

        @pl.when(h == 0)
        def _():
            low[...] = part

        @pl.when(h > 0)
        def _():
            low[...] += part

        @pl.when(h == heads - 1)
        def _():
            row = lax.broadcasted_iota(jnp.int32, (LANES, LANES), 0)
            lane = lax.broadcasted_iota(jnp.int32, (LANES, LANES), 1)
            move = jnp.where((row == lane + rank) & (lane < rank), 1.0, 0.0).astype(BF16)
            low_out[...] = nn(low[...].astype(BF16), move).astype(BF16)

    return kernel_call(
        body,
        (heads,),
        [
            (queries, by_head(rows)),
            (keys, by_head(rows)),
            (values, by_head(rows)),
            (gate_pre, by_head(rows)),
            (grad_mixed, by_head(rows)),
            (states, spec((1, blocks + 1, HEAD_V, HEAD_K), lambda h: (h, 0, 0, 0))),
            (leaving, spec((1, HEAD_V, HEAD_K), lambda h: (h, 0, 0))),
            (first, spec((HEAD_K, LANES), lambda h: (h, 2 * wide // LANES))),
            (marks, spec(marks.shape)),
            (doc_row, spec(doc_row.shape)),
        ],
        [((rows, wide), BF16, by_head(rows))] * 4 + [((rows, LANES), BF16, spec((rows, LANES)))],
        [pltpu.VMEM((HEAD_V, HEAD_K), F32), pltpu.VMEM((rows, HEAD_K), F32), pltpu.VMEM((rows, LANES), F32)],
    )


def input_back(grads, first, second, grad_rank, tokens, gain, grad_hidden):
    rows, wide = tokens.shape
    heads = wide // HEAD_K
    places = ((second, 0), (first, 0), (first, heads), (second, heads))

    def body(*refs):
        grad_refs, weight_refs = refs[:4], refs[4:8]
        low_ref, table, x_ref, gain_ref, gh_ref, out_ref, total = refs[8:]
        h = pl.program_id(0)
        part = nt(grad_refs[0][...], weight_refs[0][...])
        for g, w in zip(grad_refs[1:], weight_refs[1:]):
            part = part + nt(g[...], w[...])

        @pl.when(h == 0)
        def _():
            total[...] = part + nt(low_ref[...], table[...])

        @pl.when(h > 0)
        def _():
            total[...] += part

        @pl.when(h == heads - 1)
        def _():
            x = x_ref[...].astype(F32)
            scale = lax.rsqrt(jnp.mean(x * x, axis=1, keepdims=True) + 1e-06)
            unit = x * scale
            grad = total[...] * gain_ref[...]
            out_ref[...] = gh_ref[...] + scale * (grad - unit * jnp.mean(grad * unit, axis=1, keepdims=True))

    def strip(start):
        return spec((wide, HEAD_K), lambda h: (0, start + h))

    whole = spec((rows, wide))
    return kernel_call(
        body,
        (heads,),
        [(g, by_head(rows)) for g in grads]
        + [(w, strip(start)) for w, start in places]
        + [
            (grad_rank, spec((rows, LANES))),
            (first, spec((wide, LANES), lambda h: (0, 2 * wide // LANES))),
            (tokens, whole),
            (gain, spec((1, wide))),
            (grad_hidden, whole),
        ],
        [((rows, wide), F32, whole)],
        [pltpu.VMEM((rows, wide), F32)],
    )[0]


def then(earlier, later):
    scale = later[:, HEAD_V:].astype(F32)
    state = scale[:, :1] * earlier[:, :HEAD_V].astype(F32) + later[:, :HEAD_V].astype(F32)
    return jnp.concatenate([state, scale * earlier[:, HEAD_V:].astype(F32)], axis=1).astype(BF16)


def nothing(like):
    return jnp.concatenate([jnp.zeros_like(like[:, :HEAD_V]), jnp.ones_like(like[:, HEAD_V:])], axis=1)


class Passing:
    def __init__(self, message, backward=False):
        _, y, x, c = place()
        height = lax.axis_size("y")
        self.core, self.sign = c, -1 if backward else 1
        if backward:
            y, x, c = height - 1 - y, 1 - x, 1 - c
        self.y, self.x, self.c = y, x, c
        heads = message.shape[0]
        self.other = flip(message, "c")
        both = jnp.where(c == 0, then(message, self.other), then(self.other, message))
        self.mine = lax.dynamic_slice_in_dim(both, self.core * (heads // 2), heads // 2, 0)

    def by_x(self, done=()):
        self.beside = flip(after(done, self.mine), "x")
        return self.beside

    def by_y(self, done=()):
        beside, mine = after(done, self.beside, self.mine)
        self.before = jnp.where(self.x == 1, beside, nothing(mine))
        self.line = jnp.where(self.x == 1, then(beside, mine), then(mine, beside))
        self.far = [shift(self.line, "y", self.sign * j) for j in range(1, lax.axis_size("y"))]
        return self.far

    def entering(self, done=()):
        before, distant = after(done, self.before, self.far)
        for j, far in enumerate(distant):
            before = jnp.where(self.y > j, then(far, before), before)
        rest = flip(before, "c")
        chip = jnp.where(self.core == 0, jnp.concatenate([before, rest]), jnp.concatenate([rest, before]))
        return jnp.where(self.c == 1, then(chip, self.other), chip)[:, :HEAD_V]


def pair(value):
    return (value, flip(value, "c"))


def document_of(positions, starts):
    return jnp.sum((starts[None, :] <= positions[:, None]).astype(jnp.int32), axis=1) - 1


def documents(starts, rows):
    _, y, x, c = place()
    positions = ((y * 2 + x) * 2 + c) * rows + jnp.arange(rows, dtype=jnp.int32)
    doc = document_of(positions, starts)
    before = document_of(positions - 1, starts)
    blocks = doc.reshape(-1, GROUP)
    entering = (blocks == before.reshape(-1, GROUP)[:, :1]).reshape(-1)
    tail = (blocks == blocks[:, -1:]).reshape(-1)
    columns = [doc, entering, tail, doc == before[0], doc == doc[-1]]
    marks = jnp.stack([a.astype(F32) for a in columns] + [jnp.zeros((rows,), F32)] * 3, axis=1)
    return marks, doc.astype(F32).reshape(1, rows)


def pair(value):
    return (value, flip(value, "c"))


def shards(tokens, cotangent, doc_starts, *weights):
    (
        gain_one, w_query, w_key, w_value, w_swish, rank_in, rank_out, bias, head_gain, w_output, gain_two,
        w_gate, w_up, w_down,
    ) = weights
    rows, width = tokens.shape
    own, rank, ff = w_query.shape[0], rank_in.shape[1], w_gate.shape[1]
    devices = width // own
    _, _, _, c = place()

    table_columns = 2 * width + LANES
    square_weights = jnp.concatenate([w_query, w_swish, w_output], axis=1)

    w_both = lax.all_gather(jnp.concatenate([w_gate, w_up], axis=1), AXES, axis=0, tiled=True)
    first = first_weights(w_key, w_value, rank_in, rank_out, (bias, gain_one, gain_two, head_gain))
    marks, doc_row = documents(doc_starts[0], rows)
    fast = square_plane() and own % 16 == 0
    depth = lax.axis_size("z")
    if fast:
        one = jnp.stack([first] + [shift(first, "z", k) for k in range(1, depth)])
        half = width // 2
        keep = lax.dynamic_slice_in_dim(w_down, c * half, half, 1)
        other = flip(lax.dynamic_slice_in_dim(w_down, (1 - c) * half, half, 1), "c")
        chip_down = jnp.where(c == 0, jnp.concatenate([keep, other]), jnp.concatenate([other, keep]))
        chip_down, square_weights = after(one, chip_down, square_weights)
        one_early, one_late = cross(one, False), cross(one, True)
        two = [shift(square_weights, "z", k) for k in range(1, depth, 2)]
        now = (one_early, one_late, two)
        square_more, one_next = after(now, square_weights, one_early)
        one_corner = cross(one_next, True)
        two_more = [shift(square_more, "z", k) for k in range(2, depth, 2)]
        now = (one_corner, two_more)
        chip_down, one = after(now, chip_down, one)
        three = [shift(chip_down, "z", k) for k in range(1, depth, 2)]
        first = assemble(gathered(one, one_early, one_late, one_corner), own, (width, table_columns))

        def mixed_order(base, odd, even):
            return jnp.stack([base] + [(odd if k % 2 else even)[(k - 1) // 2] for k in range(1, depth)])

        two = mixed_order(square_weights, two, two_more)
        now = (first, three)
        first, two, chip_down = after(now, first, two, chip_down)
        two_early = cross(two, False)
        three_more = [shift(chip_down, "z", k) for k in range(2, depth, 2)]
        three = mixed_order(chip_down, three, three_more)
    else:
        first = lax.all_gather(first, AXES, axis=0, tiled=True)
        second = lax.all_gather(square_weights, AXES, axis=0, tiled=True)
        w_down_all = lax.all_gather(w_down, AXES, axis=0, tiled=True)
    normed, low, keys, values, gate_pre, message, vectors = project(tokens, first, marks, rank)
    row_one, row_two = vectors[1:2], vectors[2:3]
    row_head = vectors[3].reshape(devices, own)[:, : head_gain.shape[0]].reshape(1, HEAD_V)
    if fast:
        message, two, two_early = after(three, message, two, two_early)
    passing = Passing(message)
    if fast:
        two_late = cross(after(passing.mine, two), True)
        now = (passing.by_x(), two_late)
        two_corner = cross(after(now, two_early), True)
        now = (passing.by_y(now), two_corner)
        three = after(now, three)
        three_early = cross(three, False)
        second = assemble(gathered(two, two_early, two_late, two_corner), own, (width, 3 * width))
        now = (passing.entering(now), three_early, second)
        entered, second, three, three_early = after(now, now[0], second, three, three_early)
        three_late, three_corner = cross(three, True), cross(three_early, True)
    else:
        passing.by_x()
        passing.by_y()
        entered = passing.entering()
    both = pair(normed)
    queries, mixed, swish, gated, hidden, normed_two, states = mixer(
        normed, keys, values, gate_pre, entered, second, row_head, tokens, row_two, marks, doc_row
    )
    if fast:
        hidden, three = after((three_late, three_corner), hidden, three)
        w_down_all = assemble(
            gathered(three, three_early, three_late, three_corner), chip_down.shape[0], (ff, width), True
        )
    output, inner, grad_gate, grad_up, grad_hidden, grad_low = feed(
        normed_two, cotangent, w_both, w_down_all, hidden, row_two
    )

    down = weight_grads([(pair(inner), [pair(cotangent)])], 512, True)
    grad_low, gate_pair, up_pair, two_pair = after(down.blocks, grad_low, pair(grad_gate), pair(grad_up), pair(normed_two))
    grad_mixed, grad_swish, grad_head_gain, message_back = head_back(
        grad_low, second, mixed, swish, row_head, queries, gate_pre, message[:, HEAD_V:], marks
    )
    now = (down.first(), message_back)
    passing = Passing(after(now, message_back), True)
    now = passing.mine
    two_pair, gate_pair = after(now, two_pair, gate_pair)
    gate = weight_grads([(two_pair, [gate_pair])], ff // 2)
    now = (passing.by_x(), down.second(now), gate.blocks)
    up = weight_grads([after(now, (two_pair, [up_pair]))], ff // 2)
    now = (passing.by_y(now), gate.first(now), up.blocks)
    leaving = passing.entering(now)
    now = leaving
    down_sum = down.third(now)
    grad_query, grad_key, grad_value, grad_gate_pre, grad_rank = mixer_back(
        queries, keys, values, gate_pre, grad_mixed, states, leaving, first, marks, doc_row, rank
    )
    now = (up.first(now), grad_query)
    inside_pairs = [pair(a) for a in after(now, grad_query, grad_key, grad_value, grad_rank, grad_gate_pre)]
    swish_pair = after(now, pair(grad_swish))
    middle = weight_grads([(both, [swish_pair]), (pair(gated), [pair(grad_low)])], width)
    now = (inside_pairs, middle.blocks, gate.second(now))
    head_terms = grad_head_gain + flip(grad_head_gain, "c")
    head_terms = jnp.pad(head_terms.reshape(devices, -1), ((0, 0), (0, own - head_gain.shape[0]))).reshape(width, 1)
    base = jnp.pad(head_terms.astype(BF16), ((0, 0), (2 * rank + 3, LANES - 2 * rank - 4)))
    inside_pairs = after(now, inside_pairs)
    inside = weight_grads(
        [(both, inside_pairs[:3])],
        width,
        table=([(both, inside_pairs[3]), (inside_pairs[4], pair(low))], base),
    )
    gate_sum = gate.third(now)
    now = (inside.blocks, up.second(now), middle.first(now))
    input_grad = input_back(
        (grad_query, grad_key, grad_value, grad_swish), first, second, after(now, grad_rank), tokens, row_one,
        grad_hidden,
    )
    up_sum = up.third(now)
    now = (input_grad, inside.first(now), middle.second(now))
    inside.second(now)
    middle_sum = middle.third(now)
    inside_sum = inside.third()

    chip_half = ff // devices
    keep = lax.dynamic_slice_in_dim(down_sum, c * chip_half, chip_half, 0)
    other = flip(lax.dynamic_slice_in_dim(down_sum, (1 - c) * chip_half, chip_half, 0), "c")
    down_sum = jnp.where(c == 0, jnp.concatenate([keep, other], 1), jnp.concatenate([other, keep], 1))
    g_query, g_key, g_value = (inside_sum[:, n * width : (n + 1) * width] for n in range(3))
    g_swish, g_output = middle_sum[:, :width], middle_sum[:, width:]
    g_rank_in, g_rank_out, g_bias, g_head = (
        inside_sum[:, 3 * width + a : 3 * width + b]
        for a, b in ((0, rank), (rank, 2 * rank), (2 * rank, 2 * rank + 1), (2 * rank + 3, 2 * rank + 4))
    )
    g_gate, g_up = gate_sum, up_sum

    def gain_grad(gain, *terms):
        return sum(jnp.sum(wide(w) * g, axis=1) for w, g in terms) / wide(gain)

    g_gain_one = gain_grad(
        gain_one, (w_query, g_query), (w_key, g_key), (w_value, g_value), (w_swish, g_swish), (rank_in, g_rank_in)
    )
    g_gain_two = gain_grad(gain_two, (w_gate, g_gate), (w_up, g_up))
    return (
        output, input_grad, g_gain_one, g_query, g_key, g_value, g_swish, g_rank_in, g_rank_out.T, g_bias[:, 0],
        g_head[: head_gain.shape[0], 0], g_output, g_gain_two, g_gate, g_up, down_sum,
    )


def solution(mesh):
    fsdp, seq = mesh.shape["fsdp"], mesh.shape["seq"]
    inner = Mesh(mesh.devices.reshape(fsdp, seq // 4, 2, 2), AXES)
    rows, vector, columns = P(AXES, None), P(AXES), P(None, AXES)
    in_specs = (rows, rows, P("z", None), vector, rows, rows, rows, rows, rows, columns, vector, vector, rows, vector) + (rows,) * 3
    out_specs = (rows, rows, vector) + (rows,) * 5 + (columns, vector, vector, rows, vector) + (rows,) * 3
    return jax.shard_map(shards, mesh=inner, in_specs=in_specs, out_specs=out_specs, check_vma=False)
```

time: 2350 us -> 490 us (0.21)
  waiting for transfers between devices: 1620 us -> 177 us
  matrix products: 255 us -> 0 us
  blocking collectives: 170 us -> 0 us
  Pallas kernels: 0 us -> 150 us
  other arithmetic: 155 us -> 50 us
  local copies, waits for them, and re-layouts: 106 us -> 19.2 us
  starting transfers between devices: 1.67 us -> 74.9 us
    reduce_scatter x8 -> x5, waiting for transfers between devices: 1160 us -> 45.9 us  [third(): return wide(lax.psum_scatter(total, 'z', scatter_dimension=0, tiled=True))]
    all_gather x10 -> x1, waiting for transfers between devices: 312 us -> 0.02 us  [shards(): lax.all_gather(jnp.concatenate([w_gate, w_up], axis=1), AXES, axis=0, til...]
    dot_general x115 -> x0, matrix products: 252 us -> none  [the longest x24 44.7 us: group_step(): jnp.einsum('yaq,yap->aqp', key_finish, value_matrix, precision=MAXIMUM_AC...]
    unnamed x22 -> x6, waiting for transfers between devices: 155 us -> 0.1 us
    pallas_call x0 -> x15, Pallas kernels: none -> 150 us  [the longest x7 91.9 us: kernel_call(): pl.pallas_call(body, grid=grid, in_specs=[s for _, s in ins], out_specs=[...]
    ppermute x0 -> x66, waiting for transfers between devices: none -> 131 us  [the longest x47 98.5 us: shift(): lax.ppermute(value, axis, [(i, (i + step) % size) for i in range(size)])]
    all_gather x3 -> x0, blocking collectives: 87.5 us -> none  [the longest x1 41.1 us: gather_attention(): lax.all_gather(pieces[5], ('fsdp', 'seq'), axis=0, tiled=True)]
    unnamed x2 -> x0, blocking collectives: 82.1 us -> none
  transfers between devices with their start and end apart: 20 -> 72, of which waited for: 17 -> 35; matrix products, arithmetic and copies ran while one was open for 10% -> 10% of each run, Pallas kernels for 0% -> 26%
where the time goes in v2:
time: 490 us; the launch traced here: 486 us
  waiting for transfers between devices  177 us (36%)
  Pallas kernels  150 us (31%)
  starting transfers between devices  74.9 us (15%)
  other arithmetic  50 us (10%)
  local copies, waits for them, and re-layouts  19.2 us (4%)
  between operations  15.7 us (3%)
    ppermute x47, waiting for transfers between devices, shift(): lax.ppermute(value, axis, [(i, (i + step) % size) for i in range(size)])  98.5 us
    pallas_call x7, Pallas kernels, kernel_call(): pl.pallas_call(body, grid=grid, in_specs=[s for _, s in ins], out_specs=[...  91.9 us
    ppermute x47, starting transfers between devices, shift(): lax.ppermute(value, axis, [(i, (i + step) % size) for i in range(size)])  48.1 us
    reduce_scatter x5, waiting for transfers between devices, third(): return wide(lax.psum_scatter(total, 'z', scatter_dimension=0, tiled=True))  45.9 us
    pallas_call x5, Pallas kernels, weight_grads(): pl.pallas_call(body, grid_spec=pltpu.PrefetchScalarGridSpec(num_scalar_pr...  40.8 us
    ppermute x19, waiting for transfers between devices, cross(): return lax.ppermute(value, ('y', 'x', 'c'), perm)  32.1 us
    ppermute x19, starting transfers between devices, cross(): return lax.ppermute(value, ('y', 'x', 'c'), perm)  26.6 us
    pallas_call x3, Pallas kernels, assemble(): pl.pallas_call(body, grid_spec=pltpu.PrefetchScalarGridSpec(num_scalar_pr...  17.1 us
  transfers between devices with their start and end apart: 72, of which 35 were waited for; matrix products, arithmetic and copies ran while one was open for 10% of the time, Pallas kernels for 26%

profile of v2, /device:TPU:0, one launch (start us, length us, event | category | flops | bytes accessed | tf_op | source)
XLA Modules:
  0.0 486.2 jit_solution(15359160085815722220)
XLA Ops:
  12.5 3.0 collective-permute-start.1
  15.5 2.6 collective-permute-start.2
  19.6 2.8 collective-permute-done.1
  22.4 6.6 %collective-permute-done.2 = bf16[32,2176]{1,0:T(8,128)(2,1)S(1)} collective-permute-done((bf16[32,2176]{1,0:T(8,128)(2,1)}, bf16[32,2176]{1,0:T(8,128)(2,1)S(1)}, u32[]{:S(2)}, u32[]{:S(2)}) %collective-permute-start.2) | collective-permute-done | bytes 139296 | tf_op jit(solution)/shard_map/ppermute | solution.py:24
  33.2 8.9 %collective-permute-start.6 = (bf16[32,3072]{1,0:T(8,128)(2,1)S(1)}, bf16[32,3072]{1,0:T(8,128)(2,1)S(1)}, u32[]{:S(2)}, u32[]{:S(2)}) collective-permute-start(bf16[32,3072]{1,0:T(8,128)(2,1)S(1)} %pad_maximum_fusion.10), channel_id=1, source_target_pairs={{0,8},{8,16},{16,24},{24,0},{1,9},{9,17},{17,25},{25,1},{2,10},{10... | collective-permute-start | bytes 589832 | tf_op jit(solution)/shard_map/ppermute | solution.py:24
  43.8 7.9 %collective-permute-done.6 = bf16[32,3072]{1,0:T(8,128)(2,1)S(1)} collective-permute-done((bf16[32,3072]{1,0:T(8,128)(2,1)S(1)}, bf16[32,3072]{1,0:T(8,128)(2,1)S(1)}, u32[]{:S(2)}, u32[]{:S(2)}) %collective-permute-start.6) | collective-permute-done | bytes 196640 | tf_op jit(solution)/shard_map/ppermute | solution.py:24
  51.7 6.7 %collective-permute-done.7 = bf16[32,3072]{1,0:T(8,128)(2,1)S(1)} collective-permute-done((bf16[32,3072]{1,0:T(8,128)(2,1)S(1)}, bf16[32,3072]{1,0:T(8,128)(2,1)S(1)}, u32[]{:S(2)}, u32[]{:S(2)}) %collective-permute-start.7) | collective-permute-done | bytes 196640 | tf_op jit(solution)/shard_map/ppermute | solution.py:24
  60.5 16.3 %collective-permute-done.9 = bf16[32,3072]{1,0:T(8,128)(2,1)S(1)} collective-permute-done((bf16[32,3072]{1,0:T(8,128)(2,1)S(1)}, bf16[32,3072]{1,0:T(8,128)(2,1)S(1)}, u32[]{:S(2)}, u32[]{:S(2)}) %collective-permute-start.9) | collective-permute-done | bytes 196640 | tf_op jit(solution)/shard_map/ppermute | solution.py:24
  77.4 4.3 collective-permute-start.15
  83.7 5.1 %shard_map.289.wk.wv.table.part_ref.ro.refs_5_.refs_6_.refs_9_ = bf16[1024,2176]{1,0:T(8,128)(2,1)} custom-call(s32[64]{0:T(128)} %stack.114.where_ref, bf16[4,32,2176]{2,1,0:T(8,128)(2,1)} %copy-done.9, bf16[4,32,2176]{2,1,0:T(8,128)(2,1)} %copy-done.39, bf16[4,32,2176]{2,1,0:T(8,128)(2,1)} %copy-done.40, ...), custom_call_target="tpu_custom_call" | custom-call | tf_op jit(solution)/shard_map/pallas_call | solution.py:96
  88.8 6.2 %collective-permute-done.15 = bf16[176,512]{1,0:T(8,128)(2,1)S(1)} collective-permute-done((bf16[176,512]{1,0:T(8,128)(2,1)S(1)}, bf16[176,512]{1,0:T(8,128)(2,1)S(1)}, u32[]{:S(2)}, u32[]{:S(2)}) %collective-permute-start.15) | collective-permute-done | bytes 180256 | tf_op jit(solution)/shard_map/ppermute | solution.py:24
  101.4 9.4 %shard_map.290 = (bf16[384,1024]{1,0:T(8,128)(2,1)}, bf16[384,128]{1,0:T(8,128)(2,1)}, bf16[384,1024]{1,0:T(8,128)(2,1)}, bf16[384,1024]{1,0:T(8,128)(2,1)}, f32...) custom-call(bf16[384,1024]{1,0:T(8,128)(2,1)} %refs_10_.1, ...), custom_call_target="tpu_custom_call" | custom-call | tf_op jit(solution)/shard_map/pallas_call | solution.py:330
  110.9 8.3 %collective-permute-done.17 = bf16[176,512]{1,0:T(8,128)(2,1)S(1)} collective-permute-done((bf16[176,512]{1,0:T(8,128)(2,1)S(1)}, bf16[176,512]{1,0:T(8,128)(2,1)S(1)}, u32[]{:S(2)}, u32[]{:S(2)}) %collective-permute-start.17) | collective-permute-done | bytes 180256 | tf_op jit(solution)/shard_map/ppermute | solution.py:24
  123.8 2.1 collective-permute-start.20
  125.9 2.3 collective-permute-start.19
  128.2 7.6 %collective-permute-done.19 = bf16[2,272,256]{2,1,0:T(8,128)(2,1)S(1)} collective-permute-done((bf16[2,272,256]{2,1,0:T(8,128)(2,1)S(1)}, bf16[2,272,256]{2,1,0:T(8,128)(2,1)S(1)}, u32[]{:S(2)}, u32[]{:S(2)}) %collective-permute-start.19) | collective-permute-done | bytes 278560 | tf_op jit(solution)/shard_map/ppermute | solution.py:24
  139.1 14.8 %collective-permute-done.21 = bf16[2,272,256]{2,1,0:T(8,128)(2,1)S(1)} collective-permute-done((bf16[2,272,256]{2,1,0:T(8,128)(2,1)}, bf16[2,272,256]{2,1,0:T(8,128)(2,1)S(1)}, u32[]{:S(2)}, u32[]{:S(2)}) %collective-permute-start.21) | collective-permute-done | bytes 278560 | tf_op jit(solution)/shard_map/ppermute | solution.py:24
  155.2 2.9 collective-permute-start.28
  161.8 6.2 %shard_map.291.wq.ws.wo.refs_4_.refs_7_ = bf16[1024,3072]{1,0:T(8,128)(2,1)} custom-call(s32[64]{0:T(128)} %stack.114.where_ref, bf16[4,32,3072]{2,1,0:T(8,128)(2,1)} %copy-done.5, bf16[4,32,3072]{2,1,0:T(8,128)(2,1)} %copy-done.15, bf16[4,32,3072]{2,1,0:T(8,128)(2,1)} %collective-permute-done.20.refs_2_, ...), custom_call_target="tpu_custom_call" | custom-call | tf_op jit(solution)/shard_map/pallas_call | solution.py:96
  173.3 16.7 %shard_map.292 = (bf16[384,1024]{1,0:T(8,128)(2,1)}, f32[384,1024]{1,0:T(8,128)}, f32[384,1024]{1,0:T(8,128)}, bf16[384,1024]{1,0:T(8,128)(2,1)}, f32[384,1024]{...) custom-call(bf16[384,1024]{1,0:T(8,128)(2,1)} %get-tuple-element.154.n_ref.refs_0_.refs_8_, ...), custom_call_target="tpu_custom_call" | custom-call | tf_op jit(solution)/shard_map/pallas_call | solution.py:330
  195.3 5.9 %shard_map.293.wd = bf16[2816,1024]{1,0:T(8,128)(2,1)} custom-call(s32[64]{0:T(128)} %stack.114.where_ref, bf16[4,176,512]{2,1,0:T(8,128)(2,1)} %copy-done.8, bf16[4,176,512]{2,1,0:T(8,128)(2,1)} %collective-permute-done.28.refs_1_, bf16[4,176,512]{2,1,0:T(8,128)(2,1)} %copy-done.31, bf16[4,176,512]{2,1,0:T(8,128)(2,1)} %copy-done.32, ...), custom_call_target="tpu_custom_call" | custom-call | tf_op jit(solution)/shard_map/pallas_call | solution.py:96
  201.2 25.6 %shard_map.294 = (bf16[384,1024]{1,0:T(8,128)(2,1)}, bf16[384,2816]{1,0:T(8,128)(2,1)}, bf16[384,2816]{1,0:T(8,128)(2,1)}, bf16[384,2816]{1,0:T(8,128)(2,1)}, f3...) custom-call(bf16[384,1024]{1,0:T(8,128)(2,1)} %get-tuple-element.214.n_ref.refs_0_, bf16[384,1024]{1,0:T(8,128)(2,1)} %refs_2_.1, ...), custom_call_target="tpu_custom_call" | custom-call | tf_op jit(solution)/shard_map/pallas_call | solution.py:330
  228.5 4.5 collective-permute-done.39.refs_3_
  233.9 7.9 %shard_map.295 = (bf16[8,176,512]{2,1,0:T(8,128)(2,1)}, bf16[4,176,512]{2,1,0:T(8,128)(2,1)}, bf16[4,176,512]{2,1,0:T(8,128)(2,1)}) custom-call(s32[17]{0:T(128)} %pad_add_fusion.1.numbers_ref, bf16[384,2816]{1,0:T(8,128)(2,1)} %get-tuple-element.185.refs_0_, bf16[384,2816]{1,0:T(8,128)(2,1)} %collective-permute-done.38.refs_1_, bf16[384,1024]{1,0:T(8,128)(2,1)} %refs_2_.1, ...), custom_call_target="tpu_custom_call" | custom-call | tf_op jit(solution)/shard_map/pallas_call | solution.py:264
  241.9 2.4 collective-permute-start.40
  244.3 2.3 collective-permute-done.37.refs_1_
  246.6 9.7 %shard_map.296 = (bf16[384,1024]{1,0:T(8,128)(2,1)}, bf16[384,1024]{1,0:T(8,128)(2,1)}, f32[1,256]{1,0:T(1,128)}, bf16[4,272,256]{2,1,0:T(8,128)(2,1)}) custom-call(bf16[384,1024]{1,0:T(8,128)(2,1)} %get-tuple-element.189.gh_ref.refs_6_, bf16[1024,3072]{1,0:T(8,128)(2,1)} %shard_map.291.wq.ws.wo.refs_4_.refs_7_, f32[384,1024]{1,0:T(8,128)} %get-tuple-element.190.mixed_ref, ...), custom_call_target="tpu_custom_call" | custom-call | tf_op jit(solution)/shard_map/pallas_call | solution.py:330
  256.3 5.2 %collective-permute-done.40 = bf16[8,176,512]{2,1,0:T(8,128)(2,1)S(1)} collective-permute-done((bf16[8,176,512]{2,1,0:T(8,128)(2,1)}, bf16[8,176,512]{2,1,0:T(8,128)(2,1)S(1)}, u32[]{:S(2)}, u32[]{:S(2)}) %collective-permute-start.40) | collective-permute-done | bytes 1441824 | tf_op jit(solution)/shard_map/ppermute | solution.py:46
  270.2 7.1 %shard_map.297 = (bf16[8,32,2816]{2,1,0:T(8,128)(2,1)}, bf16[4,32,2816]{2,1,0:T(8,128)(2,1)}, bf16[4,32,2816]{2,1,0:T(8,128)(2,1)}) custom-call(s32[17]{0:T(128)} %pad_add_fusion.2.numbers_ref, bf16[384,1024]{1,0:T(8,128)(2,1)} %get-tuple-element.214.n_ref.refs_0_, bf16[384,1024]{1,0:T(8,128)(2,1)} %copy-done.4, ...), custom_call_target="tpu_custom_call" | custom-call | tf_op jit(solution)/shard_map/pallas_call | solution.py:264
  285.9 7.2 %shard_map.298 = (bf16[8,32,2816]{2,1,0:T(8,128)(2,1)}, bf16[4,32,2816]{2,1,0:T(8,128)(2,1)}, bf16[4,32,2816]{2,1,0:T(8,128)(2,1)}) custom-call(s32[17]{0:T(128)} %pad_add_fusion.2.numbers_ref, bf16[384,1024]{1,0:T(8,128)(2,1)} %get-tuple-element.214.n_ref.refs_0_, bf16[384,1024]{1,0:T(8,128)(2,1)} %copy-done.4, ...), custom_call_target="tpu_custom_call" | custom-call | tf_op jit(solution)/shard_map/pallas_call | solution.py:264
  294.4 4.0 collective-permute-done.45
  300.9 10.4 %collective-permute-start.46 = (bf16[2,272,256]{2,1,0:T(8,128)(2,1)}, bf16[2,272,256]{2,1,0:T(8,128)(2,1)}, u32[]{:S(2)}, u32[]{:S(2)}) collective-permute-start(bf16[2,272,256]{2,1,0:T(8,128)(2,1)} %maximum_select_fusion.4), channel_id=1, source_target_pairs={{0,1},{1,0},{2,3},{3,2},{4,5},{5,4},{6,7},{7,6},{8,9},{9,8},{10,11... | collective-permute-start | bytes 835592 | tf_op jit(solution)/shard_map/ppermute | solution.py:24
  317.6 17.9 %shard_map.299 = (bf16[384,1024]{1,0:T(8,128)(2,1)}, bf16[384,1024]{1,0:T(8,128)(2,1)}, bf16[384,1024]{1,0:T(8,128)(2,1)}, bf16[384,1024]{1,0:T(8,128)(2,1)}, bf16[384,128]{1,0:T(8,128)(2,1)}) custom-call(bf16[384,1024]{1,0:T(8,128)(2,1)} %get-tuple-element.181.q_ref, bf16[384,1024]{1,0:T(8,128)(2,1)} %get-tuple-element.155.k_ref, ...), custom_call_target="tpu_custom_call" | custom-call | tf_op jit(solution)/shard_map/pallas_call | solution.py:330
  337.2 3.7 collective-permute-done.52.refs_11_
  342.1 7.6 %shard_map.300 = (bf16[8,32,2048]{2,1,0:T(8,128)(2,1)}, bf16[4,32,2048]{2,1,0:T(8,128)(2,1)}, bf16[4,32,2048]{2,1,0:T(8,128)(2,1)}) custom-call(s32[17]{0:T(128)} %pad_add_fusion.2.numbers_ref, bf16[384,1024]{1,0:T(8,128)(2,1)} %get-tuple-element.154.n_ref.refs_0_.refs_8_, bf16[384,1024]{1,0:T(8,128)(2,1)} %copy-done.1, ...), custom_call_target="tpu_custom_call" | custom-call | tf_op jit(solution)/shard_map/pallas_call | solution.py:264
  349.7 2.6 collective-permute-done.57
  360.5 11.0 %shard_map.301 = (bf16[8,32,3200]{2,1,0:T(8,128)(2,1)}, bf16[4,32,3200]{2,1,0:T(8,128)(2,1)}, bf16[4,32,3200]{2,1,0:T(8,128)(2,1)}) custom-call(s32[17]{0:T(128)} %pad_add_fusion.2.numbers_ref, bf16[384,1024]{1,0:T(8,128)(2,1)} %get-tuple-element.154.n_ref.refs_0_.refs_8_, bf16[384,1024]{1,0:T(8,128)(2,1)} %copy-done.1, ...), custom_call_target="tpu_custom_call" | custom-call | tf_op jit(solution)/shard_map/pallas_call | solution.py:264
  371.4 2.2 collective-permute-done.60
  376.0 2.3 add_convert_fusion.4
  378.4 2.3 add_convert_fusion.9
  382.0 2.3 add_convert_fusion.3
  384.4 10.7 %shard_map.302 = f32[384,1024]{1,0:T(8,128)} custom-call(bf16[384,1024]{1,0:T(8,128)(2,1)} %get-tuple-element.243.refs_2_.refs_0_, bf16[384,1024]{1,0:T(8,128)(2,1)} %get-tuple-element.245.refs_4_.refs_1_, bf16[384,1024]{1,0:T(8,128)(2,1)} %get-tuple-element.247.refs_6_.refs_2_, bf16[384,1024]{1,0:T(8,128)(2,1)} %get-tuple-element.236.refs_4_.refs_3_, ...), custom_call_target="tpu_custom_call" | custom-call | tf_op jit(solution)/shard_map/pallas_call | solution.py:330
  395.9 6.3 %collective-permute-done.62 = bf16[8,32,3200]{2,1,0:T(8,128)(2,1)S(1)} collective-permute-done((bf16[8,32,3200]{2,1,0:T(8,128)(2,1)}, bf16[8,32,3200]{2,1,0:T(8,128)(2,1)S(1)}, u32[]{:S(2)}, u32[]{:S(2)}) %collective-permute-start.62) | collective-permute-done | bytes 1638432 | tf_op jit(solution)/shard_map/ppermute | solution.py:46
  404.5 2.2 add_convert_fusion.8
  406.8 9.1 %collective-permute-done.64 = bf16[4,32,3200]{2,1,0:T(8,128)(2,1)S(1)} collective-permute-done((bf16[4,32,3200]{2,1,0:T(8,128)(2,1)}, bf16[4,32,3200]{2,1,0:T(8,128)(2,1)S(1)}, u32[]{:S(2)}, u32[]{:S(2)}) %collective-permute-start.64) | collective-permute-done | bytes 819232 | tf_op jit(solution)/shard_map/ppermute | solution.py:46
  422.4 3.2 reduce-scatter.12.cloned.1.call-done
  427.9 20.4 %reduce-scatter.8.cloned.1.call-done = bf16[32,2048]{1,0:T(8,128)(2,1)} async-done(((bf16[128,2048]{1,0:T(8,128)(2,1)}), bf16[32,2048]{1,0:T(8,128)(2,1)}) %reduce-scatter.8.cloned.1.call-update) | async-done | bytes 131088 | tf_op jit(solution)/shard_map/reduce_scatter | solution.py:154
  450.0 22.2 %reduce-scatter.16.cloned.1.call-done = bf16[32,3200]{1,0:T(8,128)(2,1)} async-done(((bf16[128,3200]{1,0:T(8,128)(2,1)}), bf16[32,3200]{1,0:T(8,128)(2,1)}) %reduce-scatter.16.cloned.1.call-update) | async-done | bytes 204816 | tf_op jit(solution)/shard_map/reduce_scatter | solution.py:154
  (375 shorter events, 111.6 us)
Async XLA Ops:
  7.2 193.9 %all-gather.2.cloned.1.call-start = ((), (), s32[]{:S(2)}) async-start(), calls=%async_computation.5 | async-start | bytes 11894784 | tf_op jit(solution)/shard_map/all_gather | solution.py:866
  9.1 408.0 %reduce-scatter.14.cloned.1.call-start = ((), (), s32[]{:S(2)}) async-start(), calls=%async_computation.9 | async-start | bytes 901120 | tf_op jit(solution)/shard_map/reduce_scatter | solution.py:154
  15.5 13.5 %collective-permute-start.2 = (bf16[32,2176]{1,0:T(8,128)(2,1)}, bf16[32,2176]{1,0:T(8,128)(2,1)S(1)}, u32[]{:S(2)}, u32[]{:S(2)}) collective-permute-start(bf16[32,2176]{1,0:T(8,128)(2,1)} %shard_map.288), channel_id=1, source_target_pairs={{0,16},{8,24},{16,0},{24,8},{1,17},{9,25},{17,1},{25,9},{2,18},{10... | collective-permute-start | bytes 417800 | tf_op jit(solution)/shard_map/ppermute | solution.py:24
  19.5 13.7 %collective-permute-start = (bf16[88,512]{1,0:T(8,128)(2,1)S(1)}, bf16[88,512]{1,0:T(8,128)(2,1)S(1)}, u32[]{:S(2)}, u32[]{:S(2)}) collective-permute-start(bf16[88,512]{1,0:T(8,128)(2,1)S(1)} %get-tuple-element.425), channel_id=1, source_target_pairs={{0,1},{1,0},{2,3},{3,2},{4,5},{5,4},{6,7},{7,6},{8,9},{9,8},{10,11... | collective-permute-start | bytes 270344 | tf_op jit(solution)/shard_map/ppermute | solution.py:24
  30.0 28.4 %collective-permute-start.4 = (bf16[4,32,2176]{2,1,0:T(8,128)(2,1)S(1)}, bf16[4,32,2176]{2,1,0:T(8,128)(2,1)S(1)}, u32[]{:S(2)}, u32[]{:S(2)}) collective-permute-start(bf16[4,32,2176]{2,1,0:T(8,128)(2,1)S(1)} %pad_maximum_fusion.2.refs_0_), channel_id=1, source_target_pairs={{0,2},{1,5},{2,0},{3,7},{4,6},{5,1},{6,4},{7,3},{8,10},{9,13},{10,... | collective-permute-start | bytes 1671176 | tf_op jit(solution)/shard_map/ppermute | solution.py:46
  31.6 26.8 %collective-permute-start.5 = (bf16[4,32,2176]{2,1,0:T(8,128)(2,1)S(1)}, bf16[4,32,2176]{2,1,0:T(8,128)(2,1)S(1)}, u32[]{:S(2)}, u32[]{:S(2)}) collective-permute-start(bf16[4,32,2176]{2,1,0:T(8,128)(2,1)S(1)} %pad_maximum_fusion.2.refs_0_), channel_id=1, source_target_pairs={{0,4},{1,3},{2,6},{3,1},{4,0},{5,7},{6,2},{7,5},{8,12},{9,11},{10,... | collective-permute-start | bytes 1671176 | tf_op jit(solution)/shard_map/ppermute | solution.py:46
  33.2 18.5 %collective-permute-start.6 = (bf16[32,3072]{1,0:T(8,128)(2,1)S(1)}, bf16[32,3072]{1,0:T(8,128)(2,1)S(1)}, u32[]{:S(2)}, u32[]{:S(2)}) collective-permute-start(bf16[32,3072]{1,0:T(8,128)(2,1)S(1)} %pad_maximum_fusion.10), channel_id=1, source_target_pairs={{0,8},{8,16},{16,24},{24,0},{1,9},{9,17},{17,25},{25,1},{2,10},{10... | collective-permute-start | bytes 589832 | tf_op jit(solution)/shard_map/ppermute | solution.py:24
  42.1 16.2 %collective-permute-start.7 = (bf16[32,3072]{1,0:T(8,128)(2,1)S(1)}, bf16[32,3072]{1,0:T(8,128)(2,1)S(1)}, u32[]{:S(2)}, u32[]{:S(2)}) collective-permute-start(bf16[32,3072]{1,0:T(8,128)(2,1)S(1)} %pad_maximum_fusion.10), channel_id=1, source_target_pairs={{0,24},{8,0},{16,8},{24,16},{1,25},{9,1},{17,9},{25,17},{2,26},{10... | collective-permute-start | bytes 589832 | tf_op jit(solution)/shard_map/ppermute | solution.py:24
  58.4 18.5 %collective-permute-start.8 = (bf16[4,32,2176]{2,1,0:T(8,128)(2,1)S(1)}, bf16[4,32,2176]{2,1,0:T(8,128)(2,1)}, u32[]{:S(2)}, u32[]{:S(2)}) collective-permute-start(bf16[4,32,2176]{2,1,0:T(8,128)(2,1)S(1)} %collective-permute-done.4.refs_1_), channel_id=1, source_target_pairs={{0,4},{1,3},{2,6},{3,1},{4,0},{5,7},{6,2},{7,5},{8,12},{9,11},{10,... | collective-permute-start | bytes 1671176 | tf_op jit(solution)/shard_map/ppermute | solution.py:46
  58.5 18.9 %collective-permute-start.11 = (bf16[4,32,2176]{2,1,0:T(8,128)(2,1)S(1)}, bf16[4,32,2176]{2,1,0:T(8,128)(2,1)S(1)}, u32[]{:S(2)}, u32[]{:S(2)}) collective-permute-start(bf16[4,32,2176]{2,1,0:T(8,128)(2,1)S(1)} %collective-permute-done.4.refs_1_), channel_id=1, source_target_pairs={{0,1},{1,0},{2,3},{3,2},{4,5},{5,4},{6,7},{7,6},{8,9},{9,8},{10,11... | collective-permute-start | bytes 1671176 | tf_op jit(solution)/shard_map/ppermute | solution.py:24
  59.5 17.3 %collective-permute-start.9 = (bf16[32,3072]{1,0:T(8,128)(2,1)S(1)}, bf16[32,3072]{1,0:T(8,128)(2,1)S(1)}, u32[]{:S(2)}, u32[]{:S(2)}) collective-permute-start(bf16[32,3072]{1,0:T(8,128)(2,1)S(1)} %pad_maximum_fusion.10), channel_id=1, source_target_pairs={{0,16},{8,24},{16,0},{24,8},{1,17},{9,25},{17,1},{25,9},{2,18},{10... | collective-permute-start | bytes 589832 | tf_op jit(solution)/shard_map/ppermute | solution.py:24
  60.3 21.5 %collective-permute-start.12 = (bf16[4,32,2176]{2,1,0:T(8,128)(2,1)S(1)}, bf16[4,32,2176]{2,1,0:T(8,128)(2,1)S(1)}, u32[]{:S(2)}, u32[]{:S(2)}) collective-permute-start(bf16[4,32,2176]{2,1,0:T(8,128)(2,1)S(1)} %collective-permute-done.5.refs_2_), channel_id=1, source_target_pairs={{0,1},{1,0},{2,3},{3,2},{4,5},{5,4},{6,7},{7,6},{8,9},{9,8},{10,11... | collective-permute-start | bytes 1671176 | tf_op jit(solution)/shard_map/ppermute | solution.py:24
  77.4 11.4 %collective-permute-start.14 = (bf16[176,512]{1,0:T(8,128)(2,1)S(1)}, bf16[176,512]{1,0:T(8,128)(2,1)S(1)}, u32[]{:S(2)}, u32[]{:S(2)}) collective-permute-start(bf16[176,512]{1,0:T(8,128)(2,1)S(1)} %maximum_select_fusion.5), channel_id=1, source_target_pairs={{0,8},{8,16},{16,24},{24,0},{1,9},{9,17},{17,25},{25,1},{2,10},{10... | collective-permute-start | bytes 540680 | tf_op jit(solution)/shard_map/ppermute | solution.py:24
  77.4 17.6 %collective-permute-start.15 = (bf16[176,512]{1,0:T(8,128)(2,1)S(1)}, bf16[176,512]{1,0:T(8,128)(2,1)S(1)}, u32[]{:S(2)}, u32[]{:S(2)}) collective-permute-start(bf16[176,512]{1,0:T(8,128)(2,1)S(1)} %maximum_select_fusion.5), channel_id=1, source_target_pairs={{0,24},{8,0},{16,8},{24,16},{1,25},{9,1},{17,9},{25,17},{2,26},{10... | collective-permute-start | bytes 540680 | tf_op jit(solution)/shard_map/ppermute | solution.py:24
  95.0 24.3 %collective-permute-start.16 = (bf16[4,32,3072]{2,1,0:T(8,128)(2,1)S(1)}, bf16[4,32,3072]{2,1,0:T(8,128)(2,1)S(1)}, u32[]{:S(2)}, u32[]{:S(2)}) collective-permute-start(bf16[4,32,3072]{2,1,0:T(8,128)(2,1)S(1)} %pad_maximum_fusion.refs_0_), channel_id=1, source_target_pairs={{0,2},{1,5},{2,0},{3,7},{4,6},{5,1},{6,4},{7,3},{8,10},{9,13},{10,... | collective-permute-start | bytes 2359304 | tf_op jit(solution)/shard_map/ppermute | solution.py:46
  97.5 21.7 %collective-permute-start.17 = (bf16[176,512]{1,0:T(8,128)(2,1)S(1)}, bf16[176,512]{1,0:T(8,128)(2,1)S(1)}, u32[]{:S(2)}, u32[]{:S(2)}) collective-permute-start(bf16[176,512]{1,0:T(8,128)(2,1)S(1)} %maximum_select_fusion.5), channel_id=1, source_target_pairs={{0,16},{8,24},{16,0},{24,8},{1,17},{9,25},{17,1},{25,9},{2,18},{10... | collective-permute-start | bytes 540680 | tf_op jit(solution)/shard_map/ppermute | solution.py:24
  123.8 12.2 %collective-permute-start.20 = (bf16[4,32,3072]{2,1,0:T(8,128)(2,1)S(1)}, bf16[4,32,3072]{2,1,0:T(8,128)(2,1)}, u32[]{:S(2)}, u32[]{:S(2)}) collective-permute-start(bf16[4,32,3072]{2,1,0:T(8,128)(2,1)S(1)} %pad_maximum_fusion.refs_0_), channel_id=1, source_target_pairs={{0,4},{1,3},{2,6},{3,1},{4,0},{5,7},{6,2},{7,5},{8,12},{9,11},{10,... | collective-permute-start | bytes 2359304 | tf_op jit(solution)/shard_map/ppermute | solution.py:46
  136.0 18.0 %collective-permute-start.22 = (bf16[4,32,3072]{2,1,0:T(8,128)(2,1)S(1)}, bf16[4,32,3072]{2,1,0:T(8,128)(2,1)}, u32[]{:S(2)}, u32[]{:S(2)}) collective-permute-start(bf16[4,32,3072]{2,1,0:T(8,128)(2,1)S(1)} %collective-permute-done.16.refs_1_), channel_id=1, source_target_pairs={{0,4},{1,3},{2,6},{3,1},{4,0},{5,7},{6,2},{7,5},{8,12},{9,11},{10,... | collective-permute-start | bytes 2359304 | tf_op jit(solution)/shard_map/ppermute | solution.py:46
  139.0 15.0 %collective-permute-start.21 = (bf16[2,272,256]{2,1,0:T(8,128)(2,1)}, bf16[2,272,256]{2,1,0:T(8,128)(2,1)S(1)}, u32[]{:S(2)}, u32[]{:S(2)}) collective-permute-start(bf16[2,272,256]{2,1,0:T(8,128)(2,1)} %fusion.13), channel_id=1, source_target_pairs={{0,4},{4,0},{1,5},{5,1},{2,6},{6,2},{3,7},{7,3},{8,12},{12,8},{9,1... | collective-permute-start | bytes 835592 | tf_op jit(solution)/shard_map/ppermute | solution.py:24
  155.2 12.7 %collective-permute-start.28 = (bf16[4,176,512]{2,1,0:T(8,128)(2,1)S(1)}, bf16[4,176,512]{2,1,0:T(8,128)(2,1)}, u32[]{:S(2)}, u32[]{:S(2)}) collective-permute-start(bf16[4,176,512]{2,1,0:T(8,128)(2,1)S(1)} %pad_maximum_fusion.1.refs_0_), channel_id=1, source_target_pairs={{0,2},{1,5},{2,0},{3,7},{4,6},{5,1},{6,4},{7,3},{8,10},{9,13},{10,... | collective-permute-start | bytes 2162696 | tf_op jit(solution)/shard_map/ppermute | solution.py:46
  168.0 22.0 %collective-permute-start.29 = (bf16[4,176,512]{2,1,0:T(8,128)(2,1)S(1)}, bf16[4,176,512]{2,1,0:T(8,128)(2,1)S(1)}, u32[]{:S(2)}, u32[]{:S(2)}) collective-permute-start(bf16[4,176,512]{2,1,0:T(8,128)(2,1)S(1)} %pad_maximum_fusion.1.refs_0_), channel_id=1, source_target_pairs={{0,4},{1,3},{2,6},{3,1},{4,0},{5,7},{6,2},{7,5},{8,12},{9,11},{10,... | collective-permute-start | bytes 2162696 | tf_op jit(solution)/shard_map/ppermute | solution.py:46
  169.7 20.3 %collective-permute-start.30 = (bf16[4,176,512]{2,1,0:T(8,128)(2,1)}, bf16[4,176,512]{2,1,0:T(8,128)(2,1)S(1)}, u32[]{:S(2)}, u32[]{:S(2)}) collective-permute-start(bf16[4,176,512]{2,1,0:T(8,128)(2,1)} %collective-permute-done.28.refs_1_), channel_id=1, source_target_pairs={{0,4},{1,3},{2,6},{3,1},{4,0},{5,7},{6,2},{7,5},{8,12},{9,11},{10,... | collective-permute-start | bytes 2162696 | tf_op jit(solution)/shard_map/ppermute | solution.py:46
  172.8 17.8 %collective-permute-start.32 = (bf16[4,176,512]{2,1,0:T(8,128)(2,1)}, bf16[4,176,512]{2,1,0:T(8,128)(2,1)S(1)}, u32[]{:S(2)}, u32[]{:S(2)}) collective-permute-start(bf16[4,176,512]{2,1,0:T(8,128)(2,1)} %collective-permute-done.28.refs_1_), channel_id=1, source_target_pairs={{0,1},{1,0},{2,3},{3,2},{4,5},{5,4},{6,7},{7,6},{8,9},{9,8},{10,11... | collective-permute-start | bytes 2162696 | tf_op jit(solution)/shard_map/ppermute | solution.py:24
  227.3 19.3 %collective-permute-start.35 = (bf16[384,2816]{1,0:T(8,128)(2,1)}, bf16[384,2816]{1,0:T(8,128)(2,1)}, u32[]{:S(2)}, u32[]{:S(2)}) collective-permute-start(bf16[384,2816]{1,0:T(8,128)(2,1)} %get-tuple-element.204.refs_2_), channel_id=1, source_target_pairs={{0,1},{1,0},{2,3},{3,2},{4,5},{5,4},{6,7},{7,6},{8,9},{9,8},{10,11... | collective-permute-start | bytes 6488072 | tf_op jit(solution)/shard_map/ppermute | solution.py:24
  227.4 19.1 %collective-permute-start.36 = (bf16[384,2816]{1,0:T(8,128)(2,1)}, bf16[384,2816]{1,0:T(8,128)(2,1)}, u32[]{:S(2)}, u32[]{:S(2)}) collective-permute-start(bf16[384,2816]{1,0:T(8,128)(2,1)} %get-tuple-element.216.refs_2_), channel_id=1, source_target_pairs={{0,1},{1,0},{2,3},{3,2},{4,5},{5,4},{6,7},{7,6},{8,9},{9,8},{10,11... | collective-permute-start | bytes 6488072 | tf_op jit(solution)/shard_map/ppermute | solution.py:24
  241.9 19.6 %collective-permute-start.40 = (bf16[8,176,512]{2,1,0:T(8,128)(2,1)}, bf16[8,176,512]{2,1,0:T(8,128)(2,1)S(1)}, u32[]{:S(2)}, u32[]{:S(2)}) collective-permute-start(bf16[8,176,512]{2,1,0:T(8,128)(2,1)} %get-tuple-element.186), channel_id=1, source_target_pairs={{0,2},{1,5},{2,0},{3,7},{4,6},{5,1},{6,4},{7,3},{8,10},{9,13},{10,... | collective-permute-start | bytes 4325384 | tf_op jit(solution)/shard_map/ppermute | solution.py:46
  266.1 11.4 %collective-permute-start.43 = (bf16[4,176,512]{2,1,0:T(8,128)(2,1)S(1)}, bf16[4,176,512]{2,1,0:T(8,128)(2,1)S(1)}, u32[]{:S(2)}, u32[]{:S(2)}) collective-permute-start(bf16[4,176,512]{2,1,0:T(8,128)(2,1)S(1)} %add_convert_fusion.7), channel_id=1, source_target_pairs={{0,4},{1,3},{2,6},{3,1},{4,0},{5,7},{6,2},{7,5},{8,12},{9,11},{10,... | collective-permute-start | bytes 2162696 | tf_op jit(solution)/shard_map/ppermute | solution.py:46
  278.4 20.0 %collective-permute-start.45 = (bf16[8,32,2816]{2,1,0:T(8,128)(2,1)}, bf16[8,32,2816]{2,1,0:T(8,128)(2,1)S(1)}, u32[]{:S(2)}, u32[]{:S(2)}) collective-permute-start(bf16[8,32,2816]{2,1,0:T(8,128)(2,1)} %get-tuple-element.211), channel_id=1, source_target_pairs={{0,2},{1,5},{2,0},{3,7},{4,6},{5,1},{6,4},{7,3},{8,10},{9,13},{10,... | collective-permute-start | bytes 4325384 | tf_op jit(solution)/shard_map/ppermute | solution.py:46
  300.9 11.9 %collective-permute-start.46 = (bf16[2,272,256]{2,1,0:T(8,128)(2,1)}, bf16[2,272,256]{2,1,0:T(8,128)(2,1)}, u32[]{:S(2)}, u32[]{:S(2)}) collective-permute-start(bf16[2,272,256]{2,1,0:T(8,128)(2,1)} %maximum_select_fusion.4), channel_id=1, source_target_pairs={{0,1},{1,0},{2,3},{3,2},{4,5},{5,4},{6,7},{7,6},{8,9},{9,8},{10,11... | collective-permute-start | bytes 835592 | tf_op jit(solution)/shard_map/ppermute | solution.py:24
  315.5 20.0 %collective-permute-start.48 = (bf16[8,32,2816]{2,1,0:T(8,128)(2,1)}, bf16[8,32,2816]{2,1,0:T(8,128)(2,1)S(1)}, u32[]{:S(2)}, u32[]{:S(2)}) collective-permute-start(bf16[8,32,2816]{2,1,0:T(8,128)(2,1)} %get-tuple-element.229), channel_id=1, source_target_pairs={{0,2},{1,5},{2,0},{3,7},{4,6},{5,1},{6,4},{7,3},{8,10},{9,13},{10,... | collective-permute-start | bytes 4325384 | tf_op jit(solution)/shard_map/ppermute | solution.py:46
  316.4 19.6 %collective-permute-start.47 = (bf16[384,1024]{1,0:T(8,128)(2,1)S(1)}, bf16[384,1024]{1,0:T(8,128)(2,1)S(1)}, u32[]{:S(2)}, u32[]{:S(2)}) collective-permute-start(bf16[384,1024]{1,0:T(8,128)(2,1)S(1)} %copy-done), channel_id=1, source_target_pairs={{0,1},{1,0},{2,3},{3,2},{4,5},{5,4},{6,7},{7,6},{8,9},{9,8},{10,11... | collective-permute-start | bytes 2359304 | tf_op jit(solution)/shard_map/ppermute | solution.py:24
  317.0 19.1 %collective-permute-start.54 = (bf16[384,1024]{1,0:T(8,128)(2,1)}, bf16[384,1024]{1,0:T(8,128)(2,1)}, u32[]{:S(2)}, u32[]{:S(2)}) collective-permute-start(bf16[384,1024]{1,0:T(8,128)(2,1)} %get-tuple-element.235.refs_2_), channel_id=1, source_target_pairs={{0,1},{1,0},{2,3},{3,2},{4,5},{5,4},{6,7},{7,6},{8,9},{9,8},{10,11... | collective-permute-start | bytes 2359304 | tf_op jit(solution)/shard_map/ppermute | solution.py:24
  317.0 19.6 %collective-permute-start.55 = (bf16[384,1024]{1,0:T(8,128)(2,1)S(1)}, bf16[384,1024]{1,0:T(8,128)(2,1)}, u32[]{:S(2)}, u32[]{:S(2)}) collective-permute-start(bf16[384,1024]{1,0:T(8,128)(2,1)S(1)} %copy-done.7), channel_id=1, source_target_pairs={{0,1},{1,0},{2,3},{3,2},{4,5},{5,4},{6,7},{7,6},{8,9},{9,8},{10,11... | collective-permute-start | bytes 2359304 | tf_op jit(solution)/shard_map/ppermute | solution.py:24
  317.5 19.1 %collective-permute-start.56 = (bf16[384,1024]{1,0:T(8,128)(2,1)S(1)}, bf16[384,1024]{1,0:T(8,128)(2,1)}, u32[]{:S(2)}, u32[]{:S(2)}) collective-permute-start(bf16[384,1024]{1,0:T(8,128)(2,1)S(1)} %copy-done.3), channel_id=1, source_target_pairs={{0,1},{1,0},{2,3},{3,2},{4,5},{5,4},{6,7},{7,6},{8,9},{9,8},{10,11... | collective-permute-start | bytes 2359304 | tf_op jit(solution)/shard_map/ppermute | solution.py:24
  335.5 16.8 %collective-permute-start.49 = (bf16[384,1024]{1,0:T(8,128)(2,1)}, bf16[384,1024]{1,0:T(8,128)(2,1)}, u32[]{:S(2)}, u32[]{:S(2)}) collective-permute-start(bf16[384,1024]{1,0:T(8,128)(2,1)} %get-tuple-element.243.refs_2_.refs_0_), channel_id=1, source_target_pairs={{0,1},{1,0},{2,3},{3,2},{4,5},{5,4},{6,7},{7,6},{8,9},{9,8},{10,11... | collective-permute-start | bytes 2359304 | tf_op jit(solution)/shard_map/ppermute | solution.py:24
  336.0 16.3 %collective-permute-start.50 = (bf16[384,1024]{1,0:T(8,128)(2,1)}, bf16[384,1024]{1,0:T(8,128)(2,1)S(1)}, u32[]{:S(2)}, u32[]{:S(2)}) collective-permute-start(bf16[384,1024]{1,0:T(8,128)(2,1)} %get-tuple-element.245.refs_4_.refs_1_), channel_id=1, source_target_pairs={{0,1},{1,0},{2,3},{3,2},{4,5},{5,4},{6,7},{7,6},{8,9},{9,8},{10,11... | collective-permute-start | bytes 2359304 | tf_op jit(solution)/shard_map/ppermute | solution.py:24
  336.1 16.2 %collective-permute-start.51 = (bf16[384,1024]{1,0:T(8,128)(2,1)}, bf16[384,1024]{1,0:T(8,128)(2,1)}, u32[]{:S(2)}, u32[]{:S(2)}) collective-permute-start(bf16[384,1024]{1,0:T(8,128)(2,1)} %get-tuple-element.247.refs_6_.refs_2_), channel_id=1, source_target_pairs={{0,1},{1,0},{2,3},{3,2},{4,5},{5,4},{6,7},{7,6},{8,9},{9,8},{10,11... | collective-permute-start | bytes 2359304 | tf_op jit(solution)/shard_map/ppermute | solution.py:24
  336.5 15.8 %collective-permute-start.53 = (bf16[384,1024]{1,0:T(8,128)(2,1)}, bf16[384,1024]{1,0:T(8,128)(2,1)S(1)}, u32[]{:S(2)}, u32[]{:S(2)}) collective-permute-start(bf16[384,1024]{1,0:T(8,128)(2,1)} %get-tuple-element.251.refs_12_), channel_id=1, source_target_pairs={{0,1},{1,0},{2,3},{3,2},{4,5},{5,4},{6,7},{7,6},{8,9},{9,8},{10,11... | collective-permute-start | bytes 2359304 | tf_op jit(solution)/shard_map/ppermute | solution.py:24
  340.9 11.4 %collective-permute-start.57 = (bf16[4,32,2816]{2,1,0:T(8,128)(2,1)S(1)}, bf16[4,32,2816]{2,1,0:T(8,128)(2,1)}, u32[]{:S(2)}, u32[]{:S(2)}) collective-permute-start(bf16[4,32,2816]{2,1,0:T(8,128)(2,1)S(1)} %add_convert_fusion.6), channel_id=1, source_target_pairs={{0,4},{1,3},{2,6},{3,1},{4,0},{5,7},{6,2},{7,5},{8,12},{9,11},{10,... | collective-permute-start | bytes 2162696 | tf_op jit(solution)/shard_map/ppermute | solution.py:46
  352.4 22.9 %collective-permute-start.61 = (bf16[8,32,2048]{2,1,0:T(8,128)(2,1)}, bf16[8,32,2048]{2,1,0:T(8,128)(2,1)}, u32[]{:S(2)}, u32[]{:S(2)}) collective-permute-start(bf16[8,32,2048]{2,1,0:T(8,128)(2,1)} %get-tuple-element.260), channel_id=1, source_target_pairs={{0,2},{1,5},{2,0},{3,7},{4,6},{5,1},{6,4},{7,3},{8,10},{9,13},{10,... | collective-permute-start | bytes 3145736 | tf_op jit(solution)/shard_map/ppermute | solution.py:46
  354.3 19.4 %collective-permute-start.60 = (bf16[4,32,2816]{2,1,0:T(8,128)(2,1)}, bf16[4,32,2816]{2,1,0:T(8,128)(2,1)}, u32[]{:S(2)}, u32[]{:S(2)}) collective-permute-start(bf16[4,32,2816]{2,1,0:T(8,128)(2,1)} %add_convert_fusion.5), channel_id=1, source_target_pairs={{0,4},{1,3},{2,6},{3,1},{4,0},{5,7},{6,2},{7,5},{8,12},{9,11},{10,... | collective-permute-start | bytes 2162696 | tf_op jit(solution)/shard_map/ppermute | solution.py:46
  357.0 63.5 %reduce-scatter.10.cloned.1.call-start = ((), (), s32[]{:S(2)}) async-start(), calls=%async_computation.7 | async-start | bytes 901120 | tf_op jit(solution)/shard_map/reduce_scatter | solution.py:154
  375.3 26.9 %collective-permute-start.62 = (bf16[8,32,3200]{2,1,0:T(8,128)(2,1)}, bf16[8,32,3200]{2,1,0:T(8,128)(2,1)S(1)}, u32[]{:S(2)}, u32[]{:S(2)}) collective-permute-start(bf16[8,32,3200]{2,1,0:T(8,128)(2,1)} %get-tuple-element.263), channel_id=1, source_target_pairs={{0,2},{1,5},{2,0},{3,7},{4,6},{5,1},{6,4},{7,3},{8,10},{9,13},{10,... | collective-permute-start | bytes 4915208 | tf_op jit(solution)/shard_map/ppermute | solution.py:46
  378.4 47.2 %reduce-scatter.12.cloned.1.call-start = ((), (), s32[]{:S(2)}) async-start(), calls=%async_computation.8 | async-start | bytes 901120 | tf_op jit(solution)/shard_map/reduce_scatter | solution.py:154
  380.7 15.2 %collective-permute-start.63 = (bf16[4,32,2048]{2,1,0:T(8,128)(2,1)}, bf16[4,32,2048]{2,1,0:T(8,128)(2,1)}, u32[]{:S(2)}, u32[]{:S(2)}) collective-permute-start(bf16[4,32,2048]{2,1,0:T(8,128)(2,1)} %add_convert_fusion.9), channel_id=1, source_target_pairs={{0,4},{1,3},{2,6},{3,1},{4,0},{5,7},{6,2},{7,5},{8,12},{9,11},{10,... | collective-permute-start | bytes 1572872 | tf_op jit(solution)/shard_map/ppermute | solution.py:46
  384.3 64.0 %reduce-scatter.8.cloned.1.call-start = ((), (), s32[]{:S(2)}) async-start(), calls=%async_computation.6 | async-start | bytes 655360 | tf_op jit(solution)/shard_map/reduce_scatter | solution.py:154
  403.3 12.6 %collective-permute-start.64 = (bf16[4,32,3200]{2,1,0:T(8,128)(2,1)}, bf16[4,32,3200]{2,1,0:T(8,128)(2,1)S(1)}, u32[]{:S(2)}, u32[]{:S(2)}) collective-permute-start(bf16[4,32,3200]{2,1,0:T(8,128)(2,1)} %add_convert_fusion.1), channel_id=1, source_target_pairs={{0,4},{1,3},{2,6},{3,1},{4,0},{5,7},{6,2},{7,5},{8,12},{9,11},{10,... | collective-permute-start | bytes 2457608 | tf_op jit(solution)/shard_map/ppermute | solution.py:46
  406.7 65.5 %reduce-scatter.16.cloned.1.call-start = ((), (), s32[]{:S(2)}) async-start(), calls=%async_computation.10 | async-start | bytes 1024000 | tf_op jit(solution)/shard_map/reduce_scatter | solution.py:154
  (88 other events, 1096.4 us)
Sparse Core Ops, SparseCore 0:
  11.5 118.8 all-gather.1
  357.1 20.4 reduce-scatter.13
  379.9 21.6 reduce-scatter.9
  403.8 21.7 reduce-scatter.11
  427.7 20.5 reduce-scatter.7
  450.5 21.7 reduce-scatter.15

commit v3 on v2

--- a/solution.py
+++ b/solution.py
@@ -12,6 +12,7 @@
 HEAD_V = 256
 GROUP = 64
 LANES = 128
+TOGETHER = 2
 AXES = ("z", "y", "x", "c")
 VMEM = 56 * 1024 * 1024
 QUICK = pl.CostEstimate(flops=0, bytes_accessed=0, transcendentals=0)
@@ -133,25 +134,44 @@
         self.arrived = cross(after(done, self.blocks[0]), False) if square_plane() else ()
         return self.arrived
 
-    def second(self, done=()):
+    def second(self, done=(), *others):
+        parts = (self, *others)
         if not square_plane():
-            self.through = ()
+            for p in parts:
+                p.through = ()
             return ()
         depth = lax.axis_size("z")
-        arrived, kept = after(done, self.arrived, self.blocks[1])
-        self.through = cross((wide(kept) + wide(arrived[depth:])).astype(BF16), True)
-        return self.through
-
-    def third(self, done=()):
-        width = self.blocks[-1].shape[-1]
+        sums = []
+        for p in parts:
+            arrived, kept = after(done, p.arrived, p.blocks[1])
+            sums.append((wide(kept) + wide(arrived[depth:])).astype(BF16))
+        through = cross(sums[0] if len(sums) == 1 else jnp.concatenate(sums, axis=2), True)
+        at = 0
+        for p, part in zip(parts, sums):
+            p.through = through[:, :, at : at + part.shape[2]]
+            at += part.shape[2]
+        return through
+
+    def total(self):
+        depth = lax.axis_size("z")
+        return (wide(self.blocks[2]) + wide(self.arrived[:depth]) + wide(self.through)).astype(BF16)
+
+    def third(self, *others):
+        parts = (self, *others)
+        if square_plane():
+            axes, totals = "z", [p.total() for p in parts]
+        else:
+            axes, totals = ("z", "y", "x"), [p.blocks[0] for p in parts]
+        total = totals[0] if len(totals) == 1 else jnp.concatenate(totals, axis=2)
+        return lax.psum_scatter(total.reshape(-1, total.shape[-1]), axes, scatter_dimension=0, tiled=True)
+
+    def third_terms(self):
         if not square_plane():
-            total = self.blocks[0].reshape(-1, width)
-            return wide(lax.psum_scatter(total, ("z", "y", "x"), scatter_dimension=0, tiled=True))
+            return [self.third()]
         depth = lax.axis_size("z")
-        arrived, through = after(done, self.arrived, self.through)
-        total = wide(self.blocks[2]) + wide(arrived[:depth]) + wide(through)
-        total = total.astype(BF16).reshape(-1, width)
-        return wide(lax.psum_scatter(total, "z", scatter_dimension=0, tiled=True))
+        total, z = self.total(), lax.axis_index("z")
+        block = [lax.dynamic_index_in_dim(total, (z + k) % depth, 0, False) for k in range(depth)]
+        return [block[0]] + [shift(block[k], "z", k) for k in range(1, depth)]
 
 
 def weight_grads(groups, tile, halves=False, table=None):
@@ -163,7 +183,7 @@
     lefts = [left for left, _ in groups]
     rights = [right for _, group in groups for right in group]
     owner = [n for n, (_, group) in enumerate(groups) for _ in group]
-    tokens, height = lefts[0][0].shape
+    height, tokens = lefts[0][0].shape
     each = rights[0][0].shape[1] // (2 if halves else 1)
     width = each * len(rights)
     rows = height // (count if halves else 2 * count)
@@ -172,7 +192,7 @@
     if rows % 16:
         products = []
         for n, right in zip(owner, rights):
-            product = tn(jnp.concatenate(lefts[n]), jnp.concatenate(right)).astype(BF16)
+            product = nn(jnp.concatenate(lefts[n], axis=1), jnp.concatenate(right)).astype(BF16)
             if halves:
                 product = lax.dynamic_slice_in_dim(product, c * each, each, 1).reshape(count, rows, each)
             else:
@@ -181,7 +201,7 @@
         if table is not None:
             product = wide(table[1])
             for left, right in table[0]:
-                product = product + tn(jnp.concatenate(left), jnp.concatenate(right))
+                product = product + nn(jnp.concatenate(left, axis=1), jnp.concatenate(right))
             product = product.astype(BF16).reshape(count, 2, rows, LANES)
             products.append(lax.dynamic_index_in_dim(product, c, 1, False))
         product = jnp.take(jnp.concatenate(products, axis=2), chips, axis=0)
@@ -205,17 +225,16 @@
     def body(numbers_ref, *refs):
         left_refs, right_refs = refs[: 2 * len(lefts)], refs[2 * len(lefts) : len(flat)]
         narrow_refs = refs[len(flat) : len(flat) + len(narrow)]
-        outs, (turned, chosen, total, based) = refs[len(flat) + len(narrow) : -4], refs[-4:]
+        outs, (chosen, total, based) = refs[len(flat) + len(narrow) : -3], refs[-3:]
         step = pl.program_id(0)
 
         def start(at):
             return pl.ds(pl.multiple_of(numbers_ref[at], 16), rows)
 
-        def turn(lo_ref, ls_ref):
-            turned[:, :tokens] = lo_ref[...].T
-            turned[:, tokens:] = ls_ref[...].T
+        def choose(lo_ref, ls_ref):
             for at in range(count):
-                chosen[at * rows : (at + 1) * rows, :] = turned[start(at), :]
+                chosen[at * rows : (at + 1) * rows, :tokens] = lo_ref[start(at), :]
+                chosen[at * rows : (at + 1) * rows, tokens:] = ls_ref[start(at), :]
 
         def put(product, columns):
             at = 0
@@ -229,7 +248,7 @@
 
         def term(n):
             lo_ref, ls_ref, ro_ref, rs_ref = narrow_refs[4 * n : 4 * n + 4]
-            turn(lo_ref, ls_ref)
+            choose(lo_ref, ls_ref)
             both = jnp.concatenate([ro_ref[...], rs_ref[...]], axis=0)
             product = nn(chosen[...], both)
             if n == 0:
@@ -242,7 +261,7 @@
                 put((total[...] + wide(based[...])).astype(BF16), LANES)
 
         for n in range(len(lefts)):
-            pl.when(step == owner.index(n) * strips)(partial(turn, *left_refs[2 * n : 2 * n + 2]))
+            pl.when(step == owner.index(n) * strips)(partial(choose, *left_refs[2 * n : 2 * n + 2]))
         if len(rights) == 1:
             strip(*right_refs)
         else:
@@ -269,7 +288,6 @@
             in_specs=[full(a) for left in lefts for a in left] + right_specs + [full(a) for a in narrow],
             out_specs=[pl.BlockSpec((n, rows, tile), lambda n, s: (0, 0, jnp.minimum(n, last))) for n, _, _ in outs],
             scratch_shapes=[
-                pltpu.VMEM((height, 2 * tokens), BF16),
                 pltpu.VMEM((count * rows, 2 * tokens), BF16),
                 pltpu.VMEM((count * rows, LANES), F32),
                 pltpu.VMEM((count * rows, LANES), BF16),
@@ -322,8 +340,24 @@
     return pl.BlockSpec(shape, index)
 
 
-def by_head(rows):
-    return spec((rows, HEAD_K), lambda h: (0, h))
+def by_head(rows, start=0):
+    return spec((rows, TOGETHER * HEAD_K), lambda h: (0, start + h))
+
+
+def spans(count=TOGETHER):
+    return [slice(n * HEAD_K, (n + 1) * HEAD_K) for n in range(count)]
+
+
+def by_spans(function, *arrays):
+    return jnp.concatenate([function(*[a[:, at] for a in arrays]) for at in spans()], axis=1)
+
+
+def head_mean(values):
+    return by_spans(lambda a: jnp.broadcast_to(jnp.mean(a, axis=1, keepdims=True), a.shape), values)
+
+
+def repeated(row):
+    return jnp.concatenate([row] * TOGETHER, axis=1)
 
 
 def kernel_call(body, grid, ins, outs, scratch=()):
@@ -348,21 +382,21 @@
     return jnp.where(column == row + start, 1.0, 0.0).astype(BF16)
 
 
-def first_weights(w_key, w_value, rank_in, rank_out, vectors):
+def first_weights(w_key, w_value, turned_in, rank_out, vectors):
     rows, width = w_key.shape
-    rank = rank_in.shape[1]
+    rank = turned_in.shape[0]
 
     def body(wk, wv, ri, ro, *refs):
         vector_refs, out = refs[:-1], refs[-1]
         out[:, :width] = wk[...]
         out[:, width : 2 * width] = wv[...]
-        table = nn(ri[...], unit_columns(rank, LANES, 0)) + tn(ro[...], unit_columns(rank, LANES, rank))
+        table = tn(ri[...], unit_columns(rank, LANES, 0)) + tn(ro[...], unit_columns(rank, LANES, rank))
         for n, v in enumerate(vector_refs):
             mine = unit_columns(v.shape[1], rows, 0)
             table = table + tn(nn(v[...], mine).astype(BF16), unit_columns(1, LANES, 2 * rank + n))
         out[:, 2 * width :] = table.astype(BF16)
 
-    ins = [w_key, w_value, rank_in, rank_out, *[v.reshape(1, -1) for v in vectors]]
+    ins = [w_key, w_value, turned_in, rank_out, *[v.reshape(1, -1) for v in vectors]]
     shape = (rows, 2 * width + LANES)
     return kernel_call(body, (1,), [(a, spec(a.shape)) for a in ins], [(shape, BF16, spec(shape))])[0]
 
@@ -370,9 +404,12 @@
 def project(tokens, weights, marks, rank):
     rows, width = tokens.shape
     heads = width // HEAD_K
+    steps = heads // TOGETHER
     at_table = 2 * width // LANES
 
-    def body(x_ref, wk, wv, table, part_ref, marks_ref, n_out, low_out, k_out, v_out, g_out, m_out, vectors_out):
+    def body(
+        x_ref, wk, wv, table, part_ref, marks_ref, n_out, turned_out, low_out, k_out, v_out, g_out, m_out, vectors_out
+    ):
         @pl.when(pl.program_id(0) == 0)
         def _():
             vectors = nt(unit_columns(8, LANES, 2 * rank), table[...])
@@ -380,6 +417,7 @@
             x = x_ref[...].astype(F32)
             scale = lax.rsqrt(jnp.mean(x * x, axis=1, keepdims=True) + 1e-06)
             n_out[...] = (x * scale * vectors[1:2]).astype(BF16)
+            turned_out[...] = n_out[...].T
             low = nn(n_out[...], table[...]).astype(BF16)
             lane = lax.broadcasted_iota(jnp.int32, (LANES, LANES), 1)
             row = lax.broadcasted_iota(jnp.int32, (LANES, LANES), 0)
@@ -398,28 +436,30 @@
         later = summed(triangle(rows, lambda i, j: j > i), decay)
         last = marks_ref[:, 4:5]
         finish = (key.astype(F32) * jnp.exp(later) * last).astype(BF16)
-        m_out[0, :HEAD_V] = tn(value, finish).astype(BF16)
         total = jnp.exp(jnp.sum(decay, axis=0, keepdims=True)) * marks_ref[rows - 1 :, 3:4]
-        m_out[0, HEAD_V:] = jnp.broadcast_to(total, (MESSAGE - HEAD_V, HEAD_K)).astype(BF16)
+        for n, at in enumerate(spans()):
+            m_out[n, :HEAD_V] = tn(value[:, at], finish[:, at]).astype(BF16)
+            m_out[n, HEAD_V:] = jnp.broadcast_to(total[:, at], (MESSAGE - HEAD_V, HEAD_K)).astype(BF16)
 
     return kernel_call(
         body,
-        (heads,),
+        (steps,),
         [
             (tokens, spec((rows, width))),
             (weights, by_head(width)),
-            (weights, spec((width, HEAD_K), lambda h: (0, heads + h))),
+            (weights, by_head(width, steps)),
             (weights, spec((width, LANES), lambda h: (0, at_table))),
-            (weights, spec((HEAD_K, LANES), lambda h: (h, at_table))),
+            (weights, spec((TOGETHER * HEAD_K, LANES), lambda h: (h, at_table))),
             (marks, spec(marks.shape)),
         ],
         [
             ((rows, width), BF16, spec((rows, width))),
+            ((width, rows), BF16, spec((width, rows))),
             ((rows, LANES), BF16, spec((rows, LANES))),
             ((rows, width), BF16, by_head(rows)),
             ((rows, width), BF16, by_head(rows)),
             ((rows, width), F32, by_head(rows)),
-            ((heads, MESSAGE, HEAD_K), BF16, spec((1, MESSAGE, HEAD_K), lambda h: (h, 0, 0))),
+            ((heads, MESSAGE, HEAD_K), BF16, spec((TOGETHER, MESSAGE, HEAD_K), lambda h: (h, 0, 0))),
             ((8, width), F32, spec((8, width))),
         ],
     )
@@ -432,41 +472,46 @@
 def mixer(normed, keys, values, gate_pre, entered, weights, head_gain, tokens, gain, marks, doc_row):
     rows, wide = tokens.shape
     heads = wide // HEAD_K
+    steps = heads // TOGETHER
     blocks = rows // GROUP
 
     def body(
         n_ref, k_ref, v_ref, g_ref, s_ref, wq, ws, hg_ref, wo, x_ref, gain_ref, marks_ref, doc_ref,
-        q_ref, mixed_out, swish_out, gated_out, hidden_out, two_out, states_out, state, total,
+        q_ref, mixed_out, swish_out, gated_out, hidden_out, two_out, two_turned, states_out, state, total,
     ):
         h = pl.program_id(0)
         q_ref[...] = nn(n_ref[...], wq[...]).astype(BF16)
         swish = nn(n_ref[...], ws[...])
         swish_out[...] = swish
         along = summed(triangle(rows, lambda i, j: j <= i, GROUP), log_decay(g_ref[...]))
-        state[...] = s_ref[0].astype(F32)
         causal = triangle(GROUP, lambda i, j: j <= i) > 0
+        run_all, key_all = along, k_ref[...].astype(F32)
+        query_all = (scaled(q_ref[...]) * jnp.exp(run_all)).astype(BF16)
+        key_in_all = (key_all * jnp.exp(-run_all)).astype(BF16)
+        for head in range(TOGETHER):
+            state[head] = s_ref[head].astype(F32)
         for n in range(blocks):
             at = slice(n * GROUP, (n + 1) * GROUP)
             marks_n = marks_ref[at]
-            run = along[at]
+            allowed = causal & (marks_n[:, 0:1] == doc_ref[:, at])
+            run = run_all[at]
             end = run[GROUP - 1 :]
-            key = k_ref[at].astype(F32)
-            value = v_ref[at]
-            query_in = (scaled(q_ref[at]) * jnp.exp(run)).astype(BF16)
-            key_in = (key * jnp.exp(-run)).astype(BF16)
-            key_out = (key * jnp.exp(end - run) * marks_n[:, 2:3]).astype(BF16)
-            allowed = causal & (marks_n[:, 0:1] == doc_ref[:, at])
-            scores = jnp.where(allowed, nt(query_in, key_in), 0.0).astype(BF16)
-            before = state[...].astype(BF16)
-            states_out[0, n] = before
-            mixed_out[at] = nn(scores, value) + marks_n[:, 1:2] * nt(query_in, before)
+            key_out_all = (key_all[at] * jnp.exp(end - run) * marks_n[:, 2:3]).astype(BF16)
             kept = marks_n[GROUP - 1 :, 1:2] * jnp.exp(end)
-            state[...] = kept * state[...] + tn(value, key_out)
-        states_out[0, blocks] = state[...].astype(BF16)
+            for head, lanes in enumerate(spans()):
+                value = v_ref[at, lanes]
+                query_in = query_all[at, lanes]
+                scores = jnp.where(allowed, nt(query_in, key_in_all[at, lanes]), 0.0).astype(BF16)
+                before = state[head].astype(BF16)
+                states_out[head, n] = before
+                mixed_out[at, lanes] = nn(scores, value) + marks_n[:, 1:2] * nt(query_in, before)
+                state[head] = kept[:, lanes] * state[head] + tn(value, key_out_all[:, lanes])
+        for head in range(TOGETHER):
+            states_out[head, blocks] = state[head].astype(BF16)
         mixed = mixed_out[...]
-        norm = lax.rsqrt(jnp.mean(mixed * mixed, axis=1, keepdims=True) + 1e-05)
-        gated = (mixed * norm * hg_ref[...] * (swish * sigmoid(swish))).astype(BF16)
-        gated_out[...] = gated
+        norm = lax.rsqrt(head_mean(mixed * mixed) + 1e-05)
+        gated = (mixed * norm * repeated(hg_ref[...]) * (swish * sigmoid(swish))).astype(BF16)
+        gated_out[...] = gated.T
         part = nn(gated, wo[...])
 
         @pl.when(h == 0)
@@ -477,26 +522,27 @@
         def _():
             total[...] += part
 
-        @pl.when(h == heads - 1)
+        @pl.when(h == steps - 1)
         def _():
             hidden = total[...]
             hidden_out[...] = hidden
             scale = lax.rsqrt(jnp.mean(hidden * hidden, axis=1, keepdims=True) + 1e-06)
             two_out[...] = (hidden * scale * gain_ref[...]).astype(BF16)
+            two_turned[...] = two_out[...].T
 
     return kernel_call(
         body,
-        (heads,),
+        (steps,),
         [
             (normed, spec((rows, wide))),
             (keys, by_head(rows)),
             (values, by_head(rows)),
             (gate_pre, by_head(rows)),
-            (entered, spec((1, HEAD_V, HEAD_K), lambda h: (h, 0, 0))),
+            (entered, spec((TOGETHER, HEAD_V, HEAD_K), lambda h: (h, 0, 0))),
             (weights, by_head(wide)),
-            (weights, spec((wide, HEAD_V), lambda h: (0, heads + h))),
+            (weights, by_head(wide, steps)),
             (head_gain, spec((1, HEAD_V))),
-            (weights, spec((HEAD_V, wide), lambda h: (h, 2))),
+            (weights, spec((TOGETHER * HEAD_V, wide), lambda h: (h, 2))),
             (tokens, spec((rows, wide))),
             (gain, spec((1, wide))),
             (marks, spec(marks.shape)),
@@ -506,19 +552,20 @@
             ((rows, wide), BF16, by_head(rows)),
             ((rows, wide), F32, by_head(rows)),
             ((rows, wide), F32, by_head(rows)),
-            ((rows, wide), BF16, by_head(rows)),
+            ((wide, rows), BF16, spec((TOGETHER * HEAD_V, rows), lambda h: (h, 0))),
             ((rows, wide), F32, spec((rows, wide))),
             ((rows, wide), BF16, spec((rows, wide))),
-            ((heads, blocks + 1, HEAD_V, HEAD_K), BF16, spec((1, blocks + 1, HEAD_V, HEAD_K), lambda h: (h, 0, 0, 0))),
+            ((wide, rows), BF16, spec((wide, rows))),
+            ((heads, blocks + 1, HEAD_V, HEAD_K), BF16, spec((TOGETHER, blocks + 1, HEAD_V, HEAD_K), lambda h: (h, 0, 0, 0))),
         ],
-        [pltpu.VMEM((HEAD_V, HEAD_K), F32), pltpu.VMEM((rows, wide), F32)],
+        [pltpu.VMEM((TOGETHER, HEAD_V, HEAD_K), F32), pltpu.VMEM((rows, wide), F32)],
     )
 
 
 def feed(normed_two, cotangent, w_both, w_down, hidden, gain):
     rows, wide = hidden.shape
     inner = w_both.shape[1] // 2
-    tile = 256
+    tile = inner // 2 if inner % 256 == 0 else inner
     steps = inner // tile
 
     def body(
@@ -532,7 +579,7 @@
         soft = sigmoid(gate)
         silu = gate * soft
         product = (silu * up).astype(BF16)
-        inner_out[...] = product
+        inner_out[...] = product.T
         grad = nt(c_ref[...], wd[...])
         grad_up = (grad * silu).astype(BF16)
         grad_gate = (grad * up * (soft * (1.0 + gate * (1.0 - soft)))).astype(BF16)
@@ -580,7 +627,7 @@
         ],
         [
             ((rows, wide), BF16, whole),
-            ((rows, inner), BF16, column),
+            ((inner, rows), BF16, spec((tile, rows), lambda n: (n, 0))),
             ((rows, inner), BF16, column),
             ((rows, inner), BF16, column),
             ((rows, wide), F32, whole),
@@ -593,6 +640,7 @@
 def head_back(grad_low, weights, mixed, swish, head_gain, queries, gate_pre, decays, marks):
     rows, wide = mixed.shape
     heads = wide // HEAD_K
+    steps = heads // TOGETHER
 
     def body(gh_ref, wo, mixed_ref, swish_ref, hg_ref, q_ref, g_ref, d_ref, marks_ref, gm_out, gs_out, hg_out, m_out):
         grad = nt(gh_ref[...], wo[...])
@@ -600,11 +648,12 @@
         swish = swish_ref[...]
         soft = sigmoid(swish)
         silu = swish * soft
-        norm = lax.rsqrt(jnp.mean(mixed * mixed, axis=1, keepdims=True) + 1e-05)
+        norm = lax.rsqrt(head_mean(mixed * mixed) + 1e-05)
         unit = mixed * norm
-        gain = hg_ref[...]
+        gain = repeated(hg_ref[...])
         gs_out[...] = (grad * unit * gain * (soft * (1.0 + swish * (1.0 - soft)))).astype(BF16)
         by_gain = jnp.sum(grad * unit * silu, axis=0, keepdims=True)
+        by_gain = sum(by_gain[:, at] for at in spans())
 
         @pl.when(pl.program_id(0) == 0)
         def _():
@@ -615,32 +664,34 @@
             hg_out[...] += by_gain
 
         inner = grad * gain * silu
-        grad_mixed = norm * (inner - unit * jnp.mean(inner * unit, axis=1, keepdims=True))
+        grad_mixed = norm * (inner - unit * head_mean(inner * unit))
         gm_out[...] = grad_mixed.astype(BF16)
         along = summed(triangle(rows, lambda i, j: j <= i), log_decay(g_ref[...]))
         query_in = (scaled(q_ref[...]) * jnp.exp(along)).astype(BF16)
-        m_out[0, :HEAD_V] = tn((grad_mixed * marks_ref[:, 3:4]).astype(BF16), query_in).astype(BF16)
-        m_out[0, HEAD_V:] = d_ref[0]
+        entry = (grad_mixed * marks_ref[:, 3:4]).astype(BF16)
+        for n, at in enumerate(spans()):
+            m_out[n, :HEAD_V] = tn(entry[:, at], query_in[:, at]).astype(BF16)
+            m_out[n, HEAD_V:] = d_ref[n]
 
     return kernel_call(
         body,
-        (heads,),
+        (steps,),
         [
             (grad_low, spec((rows, wide))),
-            (weights, spec((HEAD_V, wide), lambda h: (h, 2))),
+            (weights, spec((TOGETHER * HEAD_V, wide), lambda h: (h, 2))),
             (mixed, by_head(rows)),
             (swish, by_head(rows)),
             (head_gain, spec((1, HEAD_V))),
             (queries, by_head(rows)),
             (gate_pre, by_head(rows)),
-            (decays, spec((1, MESSAGE - HEAD_V, HEAD_K), lambda h: (h, 0, 0))),
+            (decays, spec((TOGETHER, MESSAGE - HEAD_V, HEAD_K), lambda h: (h, 0, 0))),
             (marks, spec(marks.shape)),
         ],
         [
             ((rows, wide), BF16, by_head(rows)),
             ((rows, wide), BF16, by_head(rows)),
             ((1, HEAD_V), F32, spec((1, HEAD_V))),
-            ((heads, MESSAGE, HEAD_K), BF16, spec((1, MESSAGE, HEAD_K), lambda h: (h, 0, 0))),
+            ((heads, MESSAGE, HEAD_K), BF16, spec((TOGETHER, MESSAGE, HEAD_K), lambda h: (h, 0, 0))),
         ],
     )
 
@@ -648,6 +699,7 @@
 def mixer_back(queries, keys, values, gate_pre, grad_mixed, states, leaving, first, marks, doc_row, rank):
     rows, wide = queries.shape
     heads = wide // HEAD_K
+    steps = heads // TOGETHER
     blocks = rows // GROUP
 
     def body(
@@ -657,44 +709,47 @@
         h = pl.program_id(0)
         gate = g_ref[...]
         along = summed(triangle(rows, lambda i, j: j <= i, GROUP), log_decay(gate))
-        state_grad[...] = l_ref[0].astype(F32)
         causal = triangle(GROUP, lambda i, j: j <= i) > 0
         onward = triangle(GROUP, lambda i, j: j >= i)
+        for head in range(TOGETHER):
+            state_grad[head] = l_ref[head].astype(F32)
         for n in reversed(range(blocks)):
             at = slice(n * GROUP, (n + 1) * GROUP)
             marks_n = marks_ref[at]
-            run = along[at]
-            end = run[GROUP - 1 :]
-            key = k_ref[at].astype(F32)
-            value = v_ref[at]
-            grad = gm_ref[at]
             entering = marks_n[:, 1:2]
-            up, down = jnp.exp(run), jnp.exp(-run)
-            out = jnp.exp(end - run) * marks_n[:, 2:3]
-            query_in = (scaled(q_ref[at]) * up).astype(BF16)
-            key_in = (key * down).astype(BF16)
-            key_out = (key * out).astype(BF16)
             allowed = causal & (marks_n[:, 0:1] == doc_ref[:, at])
-            scores = jnp.where(allowed, nt(query_in, key_in), 0.0).astype(BF16)
-            grad_scores = jnp.where(allowed, nt(grad, value), 0.0).astype(BF16)
-            leaving = state_grad[...].astype(BF16)
-            grad_query = nn(grad_scores, key_in) + entering * nn(grad, s_ref[0, n])
-            grad_key_in = tn(grad_scores, query_in)
-            grad_key_out = nn(value, leaving)
-            gv_out[at] = (tn(scores, grad) + nt(key_out, leaving)).astype(BF16)
-            gq_out[at] = (grad_query * up * HEAD_K ** (-0.5)).astype(BF16)
-            gk_out[at] = (grad_key_in * down + grad_key_out * out).astype(BF16)
-            change = (
-                query_in.astype(F32) * grad_query
-                - key_in.astype(F32) * grad_key_in
-                - key_out.astype(F32) * grad_key_out
-            )
-            closing = jnp.sum(s_ref[0, n + 1].astype(F32) * leaving.astype(F32), axis=0, keepdims=True)
-            slope[at] = summed(onward, change) + closing
-            kept = marks_n[GROUP - 1 :, 1:2] * jnp.exp(end)
-            state_grad[...] = kept * state_grad[...] + tn(grad, (query_in.astype(F32) * entering).astype(BF16))
+            run_all = along[at]
+            for head, lanes in enumerate(spans()):
+                run = run_all[:, lanes]
+                end = run[GROUP - 1 :]
+                key = k_ref[at, lanes].astype(F32)
+                value = v_ref[at, lanes]
+                grad = gm_ref[at, lanes]
+                up, down = jnp.exp(run), jnp.exp(-run)
+                out = jnp.exp(end - run) * marks_n[:, 2:3]
+                query_in = (scaled(q_ref[at, lanes]) * up).astype(BF16)
+                key_in = (key * down).astype(BF16)
+                key_out = (key * out).astype(BF16)
+                scores = jnp.where(allowed, nt(query_in, key_in), 0.0).astype(BF16)
+                grad_scores = jnp.where(allowed, nt(grad, value), 0.0).astype(BF16)
+                leaving = state_grad[head].astype(BF16)
+                grad_query = nn(grad_scores, key_in) + entering * nn(grad, s_ref[head, n])
+                grad_key_in = tn(grad_scores, query_in)
+                grad_key_out = nn(value, leaving)
+                gv_out[at, lanes] = (tn(scores, grad) + nt(key_out, leaving)).astype(BF16)
+                gq_out[at, lanes] = (grad_query * up * HEAD_K ** (-0.5)).astype(BF16)
+                gk_out[at, lanes] = (grad_key_in * down + grad_key_out * out).astype(BF16)
+                change = (
+                    query_in.astype(F32) * grad_query
+                    - key_in.astype(F32) * grad_key_in
+                    - key_out.astype(F32) * grad_key_out
+                )
+                closing = jnp.sum(s_ref[head, n + 1].astype(F32) * leaving.astype(F32), axis=0, keepdims=True)
+                slope[at, lanes] = summed(onward, change) + closing
+                kept = marks_n[GROUP - 1 :, 1:2] * jnp.exp(end)
+                state_grad[head] = kept * state_grad[head] + tn(grad, (query_in.astype(F32) * entering).astype(BF16))
         grad_gate = (slope[...] * sigmoid(-gate) * (1.0 / 16.0)).astype(BF16)
-        gg_out[...] = grad_gate
+        gg_out[...] = grad_gate.T
         part = nn(grad_gate, ro[...])
 
         @pl.when(h == 0)
@@ -705,7 +760,7 @@
         def _():
             low[...] += part
 
-        @pl.when(h == heads - 1)
+        @pl.when(h == steps - 1)
         def _():
             row = lax.broadcasted_iota(jnp.int32, (LANES, LANES), 0)
             lane = lax.broadcasted_iota(jnp.int32, (LANES, LANES), 1)
@@ -714,28 +769,36 @@
 
     return kernel_call(
         body,
-        (heads,),
+        (steps,),
         [
             (queries, by_head(rows)),
             (keys, by_head(rows)),
             (values, by_head(rows)),
             (gate_pre, by_head(rows)),
             (grad_mixed, by_head(rows)),
-            (states, spec((1, blocks + 1, HEAD_V, HEAD_K), lambda h: (h, 0, 0, 0))),
-            (leaving, spec((1, HEAD_V, HEAD_K), lambda h: (h, 0, 0))),
-            (first, spec((HEAD_K, LANES), lambda h: (h, 2 * wide // LANES))),
+            (states, spec((TOGETHER, blocks + 1, HEAD_V, HEAD_K), lambda h: (h, 0, 0, 0))),
+            (leaving, spec((TOGETHER, HEAD_V, HEAD_K), lambda h: (h, 0, 0))),
+            (first, spec((TOGETHER * HEAD_K, LANES), lambda h: (h, 2 * wide // LANES))),
             (marks, spec(marks.shape)),
             (doc_row, spec(doc_row.shape)),
         ],
-        [((rows, wide), BF16, by_head(rows))] * 4 + [((rows, LANES), BF16, spec((rows, LANES)))],
-        [pltpu.VMEM((HEAD_V, HEAD_K), F32), pltpu.VMEM((rows, HEAD_K), F32), pltpu.VMEM((rows, LANES), F32)],
+        [((rows, wide), BF16, by_head(rows))] * 3
+        + [
+            ((wide, rows), BF16, spec((TOGETHER * HEAD_K, rows), lambda h: (h, 0))),
+            ((rows, LANES), BF16, spec((rows, LANES))),
+        ],
+        [
+            pltpu.VMEM((TOGETHER, HEAD_V, HEAD_K), F32),
+            pltpu.VMEM((rows, TOGETHER * HEAD_K), F32),
+            pltpu.VMEM((rows, LANES), F32),
+        ],
     )
 
 
 def input_back(grads, first, second, grad_rank, tokens, gain, grad_hidden):
     rows, wide = tokens.shape
-    heads = wide // HEAD_K
-    places = ((second, 0), (first, 0), (first, heads), (second, heads))
+    steps = wide // HEAD_K // TOGETHER
+    places = ((second, 0), (first, 0), (first, steps), (second, steps))
 
     def body(*refs):
         grad_refs, weight_refs = refs[:4], refs[4:8]
@@ -753,7 +816,7 @@
         def _():
             total[...] += part
 
-        @pl.when(h == heads - 1)
+        @pl.when(h == steps - 1)
         def _():
             x = x_ref[...].astype(F32)
             scale = lax.rsqrt(jnp.mean(x * x, axis=1, keepdims=True) + 1e-06)
@@ -761,15 +824,12 @@
             grad = total[...] * gain_ref[...]
             out_ref[...] = gh_ref[...] + scale * (grad - unit * jnp.mean(grad * unit, axis=1, keepdims=True))
 
-    def strip(start):
-        return spec((wide, HEAD_K), lambda h: (0, start + h))
-
     whole = spec((rows, wide))
     return kernel_call(
         body,
-        (heads,),
+        (steps,),
         [(g, by_head(rows)) for g in grads]
-        + [(w, strip(start)) for w, start in places]
+        + [(w, by_head(wide, start)) for w, start in places]
         + [
             (grad_rank, spec((rows, LANES))),
             (first, spec((wide, LANES), lambda h: (0, 2 * wide // LANES))),
@@ -780,6 +840,43 @@
         [((rows, wide), F32, whole)],
         [pltpu.VMEM((rows, wide), F32)],
     )[0]
+
+
+def finish(terms, weights, turned_in, gain, middle, w_middle, rank, head_rows):
+    rows, width = weights[0].shape
+    count = len(weights)
+
+    def body(*refs):
+        term_refs, weight_refs = refs[: len(terms)], refs[len(terms) : len(terms) + count]
+        in_ref, gain_ref, middle_ref, wm_ref = refs[len(terms) + count : len(terms) + count + 4]
+        outs, middle_outs = refs[len(terms) + count + 4 : -7], refs[-7:-5]
+        in_out, out_out, bias_out, head_out, gain_out = refs[-5:]
+
+        def summed_terms(at):
+            total = term_refs[0][:, at].astype(F32)
+            for t in term_refs[1:]:
+                total = total + t[:, at].astype(F32)
+            return total
+
+        for n, out in enumerate(middle_outs):
+            out[...] = middle_ref[:, n * width : (n + 1) * width].astype(F32)
+        by_row = jnp.sum(wm_ref[...].astype(F32) * middle_outs[0][...], axis=1, keepdims=True)
+        for n, out in enumerate(outs):
+            out[...] = summed_terms(slice(n * width, (n + 1) * width))
+            by_row = by_row + jnp.sum(weight_refs[n][...].astype(F32) * out[...], axis=1, keepdims=True)
+        table = summed_terms(slice(count * width, count * width + LANES))
+        lane = lax.broadcasted_iota(jnp.int32, (rows, LANES), 1)
+        turned = jnp.where(lane == LANES - 1, by_row, table).T
+        in_out[...] = turned[:rank]
+        out_out[...] = turned[rank : 2 * rank]
+        bias_out[...] = turned[2 * rank : 2 * rank + 1]
+        head_out[...] = turned[2 * rank + 3 : 2 * rank + 4, :head_rows]
+        by_rank = jnp.sum(in_ref[...].astype(F32) * turned[:rank], axis=0, keepdims=True)
+        gain_out[...] = (turned[LANES - 1 :] + by_rank) / gain_ref[...].astype(F32)
+
+    ins = [*terms, *weights, turned_in, gain, middle, w_middle]
+    shapes = [(rows, width)] * (count + 2) + [(rank, rows), (rank, rows), (1, rows), (1, head_rows), (1, rows)]
+    return kernel_call(body, (1,), [(a, spec(a.shape)) for a in ins], [(o, F32, spec(o)) for o in shapes])
 
 
 def then(earlier, later):
@@ -805,21 +902,36 @@
         both = jnp.where(c == 0, then(message, self.other), then(self.other, message))
         self.mine = lax.dynamic_slice_in_dim(both, self.core * (heads // 2), heads // 2, 0)
 
-    def by_x(self, done=()):
-        self.beside = flip(after(done, self.mine), "x")
-        return self.beside
-
-    def by_y(self, done=()):
-        beside, mine = after(done, self.beside, self.mine)
+    def near(self, done=()):
+        if square_plane():
+            mine = after(done, self.mine)
+            self.arrived = (cross(mine, False), cross(mine, True))
+        else:
+            self.arrived = flip(after(done, self.mine), "x")
+        return self.arrived
+
+    def distant(self, done=()):
+        if square_plane():
+            self.far = cross(after(done, self.arrived[0]), True)
+            return self.far
+        beside, mine = after(done, self.arrived, self.mine)
         self.before = jnp.where(self.x == 1, beside, nothing(mine))
         self.line = jnp.where(self.x == 1, then(beside, mine), then(mine, beside))
         self.far = [shift(self.line, "y", self.sign * j) for j in range(1, lax.axis_size("y"))]
         return self.far
 
     def entering(self, done=()):
-        before, distant = after(done, self.before, self.far)
-        for j, far in enumerate(distant):
-            before = jnp.where(self.y > j, then(far, before), before)
+        if square_plane():
+            (early, late), corner = after(done, self.arrived, self.far)
+            beside = jnp.where(self.core == 0, early, late)
+            along = jnp.where(self.core == 0, late, early)
+            line = jnp.where(self.x == 1, then(corner, along), then(along, corner))
+            before = jnp.where(self.x == 1, beside, nothing(beside))
+            before = jnp.where(self.y == 1, then(line, before), before)
+        else:
+            before, distant = after(done, self.before, self.far)
+            for j, far in enumerate(distant):
+                before = jnp.where(self.y > j, then(far, before), before)
         rest = flip(before, "c")
         chip = jnp.where(self.core == 0, jnp.concatenate([before, rest]), jnp.concatenate([rest, before]))
         return jnp.where(self.c == 1, then(chip, self.other), chip)[:, :HEAD_V]
@@ -863,65 +975,73 @@
     table_columns = 2 * width + LANES
     square_weights = jnp.concatenate([w_query, w_swish, w_output], axis=1)
 
-    w_both = lax.all_gather(jnp.concatenate([w_gate, w_up], axis=1), AXES, axis=0, tiled=True)
-    first = first_weights(w_key, w_value, rank_in, rank_out, (bias, gain_one, gain_two, head_gain))
+    first = first_weights(w_key, w_value, rank_in.T, rank_out, (bias, gain_one, gain_two, head_gain))
+    wait_for = first
     marks, doc_row = documents(doc_starts[0], rows)
     fast = square_plane() and own % 16 == 0
     depth = lax.axis_size("z")
+
+    def by_distance(base, odd, even):
+        return jnp.stack([base] + [(odd if k % 2 else even)[(k - 1) // 2] for k in range(1, depth)])
+
+    def odd_shifts(a):
+        return [shift(a, "z", k) for k in range(1, depth, 2)]
+
+    def even_shifts(a):
+        return [shift(a, "z", k) for k in range(2, depth, 2)]
+
     if fast:
-        one = jnp.stack([first] + [shift(first, "z", k) for k in range(1, depth)])
         half = width // 2
         keep = lax.dynamic_slice_in_dim(w_down, c * half, half, 1)
         other = flip(lax.dynamic_slice_in_dim(w_down, (1 - c) * half, half, 1), "c")
         chip_down = jnp.where(c == 0, jnp.concatenate([keep, other]), jnp.concatenate([other, keep]))
-        chip_down, square_weights = after(one, chip_down, square_weights)
+        one = by_distance(first, odd_shifts(first), even_shifts(first))
         one_early, one_late = cross(one, False), cross(one, True)
-        two = [shift(square_weights, "z", k) for k in range(1, depth, 2)]
-        now = (one_early, one_late, two)
-        square_more, one_next = after(now, square_weights, one_early)
+        now = (one_early, one_late)
+        square_weights, one_next = after(now, square_weights, one_early)
         one_corner = cross(one_next, True)
-        two_more = [shift(square_more, "z", k) for k in range(2, depth, 2)]
-        now = (one_corner, two_more)
-        chip_down, one = after(now, chip_down, one)
-        three = [shift(chip_down, "z", k) for k in range(1, depth, 2)]
+        two_odd = odd_shifts(square_weights)
+        now = (one_corner, two_odd)
+        square_weights, one = after(now, square_weights, one)
+        wait_for = two_even = even_shifts(square_weights)
+        two = by_distance(square_weights, two_odd, two_even)
+        one, two = after(two, one, two)
         first = assemble(gathered(one, one_early, one_late, one_corner), own, (width, table_columns))
-
-        def mixed_order(base, odd, even):
-            return jnp.stack([base] + [(odd if k % 2 else even)[(k - 1) // 2] for k in range(1, depth)])
-
-        two = mixed_order(square_weights, two, two_more)
-        now = (first, three)
-        first, two, chip_down = after(now, first, two, chip_down)
         two_early = cross(two, False)
-        three_more = [shift(chip_down, "z", k) for k in range(2, depth, 2)]
-        three = mixed_order(chip_down, three, three_more)
+        first, two, chip_down = after((first, two_early), first, two, chip_down)
+        two_late = cross(two, True)
+        three_odd = odd_shifts(chip_down)
     else:
         first = lax.all_gather(first, AXES, axis=0, tiled=True)
         second = lax.all_gather(square_weights, AXES, axis=0, tiled=True)
         w_down_all = lax.all_gather(w_down, AXES, axis=0, tiled=True)
-    normed, low, keys, values, gate_pre, message, vectors = project(tokens, first, marks, rank)
+    gate_shard, up_shard = after(wait_for, w_gate, w_up)
+    w_both = lax.all_gather(jnp.concatenate([gate_shard, up_shard], axis=1), AXES, axis=0, tiled=True)
+    normed, normed_turned, low, keys, values, gate_pre, message, vectors = project(tokens, first, marks, rank)
     row_one, row_two = vectors[1:2], vectors[2:3]
     row_head = vectors[3].reshape(devices, own)[:, : head_gain.shape[0]].reshape(1, HEAD_V)
     if fast:
-        message, two, two_early = after(three, message, two, two_early)
+        message, two_early, chip_down = after((two_late, three_odd), message, two_early, chip_down)
     passing = Passing(message)
     if fast:
-        two_late = cross(after(passing.mine, two), True)
-        now = (passing.by_x(), two_late)
-        two_corner = cross(after(now, two_early), True)
-        now = (passing.by_y(now), two_corner)
-        three = after(now, three)
+        two_next, three_next = after(passing.mine, two_early, chip_down)
+        two_corner = cross(two_next, True)
+        three_even = even_shifts(three_next)
+        now = (passing.near(), two_corner, three_even)
+        now = passing.distant(now)
+        three, two, two_early, two_late, two_corner = after(
+            now, by_distance(chip_down, three_odd, three_even), two, two_early, two_late, two_corner
+        )
         three_early = cross(three, False)
         second = assemble(gathered(two, two_early, two_late, two_corner), own, (width, 3 * width))
-        now = (passing.entering(now), three_early, second)
-        entered, second, three, three_early = after(now, now[0], second, three, three_early)
+        entered = passing.entering(now)
+        entered, second, three, three_early = after((entered, second, three_early), entered, second, three, three_early)
         three_late, three_corner = cross(three, True), cross(three_early, True)
     else:
-        passing.by_x()
-        passing.by_y()
+        passing.near()
+        passing.distant()
         entered = passing.entering()
-    both = pair(normed)
-    queries, mixed, swish, gated, hidden, normed_two, states = mixer(
+    queries, mixed, swish, gated, hidden, normed_two, two_turned, states = mixer(
         normed, keys, values, gate_pre, entered, second, row_head, tokens, row_two, marks, doc_row
     )
     if fast:
@@ -933,73 +1053,64 @@
         normed_two, cotangent, w_both, w_down_all, hidden, row_two
     )
 
+    both = pair(normed_turned)
+    two_pair = pair(two_turned)
     down = weight_grads([(pair(inner), [pair(cotangent)])], 512, True)
-    grad_low, gate_pair, up_pair, two_pair = after(down.blocks, grad_low, pair(grad_gate), pair(grad_up), pair(normed_two))
+    grad_low, gate_pair, up_pair = after(down.blocks, grad_low, pair(grad_gate), pair(grad_up))
     grad_mixed, grad_swish, grad_head_gain, message_back = head_back(
         grad_low, second, mixed, swish, row_head, queries, gate_pre, message[:, HEAD_V:], marks
     )
-    now = (down.first(), message_back)
+    gate = weight_grads([(two_pair, [gate_pair])], ff // 2)
+    now = (down.first(), message_back, gate.blocks)
     passing = Passing(after(now, message_back), True)
     now = passing.mine
-    two_pair, gate_pair = after(now, two_pair, gate_pair)
-    gate = weight_grads([(two_pair, [gate_pair])], ff // 2)
-    now = (passing.by_x(), down.second(now), gate.blocks)
-    up = weight_grads([after(now, (two_pair, [up_pair]))], ff // 2)
-    now = (passing.by_y(now), gate.first(now), up.blocks)
+    up = weight_grads([(two_pair, [after(now, up_pair)])], ff // 2)
+    now = (passing.near(), down.second(now), up.blocks)
+    down_part = down.third()
+    swish_pair, gated_pair, low_pair = after(now, pair(grad_swish), pair(gated), pair(grad_low))
+    middle = weight_grads([(both, [swish_pair]), (gated_pair, [low_pair])], width)
+    now = (passing.distant(now), gate.first(now), middle.blocks)
     leaving = passing.entering(now)
     now = leaving
-    down_sum = down.third(now)
     grad_query, grad_key, grad_value, grad_gate_pre, grad_rank = mixer_back(
         queries, keys, values, gate_pre, grad_mixed, states, leaving, first, marks, doc_row, rank
     )
     now = (up.first(now), grad_query)
+    gate.second(now, up)
     inside_pairs = [pair(a) for a in after(now, grad_query, grad_key, grad_value, grad_rank, grad_gate_pre)]
-    swish_pair = after(now, pair(grad_swish))
-    middle = weight_grads([(both, [swish_pair]), (pair(gated), [pair(grad_low)])], width)
-    now = (inside_pairs, middle.blocks, gate.second(now))
     head_terms = grad_head_gain + flip(grad_head_gain, "c")
     head_terms = jnp.pad(head_terms.reshape(devices, -1), ((0, 0), (0, own - head_gain.shape[0]))).reshape(width, 1)
     base = jnp.pad(head_terms.astype(BF16), ((0, 0), (2 * rank + 3, LANES - 2 * rank - 4)))
-    inside_pairs = after(now, inside_pairs)
     inside = weight_grads(
         [(both, inside_pairs[:3])],
         width,
         table=([(both, inside_pairs[3]), (inside_pairs[4], pair(low))], base),
     )
-    gate_sum = gate.third(now)
-    now = (inside.blocks, up.second(now), middle.first(now))
+    now = (inside.blocks, gate.through, up.through, down_part)
+    gates_part = gate.third(up)
     input_grad = input_back(
         (grad_query, grad_key, grad_value, grad_swish), first, second, after(now, grad_rank), tokens, row_one,
         grad_hidden,
     )
-    up_sum = up.third(now)
-    now = (input_grad, inside.first(now), middle.second(now))
-    inside.second(now)
-    middle_sum = middle.third(now)
-    inside_sum = inside.third()
+    now = (input_grad, middle.first(now), inside.first(now))
+    now = (inside.second(now), middle.second(now))
+    middle_part = middle.third()
+    inside_terms = inside.third_terms()
 
     chip_half = ff // devices
+    down_sum = wide(down_part)
     keep = lax.dynamic_slice_in_dim(down_sum, c * chip_half, chip_half, 0)
     other = flip(lax.dynamic_slice_in_dim(down_sum, (1 - c) * chip_half, chip_half, 0), "c")
     down_sum = jnp.where(c == 0, jnp.concatenate([keep, other], 1), jnp.concatenate([other, keep], 1))
-    g_query, g_key, g_value = (inside_sum[:, n * width : (n + 1) * width] for n in range(3))
-    g_swish, g_output = middle_sum[:, :width], middle_sum[:, width:]
-    g_rank_in, g_rank_out, g_bias, g_head = (
-        inside_sum[:, 3 * width + a : 3 * width + b]
-        for a, b in ((0, rank), (rank, 2 * rank), (2 * rank, 2 * rank + 1), (2 * rank + 3, 2 * rank + 4))
-    )
-    g_gate, g_up = gate_sum, up_sum
-
-    def gain_grad(gain, *terms):
-        return sum(jnp.sum(wide(w) * g, axis=1) for w, g in terms) / wide(gain)
-
-    g_gain_one = gain_grad(
-        gain_one, (w_query, g_query), (w_key, g_key), (w_value, g_value), (w_swish, g_swish), (rank_in, g_rank_in)
-    )
-    g_gain_two = gain_grad(gain_two, (w_gate, g_gate), (w_up, g_up))
+    g_gate, g_up = wide(gates_part[:, :ff]), wide(gates_part[:, ff:])
+    g_gain_two = (jnp.sum(wide(w_gate) * g_gate, axis=1) + jnp.sum(wide(w_up) * g_up, axis=1)) / wide(gain_two)
+    g_query, g_key, g_value, g_swish, g_output, g_rank_in, g_rank_out, g_bias, g_head, g_gain_one = finish(
+        inside_terms, (w_query, w_key, w_value), rank_in.T, gain_one.reshape(1, own), middle_part, w_swish,
+        rank, head_gain.shape[0],
+    )
     return (
-        output, input_grad, g_gain_one, g_query, g_key, g_value, g_swish, g_rank_in, g_rank_out.T, g_bias[:, 0],
-        g_head[: head_gain.shape[0], 0], g_output, g_gain_two, g_gate, g_up, down_sum,
+        output, input_grad, g_gain_one[0], g_query, g_key, g_value, g_swish, g_rank_in.T, g_rank_out, g_bias[0], g_head[0],
+        g_output, g_gain_two, g_gate, g_up, down_sum,
     )
 
 

time: 490 us -> 436 us (0.89)
  starting transfers between devices: 74.9 us -> 49.9 us
  other arithmetic: 50 us -> 32.8 us
  Pallas kernels: 150 us -> 142 us
  waiting for transfers between devices: 177 us -> 169 us
    ppermute x19 -> x24, waiting for transfers between devices: 32.1 us -> 80.9 us  [cross(): return lax.ppermute(value, ('y', 'x', 'c'), perm)]
    reduce_scatter x5 -> x3, waiting for transfers between devices: 45.9 us -> 5.94 us  [third(): lax.psum_scatter(total.reshape(-1, total.shape[-1]), axes, scatter_dimens...]
    ppermute x47 -> x46, starting transfers between devices: 48.1 us -> 27.7 us  [shift(): lax.ppermute(value, axis, [(i, (i + step) % size) for i in range(size)])]
    ppermute x47 -> x46, waiting for transfers between devices: 98.5 us -> 82.5 us  [shift(): lax.ppermute(value, axis, [(i, (i + step) % size) for i in range(size)])]
    reduce_sum x4 -> x1, other arithmetic: 7.15 us -> 2.06 us  [shards(): jnp.sum(wide(w_up) * g_up, axis=1)]
    ppermute x19 -> x24, starting transfers between devices: 26.6 us -> 22 us  [cross(): return lax.ppermute(value, ('y', 'x', 'c'), perm)]
    pallas_call x7 -> x8, Pallas kernels: 91.9 us -> 87.4 us  [kernel_call(): pl.pallas_call(body, grid=grid, in_specs=[s for _, s in ins], out_specs=[...]
    unnamed x141 -> x150, local copies, waits for them, and re-layouts: 9.25 us -> 12.4 us
  transfers between devices with their start and end apart: 72 -> 74, of which waited for: 35 -> 43; matrix products, arithmetic and copies ran while one was open for 10% -> 8% of each run, Pallas kernels for 26% -> 26%
where the time goes in v3:
time: 436 us; the launch traced here: 431 us
  waiting for transfers between devices  169 us (39%)
  Pallas kernels  142 us (33%)
  starting transfers between devices  49.9 us (11%)
  other arithmetic  32.8 us (8%)
  local copies, waits for them, and re-layouts  21.6 us (5%)
  between operations  15.2 us (3%)
    pallas_call x8, Pallas kernels, kernel_call(): pl.pallas_call(body, grid=grid, in_specs=[s for _, s in ins], out_specs=[...  87.4 us
    ppermute x46, waiting for transfers between devices, shift(): lax.ppermute(value, axis, [(i, (i + step) % size) for i in range(size)])  82.5 us
    ppermute x24, waiting for transfers between devices, cross(): return lax.ppermute(value, ('y', 'x', 'c'), perm)  80.9 us
    pallas_call x5, Pallas kernels, weight_grads(): pl.pallas_call(body, grid_spec=pltpu.PrefetchScalarGridSpec(num_scalar_pr...  37.3 us
    ppermute x46, starting transfers between devices, shift(): lax.ppermute(value, axis, [(i, (i + step) % size) for i in range(size)])  27.7 us
    ppermute x24, starting transfers between devices, cross(): return lax.ppermute(value, ('y', 'x', 'c'), perm)  22 us
    pallas_call x3, Pallas kernels, assemble(): pl.pallas_call(body, grid_spec=pltpu.PrefetchScalarGridSpec(num_scalar_pr...  17.2 us
    unnamed x150, local copies, waits for them, and re-layouts  12.4 us
  transfers between devices with their start and end apart: 74, of which 43 were waited for; matrix products, arithmetic and copies ran while one was open for 8% of the time, Pallas kernels for 26%

profile of v3, /device:TPU:0, one launch (start us, length us, event | category | flops | bytes accessed | tf_op | source)
XLA Modules:
  0.0 430.9 jit_solution(10530238787432805957)
XLA Ops:
  7.3 2.1 shard_map.288
  9.4 3.0 collective-permute-start
  12.4 2.6 collective-permute-start.1
  16.3 2.9 collective-permute-done
  19.2 5.1 %collective-permute-done.1 = bf16[32,2176]{1,0:T(8,128)(2,1)S(1)} collective-permute-done((bf16[32,2176]{1,0:T(8,128)(2,1)}, bf16[32,2176]{1,0:T(8,128)(2,1)S(1)}, u32[]{:S(2)}, u32[]{:S(2)}) %collective-permute-start.1) | collective-permute-done | bytes 139296 | tf_op jit(solution)/shard_map/ppermute | solution.py:25
  28.5 12.3 %collective-permute-done.3.refs_1_ = bf16[4,32,2176]{2,1,0:T(8,128)(2,1)S(1)} collective-permute-done((bf16[4,32,2176]{2,1,0:T(8,128)(2,1)S(1)}, bf16[4,32,2176]{2,1,0:T(8,128)(2,1)S(1)}, u32[]{:S(2)}, u32[]{:S(2)}) %collective-permute-start.3) | collective-permute-done | bytes 557088 | tf_op jit(solution)/shard_map/ppermute | solution.py:47
  41.7 3.5 collective-permute-start.6
  45.5 5.7 %collective-permute-done.6 = bf16[32,3072]{1,0:T(8,128)(2,1)S(1)} collective-permute-done((bf16[32,3072]{1,0:T(8,128)(2,1)S(1)}, bf16[32,3072]{1,0:T(8,128)(2,1)S(1)}, u32[]{:S(2)}, u32[]{:S(2)}) %collective-permute-start.6) | collective-permute-done | bytes 196640 | tf_op jit(solution)/shard_map/ppermute | solution.py:25
  51.2 3.7 collective-permute-done.7
  55.5 11.3 %collective-permute-done.8 = bf16[32,3072]{1,0:T(8,128)(2,1)S(1)} collective-permute-done((bf16[32,3072]{1,0:T(8,128)(2,1)S(1)}, bf16[32,3072]{1,0:T(8,128)(2,1)S(1)}, u32[]{:S(2)}, u32[]{:S(2)}) %collective-permute-start.8) | collective-permute-done | bytes 196640 | tf_op jit(solution)/shard_map/ppermute | solution.py:25
  73.2 5.2 %shard_map.289.wk.wv.table.part_ref.ro.refs_5_.refs_6_.refs_9_ = bf16[1024,2176]{1,0:T(8,128)(2,1)} custom-call(s32[64]{0:T(128)} %stack.114.where_ref, bf16[4,32,2176]{2,1,0:T(8,128)(2,1)} %copy-done.14, bf16[4,32,2176]{2,1,0:T(8,128)(2,1)} %copy-done.48, bf16[4,32,2176]{2,1,0:T(8,128)(2,1)} %collective-permute-done.4.refs_2_, ...), custom_call_target="tpu_custom_call" | custom-call | tf_op jit(solution)/shard_map/pallas_call | solution.py:97
  78.3 4.1 collective-permute-done.14.refs_1_
  84.4 4.3 %collective-permute-start.17 = (bf16[176,512]{1,0:T(8,128)(2,1)S(1)}, bf16[176,512]{1,0:T(8,128)(2,1)S(1)}, u32[]{:S(2)}, u32[]{:S(2)}) collective-permute-start(bf16[176,512]{1,0:T(8,128)(2,1)S(1)} %maximum_select_fusion.5), channel_id=1, source_target_pairs={{0,24},{8,0},{16,8},{24,16},{1,25},{9,1},{17,9},{25,17},{2,26},{10... | collective-permute-start | bytes 540680 | tf_op jit(solution)/shard_map/ppermute | solution.py:25
  90.9 8.2 %shard_map.290 = (bf16[384,1024]{1,0:T(8,128)(2,1)}, bf16[1024,384]{1,0:T(8,128)(2,1)}, bf16[384,128]{1,0:T(8,128)(2,1)}, bf16[384,1024]{1,0:T(8,128)(2,1)}, bf1...) custom-call(bf16[384,1024]{1,0:T(8,128)(2,1)} %refs_10_.2, ...), custom_call_target="tpu_custom_call" | custom-call | tf_op jit(solution)/shard_map/pallas_call | solution.py:364
  104.5 2.0 collective-permute-start.21
  106.9 14.9 %collective-permute-done.22 = bf16[176,512]{1,0:T(8,128)(2,1)S(1)} collective-permute-done((bf16[176,512]{1,0:T(8,128)(2,1)S(1)}, bf16[176,512]{1,0:T(8,128)(2,1)S(1)}, u32[]{:S(2)}, u32[]{:S(2)}) %collective-permute-start.22) | collective-permute-done | bytes 180256 | tf_op jit(solution)/shard_map/ppermute | solution.py:25
  124.6 11.2 %collective-permute-done.23 = bf16[2,272,256]{2,1,0:T(8,128)(2,1)S(1)} collective-permute-done((bf16[2,272,256]{2,1,0:T(8,128)(2,1)S(1)}, bf16[2,272,256]{2,1,0:T(8,128)(2,1)S(1)}, u32[]{:S(2)}, u32[]{:S(2)}) %collective-permute-start.23) | collective-permute-done | bytes 278560 | tf_op jit(solution)/shard_map/ppermute | solution.py:47
  144.7 6.1 %shard_map.291.wq.ws.wo.refs_4_.refs_7_ = bf16[1024,3072]{1,0:T(8,128)(2,1)} custom-call(s32[64]{0:T(128)} %stack.114.where_ref, bf16[4,32,3072]{2,1,0:T(8,128)(2,1)} %copy-done.5, bf16[4,32,3072]{2,1,0:T(8,128)(2,1)} %copy-done.20, bf16[4,32,3072]{2,1,0:T(8,128)(2,1)} %copy-done.22, bf16[4,32,3072]{2,1,0:T(8,128)(2,1)} %copy-done.23, ...), custom_call_target="tpu_custom_call" | custom-call | tf_op jit(solution)/shard_map/pallas_call | solution.py:97
  150.8 6.6 %collective-permute-done.29.refs_1_ = bf16[4,176,512]{2,1,0:T(8,128)(2,1)} collective-permute-done((bf16[4,176,512]{2,1,0:T(8,128)(2,1)S(1)}, bf16[4,176,512]{2,1,0:T(8,128)(2,1)}, u32[]{:S(2)}, u32[]{:S(2)}) %collective-permute-start.29) | collective-permute-done | bytes 720928 | tf_op jit(solution)/shard_map/ppermute | solution.py:47
  162.3 15.6 %shard_map.292 = (bf16[384,1024]{1,0:T(8,128)(2,1)}, f32[384,1024]{1,0:T(8,128)}, f32[384,1024]{1,0:T(8,128)}, bf16[1024,384]{1,0:T(8,128)(2,1)}, f32[384,1024]{...) custom-call(bf16[384,1024]{1,0:T(8,128)(2,1)} %get-tuple-element.148.n_ref, ...), custom_call_target="tpu_custom_call" | custom-call | tf_op jit(solution)/shard_map/pallas_call | solution.py:364
  183.4 5.9 %shard_map.293.wd = bf16[2816,1024]{1,0:T(8,128)(2,1)} custom-call(s32[64]{0:T(128)} %stack.114.where_ref, bf16[4,176,512]{2,1,0:T(8,128)(2,1)} %copy-done.11, bf16[4,176,512]{2,1,0:T(8,128)(2,1)} %collective-permute-done.29.refs_1_, bf16[4,176,512]{2,1,0:T(8,128)(2,1)} %copy-done.41, bf16[4,176,512]{2,1,0:T(8,128)(2,1)} %copy-done.42, ...), custom_call_target="tpu_custom_call" | custom-call | tf_op jit(solution)/shard_map/pallas_call | solution.py:97
  189.4 26.1 %shard_map.294 = (bf16[384,1024]{1,0:T(8,128)(2,1)}, bf16[2816,384]{1,0:T(8,128)(2,1)}, bf16[384,2816]{1,0:T(8,128)(2,1)}, bf16[384,2816]{1,0:T(8,128)(2,1)}, f3...) custom-call(bf16[384,1024]{1,0:T(8,128)(2,1)} %get-tuple-element.172.n_ref, bf16[384,1024]{1,0:T(8,128)(2,1)} %refs_2_.1, ...), custom_call_target="tpu_custom_call" | custom-call | tf_op jit(solution)/shard_map/pallas_call | solution.py:364
  217.3 4.8 %collective-permute-done.39.refs_3_ = bf16[384,1024]{1,0:T(8,128)(2,1)S(1)} collective-permute-done((bf16[384,1024]{1,0:T(8,128)(2,1)S(1)}, bf16[384,1024]{1,0:T(8,128)(2,1)S(1)}, u32[]{:S(2)}, u32[]{:S(2)}) %collective-permute-start.39) | collective-permute-done | bytes 786464 | tf_op jit(solution)/shard_map/ppermute | solution.py:25
  223.0 6.9 %shard_map.295 = (bf16[8,176,512]{2,1,0:T(8,128)(2,1)}, bf16[4,176,512]{2,1,0:T(8,128)(2,1)}, bf16[4,176,512]{2,1,0:T(8,128)(2,1)}) custom-call(s32[17]{0:T(128)} %pad_add_fusion.1.numbers_ref, bf16[2816,384]{1,0:T(8,128)(2,1)} %get-tuple-element.185.refs_0_, bf16[2816,384]{1,0:T(8,128)(2,1)} %collective-permute-done.38.refs_1_, bf16[384,1024]{1,0:T(8,128)(2,1)} %refs_2_.1, ...), custom_call_target="tpu_custom_call" | custom-call | tf_op jit(solution)/shard_map/pallas_call | solution.py:283
  231.4 8.0 %shard_map.296 = (bf16[384,1024]{1,0:T(8,128)(2,1)}, bf16[384,1024]{1,0:T(8,128)(2,1)}, f32[1,256]{1,0:T(1,128)}, bf16[4,272,256]{2,1,0:T(8,128)(2,1)}) custom-call(bf16[384,1024]{1,0:T(8,128)(2,1)} %get-tuple-element.220.gh_ref.refs_6_, bf16[1024,3072]{1,0:T(8,128)(2,1)} %shard_map.291.wq.ws.wo.refs_4_.refs_7_, f32[384,1024]{1,0:T(8,128)} %get-tuple-element.190.mixed_ref, ...), custom_call_target="tpu_custom_call" | custom-call | tf_op jit(solution)/shard_map/pallas_call | solution.py:364
  240.4 6.9 %shard_map.297 = (bf16[8,32,2816]{2,1,0:T(8,128)(2,1)}, bf16[4,32,2816]{2,1,0:T(8,128)(2,1)}, bf16[4,32,2816]{2,1,0:T(8,128)(2,1)}) custom-call(s32[17]{0:T(128)} %pad_add_fusion.2.numbers_ref, bf16[1024,384]{1,0:T(8,128)(2,1)} %get-tuple-element.195.refs_0_, bf16[1024,384]{1,0:T(8,128)(2,1)} %copy-done.4, bf16[384,2816]{1,0:T(8,128)(2,1)} %get-tuple-element.196.refs_2_, ...), custom_call_target="tpu_custom_call" | custom-call | tf_op jit(solution)/shard_map/pallas_call | solution.py:283
  247.3 1.8 collective-permute-done.40
  250.2 1.9 collective-permute-done.42
  256.6 6.7 %shard_map.298 = (bf16[8,32,2816]{2,1,0:T(8,128)(2,1)}, bf16[4,32,2816]{2,1,0:T(8,128)(2,1)}, bf16[4,32,2816]{2,1,0:T(8,128)(2,1)}) custom-call(s32[17]{0:T(128)} %pad_add_fusion.2.numbers_ref, bf16[1024,384]{1,0:T(8,128)(2,1)} %get-tuple-element.195.refs_0_, bf16[1024,384]{1,0:T(8,128)(2,1)} %copy-done.4, bf16[384,2816]{1,0:T(8,128)(2,1)} %get-tuple-element.206.refs_2_, ...), custom_call_target="tpu_custom_call" | custom-call | tf_op jit(solution)/shard_map/pallas_call | solution.py:283
  265.0 5.7 %collective-permute-done.44 = bf16[2,272,256]{2,1,0:T(8,128)(2,1)S(1)} collective-permute-done((bf16[2,272,256]{2,1,0:T(8,128)(2,1)S(1)}, bf16[2,272,256]{2,1,0:T(8,128)(2,1)S(1)}, u32[]{:S(2)}, u32[]{:S(2)}) %collective-permute-start.44) | collective-permute-done | bytes 278560 | tf_op jit(solution)/shard_map/ppermute | solution.py:47
  278.6 6.8 %shard_map.299 = (bf16[8,32,2048]{2,1,0:T(8,128)(2,1)}, bf16[4,32,2048]{2,1,0:T(8,128)(2,1)}, bf16[4,32,2048]{2,1,0:T(8,128)(2,1)}) custom-call(s32[17]{0:T(128)} %pad_add_fusion.2.numbers_ref, bf16[1024,384]{1,0:T(8,128)(2,1)} %get-tuple-element.213.refs_0_.refs_8_, bf16[1024,384]{1,0:T(8,128)(2,1)} %copy-done.1, ...), custom_call_target="tpu_custom_call" | custom-call | tf_op jit(solution)/shard_map/pallas_call | solution.py:283
  285.4 7.7 %collective-permute-done.47 = bf16[8,32,2816]{2,1,0:T(8,128)(2,1)} collective-permute-done((bf16[8,32,2816]{2,1,0:T(8,128)(2,1)}, bf16[8,32,2816]{2,1,0:T(8,128)(2,1)}, u32[]{:S(2)}, u32[]{:S(2)}) %collective-permute-start.47) | collective-permute-done | bytes 1441824 | tf_op jit(solution)/shard_map/ppermute | solution.py:47
  299.1 15.5 %shard_map.300 = (bf16[384,1024]{1,0:T(8,128)(2,1)}, bf16[384,1024]{1,0:T(8,128)(2,1)}, bf16[384,1024]{1,0:T(8,128)(2,1)}, bf16[1024,384]{1,0:T(8,128)(2,1)}, bf16[384,128]{1,0:T(8,128)(2,1)}) custom-call(bf16[384,1024]{1,0:T(8,128)(2,1)} %get-tuple-element.181.q_ref, bf16[384,1024]{1,0:T(8,128)(2,1)} %get-tuple-element.149.k_ref, ...), custom_call_target="tpu_custom_call" | custom-call | tf_op jit(solution)/shard_map/pallas_call | solution.py:364
  314.6 2.4 collective-permute-done.53
  317.0 1.8 add_convert_fusion.6
  328.1 10.0 %shard_map.301 = (bf16[8,32,3200]{2,1,0:T(8,128)(2,1)}, bf16[4,32,3200]{2,1,0:T(8,128)(2,1)}, bf16[4,32,3200]{2,1,0:T(8,128)(2,1)}) custom-call(s32[17]{0:T(128)} %pad_add_fusion.2.numbers_ref, bf16[1024,384]{1,0:T(8,128)(2,1)} %get-tuple-element.213.refs_0_.refs_8_, bf16[1024,384]{1,0:T(8,128)(2,1)} %copy-done.1, ...), custom_call_target="tpu_custom_call" | custom-call | tf_op jit(solution)/shard_map/pallas_call | solution.py:283
  339.6 5.9 %reduce-scatter.4.cloned.1.call-done = bf16[176,512]{1,0:T(8,128)(2,1)} async-done(((bf16[704,512]{1,0:T(8,128)(2,1)}), bf16[176,512]{1,0:T(8,128)(2,1)}) %reduce-scatter.4.cloned.1.call-update) | async-done | bytes 180240 | tf_op jit(solution)/shard_map/reduce_scatter | solution.py:166
  347.6 2.7 add_convert_fusion.3
  352.5 9.6 %shard_map.302 = f32[384,1024]{1,0:T(8,128)} custom-call(bf16[384,1024]{1,0:T(8,128)(2,1)} %get-tuple-element.234.refs_2_.refs_0_, bf16[384,1024]{1,0:T(8,128)(2,1)} %get-tuple-element.235.refs_4_.refs_1_, bf16[384,1024]{1,0:T(8,128)(2,1)} %get-tuple-element.236.refs_6_.refs_2_, bf16[384,1024]{1,0:T(8,128)(2,1)} %get-tuple-element.218.refs_4_.refs_3_, ...), custom_call_target="tpu_custom_call" | custom-call | tf_op jit(solution)/shard_map/pallas_call | solution.py:364
  362.2 16.0 %collective-permute-done.62 = bf16[8,32,3200]{2,1,0:T(8,128)(2,1)S(1)} collective-permute-done((bf16[8,32,3200]{2,1,0:T(8,128)(2,1)}, bf16[8,32,3200]{2,1,0:T(8,128)(2,1)S(1)}, u32[]{:S(2)}, u32[]{:S(2)}) %collective-permute-start.62) | collective-permute-done | bytes 1638432 | tf_op jit(solution)/shard_map/ppermute | solution.py:47
  385.3 3.3 collective-permute-done.68
  388.5 2.2 add_convert_fusion.8
  390.8 6.5 %collective-permute-done.64 = bf16[4,32,3200]{2,1,0:T(8,128)(2,1)} collective-permute-done((bf16[4,32,3200]{2,1,0:T(8,128)(2,1)}, bf16[4,32,3200]{2,1,0:T(8,128)(2,1)}, u32[]{:S(2)}, u32[]{:S(2)}) %collective-permute-start.64) | collective-permute-done | bytes 819232 | tf_op jit(solution)/shard_map/ppermute | solution.py:47
  399.8 2.1 collective-permute-start.66
  403.6 2.1 multiply_reduce_fusion
  406.2 7.8 %collective-permute-done.65.refs_1_ = bf16[32,3200]{1,0:T(8,128)(2,1)S(1)} collective-permute-done((bf16[32,3200]{1,0:T(8,128)(2,1)S(1)}, bf16[32,3200]{1,0:T(8,128)(2,1)S(1)}, u32[]{:S(2)}, u32[]{:S(2)}) %collective-permute-start.65) | collective-permute-done | bytes 204832 | tf_op jit(solution)/shard_map/ppermute | solution.py:25
  414.1 7.0 %collective-permute-done.66.refs_2_ = bf16[32,3200]{1,0:T(8,128)(2,1)S(1)} collective-permute-done((bf16[32,3200]{1,0:T(8,128)(2,1)S(1)}, bf16[32,3200]{1,0:T(8,128)(2,1)S(1)}, u32[]{:S(2)}, u32[]{:S(2)}) %collective-permute-start.66) | collective-permute-done | bytes 204832 | tf_op jit(solution)/shard_map/ppermute | solution.py:25
  421.9 2.2 shard_map.303
  (380 shorter events, 98.7 us)
Async XLA Ops:
  7.2 182.1 %all-gather.2.cloned.1.call-start = ((), (), s32[]{:S(2)}) async-start(), calls=%async_computation.3 | async-start | bytes 11894784 | tf_op jit(solution)/shard_map/all_gather | solution.py:1019
  9.4 9.9 %collective-permute-start = (bf16[32,2176]{1,0:T(8,128)(2,1)}, bf16[32,2176]{1,0:T(8,128)(2,1)S(1)}, u32[]{:S(2)}, u32[]{:S(2)}) collective-permute-start(bf16[32,2176]{1,0:T(8,128)(2,1)} %shard_map.288), channel_id=1, source_target_pairs={{0,8},{8,16},{16,24},{24,0},{1,9},{9,17},{17,25},{25,1},{2,10},{10... | collective-permute-start | bytes 417800 | tf_op jit(solution)/shard_map/ppermute | solution.py:25
  12.4 12.0 %collective-permute-start.1 = (bf16[32,2176]{1,0:T(8,128)(2,1)}, bf16[32,2176]{1,0:T(8,128)(2,1)S(1)}, u32[]{:S(2)}, u32[]{:S(2)}) collective-permute-start(bf16[32,2176]{1,0:T(8,128)(2,1)} %shard_map.288), channel_id=1, source_target_pairs={{0,16},{8,24},{16,0},{24,8},{1,17},{9,25},{17,1},{25,9},{2,18},{10... | collective-permute-start | bytes 417800 | tf_op jit(solution)/shard_map/ppermute | solution.py:25
  15.0 9.4 %collective-permute-start.2 = (bf16[32,2176]{1,0:T(8,128)(2,1)}, bf16[32,2176]{1,0:T(8,128)(2,1)S(1)}, u32[]{:S(2)}, u32[]{:S(2)}) collective-permute-start(bf16[32,2176]{1,0:T(8,128)(2,1)} %shard_map.288), channel_id=1, source_target_pairs={{0,24},{8,0},{16,8},{24,16},{1,25},{9,1},{17,9},{25,17},{2,26},{10... | collective-permute-start | bytes 417800 | tf_op jit(solution)/shard_map/ppermute | solution.py:25
  25.4 15.4 %collective-permute-start.3 = (bf16[4,32,2176]{2,1,0:T(8,128)(2,1)S(1)}, bf16[4,32,2176]{2,1,0:T(8,128)(2,1)S(1)}, u32[]{:S(2)}, u32[]{:S(2)}) collective-permute-start(bf16[4,32,2176]{2,1,0:T(8,128)(2,1)S(1)} %pad_maximum_fusion.4.refs_0_), channel_id=1, source_target_pairs={{0,2},{1,5},{2,0},{3,7},{4,6},{5,1},{6,4},{7,3},{8,10},{9,13},{10,... | collective-permute-start | bytes 1671176 | tf_op jit(solution)/shard_map/ppermute | solution.py:47
  26.9 13.8 %collective-permute-start.4 = (bf16[4,32,2176]{2,1,0:T(8,128)(2,1)S(1)}, bf16[4,32,2176]{2,1,0:T(8,128)(2,1)}, u32[]{:S(2)}, u32[]{:S(2)}) collective-permute-start(bf16[4,32,2176]{2,1,0:T(8,128)(2,1)S(1)} %pad_maximum_fusion.4.refs_0_), channel_id=1, source_target_pairs={{0,4},{1,3},{2,6},{3,1},{4,0},{5,7},{6,2},{7,5},{8,12},{9,11},{10,... | collective-permute-start | bytes 1671176 | tf_op jit(solution)/shard_map/ppermute | solution.py:47
  40.8 14.2 %collective-permute-start.5 = (bf16[4,32,2176]{2,1,0:T(8,128)(2,1)S(1)}, bf16[4,32,2176]{2,1,0:T(8,128)(2,1)}, u32[]{:S(2)}, u32[]{:S(2)}) collective-permute-start(bf16[4,32,2176]{2,1,0:T(8,128)(2,1)S(1)} %collective-permute-done.3.refs_1_), channel_id=1, source_target_pairs={{0,4},{1,3},{2,6},{3,1},{4,0},{5,7},{6,2},{7,5},{8,12},{9,11},{10,... | collective-permute-start | bytes 1671176 | tf_op jit(solution)/shard_map/ppermute | solution.py:47
  41.7 9.5 %collective-permute-start.6 = (bf16[32,3072]{1,0:T(8,128)(2,1)S(1)}, bf16[32,3072]{1,0:T(8,128)(2,1)S(1)}, u32[]{:S(2)}, u32[]{:S(2)}) collective-permute-start(bf16[32,3072]{1,0:T(8,128)(2,1)S(1)} %pad_maximum_fusion.12), channel_id=1, source_target_pairs={{0,8},{8,16},{16,24},{24,0},{1,9},{9,17},{17,25},{25,1},{2,10},{10... | collective-permute-start | bytes 589832 | tf_op jit(solution)/shard_map/ppermute | solution.py:25
  45.2 9.7 %collective-permute-start.7 = (bf16[32,3072]{1,0:T(8,128)(2,1)S(1)}, bf16[32,3072]{1,0:T(8,128)(2,1)S(1)}, u32[]{:S(2)}, u32[]{:S(2)}) collective-permute-start(bf16[32,3072]{1,0:T(8,128)(2,1)S(1)} %pad_maximum_fusion.12), channel_id=1, source_target_pairs={{0,24},{8,0},{16,8},{24,16},{1,25},{9,1},{17,9},{25,17},{2,26},{10... | collective-permute-start | bytes 589832 | tf_op jit(solution)/shard_map/ppermute | solution.py:25
  54.9 11.9 %collective-permute-start.8 = (bf16[32,3072]{1,0:T(8,128)(2,1)S(1)}, bf16[32,3072]{1,0:T(8,128)(2,1)S(1)}, u32[]{:S(2)}, u32[]{:S(2)}) collective-permute-start(bf16[32,3072]{1,0:T(8,128)(2,1)S(1)} %pad_maximum_fusion.12), channel_id=1, source_target_pairs={{0,16},{8,24},{16,0},{24,8},{1,17},{9,25},{17,1},{25,9},{2,18},{10... | collective-permute-start | bytes 589832 | tf_op jit(solution)/shard_map/ppermute | solution.py:25
  67.6 277.9 %reduce-scatter.4.cloned.1.call-start = ((), (), s32[]{:S(2)}) async-start(), calls=%async_computation.4 | async-start | bytes 901120 | tf_op jit(solution)/shard_map/reduce_scatter | solution.py:166
  67.8 14.6 %collective-permute-start.14 = (bf16[4,32,3072]{2,1,0:T(8,128)(2,1)S(1)}, bf16[4,32,3072]{2,1,0:T(8,128)(2,1)S(1)}, u32[]{:S(2)}, u32[]{:S(2)}) collective-permute-start(bf16[4,32,3072]{2,1,0:T(8,128)(2,1)S(1)} %pad_maximum_fusion.2.refs_0_), channel_id=1, source_target_pairs={{0,2},{1,5},{2,0},{3,7},{4,6},{5,1},{6,4},{7,3},{8,10},{9,13},{10,... | collective-permute-start | bytes 2359304 | tf_op jit(solution)/shard_map/ppermute | solution.py:47
  82.5 16.7 %collective-permute-start.15 = (bf16[4,32,3072]{2,1,0:T(8,128)(2,1)S(1)}, bf16[4,32,3072]{2,1,0:T(8,128)(2,1)S(1)}, u32[]{:S(2)}, u32[]{:S(2)}) collective-permute-start(bf16[4,32,3072]{2,1,0:T(8,128)(2,1)S(1)} %pad_maximum_fusion.2.refs_0_), channel_id=1, source_target_pairs={{0,4},{1,3},{2,6},{3,1},{4,0},{5,7},{6,2},{7,5},{8,12},{9,11},{10,... | collective-permute-start | bytes 2359304 | tf_op jit(solution)/shard_map/ppermute | solution.py:47
  84.4 14.7 %collective-permute-start.16 = (bf16[176,512]{1,0:T(8,128)(2,1)S(1)}, bf16[176,512]{1,0:T(8,128)(2,1)S(1)}, u32[]{:S(2)}, u32[]{:S(2)}) collective-permute-start(bf16[176,512]{1,0:T(8,128)(2,1)S(1)} %maximum_select_fusion.5), channel_id=1, source_target_pairs={{0,8},{8,16},{16,24},{24,0},{1,9},{9,17},{17,25},{25,1},{2,10},{10... | collective-permute-start | bytes 540680 | tf_op jit(solution)/shard_map/ppermute | solution.py:25
  84.4 14.7 %collective-permute-start.17 = (bf16[176,512]{1,0:T(8,128)(2,1)S(1)}, bf16[176,512]{1,0:T(8,128)(2,1)S(1)}, u32[]{:S(2)}, u32[]{:S(2)}) collective-permute-start(bf16[176,512]{1,0:T(8,128)(2,1)S(1)} %maximum_select_fusion.5), channel_id=1, source_target_pairs={{0,24},{8,0},{16,8},{24,16},{1,25},{9,1},{17,9},{25,17},{2,26},{10... | collective-permute-start | bytes 540680 | tf_op jit(solution)/shard_map/ppermute | solution.py:25
  104.5 17.5 %collective-permute-start.21 = (bf16[4,32,3072]{2,1,0:T(8,128)(2,1)S(1)}, bf16[4,32,3072]{2,1,0:T(8,128)(2,1)S(1)}, u32[]{:S(2)}, u32[]{:S(2)}) collective-permute-start(bf16[4,32,3072]{2,1,0:T(8,128)(2,1)S(1)} %collective-permute-done.14.refs_1_), channel_id=1, source_target_pairs={{0,4},{1,3},{2,6},{3,1},{4,0},{5,7},{6,2},{7,5},{8,12},{9,11},{10,... | collective-permute-start | bytes 2359304 | tf_op jit(solution)/shard_map/ppermute | solution.py:47
  106.5 15.4 %collective-permute-start.19 = (bf16[2,272,256]{2,1,0:T(8,128)(2,1)S(1)}, bf16[2,272,256]{2,1,0:T(8,128)(2,1)S(1)}, u32[]{:S(2)}, u32[]{:S(2)}) collective-permute-start(bf16[2,272,256]{2,1,0:T(8,128)(2,1)S(1)} %fusion.18), channel_id=1, source_target_pairs={{0,2},{1,5},{2,0},{3,7},{4,6},{5,1},{6,4},{7,3},{8,10},{9,13},{10,... | collective-permute-start | bytes 835592 | tf_op jit(solution)/shard_map/ppermute | solution.py:47
  106.8 15.1 %collective-permute-start.20 = (bf16[2,272,256]{2,1,0:T(8,128)(2,1)S(1)}, bf16[2,272,256]{2,1,0:T(8,128)(2,1)S(1)}, u32[]{:S(2)}, u32[]{:S(2)}) collective-permute-start(bf16[2,272,256]{2,1,0:T(8,128)(2,1)S(1)} %fusion.18), channel_id=1, source_target_pairs={{0,4},{1,3},{2,6},{3,1},{4,0},{5,7},{6,2},{7,5},{8,12},{9,11},{10,... | collective-permute-start | bytes 835592 | tf_op jit(solution)/shard_map/ppermute | solution.py:47
  106.9 14.9 %collective-permute-start.22 = (bf16[176,512]{1,0:T(8,128)(2,1)S(1)}, bf16[176,512]{1,0:T(8,128)(2,1)S(1)}, u32[]{:S(2)}, u32[]{:S(2)}) collective-permute-start(bf16[176,512]{1,0:T(8,128)(2,1)S(1)} %maximum_select_fusion.5), channel_id=1, source_target_pairs={{0,16},{8,24},{16,0},{24,8},{1,17},{9,25},{17,1},{25,9},{2,18},{10... | collective-permute-start | bytes 540680 | tf_op jit(solution)/shard_map/ppermute | solution.py:25
  123.4 12.3 %collective-permute-start.23 = (bf16[2,272,256]{2,1,0:T(8,128)(2,1)S(1)}, bf16[2,272,256]{2,1,0:T(8,128)(2,1)S(1)}, u32[]{:S(2)}, u32[]{:S(2)}) collective-permute-start(bf16[2,272,256]{2,1,0:T(8,128)(2,1)S(1)} %collective-permute-done.19), channel_id=1, source_target_pairs={{0,4},{1,3},{2,6},{3,1},{4,0},{5,7},{6,2},{7,5},{8,12},{9,11},{10,... | collective-permute-start | bytes 835592 | tf_op jit(solution)/shard_map/ppermute | solution.py:47
  138.7 18.7 %collective-permute-start.29 = (bf16[4,176,512]{2,1,0:T(8,128)(2,1)S(1)}, bf16[4,176,512]{2,1,0:T(8,128)(2,1)}, u32[]{:S(2)}, u32[]{:S(2)}) collective-permute-start(bf16[4,176,512]{2,1,0:T(8,128)(2,1)S(1)} %pad_maximum_fusion.3.refs_0_), channel_id=1, source_target_pairs={{0,2},{1,5},{2,0},{3,7},{4,6},{5,1},{6,4},{7,3},{8,10},{9,13},{10,... | collective-permute-start | bytes 2162696 | tf_op jit(solution)/shard_map/ppermute | solution.py:47
  157.5 20.5 %collective-permute-start.30 = (bf16[4,176,512]{2,1,0:T(8,128)(2,1)S(1)}, bf16[4,176,512]{2,1,0:T(8,128)(2,1)S(1)}, u32[]{:S(2)}, u32[]{:S(2)}) collective-permute-start(bf16[4,176,512]{2,1,0:T(8,128)(2,1)S(1)} %pad_maximum_fusion.3.refs_0_), channel_id=1, source_target_pairs={{0,4},{1,3},{2,6},{3,1},{4,0},{5,7},{6,2},{7,5},{8,12},{9,11},{10,... | collective-permute-start | bytes 2162696 | tf_op jit(solution)/shard_map/ppermute | solution.py:47
  158.6 19.4 %collective-permute-start.31 = (bf16[4,176,512]{2,1,0:T(8,128)(2,1)}, bf16[4,176,512]{2,1,0:T(8,128)(2,1)S(1)}, u32[]{:S(2)}, u32[]{:S(2)}) collective-permute-start(bf16[4,176,512]{2,1,0:T(8,128)(2,1)} %collective-permute-done.29.refs_1_), channel_id=1, source_target_pairs={{0,4},{1,3},{2,6},{3,1},{4,0},{5,7},{6,2},{7,5},{8,12},{9,11},{10,... | collective-permute-start | bytes 2162696 | tf_op jit(solution)/shard_map/ppermute | solution.py:47
  162.3 16.9 %collective-permute-start.33 = (bf16[4,176,512]{2,1,0:T(8,128)(2,1)}, bf16[4,176,512]{2,1,0:T(8,128)(2,1)S(1)}, u32[]{:S(2)}, u32[]{:S(2)}) collective-permute-start(bf16[4,176,512]{2,1,0:T(8,128)(2,1)} %collective-permute-done.29.refs_1_), channel_id=1, source_target_pairs={{0,1},{1,0},{2,3},{3,2},{4,5},{5,4},{6,7},{7,6},{8,9},{9,8},{10,11... | collective-permute-start | bytes 2162696 | tf_op jit(solution)/shard_map/ppermute | solution.py:25
  215.5 6.6 %collective-permute-start.38 = (bf16[2816,384]{1,0:T(8,128)(2,1)}, bf16[2816,384]{1,0:T(8,128)(2,1)}, u32[]{:S(2)}, u32[]{:S(2)}) collective-permute-start(bf16[2816,384]{1,0:T(8,128)(2,1)} %get-tuple-element.185.refs_0_), channel_id=1, source_target_pairs={{0,1},{1,0},{2,3},{3,2},{4,5},{5,4},{6,7},{7,6},{8,9},{9,8},{10,11... | collective-permute-start | bytes 6488072 | tf_op jit(solution)/shard_map/ppermute | solution.py:25
  216.0 6.1 %collective-permute-start.39 = (bf16[384,1024]{1,0:T(8,128)(2,1)S(1)}, bf16[384,1024]{1,0:T(8,128)(2,1)S(1)}, u32[]{:S(2)}, u32[]{:S(2)}) collective-permute-start(bf16[384,1024]{1,0:T(8,128)(2,1)S(1)} %copy-done.6), channel_id=1, source_target_pairs={{0,1},{1,0},{2,3},{3,2},{4,5},{5,4},{6,7},{7,6},{8,9},{9,8},{10,11... | collective-permute-start | bytes 2359304 | tf_op jit(solution)/shard_map/ppermute | solution.py:25
  216.1 15.3 %collective-permute-start.36 = (bf16[384,2816]{1,0:T(8,128)(2,1)}, bf16[384,2816]{1,0:T(8,128)(2,1)}, u32[]{:S(2)}, u32[]{:S(2)}) collective-permute-start(bf16[384,2816]{1,0:T(8,128)(2,1)} %get-tuple-element.196.refs_2_), channel_id=1, source_target_pairs={{0,1},{1,0},{2,3},{3,2},{4,5},{5,4},{6,7},{7,6},{8,9},{9,8},{10,11... | collective-permute-start | bytes 6488072 | tf_op jit(solution)/shard_map/ppermute | solution.py:25
  216.5 15.0 %collective-permute-start.37 = (bf16[384,2816]{1,0:T(8,128)(2,1)}, bf16[384,2816]{1,0:T(8,128)(2,1)}, u32[]{:S(2)}, u32[]{:S(2)}) collective-permute-start(bf16[384,2816]{1,0:T(8,128)(2,1)} %get-tuple-element.206.refs_2_), channel_id=1, source_target_pairs={{0,1},{1,0},{2,3},{3,2},{4,5},{5,4},{6,7},{7,6},{8,9},{9,8},{10,11... | collective-permute-start | bytes 6488072 | tf_op jit(solution)/shard_map/ppermute | solution.py:25
  229.8 19.2 %collective-permute-start.40 = (bf16[8,176,512]{2,1,0:T(8,128)(2,1)}, bf16[8,176,512]{2,1,0:T(8,128)(2,1)S(1)}, u32[]{:S(2)}, u32[]{:S(2)}) collective-permute-start(bf16[8,176,512]{2,1,0:T(8,128)(2,1)} %get-tuple-element.186), channel_id=1, source_target_pairs={{0,2},{1,5},{2,0},{3,7},{4,6},{5,1},{6,4},{7,3},{8,10},{9,13},{10,... | collective-permute-start | bytes 4325384 | tf_op jit(solution)/shard_map/ppermute | solution.py:47
  230.2 9.3 %collective-permute-start.41 = (bf16[1024,384]{1,0:T(8,128)(2,1)S(1)}, bf16[1024,384]{1,0:T(8,128)(2,1)S(1)}, u32[]{:S(2)}, u32[]{:S(2)}) collective-permute-start(bf16[1024,384]{1,0:T(8,128)(2,1)S(1)} %copy-done.3), channel_id=1, source_target_pairs={{0,1},{1,0},{2,3},{3,2},{4,5},{5,4},{6,7},{7,6},{8,9},{9,8},{10,11... | collective-permute-start | bytes 2359304 | tf_op jit(solution)/shard_map/ppermute | solution.py:25
  254.1 16.6 %collective-permute-start.45 = (bf16[4,176,512]{2,1,0:T(8,128)(2,1)S(1)}, bf16[4,176,512]{2,1,0:T(8,128)(2,1)S(1)}, u32[]{:S(2)}, u32[]{:S(2)}) collective-permute-start(bf16[4,176,512]{2,1,0:T(8,128)(2,1)S(1)} %add_convert_fusion.7), channel_id=1, source_target_pairs={{0,4},{1,3},{2,6},{3,1},{4,0},{5,7},{6,2},{7,5},{8,12},{9,11},{10,... | collective-permute-start | bytes 2162696 | tf_op jit(solution)/shard_map/ppermute | solution.py:47
  255.3 9.7 %collective-permute-start.43 = (bf16[2,272,256]{2,1,0:T(8,128)(2,1)S(1)}, bf16[2,272,256]{2,1,0:T(8,128)(2,1)}, u32[]{:S(2)}, u32[]{:S(2)}) collective-permute-start(bf16[2,272,256]{2,1,0:T(8,128)(2,1)S(1)} %fusion.15), channel_id=1, source_target_pairs={{0,2},{1,5},{2,0},{3,7},{4,6},{5,1},{6,4},{7,3},{8,10},{9,13},{10,... | collective-permute-start | bytes 835592 | tf_op jit(solution)/shard_map/ppermute | solution.py:47
  255.9 14.8 %collective-permute-start.44 = (bf16[2,272,256]{2,1,0:T(8,128)(2,1)S(1)}, bf16[2,272,256]{2,1,0:T(8,128)(2,1)S(1)}, u32[]{:S(2)}, u32[]{:S(2)}) collective-permute-start(bf16[2,272,256]{2,1,0:T(8,128)(2,1)S(1)} %fusion.15), channel_id=1, source_target_pairs={{0,4},{1,3},{2,6},{3,1},{4,0},{5,7},{6,2},{7,5},{8,12},{9,11},{10,... | collective-permute-start | bytes 835592 | tf_op jit(solution)/shard_map/ppermute | solution.py:47
  270.7 22.4 %collective-permute-start.47 = (bf16[8,32,2816]{2,1,0:T(8,128)(2,1)}, bf16[8,32,2816]{2,1,0:T(8,128)(2,1)}, u32[]{:S(2)}, u32[]{:S(2)}) collective-permute-start(bf16[8,32,2816]{2,1,0:T(8,128)(2,1)} %get-tuple-element.212), channel_id=1, source_target_pairs={{0,2},{1,5},{2,0},{3,7},{4,6},{5,1},{6,4},{7,3},{8,10},{9,13},{10,... | collective-permute-start | bytes 4325384 | tf_op jit(solution)/shard_map/ppermute | solution.py:47
  272.4 5.3 %collective-permute-start.51 = (bf16[384,1024]{1,0:T(8,128)(2,1)S(1)}, bf16[384,1024]{1,0:T(8,128)(2,1)}, u32[]{:S(2)}, u32[]{:S(2)}) collective-permute-start(bf16[384,1024]{1,0:T(8,128)(2,1)S(1)} %copy-done.2), channel_id=1, source_target_pairs={{0,1},{1,0},{2,3},{3,2},{4,5},{5,4},{6,7},{7,6},{8,9},{9,8},{10,11... | collective-permute-start | bytes 2359304 | tf_op jit(solution)/shard_map/ppermute | solution.py:25
  272.5 5.2 %collective-permute-start.48 = (bf16[1024,384]{1,0:T(8,128)(2,1)S(1)}, bf16[1024,384]{1,0:T(8,128)(2,1)S(1)}, u32[]{:S(2)}, u32[]{:S(2)}) collective-permute-start(bf16[1024,384]{1,0:T(8,128)(2,1)S(1)} %copy-done), channel_id=1, source_target_pairs={{0,1},{1,0},{2,3},{3,2},{4,5},{5,4},{6,7},{7,6},{8,9},{9,8},{10,11... | collective-permute-start | bytes 2359304 | tf_op jit(solution)/shard_map/ppermute | solution.py:25
  275.4 9.9 %collective-permute-start.46 = (bf16[2,272,256]{2,1,0:T(8,128)(2,1)}, bf16[2,272,256]{2,1,0:T(8,128)(2,1)S(1)}, u32[]{:S(2)}, u32[]{:S(2)}) collective-permute-start(bf16[2,272,256]{2,1,0:T(8,128)(2,1)} %collective-permute-done.43), channel_id=1, source_target_pairs={{0,4},{1,3},{2,6},{3,1},{4,0},{5,7},{6,2},{7,5},{8,12},{9,11},{10,... | collective-permute-start | bytes 835592 | tf_op jit(solution)/shard_map/ppermute | solution.py:47
  298.0 19.0 %collective-permute-start.53 = (bf16[8,32,2816]{2,1,0:T(8,128)(2,1)S(1)}, bf16[8,32,2816]{2,1,0:T(8,128)(2,1)S(1)}, u32[]{:S(2)}, u32[]{:S(2)}) collective-permute-start(bf16[8,32,2816]{2,1,0:T(8,128)(2,1)S(1)} %copy-done.69), channel_id=1, source_target_pairs={{0,2},{1,5},{2,0},{3,7},{4,6},{5,1},{6,4},{7,3},{8,10},{9,13},{10,... | collective-permute-start | bytes 4325384 | tf_op jit(solution)/shard_map/ppermute | solution.py:47
  320.3 19.3 %collective-permute-start.61 = (bf16[4,32,5632]{2,1,0:T(8,128)(2,1)}, bf16[4,32,5632]{2,1,0:T(8,128)(2,1)}, u32[]{:S(2)}, u32[]{:S(2)}) collective-permute-start(bf16[4,32,5632]{2,1,0:T(8,128)(2,1)} %pad_maximum_fusion), channel_id=1, source_target_pairs={{0,4},{1,3},{2,6},{3,1},{4,0},{5,7},{6,2},{7,5},{8,12},{9,11},{10,... | collective-permute-start | bytes 4325384 | tf_op jit(solution)/shard_map/ppermute | solution.py:47
  325.1 78.5 %reduce-scatter.8.cloned.1.call-start = ((), (), s32[]{:S(2)}) async-start(), calls=%async_computation.6 | async-start | bytes 1802240 | tf_op jit(solution)/shard_map/reduce_scatter | solution.py:166
  345.6 16.6 %collective-permute-start.63 = (bf16[8,32,2048]{2,1,0:T(8,128)(2,1)}, bf16[8,32,2048]{2,1,0:T(8,128)(2,1)S(1)}, u32[]{:S(2)}, u32[]{:S(2)}) collective-permute-start(bf16[8,32,2048]{2,1,0:T(8,128)(2,1)} %get-tuple-element.251), channel_id=1, source_target_pairs={{0,2},{1,5},{2,0},{3,7},{4,6},{5,1},{6,4},{7,3},{8,10},{9,13},{10,... | collective-permute-start | bytes 3145736 | tf_op jit(solution)/shard_map/ppermute | solution.py:47
  347.1 31.0 %collective-permute-start.62 = (bf16[8,32,3200]{2,1,0:T(8,128)(2,1)}, bf16[8,32,3200]{2,1,0:T(8,128)(2,1)S(1)}, u32[]{:S(2)}, u32[]{:S(2)}) collective-permute-start(bf16[8,32,3200]{2,1,0:T(8,128)(2,1)} %get-tuple-element.250), channel_id=1, source_target_pairs={{0,2},{1,5},{2,0},{3,7},{4,6},{5,1},{6,4},{7,3},{8,10},{9,13},{10,... | collective-permute-start | bytes 4915208 | tf_op jit(solution)/shard_map/ppermute | solution.py:47
  351.6 69.5 %reduce-scatter.6.cloned.1.call-start = ((), (), s32[]{:S(2)}) async-start(), calls=%async_computation.5 | async-start | bytes 655360 | tf_op jit(solution)/shard_map/reduce_scatter | solution.py:166
  379.0 9.5 %collective-permute-start.68 = (bf16[4,32,2048]{2,1,0:T(8,128)(2,1)}, bf16[4,32,2048]{2,1,0:T(8,128)(2,1)}, u32[]{:S(2)}, u32[]{:S(2)}) collective-permute-start(bf16[4,32,2048]{2,1,0:T(8,128)(2,1)} %add_convert_fusion.9), channel_id=1, source_target_pairs={{0,4},{1,3},{2,6},{3,1},{4,0},{5,7},{6,2},{7,5},{8,12},{9,11},{10,... | collective-permute-start | bytes 1572872 | tf_op jit(solution)/shard_map/ppermute | solution.py:47
  381.7 15.6 %collective-permute-start.64 = (bf16[4,32,3200]{2,1,0:T(8,128)(2,1)}, bf16[4,32,3200]{2,1,0:T(8,128)(2,1)}, u32[]{:S(2)}, u32[]{:S(2)}) collective-permute-start(bf16[4,32,3200]{2,1,0:T(8,128)(2,1)} %add_convert_fusion.1), channel_id=1, source_target_pairs={{0,4},{1,3},{2,6},{3,1},{4,0},{5,7},{6,2},{7,5},{8,12},{9,11},{10,... | collective-permute-start | bytes 2457608 | tf_op jit(solution)/shard_map/ppermute | solution.py:47
  399.8 14.2 %collective-permute-start.65 = (bf16[32,3200]{1,0:T(8,128)(2,1)S(1)}, bf16[32,3200]{1,0:T(8,128)(2,1)S(1)}, u32[]{:S(2)}, u32[]{:S(2)}) collective-permute-start(bf16[32,3200]{1,0:T(8,128)(2,1)S(1)} %get-tuple-element.284), channel_id=1, source_target_pairs={{0,8},{8,16},{16,24},{24,0},{1,9},{9,17},{17,25},{25,1},{2,10},{10... | collective-permute-start | bytes 614408 | tf_op jit(solution)/shard_map/ppermute | solution.py:25
  399.8 21.3 %collective-permute-start.66 = (bf16[32,3200]{1,0:T(8,128)(2,1)S(1)}, bf16[32,3200]{1,0:T(8,128)(2,1)S(1)}, u32[]{:S(2)}, u32[]{:S(2)}) collective-permute-start(bf16[32,3200]{1,0:T(8,128)(2,1)S(1)} %get-tuple-element.283), channel_id=1, source_target_pairs={{0,16},{8,24},{16,0},{24,8},{1,17},{9,25},{17,1},{25,9},{2,18},{10... | collective-permute-start | bytes 614408 | tf_op jit(solution)/shard_map/ppermute | solution.py:25
  401.9 19.2 %collective-permute-start.67 = (bf16[32,3200]{1,0:T(8,128)(2,1)S(1)}, bf16[32,3200]{1,0:T(8,128)(2,1)S(1)}, u32[]{:S(2)}, u32[]{:S(2)}) collective-permute-start(bf16[32,3200]{1,0:T(8,128)(2,1)S(1)} %get-tuple-element.282), channel_id=1, source_target_pairs={{0,24},{8,0},{16,8},{24,16},{1,25},{9,1},{17,9},{25,17},{2,26},{10... | collective-permute-start | bytes 614408 | tf_op jit(solution)/shard_map/ppermute | solution.py:25
  (96 other events, 868.9 us)
Sparse Core Ops, SparseCore 0:
  67.8 103.1 all-gather.1
  325.3 20.2 reduce-scatter.3
  351.7 32.2 reduce-scatter.7
  390.9 26.0 reduce-scatter.5

commit v4 on v3

--- a/solution.py
+++ b/solution.py
@@ -54,9 +54,10 @@
     return (y + by_y) % 2, (x + by_x) % 2
 
 
-def gathered(own, early, late, corner):
+def gathered(own, early, late, corner, others=()):
     pieces = [(own, 0, 0, 0), (early, 1, 0, 0), (late, 0, 1, 0), (corner, 1, 1, 0)]
-    return pieces + [(flip(a, "c"), i, j, 1) for a, i, j, _ in pieces]
+    others = list(others) + [flip(a, "c") for a, _, _, _ in pieces[len(others) :]]
+    return pieces + [(a, i, j, 1) for a, (_, i, j, _) in zip(others, pieces)]
 
 
 def sources(pieces):
@@ -109,7 +110,7 @@
     )(where, *arrays)
 
 
-def layout():
+def layout(by_z):
     _, _, _, c = place()
     depth, height = lax.axis_size("z"), lax.axis_size("y")
     if not square_plane():
@@ -119,7 +120,10 @@
         y, x = neighbour(early, late, c)
         return (jnp.arange(depth, dtype=jnp.int32) * 2 + y) * 2 + x
 
-    return [jnp.concatenate([column(1, 0), column(1, 1)]), column(0, 1), column(0, 0)]
+    columns = [column(1, 0), column(1, 1), column(0, 1), column(0, 0)]
+    if by_z:
+        return [jnp.stack(columns, axis=1).reshape(-1)]
+    return [jnp.concatenate(columns[:2]), *columns[2:]]
 
 
 def wide(a):
@@ -129,6 +133,16 @@
 class Sum:
     def __init__(self, blocks):
         self.blocks = blocks
+        self.depth = lax.axis_size("z")
+
+    def zeroth(self, done=()):
+        if square_plane():
+            (blocks,) = after(done, self.blocks, ())[0]
+            _, rows, width = blocks.shape
+            part = lax.psum_scatter(blocks.reshape(-1, width), "z", scatter_dimension=0, tiled=True)
+            part = part.reshape(4, rows, width)
+            self.blocks, self.depth = [part[:2], part[2:3], part[3:]], 1
+        return self.blocks
 
     def first(self, done=()):
         self.arrived = cross(after(done, self.blocks[0]), False) if square_plane() else ()
@@ -140,11 +154,10 @@
             for p in parts:
                 p.through = ()
             return ()
-        depth = lax.axis_size("z")
         sums = []
         for p in parts:
             arrived, kept = after(done, p.arrived, p.blocks[1])
-            sums.append((wide(kept) + wide(arrived[depth:])).astype(BF16))
+            sums.append((wide(kept) + wide(arrived[p.depth :])).astype(BF16))
         through = cross(sums[0] if len(sums) == 1 else jnp.concatenate(sums, axis=2), True)
         at = 0
         for p, part in zip(parts, sums):
@@ -153,8 +166,10 @@
         return through
 
     def total(self):
-        depth = lax.axis_size("z")
-        return (wide(self.blocks[2]) + wide(self.arrived[:depth]) + wide(self.through)).astype(BF16)
+        return (wide(self.blocks[2]) + wide(self.arrived[: self.depth]) + wide(self.through)).astype(BF16)
+
+    def result(self):
+        return self.total()[0] if square_plane() else self.third()
 
     def third(self, *others):
         parts = (self, *others)
@@ -174,9 +189,9 @@
         return [block[0]] + [shift(block[k], "z", k) for k in range(1, depth)]
 
 
-def weight_grads(groups, tile, halves=False, table=None):
+def weight_grads(groups, tile, halves=False, table=None, by_z=False):
     _, _, _, c = place()
-    chips = layout()
+    chips = layout(by_z)
     spans = [a.shape[0] for a in chips]
     chips = jnp.concatenate(chips)
     count = chips.shape[0]
@@ -848,18 +863,19 @@
 
     def body(*refs):
         term_refs, weight_refs = refs[: len(terms)], refs[len(terms) : len(terms) + count]
-        in_ref, gain_ref, middle_ref, wm_ref = refs[len(terms) + count : len(terms) + count + 4]
-        outs, middle_outs = refs[len(terms) + count + 4 : -7], refs[-7:-5]
+        in_ref, gain_ref, wm_ref = refs[len(terms) + count : len(terms) + count + 3]
+        middle_refs = refs[len(terms) + count + 3 : len(terms) + count + 3 + len(middle)]
+        outs, middle_outs = refs[len(terms) + count + 3 + len(middle) : -7], refs[-7:-5]
         in_out, out_out, bias_out, head_out, gain_out = refs[-5:]
 
-        def summed_terms(at):
+        def summed_terms(at, term_refs=term_refs):
             total = term_refs[0][:, at].astype(F32)
             for t in term_refs[1:]:
                 total = total + t[:, at].astype(F32)
             return total
 
         for n, out in enumerate(middle_outs):
-            out[...] = middle_ref[:, n * width : (n + 1) * width].astype(F32)
+            out[...] = summed_terms(slice(n * width, (n + 1) * width), middle_refs)
         by_row = jnp.sum(wm_ref[...].astype(F32) * middle_outs[0][...], axis=1, keepdims=True)
         for n, out in enumerate(outs):
             out[...] = summed_terms(slice(n * width, (n + 1) * width))
@@ -874,7 +890,7 @@
         by_rank = jnp.sum(in_ref[...].astype(F32) * turned[:rank], axis=0, keepdims=True)
         gain_out[...] = (turned[LANES - 1 :] + by_rank) / gain_ref[...].astype(F32)
 
-    ins = [*terms, *weights, turned_in, gain, middle, w_middle]
+    ins = [*terms, *weights, turned_in, gain, w_middle, *middle]
     shapes = [(rows, width)] * (count + 2) + [(rank, rows), (rank, rows), (1, rows), (1, head_rows), (1, rows)]
     return kernel_call(body, (1,), [(a, spec(a.shape)) for a in ins], [(o, F32, spec(o)) for o in shapes])
 
@@ -912,7 +928,7 @@
 
     def distant(self, done=()):
         if square_plane():
-            self.far = cross(after(done, self.arrived[0]), True)
+            self.far = cross(after(done, self.arrived[1]), False)
             return self.far
         beside, mine = after(done, self.arrived, self.mine)
         self.before = jnp.where(self.x == 1, beside, nothing(mine))
@@ -996,21 +1012,22 @@
         other = flip(lax.dynamic_slice_in_dim(w_down, (1 - c) * half, half, 1), "c")
         chip_down = jnp.where(c == 0, jnp.concatenate([keep, other]), jnp.concatenate([other, keep]))
         one = by_distance(first, odd_shifts(first), even_shifts(first))
-        one_early, one_late = cross(one, False), cross(one, True)
-        now = (one_early, one_late)
-        square_weights, one_next = after(now, square_weights, one_early)
+        square_next = after(one, square_weights)
+        one_early, one_late, one_other = cross(one, False), cross(one, True), flip(one, "c")
+        two_odd = odd_shifts(square_next)
+        now = (one_early, one_late, two_odd, one_other)
+        one_next, one_late, square_next = after(now, one_early, one_late, square_weights)
         one_corner = cross(one_next, True)
-        two_odd = odd_shifts(square_weights)
-        now = (one_corner, two_odd)
-        square_weights, one = after(now, square_weights, one)
-        wait_for = two_even = even_shifts(square_weights)
-        two = by_distance(square_weights, two_odd, two_even)
-        one, two = after(two, one, two)
-        first = assemble(gathered(one, one_early, one_late, one_corner), own, (width, table_columns))
+        two_even = even_shifts(square_next)
+        one_others = [one_other, flip(one_next, "c"), flip(one_late, "c")]
+        wait_for = now = (one_corner, two_even, one_others)
+        one, two, chip_down = after(now, one, by_distance(square_weights, two_odd, two_even), chip_down)
+        first = assemble(gathered(one, one_early, one_late, one_corner, one_others), own, (width, table_columns))
         two_early = cross(two, False)
-        first, two, chip_down = after((first, two_early), first, two, chip_down)
+        three_odd = odd_shifts(chip_down)
+        first, two, chip_down = after((first, two_early, three_odd), first, two, chip_down)
         two_late = cross(two, True)
-        three_odd = odd_shifts(chip_down)
+        three_even = even_shifts(chip_down)
     else:
         first = lax.all_gather(first, AXES, axis=0, tiled=True)
         second = lax.all_gather(square_weights, AXES, axis=0, tiled=True)
@@ -1021,21 +1038,24 @@
     row_one, row_two = vectors[1:2], vectors[2:3]
     row_head = vectors[3].reshape(devices, own)[:, : head_gain.shape[0]].reshape(1, HEAD_V)
     if fast:
-        message, two_early, chip_down = after((two_late, three_odd), message, two_early, chip_down)
+        message, two_early, two_late = after((two_late, three_even), message, two_early, two_late)
+    both, down_pair = pair(normed_turned), pair(cotangent)
     passing = Passing(message)
     if fast:
-        two_next, three_next = after(passing.mine, two_early, chip_down)
+        two_next, two_late = after(passing.mine, two_early, two_late)
         two_corner = cross(two_next, True)
-        three_even = even_shifts(three_next)
-        now = (passing.near(), two_corner, three_even)
-        now = passing.distant(now)
-        three, two, two_early, two_late, two_corner = after(
-            now, by_distance(chip_down, three_odd, three_even), two, two_early, two_late, two_corner
-        )
+        two_others = [flip(a, "c") for a in (two, two_next, two_late)]
+        now = (passing.near(), two_corner, both, down_pair, two_others)
+        two_corner = after(now, two_corner)
+        two_others.append(flip(two_corner, "c"))
+        three = by_distance(chip_down, three_odd, three_even)
+        now = (passing.distant(now), two_others, three)
+        three, two = after(now, three, two)
         three_early = cross(three, False)
-        second = assemble(gathered(two, two_early, two_late, two_corner), own, (width, 3 * width))
+        second = assemble(gathered(two, two_early, two_late, two_corner, two_others), own, (width, 3 * width))
         entered = passing.entering(now)
-        entered, second, three, three_early = after((entered, second, three_early), entered, second, three, three_early)
+        now = (entered, second, three_early)
+        entered, second, three, three_early = after(now, entered, second, three, three_early)
         three_late, three_corner = cross(three, True), cross(three_early, True)
     else:
         passing.near()
@@ -1049,34 +1069,39 @@
         w_down_all = assemble(
             gathered(three, three_early, three_late, three_corner), chip_down.shape[0], (ff, width), True
         )
+    two_pair, gated_pair = pair(two_turned), pair(gated)
     output, inner, grad_gate, grad_up, grad_hidden, grad_low = feed(
         normed_two, cotangent, w_both, w_down_all, hidden, row_two
     )
 
-    both = pair(normed_turned)
-    two_pair = pair(two_turned)
-    down = weight_grads([(pair(inner), [pair(cotangent)])], 512, True)
-    grad_low, gate_pair, up_pair = after(down.blocks, grad_low, pair(grad_gate), pair(grad_up))
+    gate_pair = pair(grad_gate)
+    inner, grad_up, grad_low = after(gate_pair, inner, grad_up, grad_low)
+    gate = weight_grads([(two_pair, [gate_pair])], ff // 2)
+    inner_pair, up_pair = pair(inner), pair(grad_up)
+    inner_pair, grad_low = after(gate.blocks, inner_pair, grad_low)
+    down = weight_grads([(inner_pair, [down_pair])], 512, True, by_z=True)
+    down_blocks = down.blocks
+    down.zeroth()
+    grad_low = after(down_blocks, grad_low)
     grad_mixed, grad_swish, grad_head_gain, message_back = head_back(
         grad_low, second, mixed, swish, row_head, queries, gate_pre, message[:, HEAD_V:], marks
     )
-    gate = weight_grads([(two_pair, [gate_pair])], ff // 2)
-    now = (down.first(), message_back, gate.blocks)
+    now = (gate.first(), message_back)
     passing = Passing(after(now, message_back), True)
     now = passing.mine
+    swish_pair, low_pair = pair(after(now, grad_swish)), pair(after(now, grad_low))
     up = weight_grads([(two_pair, [after(now, up_pair)])], ff // 2)
-    now = (passing.near(), down.second(now), up.blocks)
-    down_part = down.third()
-    swish_pair, gated_pair, low_pair = after(now, pair(grad_swish), pair(gated), pair(grad_low))
     middle = weight_grads([(both, [swish_pair]), (gated_pair, [low_pair])], width)
-    now = (passing.distant(now), gate.first(now), middle.blocks)
+    now = (passing.near(), gate.second(now), up.blocks, middle.blocks)
+    now = passing.distant(now)
     leaving = passing.entering(now)
     now = leaving
     grad_query, grad_key, grad_value, grad_gate_pre, grad_rank = mixer_back(
         queries, keys, values, gate_pre, grad_mixed, states, leaving, first, marks, doc_row, rank
     )
     now = (up.first(now), grad_query)
-    gate.second(now, up)
+    up.second(now)
+    middle.first(now)
     inside_pairs = [pair(a) for a in after(now, grad_query, grad_key, grad_value, grad_rank, grad_gate_pre)]
     head_terms = grad_head_gain + flip(grad_head_gain, "c")
     head_terms = jnp.pad(head_terms.reshape(devices, -1), ((0, 0), (0, own - head_gain.shape[0]))).reshape(width, 1)
@@ -1086,16 +1111,20 @@
         width,
         table=([(both, inside_pairs[3]), (inside_pairs[4], pair(low))], base),
     )
-    now = (inside.blocks, gate.through, up.through, down_part)
+    now = (inside.blocks, middle.arrived, up.through)
+    gate.through, up.through = after(inside.blocks, gate.through, up.through)
     gates_part = gate.third(up)
     input_grad = input_back(
         (grad_query, grad_key, grad_value, grad_swish), first, second, after(now, grad_rank), tokens, row_one,
         grad_hidden,
     )
-    now = (input_grad, middle.first(now), inside.first(now))
-    now = (inside.second(now), middle.second(now))
-    middle_part = middle.third()
+    now = (input_grad, inside.first(now), middle.second(now))
+    down.first(now)
+    middle_terms = middle.third_terms()
+    inside.second(now)
+    down.second(inside.through)
     inside_terms = inside.third_terms()
+    down_part = down.result()
 
     chip_half = ff // devices
     down_sum = wide(down_part)
@@ -1105,7 +1134,7 @@
     g_gate, g_up = wide(gates_part[:, :ff]), wide(gates_part[:, ff:])
     g_gain_two = (jnp.sum(wide(w_gate) * g_gate, axis=1) + jnp.sum(wide(w_up) * g_up, axis=1)) / wide(gain_two)
     g_query, g_key, g_value, g_swish, g_output, g_rank_in, g_rank_out, g_bias, g_head, g_gain_one = finish(
-        inside_terms, (w_query, w_key, w_value), rank_in.T, gain_one.reshape(1, own), middle_part, w_swish,
+        inside_terms, (w_query, w_key, w_value), rank_in.T, gain_one.reshape(1, own), middle_terms, w_swish,
         rank, head_gain.shape[0],
     )
     return (

time: 436 us -> 412 us (0.945)
  waiting for transfers between devices: 169 us -> 130 us
  starting transfers between devices: 49.9 us -> 56.3 us
    ppermute x46 -> x49, waiting for transfers between devices: 82.5 us -> 60 us  [shift(): lax.ppermute(value, axis, [(i, (i + step) % size) for i in range(size)])]
    ppermute x24 -> x25, waiting for transfers between devices: 80.9 us -> 70.3 us  [cross(): return lax.ppermute(value, ('y', 'x', 'c'), perm)]
    reduce_scatter x3 -> x1, waiting for transfers between devices: 5.94 us -> 0.01 us  [third(): lax.psum_scatter(total.reshape(-1, total.shape[-1]), axes, scatter_dimens...]
    ppermute x46 -> x49, starting transfers between devices: 27.7 us -> 33 us  [shift(): lax.ppermute(value, axis, [(i, (i + step) % size) for i in range(size)])]
    unnamed x150 -> x158, local copies, waits for them, and re-layouts: 12.4 us -> 14.1 us
    ppermute x24 -> x25, starting transfers between devices: 22 us -> 23.1 us  [cross(): return lax.ppermute(value, ('y', 'x', 'c'), perm)]
  transfers between devices with their start and end apart: 74 -> 77, of which waited for: 43 -> 33; matrix products, arithmetic and copies ran while one was open for 8% -> 11% of each run, Pallas kernels for 26% -> 28%
where the time goes in v4:
time: 412 us; the launch traced here: 405 us
  Pallas kernels  142 us (34%)
  waiting for transfers between devices  130 us (32%)
  starting transfers between devices  56.3 us (14%)
  other arithmetic  36.3 us (9%)
  local copies, waits for them, and re-layouts  25.5 us (6%)
  between operations  15.3 us (4%)
    pallas_call x8, Pallas kernels, kernel_call(): pl.pallas_call(body, grid=grid, in_specs=[s for _, s in ins], out_specs=[...  87 us
    ppermute x25, waiting for transfers between devices, cross(): return lax.ppermute(value, ('y', 'x', 'c'), perm)  70.3 us
    ppermute x49, waiting for transfers between devices, shift(): lax.ppermute(value, axis, [(i, (i + step) % size) for i in range(size)])  60 us
    pallas_call x5, Pallas kernels, weight_grads(): pl.pallas_call(body, grid_spec=pltpu.PrefetchScalarGridSpec(num_scalar_pr...  37.4 us
    ppermute x49, starting transfers between devices, shift(): lax.ppermute(value, axis, [(i, (i + step) % size) for i in range(size)])  33 us
    ppermute x25, starting transfers between devices, cross(): return lax.ppermute(value, ('y', 'x', 'c'), perm)  23.1 us
    pallas_call x3, Pallas kernels, assemble(): pl.pallas_call(body, grid_spec=pltpu.PrefetchScalarGridSpec(num_scalar_pr...  17.3 us
    unnamed x158, local copies, waits for them, and re-layouts  14.1 us
  transfers between devices with their start and end apart: 77, of which 33 were waited for; matrix products, arithmetic and copies ran while one was open for 11% of the time, Pallas kernels for 28%

profile of v4, /device:TPU:0, one launch (start us, length us, event | category | flops | bytes accessed | tf_op | source)
XLA Modules:
  0.0 405.5 jit_solution(11149652895361416956)
XLA Ops:
  7.3 2.1 shard_map.288
  9.4 3.0 collective-permute-start
  12.4 2.6 collective-permute-start.1
  16.3 2.9 collective-permute-done
  19.2 5.1 %collective-permute-done.1 = bf16[32,2176]{1,0:T(8,128)(2,1)S(1)} collective-permute-done((bf16[32,2176]{1,0:T(8,128)(2,1)}, bf16[32,2176]{1,0:T(8,128)(2,1)S(1)}, u32[]{:S(2)}, u32[]{:S(2)}) %collective-permute-start.1) | collective-permute-done | bytes 139296 | tf_op jit(solution)/shard_map/ppermute | solution.py:25
  29.4 3.5 collective-permute-start.3
  34.1 5.7 %collective-permute-done.3 = bf16[32,3072]{1,0:T(8,128)(2,1)S(1)} collective-permute-done((bf16[32,3072]{1,0:T(8,128)(2,1)S(1)}, bf16[32,3072]{1,0:T(8,128)(2,1)S(1)}, u32[]{:S(2)}, u32[]{:S(2)}) %collective-permute-start.3) | collective-permute-done | bytes 196640 | tf_op jit(solution)/shard_map/ppermute | solution.py:25
  39.8 3.4 collective-permute-done.6
  45.3 10.8 %collective-permute-done.8 = bf16[32,3072]{1,0:T(8,128)(2,1)S(1)} collective-permute-done((bf16[32,3072]{1,0:T(8,128)(2,1)S(1)}, bf16[32,3072]{1,0:T(8,128)(2,1)S(1)}, u32[]{:S(2)}, u32[]{:S(2)}) %collective-permute-start.8) | collective-permute-done | bytes 196640 | tf_op jit(solution)/shard_map/ppermute | solution.py:25
  63.2 4.0 collective-permute-start.16
  68.1 5.2 %shard_map.289.wk.wv.table.part_ref.ro.refs_5_.refs_6_.refs_9_ = bf16[1024,2176]{1,0:T(8,128)(2,1)} custom-call(s32[64]{0:T(128)} %stack.116.where_ref, bf16[4,32,2176]{2,1,0:T(8,128)(2,1)} %copy-done.8, bf16[4,32,2176]{2,1,0:T(8,128)(2,1)} %copy-done.44, bf16[4,32,2176]{2,1,0:T(8,128)(2,1)} %copy-done.45, ...), custom_call_target="tpu_custom_call" | custom-call | tf_op jit(solution)/shard_map/pallas_call | solution.py:98
  74.2 4.9 %collective-permute-done.16 = bf16[176,512]{1,0:T(8,128)(2,1)S(1)} collective-permute-done((bf16[176,512]{1,0:T(8,128)(2,1)S(1)}, bf16[176,512]{1,0:T(8,128)(2,1)S(1)}, u32[]{:S(2)}, u32[]{:S(2)}) %collective-permute-start.16) | collective-permute-done | bytes 180256 | tf_op jit(solution)/shard_map/ppermute | solution.py:25
  82.0 2.2 collective-permute-start.18
  86.4 8.2 %shard_map.290 = (bf16[384,1024]{1,0:T(8,128)(2,1)}, bf16[1024,384]{1,0:T(8,128)(2,1)}, bf16[384,128]{1,0:T(8,128)(2,1)}, bf16[384,1024]{1,0:T(8,128)(2,1)}, bf1...) custom-call(bf16[384,1024]{1,0:T(8,128)(2,1)} %refs_10_.1, ...), custom_call_target="tpu_custom_call" | custom-call | tf_op jit(solution)/shard_map/pallas_call | solution.py:379
  104.8 7.6 %collective-permute-done.20 = bf16[2,272,256]{2,1,0:T(8,128)(2,1)S(1)} collective-permute-done((bf16[2,272,256]{2,1,0:T(8,128)(2,1)S(1)}, bf16[2,272,256]{2,1,0:T(8,128)(2,1)S(1)}, u32[]{:S(2)}, u32[]{:S(2)}) %collective-permute-start.20) | collective-permute-done | bytes 278560 | tf_op jit(solution)/shard_map/ppermute | solution.py:47
  112.5 12.8 %collective-permute-done.21 = bf16[2,272,256]{2,1,0:T(8,128)(2,1)} collective-permute-done((bf16[2,272,256]{2,1,0:T(8,128)(2,1)S(1)}, bf16[2,272,256]{2,1,0:T(8,128)(2,1)}, u32[]{:S(2)}, u32[]{:S(2)}) %collective-permute-start.21) | collective-permute-done | bytes 278560 | tf_op jit(solution)/shard_map/ppermute | solution.py:47
  129.7 10.7 %collective-permute-done.29 = bf16[2,272,256]{2,1,0:T(8,128)(2,1)S(1)} collective-permute-done((bf16[2,272,256]{2,1,0:T(8,128)(2,1)}, bf16[2,272,256]{2,1,0:T(8,128)(2,1)S(1)}, u32[]{:S(2)}, u32[]{:S(2)}) %collective-permute-start.29) | collective-permute-done | bytes 278560 | tf_op jit(solution)/shard_map/ppermute | solution.py:47
  142.6 6.3 %shard_map.291.wq.ws.wo.refs_4_.refs_7_ = bf16[1024,3072]{1,0:T(8,128)(2,1)} custom-call(s32[64]{0:T(128)} %stack.116.where_ref, bf16[4,32,3072]{2,1,0:T(8,128)(2,1)} %copy-done.4, bf16[4,32,3072]{2,1,0:T(8,128)(2,1)} %copy-done.15, bf16[4,32,3072]{2,1,0:T(8,128)(2,1)} %copy-done.17, bf16[4,32,3072]{2,1,0:T(8,128)(2,1)} %copy-done.22, ...), custom_call_target="tpu_custom_call" | custom-call | tf_op jit(solution)/shard_map/pallas_call | solution.py:98
  150.1 3.6 collective-permute-done.31.refs_1_
  153.7 2.5 collective-permute-start.32
  159.0 15.4 %shard_map.292 = (bf16[384,1024]{1,0:T(8,128)(2,1)}, f32[384,1024]{1,0:T(8,128)}, f32[384,1024]{1,0:T(8,128)}, bf16[1024,384]{1,0:T(8,128)(2,1)}, f32[384,1024]{...) custom-call(bf16[384,1024]{1,0:T(8,128)(2,1)} %get-tuple-element.145.n_ref, ...), custom_call_target="tpu_custom_call" | custom-call | tf_op jit(solution)/shard_map/pallas_call | solution.py:379
  179.7 5.9 %shard_map.293.wd = bf16[2816,1024]{1,0:T(8,128)(2,1)} custom-call(s32[64]{0:T(128)} %stack.116.where_ref, bf16[4,176,512]{2,1,0:T(8,128)(2,1)} %copy-done.7, bf16[4,176,512]{2,1,0:T(8,128)(2,1)} %collective-permute-done.31.refs_1_, bf16[4,176,512]{2,1,0:T(8,128)(2,1)} %copy-done.37, bf16[4,176,512]{2,1,0:T(8,128)(2,1)} %copy-done.38, ...), custom_call_target="tpu_custom_call" | custom-call | tf_op jit(solution)/shard_map/pallas_call | solution.py:98
  185.6 25.0 %shard_map.294 = (bf16[384,1024]{1,0:T(8,128)(2,1)}, bf16[2816,384]{1,0:T(8,128)(2,1)}, bf16[384,2816]{1,0:T(8,128)(2,1)}, bf16[384,2816]{1,0:T(8,128)(2,1)}, f3...) custom-call(bf16[384,1024]{1,0:T(8,128)(2,1)} %get-tuple-element.168.n_ref, bf16[384,1024]{1,0:T(8,128)(2,1)} %refs_2_.1, ...), custom_call_target="tpu_custom_call" | custom-call | tf_op jit(solution)/shard_map/pallas_call | solution.py:379
  211.3 5.2 %collective-permute-done.38.refs_3_ = bf16[384,2816]{1,0:T(8,128)(2,1)} collective-permute-done((bf16[384,2816]{1,0:T(8,128)(2,1)}, bf16[384,2816]{1,0:T(8,128)(2,1)}, u32[]{:S(2)}, u32[]{:S(2)}) %collective-permute-start.38) | collective-permute-done | bytes 2162720 | tf_op jit(solution)/shard_map/ppermute | solution.py:25
  218.4 6.8 %shard_map.295 = (bf16[8,32,2816]{2,1,0:T(8,128)(2,1)}, bf16[4,32,2816]{2,1,0:T(8,128)(2,1)}, bf16[4,32,2816]{2,1,0:T(8,128)(2,1)}) custom-call(s32[17]{0:T(128)} %pad_add_fusion.numbers_ref, bf16[1024,384]{1,0:T(8,128)(2,1)} %get-tuple-element.184.refs_0_, bf16[1024,384]{1,0:T(8,128)(2,1)} %copy-done.3, bf16[384,2816]{1,0:T(8,128)(2,1)} %get-tuple-element.181.refs_2_, ...), custom_call_target="tpu_custom_call" | custom-call | tf_op jit(solution)/shard_map/pallas_call | solution.py:298
  226.0 7.1 %shard_map.296 = bf16[16,176,512]{2,1,0:T(8,128)(2,1)} custom-call(s32[17]{0:T(128)} %pad_add_fusion.1.numbers_ref, bf16[2816,384]{1,0:T(8,128)(2,1)} %get-tuple-element.189.refs_0_, bf16[2816,384]{1,0:T(8,128)(2,1)} %collective-permute-done.39.refs_1_, bf16[384,1024]{1,0:T(8,128)(2,1)} %refs_2_.1, bf16[384,1024]{1,0:T(8,128)(2,1)} %collective-permute-done.24.refs_3_), custom_call_target="tpu_custom_call" | custom-call | tf_op jit(solution)/shard_map/pallas_call | solution.py:298
  233.1 8.6 %shard_map.297 = (bf16[384,1024]{1,0:T(8,128)(2,1)}, bf16[384,1024]{1,0:T(8,128)(2,1)}, f32[1,256]{1,0:T(1,128)}, bf16[4,272,256]{2,1,0:T(8,128)(2,1)}) custom-call(bf16[384,1024]{1,0:T(8,128)(2,1)} %get-tuple-element.209.gh_ref.refs_6_, bf16[1024,3072]{1,0:T(8,128)(2,1)} %shard_map.291.wq.ws.wo.refs_4_.refs_7_, f32[384,1024]{1,0:T(8,128)} %get-tuple-element.192.mixed_ref, ...), custom_call_target="tpu_custom_call" | custom-call | tf_op jit(solution)/shard_map/pallas_call | solution.py:379
  241.8 2.8 collective-permute-done.41
  250.3 2.1 add_convert_fusion.5
  252.4 2.0 collective-permute-start.45
  256.7 6.8 %shard_map.298 = (bf16[8,32,2816]{2,1,0:T(8,128)(2,1)}, bf16[4,32,2816]{2,1,0:T(8,128)(2,1)}, bf16[4,32,2816]{2,1,0:T(8,128)(2,1)}) custom-call(s32[17]{0:T(128)} %pad_add_fusion.numbers_ref, bf16[1024,384]{1,0:T(8,128)(2,1)} %get-tuple-element.184.refs_0_, bf16[1024,384]{1,0:T(8,128)(2,1)} %copy-done.3, bf16[384,2816]{1,0:T(8,128)(2,1)} %get-tuple-element.201.refs_2_, ...), custom_call_target="tpu_custom_call" | custom-call | tf_op jit(solution)/shard_map/pallas_call | solution.py:298
  265.3 6.7 %shard_map.299 = (bf16[8,32,2048]{2,1,0:T(8,128)(2,1)}, bf16[4,32,2048]{2,1,0:T(8,128)(2,1)}, bf16[4,32,2048]{2,1,0:T(8,128)(2,1)}) custom-call(s32[17]{0:T(128)} %pad_add_fusion.numbers_ref, bf16[1024,384]{1,0:T(8,128)(2,1)} %get-tuple-element.156.refs_0_.refs_8_, bf16[1024,384]{1,0:T(8,128)(2,1)} %copy-done, bf16[1024,384]{1,0:T(8,128)(2,1)} %get-tuple-element.206.refs_2_, ...), custom_call_target="tpu_custom_call" | custom-call | tf_op jit(solution)/shard_map/pallas_call | solution.py:298
  273.2 5.4 %collective-permute-done.50 = bf16[2,272,256]{2,1,0:T(8,128)(2,1)S(1)} collective-permute-done((bf16[2,272,256]{2,1,0:T(8,128)(2,1)S(1)}, bf16[2,272,256]{2,1,0:T(8,128)(2,1)S(1)}, u32[]{:S(2)}, u32[]{:S(2)}) %collective-permute-start.50) | collective-permute-done | bytes 278560 | tf_op jit(solution)/shard_map/ppermute | solution.py:47
  285.1 15.4 %shard_map.300 = (bf16[384,1024]{1,0:T(8,128)(2,1)}, bf16[384,1024]{1,0:T(8,128)(2,1)}, bf16[384,1024]{1,0:T(8,128)(2,1)}, bf16[1024,384]{1,0:T(8,128)(2,1)}, bf16[384,128]{1,0:T(8,128)(2,1)}) custom-call(bf16[384,1024]{1,0:T(8,128)(2,1)} %get-tuple-element.177.q_ref, bf16[384,1024]{1,0:T(8,128)(2,1)} %get-tuple-element.146.k_ref, ...), custom_call_target="tpu_custom_call" | custom-call | tf_op jit(solution)/shard_map/pallas_call | solution.py:379
  304.6 2.9 collective-permute-done.56.refs_11_
  311.8 10.0 %shard_map.301 = (bf16[8,32,3200]{2,1,0:T(8,128)(2,1)}, bf16[4,32,3200]{2,1,0:T(8,128)(2,1)}, bf16[4,32,3200]{2,1,0:T(8,128)(2,1)}) custom-call(s32[17]{0:T(128)} %pad_add_fusion.numbers_ref, bf16[1024,384]{1,0:T(8,128)(2,1)} %get-tuple-element.156.refs_0_.refs_8_, bf16[1024,384]{1,0:T(8,128)(2,1)} %copy-done, ...), custom_call_target="tpu_custom_call" | custom-call | tf_op jit(solution)/shard_map/pallas_call | solution.py:298
  321.8 5.0 %collective-permute-done.61 = bf16[4,32,2816]{2,1,0:T(8,128)(2,1)} collective-permute-done((bf16[4,32,2816]{2,1,0:T(8,128)(2,1)}, bf16[4,32,2816]{2,1,0:T(8,128)(2,1)}, u32[]{:S(2)}, u32[]{:S(2)}) %collective-permute-start.61) | collective-permute-done | bytes 720928 | tf_op jit(solution)/shard_map/ppermute | solution.py:47
  334.1 9.8 %shard_map.302 = f32[384,1024]{1,0:T(8,128)} custom-call(bf16[384,1024]{1,0:T(8,128)(2,1)} %get-tuple-element.223.refs_2_.refs_0_, bf16[384,1024]{1,0:T(8,128)(2,1)} %get-tuple-element.224.refs_4_.refs_1_, bf16[384,1024]{1,0:T(8,128)(2,1)} %get-tuple-element.225.refs_6_.refs_2_, bf16[384,1024]{1,0:T(8,128)(2,1)} %get-tuple-element.208.refs_4_.refs_3_, ...), custom_call_target="tpu_custom_call" | custom-call | tf_op jit(solution)/shard_map/pallas_call | solution.py:379
  343.9 3.2 collective-permute-done.63
  347.1 9.3 %collective-permute-done.62 = bf16[8,32,3200]{2,1,0:T(8,128)(2,1)S(1)} collective-permute-done((bf16[8,32,3200]{2,1,0:T(8,128)(2,1)}, bf16[8,32,3200]{2,1,0:T(8,128)(2,1)S(1)}, u32[]{:S(2)}, u32[]{:S(2)}) %collective-permute-start.62) | collective-permute-done | bytes 1638432 | tf_op jit(solution)/shard_map/ppermute | solution.py:47
  362.5 3.8 collective-permute-start.70
  367.3 4.6 %collective-permute-done.71 = bf16[2,176,512]{2,1,0:T(8,128)(2,1)S(1)} collective-permute-done((bf16[2,176,512]{2,1,0:T(8,128)(2,1)S(1)}, bf16[2,176,512]{2,1,0:T(8,128)(2,1)S(1)}, u32[]{:S(2)}, u32[]{:S(2)}) %collective-permute-start.71) | collective-permute-done | bytes 360480 | tf_op jit(solution)/shard_map/ppermute | solution.py:47
  371.9 2.0 collective-permute-done.64
  377.8 2.1 multiply_reduce_fusion
  381.9 2.7 collective-permute-start.67
  385.1 2.3 collective-permute-done.65.refs_1_
  387.4 7.2 %collective-permute-done.66.refs_2_ = bf16[32,3200]{1,0:T(8,128)(2,1)S(1)} collective-permute-done((bf16[32,3200]{1,0:T(8,128)(2,1)S(1)}, bf16[32,3200]{1,0:T(8,128)(2,1)S(1)}, u32[]{:S(2)}, u32[]{:S(2)}) %collective-permute-start.66) | collective-permute-done | bytes 204832 | tf_op jit(solution)/shard_map/ppermute | solution.py:25
  395.5 2.4 shard_map.303
  (398 shorter events, 100.6 us)
Async XLA Ops:
  7.2 178.4 %all-gather.2.cloned.1.call-start = ((), (), s32[]{:S(2)}) async-start(), calls=%async_computation.2 | async-start | bytes 11894784 | tf_op jit(solution)/shard_map/all_gather | solution.py:1036
  12.4 12.0 %collective-permute-start.1 = (bf16[32,2176]{1,0:T(8,128)(2,1)}, bf16[32,2176]{1,0:T(8,128)(2,1)S(1)}, u32[]{:S(2)}, u32[]{:S(2)}) collective-permute-start(bf16[32,2176]{1,0:T(8,128)(2,1)} %shard_map.288), channel_id=1, source_target_pairs={{0,16},{8,24},{16,0},{24,8},{1,17},{9,25},{17,1},{25,9},{2,18},{10... | collective-permute-start | bytes 417800 | tf_op jit(solution)/shard_map/ppermute | solution.py:25
  25.4 17.8 %collective-permute-start.7 = (bf16[4,32,2176]{2,1,0:T(8,128)(2,1)S(1)}, bf16[4,32,2176]{2,1,0:T(8,128)(2,1)S(1)}, u32[]{:S(2)}, u32[]{:S(2)}) collective-permute-start(bf16[4,32,2176]{2,1,0:T(8,128)(2,1)S(1)} %pad_maximum_fusion.3.refs_0_), channel_id=1, source_target_pairs={{0,1},{1,0},{2,3},{3,2},{4,5},{5,4},{6,7},{7,6},{8,9},{9,8},{10,11... | collective-permute-start | bytes 1671176 | tf_op jit(solution)/shard_map/ppermute | solution.py:25
  25.5 17.7 %collective-permute-start.4 = (bf16[4,32,2176]{2,1,0:T(8,128)(2,1)S(1)}, bf16[4,32,2176]{2,1,0:T(8,128)(2,1)S(1)}, u32[]{:S(2)}, u32[]{:S(2)}) collective-permute-start(bf16[4,32,2176]{2,1,0:T(8,128)(2,1)S(1)} %pad_maximum_fusion.3.refs_0_), channel_id=1, source_target_pairs={{0,2},{1,5},{2,0},{3,7},{4,6},{5,1},{6,4},{7,3},{8,10},{9,13},{10,... | collective-permute-start | bytes 1671176 | tf_op jit(solution)/shard_map/ppermute | solution.py:47
  27.0 16.2 %collective-permute-start.5 = (bf16[4,32,2176]{2,1,0:T(8,128)(2,1)S(1)}, bf16[4,32,2176]{2,1,0:T(8,128)(2,1)S(1)}, u32[]{:S(2)}, u32[]{:S(2)}) collective-permute-start(bf16[4,32,2176]{2,1,0:T(8,128)(2,1)S(1)} %pad_maximum_fusion.3.refs_0_), channel_id=1, source_target_pairs={{0,4},{1,3},{2,6},{3,1},{4,0},{5,7},{6,2},{7,5},{8,12},{9,11},{10,... | collective-permute-start | bytes 1671176 | tf_op jit(solution)/shard_map/ppermute | solution.py:47
  29.4 10.3 %collective-permute-start.3 = (bf16[32,3072]{1,0:T(8,128)(2,1)S(1)}, bf16[32,3072]{1,0:T(8,128)(2,1)S(1)}, u32[]{:S(2)}, u32[]{:S(2)}) collective-permute-start(bf16[32,3072]{1,0:T(8,128)(2,1)S(1)} %constant_dynamic-update-slice_fusion), channel_id=1, source_target_pairs={{0,8},{8,16},{16,24},{24,0},{1,9},{9,17},{17,25},{25,1},{2,10},{10... | collective-permute-start | bytes 589832 | tf_op jit(solution)/shard_map/ppermute | solution.py:25
  32.9 10.2 %collective-permute-start.6 = (bf16[32,3072]{1,0:T(8,128)(2,1)S(1)}, bf16[32,3072]{1,0:T(8,128)(2,1)S(1)}, u32[]{:S(2)}, u32[]{:S(2)}) collective-permute-start(bf16[32,3072]{1,0:T(8,128)(2,1)S(1)} %constant_dynamic-update-slice_fusion), channel_id=1, source_target_pairs={{0,24},{8,0},{16,8},{24,16},{1,25},{9,1},{17,9},{25,17},{2,26},{10... | collective-permute-start | bytes 589832 | tf_op jit(solution)/shard_map/ppermute | solution.py:25
  43.2 13.0 %collective-permute-start.10 = (bf16[4,32,2176]{2,1,0:T(8,128)(2,1)S(1)}, bf16[4,32,2176]{2,1,0:T(8,128)(2,1)}, u32[]{:S(2)}, u32[]{:S(2)}) collective-permute-start(bf16[4,32,2176]{2,1,0:T(8,128)(2,1)S(1)} %collective-permute-done.4.refs_1_), channel_id=1, source_target_pairs={{0,4},{1,3},{2,6},{3,1},{4,0},{5,7},{6,2},{7,5},{8,12},{9,11},{10,... | collective-permute-start | bytes 1671176 | tf_op jit(solution)/shard_map/ppermute | solution.py:47
  43.8 12.4 %collective-permute-start.11 = (bf16[4,32,2176]{2,1,0:T(8,128)(2,1)S(1)}, bf16[4,32,2176]{2,1,0:T(8,128)(2,1)S(1)}, u32[]{:S(2)}, u32[]{:S(2)}) collective-permute-start(bf16[4,32,2176]{2,1,0:T(8,128)(2,1)S(1)} %collective-permute-done.4.refs_1_), channel_id=1, source_target_pairs={{0,1},{1,0},{2,3},{3,2},{4,5},{5,4},{6,7},{7,6},{8,9},{9,8},{10,11... | collective-permute-start | bytes 1671176 | tf_op jit(solution)/shard_map/ppermute | solution.py:25
  43.8 13.9 %collective-permute-start.12 = (bf16[4,32,2176]{2,1,0:T(8,128)(2,1)S(1)}, bf16[4,32,2176]{2,1,0:T(8,128)(2,1)}, u32[]{:S(2)}, u32[]{:S(2)}) collective-permute-start(bf16[4,32,2176]{2,1,0:T(8,128)(2,1)S(1)} %collective-permute-done.5.refs_2_), channel_id=1, source_target_pairs={{0,1},{1,0},{2,3},{3,2},{4,5},{5,4},{6,7},{7,6},{8,9},{9,8},{10,11... | collective-permute-start | bytes 1671176 | tf_op jit(solution)/shard_map/ppermute | solution.py:25
  44.3 11.9 %collective-permute-start.8 = (bf16[32,3072]{1,0:T(8,128)(2,1)S(1)}, bf16[32,3072]{1,0:T(8,128)(2,1)S(1)}, u32[]{:S(2)}, u32[]{:S(2)}) collective-permute-start(bf16[32,3072]{1,0:T(8,128)(2,1)S(1)} %constant_dynamic-update-slice_fusion), channel_id=1, source_target_pairs={{0,16},{8,24},{16,0},{24,8},{1,17},{9,25},{17,1},{25,9},{2,18},{10... | collective-permute-start | bytes 589832 | tf_op jit(solution)/shard_map/ppermute | solution.py:25
  58.5 300.9 %reduce-scatter.5.cloned.1.call-start = ((), (), s32[]{:S(2)}) async-start(), calls=%async_computation.4 | async-start | bytes 3604480 | tf_op jit(solution)/shard_map/reduce_scatter | solution.py:142
  61.0 18.0 %collective-permute-start.14 = (bf16[4,32,3072]{2,1,0:T(8,128)(2,1)S(1)}, bf16[4,32,3072]{2,1,0:T(8,128)(2,1)S(1)}, u32[]{:S(2)}, u32[]{:S(2)}) collective-permute-start(bf16[4,32,3072]{2,1,0:T(8,128)(2,1)S(1)} %pad_maximum_fusion.1.refs_0_), channel_id=1, source_target_pairs={{0,2},{1,5},{2,0},{3,7},{4,6},{5,1},{6,4},{7,3},{8,10},{9,13},{10,... | collective-permute-start | bytes 2359304 | tf_op jit(solution)/shard_map/ppermute | solution.py:47
  63.2 10.9 %collective-permute-start.15 = (bf16[176,512]{1,0:T(8,128)(2,1)S(1)}, bf16[176,512]{1,0:T(8,128)(2,1)S(1)}, u32[]{:S(2)}, u32[]{:S(2)}) collective-permute-start(bf16[176,512]{1,0:T(8,128)(2,1)S(1)} %maximum_select_fusion.5), channel_id=1, source_target_pairs={{0,8},{8,16},{16,24},{24,0},{1,9},{9,17},{17,25},{25,1},{2,10},{10... | collective-permute-start | bytes 540680 | tf_op jit(solution)/shard_map/ppermute | solution.py:25
  63.2 15.8 %collective-permute-start.16 = (bf16[176,512]{1,0:T(8,128)(2,1)S(1)}, bf16[176,512]{1,0:T(8,128)(2,1)S(1)}, u32[]{:S(2)}, u32[]{:S(2)}) collective-permute-start(bf16[176,512]{1,0:T(8,128)(2,1)S(1)} %maximum_select_fusion.5), channel_id=1, source_target_pairs={{0,24},{8,0},{16,8},{24,16},{1,25},{9,1},{17,9},{25,17},{2,26},{10... | collective-permute-start | bytes 540680 | tf_op jit(solution)/shard_map/ppermute | solution.py:25
  79.0 15.6 %collective-permute-start.17 = (bf16[4,32,3072]{2,1,0:T(8,128)(2,1)S(1)}, bf16[4,32,3072]{2,1,0:T(8,128)(2,1)S(1)}, u32[]{:S(2)}, u32[]{:S(2)}) collective-permute-start(bf16[4,32,3072]{2,1,0:T(8,128)(2,1)S(1)} %pad_maximum_fusion.1.refs_0_), channel_id=1, source_target_pairs={{0,4},{1,3},{2,6},{3,1},{4,0},{5,7},{6,2},{7,5},{8,12},{9,11},{10,... | collective-permute-start | bytes 2359304 | tf_op jit(solution)/shard_map/ppermute | solution.py:47
  82.0 12.7 %collective-permute-start.18 = (bf16[176,512]{1,0:T(8,128)(2,1)S(1)}, bf16[176,512]{1,0:T(8,128)(2,1)S(1)}, u32[]{:S(2)}, u32[]{:S(2)}) collective-permute-start(bf16[176,512]{1,0:T(8,128)(2,1)S(1)} %maximum_select_fusion.5), channel_id=1, source_target_pairs={{0,16},{8,24},{16,0},{24,8},{1,17},{9,25},{17,1},{25,9},{2,18},{10... | collective-permute-start | bytes 540680 | tf_op jit(solution)/shard_map/ppermute | solution.py:25
  100.7 24.6 %collective-permute-start.22 = (bf16[4,32,3072]{2,1,0:T(8,128)(2,1)S(1)}, bf16[4,32,3072]{2,1,0:T(8,128)(2,1)S(1)}, u32[]{:S(2)}, u32[]{:S(2)}) collective-permute-start(bf16[4,32,3072]{2,1,0:T(8,128)(2,1)S(1)} %copy-done.16), channel_id=1, source_target_pairs={{0,4},{1,3},{2,6},{3,1},{4,0},{5,7},{6,2},{7,5},{8,12},{9,11},{10,... | collective-permute-start | bytes 2359304 | tf_op jit(solution)/shard_map/ppermute | solution.py:47
  102.3 22.9 %collective-permute-start.26 = (bf16[4,32,3072]{2,1,0:T(8,128)(2,1)S(1)}, bf16[4,32,3072]{2,1,0:T(8,128)(2,1)S(1)}, u32[]{:S(2)}, u32[]{:S(2)}) collective-permute-start(bf16[4,32,3072]{2,1,0:T(8,128)(2,1)S(1)} %copy-done.16), channel_id=1, source_target_pairs={{0,1},{1,0},{2,3},{3,2},{4,5},{5,4},{6,7},{7,6},{8,9},{9,8},{10,11... | collective-permute-start | bytes 2359304 | tf_op jit(solution)/shard_map/ppermute | solution.py:25
  102.4 22.9 %collective-permute-start.27 = (bf16[4,32,3072]{2,1,0:T(8,128)(2,1)S(1)}, bf16[4,32,3072]{2,1,0:T(8,128)(2,1)S(1)}, u32[]{:S(2)}, u32[]{:S(2)}) collective-permute-start(bf16[4,32,3072]{2,1,0:T(8,128)(2,1)S(1)} %copy-done.18), channel_id=1, source_target_pairs={{0,1},{1,0},{2,3},{3,2},{4,5},{5,4},{6,7},{7,6},{8,9},{9,8},{10,11... | collective-permute-start | bytes 2359304 | tf_op jit(solution)/shard_map/ppermute | solution.py:25
  103.2 22.1 %collective-permute-start.21 = (bf16[2,272,256]{2,1,0:T(8,128)(2,1)S(1)}, bf16[2,272,256]{2,1,0:T(8,128)(2,1)}, u32[]{:S(2)}, u32[]{:S(2)}) collective-permute-start(bf16[2,272,256]{2,1,0:T(8,128)(2,1)S(1)} %fusion.20), channel_id=1, source_target_pairs={{0,4},{1,3},{2,6},{3,1},{4,0},{5,7},{6,2},{7,5},{8,12},{9,11},{10,... | collective-permute-start | bytes 835592 | tf_op jit(solution)/shard_map/ppermute | solution.py:47
  127.6 12.8 %collective-permute-start.29 = (bf16[2,272,256]{2,1,0:T(8,128)(2,1)}, bf16[2,272,256]{2,1,0:T(8,128)(2,1)S(1)}, u32[]{:S(2)}, u32[]{:S(2)}) collective-permute-start(bf16[2,272,256]{2,1,0:T(8,128)(2,1)} %collective-permute-done.21), channel_id=1, source_target_pairs={{0,2},{1,5},{2,0},{3,7},{4,6},{5,1},{6,4},{7,3},{8,10},{9,13},{10,... | collective-permute-start | bytes 835592 | tf_op jit(solution)/shard_map/ppermute | solution.py:47
  142.3 11.4 %collective-permute-start.31 = (bf16[4,176,512]{2,1,0:T(8,128)(2,1)S(1)}, bf16[4,176,512]{2,1,0:T(8,128)(2,1)}, u32[]{:S(2)}, u32[]{:S(2)}) collective-permute-start(bf16[4,176,512]{2,1,0:T(8,128)(2,1)S(1)} %pad_maximum_fusion.2.refs_0_), channel_id=1, source_target_pairs={{0,2},{1,5},{2,0},{3,7},{4,6},{5,1},{6,4},{7,3},{8,10},{9,13},{10,... | collective-permute-start | bytes 2162696 | tf_op jit(solution)/shard_map/ppermute | solution.py:47
  153.7 20.7 %collective-permute-start.32 = (bf16[4,176,512]{2,1,0:T(8,128)(2,1)S(1)}, bf16[4,176,512]{2,1,0:T(8,128)(2,1)S(1)}, u32[]{:S(2)}, u32[]{:S(2)}) collective-permute-start(bf16[4,176,512]{2,1,0:T(8,128)(2,1)S(1)} %pad_maximum_fusion.2.refs_0_), channel_id=1, source_target_pairs={{0,4},{1,3},{2,6},{3,1},{4,0},{5,7},{6,2},{7,5},{8,12},{9,11},{10,... | collective-permute-start | bytes 2162696 | tf_op jit(solution)/shard_map/ppermute | solution.py:47
  156.2 18.2 %collective-permute-start.33 = (bf16[4,176,512]{2,1,0:T(8,128)(2,1)}, bf16[4,176,512]{2,1,0:T(8,128)(2,1)S(1)}, u32[]{:S(2)}, u32[]{:S(2)}) collective-permute-start(bf16[4,176,512]{2,1,0:T(8,128)(2,1)} %collective-permute-done.31.refs_1_), channel_id=1, source_target_pairs={{0,4},{1,3},{2,6},{3,1},{4,0},{5,7},{6,2},{7,5},{8,12},{9,11},{10,... | collective-permute-start | bytes 2162696 | tf_op jit(solution)/shard_map/ppermute | solution.py:47
  159.0 16.5 %collective-permute-start.35 = (bf16[4,176,512]{2,1,0:T(8,128)(2,1)}, bf16[4,176,512]{2,1,0:T(8,128)(2,1)S(1)}, u32[]{:S(2)}, u32[]{:S(2)}) collective-permute-start(bf16[4,176,512]{2,1,0:T(8,128)(2,1)} %collective-permute-done.31.refs_1_), channel_id=1, source_target_pairs={{0,1},{1,0},{2,3},{3,2},{4,5},{5,4},{6,7},{7,6},{8,9},{9,8},{10,11... | collective-permute-start | bytes 2162696 | tf_op jit(solution)/shard_map/ppermute | solution.py:25
  225.2 19.3 %collective-permute-start.41 = (bf16[8,32,2816]{2,1,0:T(8,128)(2,1)}, bf16[8,32,2816]{2,1,0:T(8,128)(2,1)}, u32[]{:S(2)}, u32[]{:S(2)}) collective-permute-start(bf16[8,32,2816]{2,1,0:T(8,128)(2,1)} %get-tuple-element.185), channel_id=1, source_target_pairs={{0,2},{1,5},{2,0},{3,7},{4,6},{5,1},{6,4},{7,3},{8,10},{9,13},{10,... | collective-permute-start | bytes 4325384 | tf_op jit(solution)/shard_map/ppermute | solution.py:47
  249.8 13.7 %collective-permute-start.49 = (bf16[384,1024]{1,0:T(8,128)(2,1)S(1)}, bf16[384,1024]{1,0:T(8,128)(2,1)S(1)}, u32[]{:S(2)}, u32[]{:S(2)}) collective-permute-start(bf16[384,1024]{1,0:T(8,128)(2,1)S(1)} %copy-done.2), channel_id=1, source_target_pairs={{0,1},{1,0},{2,3},{3,2},{4,5},{5,4},{6,7},{7,6},{8,9},{9,8},{10,11... | collective-permute-start | bytes 2359304 | tf_op jit(solution)/shard_map/ppermute | solution.py:25
  249.9 13.6 %collective-permute-start.48 = (bf16[384,1024]{1,0:T(8,128)(2,1)S(1)}, bf16[384,1024]{1,0:T(8,128)(2,1)S(1)}, u32[]{:S(2)}, u32[]{:S(2)}) collective-permute-start(bf16[384,1024]{1,0:T(8,128)(2,1)S(1)} %copy-done.6), channel_id=1, source_target_pairs={{0,1},{1,0},{2,3},{3,2},{4,5},{5,4},{6,7},{7,6},{8,9},{9,8},{10,11... | collective-permute-start | bytes 2359304 | tf_op jit(solution)/shard_map/ppermute | solution.py:25
  252.4 19.6 %collective-permute-start.45 = (bf16[4,32,2816]{2,1,0:T(8,128)(2,1)}, bf16[4,32,2816]{2,1,0:T(8,128)(2,1)}, u32[]{:S(2)}, u32[]{:S(2)}) collective-permute-start(bf16[4,32,2816]{2,1,0:T(8,128)(2,1)} %add_convert_fusion.5), channel_id=1, source_target_pairs={{0,4},{1,3},{2,6},{3,1},{4,0},{5,7},{6,2},{7,5},{8,12},{9,11},{10,... | collective-permute-start | bytes 2162696 | tf_op jit(solution)/shard_map/ppermute | solution.py:47
  254.4 17.6 %collective-permute-start.43 = (bf16[2,272,256]{2,1,0:T(8,128)(2,1)}, bf16[2,272,256]{2,1,0:T(8,128)(2,1)}, u32[]{:S(2)}, u32[]{:S(2)}) collective-permute-start(bf16[2,272,256]{2,1,0:T(8,128)(2,1)} %fusion.17), channel_id=1, source_target_pairs={{0,2},{1,5},{2,0},{3,7},{4,6},{5,1},{6,4},{7,3},{8,10},{9,13},{10,... | collective-permute-start | bytes 835592 | tf_op jit(solution)/shard_map/ppermute | solution.py:47
  255.3 16.7 %collective-permute-start.44 = (bf16[2,272,256]{2,1,0:T(8,128)(2,1)}, bf16[2,272,256]{2,1,0:T(8,128)(2,1)S(1)}, u32[]{:S(2)}, u32[]{:S(2)}) collective-permute-start(bf16[2,272,256]{2,1,0:T(8,128)(2,1)} %fusion.17), channel_id=1, source_target_pairs={{0,4},{1,3},{2,6},{3,1},{4,0},{5,7},{6,2},{7,5},{8,12},{9,11},{10,... | collective-permute-start | bytes 835592 | tf_op jit(solution)/shard_map/ppermute | solution.py:47
  280.3 97.2 %reduce-scatter.3.cloned.1.call-start = ((), (), s32[]{:S(2)}) async-start(), calls=%async_computation.3 | async-start | bytes 1802240 | tf_op jit(solution)/shard_map/reduce_scatter | solution.py:181
  283.4 19.0 %collective-permute-start.52 = (bf16[8,32,2816]{2,1,0:T(8,128)(2,1)S(1)}, bf16[8,32,2816]{2,1,0:T(8,128)(2,1)S(1)}, u32[]{:S(2)}, u32[]{:S(2)}) collective-permute-start(bf16[8,32,2816]{2,1,0:T(8,128)(2,1)S(1)} %copy-done.72), channel_id=1, source_target_pairs={{0,2},{1,5},{2,0},{3,7},{4,6},{5,1},{6,4},{7,3},{8,10},{9,13},{10,... | collective-permute-start | bytes 4325384 | tf_op jit(solution)/shard_map/ppermute | solution.py:47
  284.6 18.4 %collective-permute-start.58 = (bf16[384,128]{1,0:T(8,128)(2,1)S(1)}, bf16[384,128]{1,0:T(8,128)(2,1)S(1)}, u32[]{:S(2)}, u32[]{:S(2)}) collective-permute-start(bf16[384,128]{1,0:T(8,128)(2,1)S(1)} %copy-done.60), channel_id=1, source_target_pairs={{0,1},{1,0},{2,3},{3,2},{4,5},{5,4},{6,7},{7,6},{8,9},{9,8},{10,11... | collective-permute-start | bytes 294920 | tf_op jit(solution)/shard_map/ppermute | solution.py:25
  284.6 18.9 %collective-permute-start.59 = (f32[1,256]{1,0:T(1,128)S(1)}, f32[1,256]{1,0:T(1,128)S(1)}, u32[]{:S(2)}, u32[]{:S(2)}) collective-permute-start(f32[1,256]{1,0:T(1,128)S(1)} %copy-done.70), channel_id=1, source_target_pairs={{0,1},{1,0},{2,3},{3,2},{4,5},{5,4},{6,7},{7,6},{8,9},{9,8},{10,11... | collective-permute-start | bytes 3080 | tf_op jit(solution)/shard_map/ppermute | solution.py:25
  307.5 19.3 %collective-permute-start.61 = (bf16[4,32,2816]{2,1,0:T(8,128)(2,1)}, bf16[4,32,2816]{2,1,0:T(8,128)(2,1)}, u32[]{:S(2)}, u32[]{:S(2)}) collective-permute-start(bf16[4,32,2816]{2,1,0:T(8,128)(2,1)} %add_convert_fusion.4), channel_id=1, source_target_pairs={{0,4},{1,3},{2,6},{3,1},{4,0},{5,7},{6,2},{7,5},{8,12},{9,11},{10,... | collective-permute-start | bytes 2162696 | tf_op jit(solution)/shard_map/ppermute | solution.py:47
  308.1 21.2 %collective-permute-start.60 = (bf16[8,32,2048]{2,1,0:T(8,128)(2,1)}, bf16[8,32,2048]{2,1,0:T(8,128)(2,1)S(1)}, u32[]{:S(2)}, u32[]{:S(2)}) collective-permute-start(bf16[8,32,2048]{2,1,0:T(8,128)(2,1)} %get-tuple-element.233), channel_id=1, source_target_pairs={{0,2},{1,5},{2,0},{3,7},{4,6},{5,1},{6,4},{7,3},{8,10},{9,13},{10,... | collective-permute-start | bytes 3145736 | tf_op jit(solution)/shard_map/ppermute | solution.py:47
  329.4 26.9 %collective-permute-start.62 = (bf16[8,32,3200]{2,1,0:T(8,128)(2,1)}, bf16[8,32,3200]{2,1,0:T(8,128)(2,1)S(1)}, u32[]{:S(2)}, u32[]{:S(2)}) collective-permute-start(bf16[8,32,3200]{2,1,0:T(8,128)(2,1)} %get-tuple-element.238), channel_id=1, source_target_pairs={{0,2},{1,5},{2,0},{3,7},{4,6},{5,1},{6,4},{7,3},{8,10},{9,13},{10,... | collective-permute-start | bytes 4915208 | tf_op jit(solution)/shard_map/ppermute | solution.py:47
  332.0 15.0 %collective-permute-start.63 = (bf16[4,32,2048]{2,1,0:T(8,128)(2,1)S(1)}, bf16[4,32,2048]{2,1,0:T(8,128)(2,1)}, u32[]{:S(2)}, u32[]{:S(2)}) collective-permute-start(bf16[4,32,2048]{2,1,0:T(8,128)(2,1)S(1)} %add_convert_fusion.7), channel_id=1, source_target_pairs={{0,4},{1,3},{2,6},{3,1},{4,0},{5,7},{6,2},{7,5},{8,12},{9,11},{10,... | collective-permute-start | bytes 1572872 | tf_op jit(solution)/shard_map/ppermute | solution.py:47
  357.4 16.5 %collective-permute-start.64 = (bf16[4,32,3200]{2,1,0:T(8,128)(2,1)}, bf16[4,32,3200]{2,1,0:T(8,128)(2,1)}, u32[]{:S(2)}, u32[]{:S(2)}) collective-permute-start(bf16[4,32,3200]{2,1,0:T(8,128)(2,1)} %add_convert_fusion.1), channel_id=1, source_target_pairs={{0,4},{1,3},{2,6},{3,1},{4,0},{5,7},{6,2},{7,5},{8,12},{9,11},{10,... | collective-permute-start | bytes 2457608 | tf_op jit(solution)/shard_map/ppermute | solution.py:47
  360.5 11.4 %collective-permute-start.71 = (bf16[2,176,512]{2,1,0:T(8,128)(2,1)S(1)}, bf16[2,176,512]{2,1,0:T(8,128)(2,1)S(1)}, u32[]{:S(2)}, u32[]{:S(2)}) collective-permute-start(bf16[2,176,512]{2,1,0:T(8,128)(2,1)S(1)} %bitcast.116), channel_id=1, source_target_pairs={{0,2},{1,5},{2,0},{3,7},{4,6},{5,1},{6,4},{7,3},{8,10},{9,13},{10,... | collective-permute-start | bytes 1081352 | tf_op jit(solution)/shard_map/ppermute | solution.py:47
  362.5 19.4 %collective-permute-start.68 = (bf16[32,2048]{1,0:T(8,128)(2,1)}, bf16[32,2048]{1,0:T(8,128)(2,1)}, u32[]{:S(2)}, u32[]{:S(2)}) collective-permute-start(bf16[32,2048]{1,0:T(8,128)(2,1)} %get-tuple-element.284), channel_id=1, source_target_pairs={{0,8},{8,16},{16,24},{24,0},{1,9},{9,17},{17,25},{25,1},{2,10},{10... | collective-permute-start | bytes 393224 | tf_op jit(solution)/shard_map/ppermute | solution.py:25
  362.5 22.1 %collective-permute-start.69 = (bf16[32,2048]{1,0:T(8,128)(2,1)}, bf16[32,2048]{1,0:T(8,128)(2,1)}, u32[]{:S(2)}, u32[]{:S(2)}) collective-permute-start(bf16[32,2048]{1,0:T(8,128)(2,1)} %get-tuple-element.283), channel_id=1, source_target_pairs={{0,16},{8,24},{16,0},{24,8},{1,17},{9,25},{17,1},{25,9},{2,18},{10... | collective-permute-start | bytes 393224 | tf_op jit(solution)/shard_map/ppermute | solution.py:25
  362.5 22.6 %collective-permute-start.70 = (bf16[32,2048]{1,0:T(8,128)(2,1)}, bf16[32,2048]{1,0:T(8,128)(2,1)}, u32[]{:S(2)}, u32[]{:S(2)}) collective-permute-start(bf16[32,2048]{1,0:T(8,128)(2,1)} %get-tuple-element.282), channel_id=1, source_target_pairs={{0,24},{8,0},{16,8},{24,16},{1,25},{9,1},{17,9},{25,17},{2,26},{10... | collective-permute-start | bytes 393224 | tf_op jit(solution)/shard_map/ppermute | solution.py:25
  380.4 14.3 %collective-permute-start.66 = (bf16[32,3200]{1,0:T(8,128)(2,1)S(1)}, bf16[32,3200]{1,0:T(8,128)(2,1)S(1)}, u32[]{:S(2)}, u32[]{:S(2)}) collective-permute-start(bf16[32,3200]{1,0:T(8,128)(2,1)S(1)} %get-tuple-element.269), channel_id=1, source_target_pairs={{0,16},{8,24},{16,0},{24,8},{1,17},{9,25},{17,1},{25,9},{2,18},{10... | collective-permute-start | bytes 614408 | tf_op jit(solution)/shard_map/ppermute | solution.py:25
  381.9 12.9 %collective-permute-start.67 = (bf16[32,3200]{1,0:T(8,128)(2,1)S(1)}, bf16[32,3200]{1,0:T(8,128)(2,1)S(1)}, u32[]{:S(2)}, u32[]{:S(2)}) collective-permute-start(bf16[32,3200]{1,0:T(8,128)(2,1)S(1)} %get-tuple-element.268), channel_id=1, source_target_pairs={{0,24},{8,0},{16,8},{24,16},{1,25},{9,1},{17,9},{25,17},{2,26},{10... | collective-permute-start | bytes 614408 | tf_op jit(solution)/shard_map/ppermute | solution.py:25
  384.6 13.4 %collective-permute-start.73 = (f32[88,512]{1,0:T(8,128)S(1)}, f32[88,512]{1,0:T(8,128)S(1)}, u32[]{:S(2)}, u32[]{:S(2)}) collective-permute-start(f32[88,512]{1,0:T(8,128)S(1)} %get-tuple-element.287), channel_id=1, source_target_pairs={{0,1},{1,0},{2,3},{3,2},{4,5},{5,4},{6,7},{7,6},{8,9},{9,8},{10,11... | collective-permute-start | bytes 540680 | tf_op jit(solution)/shard_map/ppermute | solution.py:25
  (102 other events, 946.0 us)
Sparse Core Ops, SparseCore 0:
  58.6 98.6 all-gather.1
  280.4 53.3 reduce-scatter.4
  336.2 34.1 reduce-scatter.2

commit v5 on v4

--- a/solution.py
+++ b/solution.py
@@ -1075,18 +1075,16 @@
     )
 
     gate_pair = pair(grad_gate)
-    inner, grad_up, grad_low = after(gate_pair, inner, grad_up, grad_low)
+    grad_mixed, grad_swish, grad_head_gain, message_back = head_back(
+        grad_low, second, mixed, swish, row_head, queries, gate_pre, message[:, HEAD_V:], marks
+    )
+    gate_pair, inner, grad_up = after((message_back, gate_pair), gate_pair, inner, grad_up)
     gate = weight_grads([(two_pair, [gate_pair])], ff // 2)
     inner_pair, up_pair = pair(inner), pair(grad_up)
-    inner_pair, grad_low = after(gate.blocks, inner_pair, grad_low)
-    down = weight_grads([(inner_pair, [down_pair])], 512, True, by_z=True)
+    down = weight_grads([(after(gate.blocks, inner_pair), [down_pair])], 512, True, by_z=True)
     down_blocks = down.blocks
     down.zeroth()
-    grad_low = after(down_blocks, grad_low)
-    grad_mixed, grad_swish, grad_head_gain, message_back = head_back(
-        grad_low, second, mixed, swish, row_head, queries, gate_pre, message[:, HEAD_V:], marks
-    )
-    now = (gate.first(), message_back)
+    now = (gate.first(), message_back, down_blocks)
     passing = Passing(after(now, message_back), True)
     now = passing.mine
     swish_pair, low_pair = pair(after(now, grad_swish)), pair(after(now, grad_low))

time: 412 us -> 415 us (level)
    ppermute x25, waiting for transfers between devices: 70.3 us -> 78.3 us  [cross(): return lax.ppermute(value, ('y', 'x', 'c'), perm)]
    unnamed x158 -> x160, local copies, waits for them, and re-layouts: 14.1 us -> 13.9 us
  transfers between devices with their start and end apart: 77 -> 77, of which waited for: 33 -> 32; matrix products, arithmetic and copies ran while one was open for 11% -> 11% of each run, Pallas kernels for 28% -> 28%
where the time goes in v5:
time: 415 us; the launch traced here: 408 us
  Pallas kernels  142 us (34%)
  waiting for transfers between devices  134 us (32%)
  starting transfers between devices  56.8 us (14%)
  other arithmetic  34.8 us (8%)
  local copies, waits for them, and re-layouts  25.2 us (6%)
  between operations  15.3 us (4%)
    pallas_call x8, Pallas kernels, kernel_call(): pl.pallas_call(body, grid=grid, in_specs=[s for _, s in ins], out_specs=[...  86.5 us
    ppermute x25, waiting for transfers between devices, cross(): return lax.ppermute(value, ('y', 'x', 'c'), perm)  78.3 us
    ppermute x49, waiting for transfers between devices, shift(): lax.ppermute(value, axis, [(i, (i + step) % size) for i in range(size)])  56.1 us
    pallas_call x5, Pallas kernels, weight_grads(): pl.pallas_call(body, grid_spec=pltpu.PrefetchScalarGridSpec(num_scalar_pr...  37.9 us
    ppermute x49, starting transfers between devices, shift(): lax.ppermute(value, axis, [(i, (i + step) % size) for i in range(size)])  33.1 us
    ppermute x25, starting transfers between devices, cross(): return lax.ppermute(value, ('y', 'x', 'c'), perm)  23.7 us
    pallas_call x3, Pallas kernels, assemble(): pl.pallas_call(body, grid_spec=pltpu.PrefetchScalarGridSpec(num_scalar_pr...  17.4 us
    unnamed x160, local copies, waits for them, and re-layouts  13.9 us
  transfers between devices with their start and end apart: 77, of which 32 were waited for; matrix products, arithmetic and copies ran while one was open for 11% of the time, Pallas kernels for 28%

profile of v5, /device:TPU:0, one launch (start us, length us, event | category | flops | bytes accessed | tf_op | source)
XLA Modules:
  0.0 408.4 jit_solution(11710473501998702038)
XLA Ops:
  7.3 2.1 shard_map.288
  9.4 3.0 collective-permute-start
  12.4 2.6 collective-permute-start.1
  16.3 2.9 collective-permute-done
  19.2 5.1 %collective-permute-done.1 = bf16[32,2176]{1,0:T(8,128)(2,1)S(1)} collective-permute-done((bf16[32,2176]{1,0:T(8,128)(2,1)}, bf16[32,2176]{1,0:T(8,128)(2,1)S(1)}, u32[]{:S(2)}, u32[]{:S(2)}) %collective-permute-start.1) | collective-permute-done | bytes 139296 | tf_op jit(solution)/shard_map/ppermute | solution.py:25
  29.4 3.5 collective-permute-start.3
  34.1 5.7 %collective-permute-done.3 = bf16[32,3072]{1,0:T(8,128)(2,1)S(1)} collective-permute-done((bf16[32,3072]{1,0:T(8,128)(2,1)S(1)}, bf16[32,3072]{1,0:T(8,128)(2,1)S(1)}, u32[]{:S(2)}, u32[]{:S(2)}) %collective-permute-start.3) | collective-permute-done | bytes 196640 | tf_op jit(solution)/shard_map/ppermute | solution.py:25
  39.8 3.4 collective-permute-done.6
  45.3 10.8 %collective-permute-done.8 = bf16[32,3072]{1,0:T(8,128)(2,1)S(1)} collective-permute-done((bf16[32,3072]{1,0:T(8,128)(2,1)S(1)}, bf16[32,3072]{1,0:T(8,128)(2,1)S(1)}, u32[]{:S(2)}, u32[]{:S(2)}) %collective-permute-start.8) | collective-permute-done | bytes 196640 | tf_op jit(solution)/shard_map/ppermute | solution.py:25
  63.2 4.0 collective-permute-start.16
  68.1 5.2 %shard_map.289.wk.wv.table.part_ref.ro.refs_5_.refs_6_.refs_9_ = bf16[1024,2176]{1,0:T(8,128)(2,1)} custom-call(s32[64]{0:T(128)} %stack.116.where_ref, bf16[4,32,2176]{2,1,0:T(8,128)(2,1)} %copy-done.8, bf16[4,32,2176]{2,1,0:T(8,128)(2,1)} %copy-done.45, bf16[4,32,2176]{2,1,0:T(8,128)(2,1)} %copy-done.46, ...), custom_call_target="tpu_custom_call" | custom-call | tf_op jit(solution)/shard_map/pallas_call | solution.py:98
  74.1 4.9 %collective-permute-done.16 = bf16[176,512]{1,0:T(8,128)(2,1)S(1)} collective-permute-done((bf16[176,512]{1,0:T(8,128)(2,1)S(1)}, bf16[176,512]{1,0:T(8,128)(2,1)S(1)}, u32[]{:S(2)}, u32[]{:S(2)}) %collective-permute-start.16) | collective-permute-done | bytes 180256 | tf_op jit(solution)/shard_map/ppermute | solution.py:25
  82.0 2.2 collective-permute-start.18
  86.3 8.2 %shard_map.290 = (bf16[384,1024]{1,0:T(8,128)(2,1)}, bf16[1024,384]{1,0:T(8,128)(2,1)}, bf16[384,128]{1,0:T(8,128)(2,1)}, bf16[384,1024]{1,0:T(8,128)(2,1)}, bf1...) custom-call(bf16[384,1024]{1,0:T(8,128)(2,1)} %refs_10_.1, ...), custom_call_target="tpu_custom_call" | custom-call | tf_op jit(solution)/shard_map/pallas_call | solution.py:379
  104.7 7.6 %collective-permute-done.20 = bf16[2,272,256]{2,1,0:T(8,128)(2,1)S(1)} collective-permute-done((bf16[2,272,256]{2,1,0:T(8,128)(2,1)S(1)}, bf16[2,272,256]{2,1,0:T(8,128)(2,1)S(1)}, u32[]{:S(2)}, u32[]{:S(2)}) %collective-permute-start.20) | collective-permute-done | bytes 278560 | tf_op jit(solution)/shard_map/ppermute | solution.py:47
  112.3 12.5 %collective-permute-done.21 = bf16[2,272,256]{2,1,0:T(8,128)(2,1)} collective-permute-done((bf16[2,272,256]{2,1,0:T(8,128)(2,1)S(1)}, bf16[2,272,256]{2,1,0:T(8,128)(2,1)}, u32[]{:S(2)}, u32[]{:S(2)}) %collective-permute-start.21) | collective-permute-done | bytes 278560 | tf_op jit(solution)/shard_map/ppermute | solution.py:47
  129.3 10.7 %collective-permute-done.29 = bf16[2,272,256]{2,1,0:T(8,128)(2,1)S(1)} collective-permute-done((bf16[2,272,256]{2,1,0:T(8,128)(2,1)}, bf16[2,272,256]{2,1,0:T(8,128)(2,1)S(1)}, u32[]{:S(2)}, u32[]{:S(2)}) %collective-permute-start.29) | collective-permute-done | bytes 278560 | tf_op jit(solution)/shard_map/ppermute | solution.py:47
  142.4 6.3 %shard_map.291.wq.ws.wo.refs_4_.refs_7_ = bf16[1024,3072]{1,0:T(8,128)(2,1)} custom-call(s32[64]{0:T(128)} %stack.116.where_ref, bf16[4,32,3072]{2,1,0:T(8,128)(2,1)} %copy-done.4, bf16[4,32,3072]{2,1,0:T(8,128)(2,1)} %copy-done.15, bf16[4,32,3072]{2,1,0:T(8,128)(2,1)} %copy-done.17, bf16[4,32,3072]{2,1,0:T(8,128)(2,1)} %copy-done.22, ...), custom_call_target="tpu_custom_call" | custom-call | tf_op jit(solution)/shard_map/pallas_call | solution.py:98
  150.0 3.3 collective-permute-done.31.refs_1_
  153.2 2.5 collective-permute-start.32
  158.5 15.4 %shard_map.292 = (bf16[384,1024]{1,0:T(8,128)(2,1)}, f32[384,1024]{1,0:T(8,128)}, f32[384,1024]{1,0:T(8,128)}, bf16[1024,384]{1,0:T(8,128)(2,1)}, f32[384,1024]{...) custom-call(bf16[384,1024]{1,0:T(8,128)(2,1)} %get-tuple-element.144.n_ref, ...), custom_call_target="tpu_custom_call" | custom-call | tf_op jit(solution)/shard_map/pallas_call | solution.py:379
  179.3 5.9 %shard_map.293.wd = bf16[2816,1024]{1,0:T(8,128)(2,1)} custom-call(s32[64]{0:T(128)} %stack.116.where_ref, bf16[4,176,512]{2,1,0:T(8,128)(2,1)} %copy-done.7, bf16[4,176,512]{2,1,0:T(8,128)(2,1)} %collective-permute-done.31.refs_1_, bf16[4,176,512]{2,1,0:T(8,128)(2,1)} %copy-done.37, bf16[4,176,512]{2,1,0:T(8,128)(2,1)} %copy-done.38, ...), custom_call_target="tpu_custom_call" | custom-call | tf_op jit(solution)/shard_map/pallas_call | solution.py:98
  185.3 25.0 %shard_map.294 = (bf16[384,1024]{1,0:T(8,128)(2,1)}, bf16[2816,384]{1,0:T(8,128)(2,1)}, bf16[384,2816]{1,0:T(8,128)(2,1)}, bf16[384,2816]{1,0:T(8,128)(2,1)}, f3...) custom-call(bf16[384,1024]{1,0:T(8,128)(2,1)} %get-tuple-element.167.n_ref, bf16[384,1024]{1,0:T(8,128)(2,1)} %refs_2_.1, ...), custom_call_target="tpu_custom_call" | custom-call | tf_op jit(solution)/shard_map/pallas_call | solution.py:379
  210.9 8.1 %shard_map.295 = (bf16[384,1024]{1,0:T(8,128)(2,1)}, bf16[384,1024]{1,0:T(8,128)(2,1)}, f32[1,256]{1,0:T(1,128)}, bf16[4,272,256]{2,1,0:T(8,128)(2,1)}) custom-call(bf16[384,1024]{1,0:T(8,128)(2,1)} %get-tuple-element.207.gh_ref.refs_6_, bf16[1024,3072]{1,0:T(8,128)(2,1)} %shard_map.291.wq.ws.wo.refs_4_.refs_7_, f32[384,1024]{1,0:T(8,128)} %get-tuple-element.178.mixed_ref, ...), custom_call_target="tpu_custom_call" | custom-call | tf_op jit(solution)/shard_map/pallas_call | solution.py:379
  221.1 7.2 %shard_map.296 = (bf16[8,32,2816]{2,1,0:T(8,128)(2,1)}, bf16[4,32,2816]{2,1,0:T(8,128)(2,1)}, bf16[4,32,2816]{2,1,0:T(8,128)(2,1)}) custom-call(s32[17]{0:T(128)} %pad_add_fusion.numbers_ref, bf16[1024,384]{1,0:T(8,128)(2,1)} %get-tuple-element.183.refs_0_, bf16[1024,384]{1,0:T(8,128)(2,1)} %copy-done.3, bf16[384,2816]{1,0:T(8,128)(2,1)} %get-tuple-element.187.refs_2_, ...), custom_call_target="tpu_custom_call" | custom-call | tf_op jit(solution)/shard_map/pallas_call | solution.py:298
  229.1 7.3 %shard_map.297 = bf16[16,176,512]{2,1,0:T(8,128)(2,1)} custom-call(s32[17]{0:T(128)} %pad_add_fusion.1.numbers_ref, bf16[2816,384]{1,0:T(8,128)(2,1)} %get-tuple-element.193.refs_0_, bf16[2816,384]{1,0:T(8,128)(2,1)} %collective-permute-done.41.refs_1_, bf16[384,1024]{1,0:T(8,128)(2,1)} %refs_2_.1, bf16[384,1024]{1,0:T(8,128)(2,1)} %collective-permute-done.24.refs_3_), custom_call_target="tpu_custom_call" | custom-call | tf_op jit(solution)/shard_map/pallas_call | solution.py:298
  236.4 11.2 %collective-permute-done.40 = bf16[8,32,2816]{2,1,0:T(8,128)(2,1)} collective-permute-done((bf16[8,32,2816]{2,1,0:T(8,128)(2,1)}, bf16[8,32,2816]{2,1,0:T(8,128)(2,1)}, u32[]{:S(2)}, u32[]{:S(2)}) %collective-permute-start.40) | collective-permute-done | bytes 1441824 | tf_op jit(solution)/shard_map/ppermute | solution.py:47
  248.2 2.2 collective-permute-done.42
  253.2 2.1 add_convert_fusion.5
  259.6 6.7 %shard_map.298 = (bf16[8,32,2816]{2,1,0:T(8,128)(2,1)}, bf16[4,32,2816]{2,1,0:T(8,128)(2,1)}, bf16[4,32,2816]{2,1,0:T(8,128)(2,1)}) custom-call(s32[17]{0:T(128)} %pad_add_fusion.numbers_ref, bf16[1024,384]{1,0:T(8,128)(2,1)} %get-tuple-element.183.refs_0_, bf16[1024,384]{1,0:T(8,128)(2,1)} %copy-done.3, bf16[384,2816]{1,0:T(8,128)(2,1)} %get-tuple-element.199.refs_2_, ...), custom_call_target="tpu_custom_call" | custom-call | tf_op jit(solution)/shard_map/pallas_call | solution.py:298
  268.1 6.7 %shard_map.299 = (bf16[8,32,2048]{2,1,0:T(8,128)(2,1)}, bf16[4,32,2048]{2,1,0:T(8,128)(2,1)}, bf16[4,32,2048]{2,1,0:T(8,128)(2,1)}) custom-call(s32[17]{0:T(128)} %pad_add_fusion.numbers_ref, bf16[1024,384]{1,0:T(8,128)(2,1)} %get-tuple-element.155.refs_0_.refs_8_, bf16[1024,384]{1,0:T(8,128)(2,1)} %copy-done, bf16[1024,384]{1,0:T(8,128)(2,1)} %get-tuple-element.204.refs_2_, ...), custom_call_target="tpu_custom_call" | custom-call | tf_op jit(solution)/shard_map/pallas_call | solution.py:298
  276.0 5.4 %collective-permute-done.50 = bf16[2,272,256]{2,1,0:T(8,128)(2,1)S(1)} collective-permute-done((bf16[2,272,256]{2,1,0:T(8,128)(2,1)S(1)}, bf16[2,272,256]{2,1,0:T(8,128)(2,1)S(1)}, u32[]{:S(2)}, u32[]{:S(2)}) %collective-permute-start.50) | collective-permute-done | bytes 278560 | tf_op jit(solution)/shard_map/ppermute | solution.py:47
  287.9 15.4 %shard_map.300 = (bf16[384,1024]{1,0:T(8,128)(2,1)}, bf16[384,1024]{1,0:T(8,128)(2,1)}, bf16[384,1024]{1,0:T(8,128)(2,1)}, bf16[1024,384]{1,0:T(8,128)(2,1)}, bf16[384,128]{1,0:T(8,128)(2,1)}) custom-call(bf16[384,1024]{1,0:T(8,128)(2,1)} %get-tuple-element.176.q_ref, bf16[384,1024]{1,0:T(8,128)(2,1)} %get-tuple-element.145.k_ref, ...), custom_call_target="tpu_custom_call" | custom-call | tf_op jit(solution)/shard_map/pallas_call | solution.py:379
  303.3 2.0 collective-permute-done.52
  307.5 2.9 collective-permute-done.56.refs_11_
  314.7 10.0 %shard_map.301 = (bf16[8,32,3200]{2,1,0:T(8,128)(2,1)}, bf16[4,32,3200]{2,1,0:T(8,128)(2,1)}, bf16[4,32,3200]{2,1,0:T(8,128)(2,1)}) custom-call(s32[17]{0:T(128)} %pad_add_fusion.numbers_ref, bf16[1024,384]{1,0:T(8,128)(2,1)} %get-tuple-element.155.refs_0_.refs_8_, bf16[1024,384]{1,0:T(8,128)(2,1)} %copy-done, ...), custom_call_target="tpu_custom_call" | custom-call | tf_op jit(solution)/shard_map/pallas_call | solution.py:298
  324.7 5.0 %collective-permute-done.61 = bf16[4,32,2816]{2,1,0:T(8,128)(2,1)} collective-permute-done((bf16[4,32,2816]{2,1,0:T(8,128)(2,1)}, bf16[4,32,2816]{2,1,0:T(8,128)(2,1)}, u32[]{:S(2)}, u32[]{:S(2)}) %collective-permute-start.61) | collective-permute-done | bytes 720928 | tf_op jit(solution)/shard_map/ppermute | solution.py:47
  336.9 9.8 %shard_map.302 = f32[384,1024]{1,0:T(8,128)} custom-call(bf16[384,1024]{1,0:T(8,128)(2,1)} %get-tuple-element.221.refs_2_.refs_0_, bf16[384,1024]{1,0:T(8,128)(2,1)} %get-tuple-element.222.refs_4_.refs_1_, bf16[384,1024]{1,0:T(8,128)(2,1)} %get-tuple-element.223.refs_6_.refs_2_, bf16[384,1024]{1,0:T(8,128)(2,1)} %get-tuple-element.206.refs_4_.refs_3_, ...), custom_call_target="tpu_custom_call" | custom-call | tf_op jit(solution)/shard_map/pallas_call | solution.py:379
  346.7 3.2 collective-permute-done.63
  349.9 9.3 %collective-permute-done.62 = bf16[8,32,3200]{2,1,0:T(8,128)(2,1)S(1)} collective-permute-done((bf16[8,32,3200]{2,1,0:T(8,128)(2,1)}, bf16[8,32,3200]{2,1,0:T(8,128)(2,1)S(1)}, u32[]{:S(2)}, u32[]{:S(2)}) %collective-permute-start.62) | collective-permute-done | bytes 1638432 | tf_op jit(solution)/shard_map/ppermute | solution.py:47
  365.4 3.8 collective-permute-start.70
  370.1 4.6 %collective-permute-done.71 = bf16[2,176,512]{2,1,0:T(8,128)(2,1)S(1)} collective-permute-done((bf16[2,176,512]{2,1,0:T(8,128)(2,1)S(1)}, bf16[2,176,512]{2,1,0:T(8,128)(2,1)S(1)}, u32[]{:S(2)}, u32[]{:S(2)}) %collective-permute-start.71) | collective-permute-done | bytes 360480 | tf_op jit(solution)/shard_map/ppermute | solution.py:47
  374.8 2.0 collective-permute-done.64
  380.7 2.1 multiply_reduce_fusion
  384.4 3.0 collective-permute-start.67
  388.0 2.3 collective-permute-done.65.refs_1_
  390.3 7.2 %collective-permute-done.66.refs_2_ = bf16[32,3200]{1,0:T(8,128)(2,1)S(1)} collective-permute-done((bf16[32,3200]{1,0:T(8,128)(2,1)S(1)}, bf16[32,3200]{1,0:T(8,128)(2,1)S(1)}, u32[]{:S(2)}, u32[]{:S(2)}) %collective-permute-start.66) | collective-permute-done | bytes 204832 | tf_op jit(solution)/shard_map/ppermute | solution.py:25
  398.4 2.4 shard_map.303
  (400 shorter events, 98.3 us)
Async XLA Ops:
  7.2 178.0 %all-gather.2.cloned.1.call-start = ((), (), s32[]{:S(2)}) async-start(), calls=%async_computation.2 | async-start | bytes 11894784 | tf_op jit(solution)/shard_map/all_gather | solution.py:1036
  12.4 12.0 %collective-permute-start.1 = (bf16[32,2176]{1,0:T(8,128)(2,1)}, bf16[32,2176]{1,0:T(8,128)(2,1)S(1)}, u32[]{:S(2)}, u32[]{:S(2)}) collective-permute-start(bf16[32,2176]{1,0:T(8,128)(2,1)} %shard_map.288), channel_id=1, source_target_pairs={{0,16},{8,24},{16,0},{24,8},{1,17},{9,25},{17,1},{25,9},{2,18},{10... | collective-permute-start | bytes 417800 | tf_op jit(solution)/shard_map/ppermute | solution.py:25
  25.4 17.8 %collective-permute-start.7 = (bf16[4,32,2176]{2,1,0:T(8,128)(2,1)S(1)}, bf16[4,32,2176]{2,1,0:T(8,128)(2,1)S(1)}, u32[]{:S(2)}, u32[]{:S(2)}) collective-permute-start(bf16[4,32,2176]{2,1,0:T(8,128)(2,1)S(1)} %pad_maximum_fusion.3.refs_0_), channel_id=1, source_target_pairs={{0,1},{1,0},{2,3},{3,2},{4,5},{5,4},{6,7},{7,6},{8,9},{9,8},{10,11... | collective-permute-start | bytes 1671176 | tf_op jit(solution)/shard_map/ppermute | solution.py:25
  25.5 17.7 %collective-permute-start.4 = (bf16[4,32,2176]{2,1,0:T(8,128)(2,1)S(1)}, bf16[4,32,2176]{2,1,0:T(8,128)(2,1)S(1)}, u32[]{:S(2)}, u32[]{:S(2)}) collective-permute-start(bf16[4,32,2176]{2,1,0:T(8,128)(2,1)S(1)} %pad_maximum_fusion.3.refs_0_), channel_id=1, source_target_pairs={{0,2},{1,5},{2,0},{3,7},{4,6},{5,1},{6,4},{7,3},{8,10},{9,13},{10,... | collective-permute-start | bytes 1671176 | tf_op jit(solution)/shard_map/ppermute | solution.py:47
  27.0 16.2 %collective-permute-start.5 = (bf16[4,32,2176]{2,1,0:T(8,128)(2,1)S(1)}, bf16[4,32,2176]{2,1,0:T(8,128)(2,1)S(1)}, u32[]{:S(2)}, u32[]{:S(2)}) collective-permute-start(bf16[4,32,2176]{2,1,0:T(8,128)(2,1)S(1)} %pad_maximum_fusion.3.refs_0_), channel_id=1, source_target_pairs={{0,4},{1,3},{2,6},{3,1},{4,0},{5,7},{6,2},{7,5},{8,12},{9,11},{10,... | collective-permute-start | bytes 1671176 | tf_op jit(solution)/shard_map/ppermute | solution.py:47
  29.4 10.3 %collective-permute-start.3 = (bf16[32,3072]{1,0:T(8,128)(2,1)S(1)}, bf16[32,3072]{1,0:T(8,128)(2,1)S(1)}, u32[]{:S(2)}, u32[]{:S(2)}) collective-permute-start(bf16[32,3072]{1,0:T(8,128)(2,1)S(1)} %constant_dynamic-update-slice_fusion), channel_id=1, source_target_pairs={{0,8},{8,16},{16,24},{24,0},{1,9},{9,17},{17,25},{25,1},{2,10},{10... | collective-permute-start | bytes 589832 | tf_op jit(solution)/shard_map/ppermute | solution.py:25
  32.9 10.2 %collective-permute-start.6 = (bf16[32,3072]{1,0:T(8,128)(2,1)S(1)}, bf16[32,3072]{1,0:T(8,128)(2,1)S(1)}, u32[]{:S(2)}, u32[]{:S(2)}) collective-permute-start(bf16[32,3072]{1,0:T(8,128)(2,1)S(1)} %constant_dynamic-update-slice_fusion), channel_id=1, source_target_pairs={{0,24},{8,0},{16,8},{24,16},{1,25},{9,1},{17,9},{25,17},{2,26},{10... | collective-permute-start | bytes 589832 | tf_op jit(solution)/shard_map/ppermute | solution.py:25
  43.2 13.0 %collective-permute-start.10 = (bf16[4,32,2176]{2,1,0:T(8,128)(2,1)S(1)}, bf16[4,32,2176]{2,1,0:T(8,128)(2,1)}, u32[]{:S(2)}, u32[]{:S(2)}) collective-permute-start(bf16[4,32,2176]{2,1,0:T(8,128)(2,1)S(1)} %collective-permute-done.4.refs_1_), channel_id=1, source_target_pairs={{0,4},{1,3},{2,6},{3,1},{4,0},{5,7},{6,2},{7,5},{8,12},{9,11},{10,... | collective-permute-start | bytes 1671176 | tf_op jit(solution)/shard_map/ppermute | solution.py:47
  43.8 12.4 %collective-permute-start.11 = (bf16[4,32,2176]{2,1,0:T(8,128)(2,1)S(1)}, bf16[4,32,2176]{2,1,0:T(8,128)(2,1)S(1)}, u32[]{:S(2)}, u32[]{:S(2)}) collective-permute-start(bf16[4,32,2176]{2,1,0:T(8,128)(2,1)S(1)} %collective-permute-done.4.refs_1_), channel_id=1, source_target_pairs={{0,1},{1,0},{2,3},{3,2},{4,5},{5,4},{6,7},{7,6},{8,9},{9,8},{10,11... | collective-permute-start | bytes 1671176 | tf_op jit(solution)/shard_map/ppermute | solution.py:25
  43.8 13.9 %collective-permute-start.12 = (bf16[4,32,2176]{2,1,0:T(8,128)(2,1)S(1)}, bf16[4,32,2176]{2,1,0:T(8,128)(2,1)}, u32[]{:S(2)}, u32[]{:S(2)}) collective-permute-start(bf16[4,32,2176]{2,1,0:T(8,128)(2,1)S(1)} %collective-permute-done.5.refs_2_), channel_id=1, source_target_pairs={{0,1},{1,0},{2,3},{3,2},{4,5},{5,4},{6,7},{7,6},{8,9},{9,8},{10,11... | collective-permute-start | bytes 1671176 | tf_op jit(solution)/shard_map/ppermute | solution.py:25
  44.3 11.9 %collective-permute-start.8 = (bf16[32,3072]{1,0:T(8,128)(2,1)S(1)}, bf16[32,3072]{1,0:T(8,128)(2,1)S(1)}, u32[]{:S(2)}, u32[]{:S(2)}) collective-permute-start(bf16[32,3072]{1,0:T(8,128)(2,1)S(1)} %constant_dynamic-update-slice_fusion), channel_id=1, source_target_pairs={{0,16},{8,24},{16,0},{24,8},{1,17},{9,25},{17,1},{25,9},{2,18},{10... | collective-permute-start | bytes 589832 | tf_op jit(solution)/shard_map/ppermute | solution.py:25
  58.5 303.8 %reduce-scatter.5.cloned.1.call-start = ((), (), s32[]{:S(2)}) async-start(), calls=%async_computation.4 | async-start | bytes 3604480 | tf_op jit(solution)/shard_map/reduce_scatter | solution.py:142
  61.1 18.0 %collective-permute-start.14 = (bf16[4,32,3072]{2,1,0:T(8,128)(2,1)S(1)}, bf16[4,32,3072]{2,1,0:T(8,128)(2,1)S(1)}, u32[]{:S(2)}, u32[]{:S(2)}) collective-permute-start(bf16[4,32,3072]{2,1,0:T(8,128)(2,1)S(1)} %pad_maximum_fusion.1.refs_0_), channel_id=1, source_target_pairs={{0,2},{1,5},{2,0},{3,7},{4,6},{5,1},{6,4},{7,3},{8,10},{9,13},{10,... | collective-permute-start | bytes 2359304 | tf_op jit(solution)/shard_map/ppermute | solution.py:47
  63.2 10.9 %collective-permute-start.15 = (bf16[176,512]{1,0:T(8,128)(2,1)S(1)}, bf16[176,512]{1,0:T(8,128)(2,1)S(1)}, u32[]{:S(2)}, u32[]{:S(2)}) collective-permute-start(bf16[176,512]{1,0:T(8,128)(2,1)S(1)} %maximum_select_fusion.5), channel_id=1, source_target_pairs={{0,8},{8,16},{16,24},{24,0},{1,9},{9,17},{17,25},{25,1},{2,10},{10... | collective-permute-start | bytes 540680 | tf_op jit(solution)/shard_map/ppermute | solution.py:25
  63.2 15.8 %collective-permute-start.16 = (bf16[176,512]{1,0:T(8,128)(2,1)S(1)}, bf16[176,512]{1,0:T(8,128)(2,1)S(1)}, u32[]{:S(2)}, u32[]{:S(2)}) collective-permute-start(bf16[176,512]{1,0:T(8,128)(2,1)S(1)} %maximum_select_fusion.5), channel_id=1, source_target_pairs={{0,24},{8,0},{16,8},{24,16},{1,25},{9,1},{17,9},{25,17},{2,26},{10... | collective-permute-start | bytes 540680 | tf_op jit(solution)/shard_map/ppermute | solution.py:25
  79.0 15.6 %collective-permute-start.17 = (bf16[4,32,3072]{2,1,0:T(8,128)(2,1)S(1)}, bf16[4,32,3072]{2,1,0:T(8,128)(2,1)S(1)}, u32[]{:S(2)}, u32[]{:S(2)}) collective-permute-start(bf16[4,32,3072]{2,1,0:T(8,128)(2,1)S(1)} %pad_maximum_fusion.1.refs_0_), channel_id=1, source_target_pairs={{0,4},{1,3},{2,6},{3,1},{4,0},{5,7},{6,2},{7,5},{8,12},{9,11},{10,... | collective-permute-start | bytes 2359304 | tf_op jit(solution)/shard_map/ppermute | solution.py:47
  82.0 12.6 %collective-permute-start.18 = (bf16[176,512]{1,0:T(8,128)(2,1)S(1)}, bf16[176,512]{1,0:T(8,128)(2,1)S(1)}, u32[]{:S(2)}, u32[]{:S(2)}) collective-permute-start(bf16[176,512]{1,0:T(8,128)(2,1)S(1)} %maximum_select_fusion.5), channel_id=1, source_target_pairs={{0,16},{8,24},{16,0},{24,8},{1,17},{9,25},{17,1},{25,9},{2,18},{10... | collective-permute-start | bytes 540680 | tf_op jit(solution)/shard_map/ppermute | solution.py:25
  100.6 24.2 %collective-permute-start.22 = (bf16[4,32,3072]{2,1,0:T(8,128)(2,1)S(1)}, bf16[4,32,3072]{2,1,0:T(8,128)(2,1)S(1)}, u32[]{:S(2)}, u32[]{:S(2)}) collective-permute-start(bf16[4,32,3072]{2,1,0:T(8,128)(2,1)S(1)} %copy-done.16), channel_id=1, source_target_pairs={{0,4},{1,3},{2,6},{3,1},{4,0},{5,7},{6,2},{7,5},{8,12},{9,11},{10,... | collective-permute-start | bytes 2359304 | tf_op jit(solution)/shard_map/ppermute | solution.py:47
  102.2 22.6 %collective-permute-start.26 = (bf16[4,32,3072]{2,1,0:T(8,128)(2,1)S(1)}, bf16[4,32,3072]{2,1,0:T(8,128)(2,1)S(1)}, u32[]{:S(2)}, u32[]{:S(2)}) collective-permute-start(bf16[4,32,3072]{2,1,0:T(8,128)(2,1)S(1)} %copy-done.16), channel_id=1, source_target_pairs={{0,1},{1,0},{2,3},{3,2},{4,5},{5,4},{6,7},{7,6},{8,9},{9,8},{10,11... | collective-permute-start | bytes 2359304 | tf_op jit(solution)/shard_map/ppermute | solution.py:25
  102.3 22.5 %collective-permute-start.27 = (bf16[4,32,3072]{2,1,0:T(8,128)(2,1)S(1)}, bf16[4,32,3072]{2,1,0:T(8,128)(2,1)S(1)}, u32[]{:S(2)}, u32[]{:S(2)}) collective-permute-start(bf16[4,32,3072]{2,1,0:T(8,128)(2,1)S(1)} %copy-done.18), channel_id=1, source_target_pairs={{0,1},{1,0},{2,3},{3,2},{4,5},{5,4},{6,7},{7,6},{8,9},{9,8},{10,11... | collective-permute-start | bytes 2359304 | tf_op jit(solution)/shard_map/ppermute | solution.py:25
  103.1 21.7 %collective-permute-start.21 = (bf16[2,272,256]{2,1,0:T(8,128)(2,1)S(1)}, bf16[2,272,256]{2,1,0:T(8,128)(2,1)}, u32[]{:S(2)}, u32[]{:S(2)}) collective-permute-start(bf16[2,272,256]{2,1,0:T(8,128)(2,1)S(1)} %fusion.20), channel_id=1, source_target_pairs={{0,4},{1,3},{2,6},{3,1},{4,0},{5,7},{6,2},{7,5},{8,12},{9,11},{10,... | collective-permute-start | bytes 835592 | tf_op jit(solution)/shard_map/ppermute | solution.py:47
  127.2 12.8 %collective-permute-start.29 = (bf16[2,272,256]{2,1,0:T(8,128)(2,1)}, bf16[2,272,256]{2,1,0:T(8,128)(2,1)S(1)}, u32[]{:S(2)}, u32[]{:S(2)}) collective-permute-start(bf16[2,272,256]{2,1,0:T(8,128)(2,1)} %collective-permute-done.21), channel_id=1, source_target_pairs={{0,2},{1,5},{2,0},{3,7},{4,6},{5,1},{6,4},{7,3},{8,10},{9,13},{10,... | collective-permute-start | bytes 835592 | tf_op jit(solution)/shard_map/ppermute | solution.py:47
  141.8 11.4 %collective-permute-start.31 = (bf16[4,176,512]{2,1,0:T(8,128)(2,1)S(1)}, bf16[4,176,512]{2,1,0:T(8,128)(2,1)}, u32[]{:S(2)}, u32[]{:S(2)}) collective-permute-start(bf16[4,176,512]{2,1,0:T(8,128)(2,1)S(1)} %pad_maximum_fusion.2.refs_0_), channel_id=1, source_target_pairs={{0,2},{1,5},{2,0},{3,7},{4,6},{5,1},{6,4},{7,3},{8,10},{9,13},{10,... | collective-permute-start | bytes 2162696 | tf_op jit(solution)/shard_map/ppermute | solution.py:47
  153.2 20.7 %collective-permute-start.32 = (bf16[4,176,512]{2,1,0:T(8,128)(2,1)S(1)}, bf16[4,176,512]{2,1,0:T(8,128)(2,1)S(1)}, u32[]{:S(2)}, u32[]{:S(2)}) collective-permute-start(bf16[4,176,512]{2,1,0:T(8,128)(2,1)S(1)} %pad_maximum_fusion.2.refs_0_), channel_id=1, source_target_pairs={{0,4},{1,3},{2,6},{3,1},{4,0},{5,7},{6,2},{7,5},{8,12},{9,11},{10,... | collective-permute-start | bytes 2162696 | tf_op jit(solution)/shard_map/ppermute | solution.py:47
  155.7 18.2 %collective-permute-start.33 = (bf16[4,176,512]{2,1,0:T(8,128)(2,1)}, bf16[4,176,512]{2,1,0:T(8,128)(2,1)S(1)}, u32[]{:S(2)}, u32[]{:S(2)}) collective-permute-start(bf16[4,176,512]{2,1,0:T(8,128)(2,1)} %collective-permute-done.31.refs_1_), channel_id=1, source_target_pairs={{0,4},{1,3},{2,6},{3,1},{4,0},{5,7},{6,2},{7,5},{8,12},{9,11},{10,... | collective-permute-start | bytes 2162696 | tf_op jit(solution)/shard_map/ppermute | solution.py:47
  158.5 16.5 %collective-permute-start.35 = (bf16[4,176,512]{2,1,0:T(8,128)(2,1)}, bf16[4,176,512]{2,1,0:T(8,128)(2,1)S(1)}, u32[]{:S(2)}, u32[]{:S(2)}) collective-permute-start(bf16[4,176,512]{2,1,0:T(8,128)(2,1)} %collective-permute-done.31.refs_1_), channel_id=1, source_target_pairs={{0,1},{1,0},{2,3},{3,2},{4,5},{5,4},{6,7},{7,6},{8,9},{9,8},{10,11... | collective-permute-start | bytes 2162696 | tf_op jit(solution)/shard_map/ppermute | solution.py:25
  228.2 19.4 %collective-permute-start.40 = (bf16[8,32,2816]{2,1,0:T(8,128)(2,1)}, bf16[8,32,2816]{2,1,0:T(8,128)(2,1)}, u32[]{:S(2)}, u32[]{:S(2)}) collective-permute-start(bf16[8,32,2816]{2,1,0:T(8,128)(2,1)} %get-tuple-element.189), channel_id=1, source_target_pairs={{0,2},{1,5},{2,0},{3,7},{4,6},{5,1},{6,4},{7,3},{8,10},{9,13},{10,... | collective-permute-start | bytes 4325384 | tf_op jit(solution)/shard_map/ppermute | solution.py:47
  252.7 13.7 %collective-permute-start.49 = (bf16[384,1024]{1,0:T(8,128)(2,1)S(1)}, bf16[384,1024]{1,0:T(8,128)(2,1)S(1)}, u32[]{:S(2)}, u32[]{:S(2)}) collective-permute-start(bf16[384,1024]{1,0:T(8,128)(2,1)S(1)} %copy-done.2), channel_id=1, source_target_pairs={{0,1},{1,0},{2,3},{3,2},{4,5},{5,4},{6,7},{7,6},{8,9},{9,8},{10,11... | collective-permute-start | bytes 2359304 | tf_op jit(solution)/shard_map/ppermute | solution.py:25
  252.8 13.5 %collective-permute-start.48 = (bf16[384,1024]{1,0:T(8,128)(2,1)S(1)}, bf16[384,1024]{1,0:T(8,128)(2,1)S(1)}, u32[]{:S(2)}, u32[]{:S(2)}) collective-permute-start(bf16[384,1024]{1,0:T(8,128)(2,1)S(1)} %copy-done.6), channel_id=1, source_target_pairs={{0,1},{1,0},{2,3},{3,2},{4,5},{5,4},{6,7},{7,6},{8,9},{9,8},{10,11... | collective-permute-start | bytes 2359304 | tf_op jit(solution)/shard_map/ppermute | solution.py:25
  255.3 19.5 %collective-permute-start.45 = (bf16[4,32,2816]{2,1,0:T(8,128)(2,1)}, bf16[4,32,2816]{2,1,0:T(8,128)(2,1)}, u32[]{:S(2)}, u32[]{:S(2)}) collective-permute-start(bf16[4,32,2816]{2,1,0:T(8,128)(2,1)} %add_convert_fusion.5), channel_id=1, source_target_pairs={{0,4},{1,3},{2,6},{3,1},{4,0},{5,7},{6,2},{7,5},{8,12},{9,11},{10,... | collective-permute-start | bytes 2162696 | tf_op jit(solution)/shard_map/ppermute | solution.py:47
  257.3 17.5 %collective-permute-start.43 = (bf16[2,272,256]{2,1,0:T(8,128)(2,1)}, bf16[2,272,256]{2,1,0:T(8,128)(2,1)}, u32[]{:S(2)}, u32[]{:S(2)}) collective-permute-start(bf16[2,272,256]{2,1,0:T(8,128)(2,1)} %fusion.17), channel_id=1, source_target_pairs={{0,2},{1,5},{2,0},{3,7},{4,6},{5,1},{6,4},{7,3},{8,10},{9,13},{10,... | collective-permute-start | bytes 835592 | tf_op jit(solution)/shard_map/ppermute | solution.py:47
  258.2 16.6 %collective-permute-start.44 = (bf16[2,272,256]{2,1,0:T(8,128)(2,1)}, bf16[2,272,256]{2,1,0:T(8,128)(2,1)S(1)}, u32[]{:S(2)}, u32[]{:S(2)}) collective-permute-start(bf16[2,272,256]{2,1,0:T(8,128)(2,1)} %fusion.17), channel_id=1, source_target_pairs={{0,4},{1,3},{2,6},{3,1},{4,0},{5,7},{6,2},{7,5},{8,12},{9,11},{10,... | collective-permute-start | bytes 835592 | tf_op jit(solution)/shard_map/ppermute | solution.py:47
  283.2 97.2 %reduce-scatter.3.cloned.1.call-start = ((), (), s32[]{:S(2)}) async-start(), calls=%async_computation.3 | async-start | bytes 1802240 | tf_op jit(solution)/shard_map/reduce_scatter | solution.py:181
  286.3 19.0 %collective-permute-start.52 = (bf16[8,32,2816]{2,1,0:T(8,128)(2,1)S(1)}, bf16[8,32,2816]{2,1,0:T(8,128)(2,1)S(1)}, u32[]{:S(2)}, u32[]{:S(2)}) collective-permute-start(bf16[8,32,2816]{2,1,0:T(8,128)(2,1)S(1)} %copy-done.73), channel_id=1, source_target_pairs={{0,2},{1,5},{2,0},{3,7},{4,6},{5,1},{6,4},{7,3},{8,10},{9,13},{10,... | collective-permute-start | bytes 4325384 | tf_op jit(solution)/shard_map/ppermute | solution.py:47
  287.4 18.4 %collective-permute-start.58 = (bf16[384,128]{1,0:T(8,128)(2,1)S(1)}, bf16[384,128]{1,0:T(8,128)(2,1)S(1)}, u32[]{:S(2)}, u32[]{:S(2)}) collective-permute-start(bf16[384,128]{1,0:T(8,128)(2,1)S(1)} %copy-done.61), channel_id=1, source_target_pairs={{0,1},{1,0},{2,3},{3,2},{4,5},{5,4},{6,7},{7,6},{8,9},{9,8},{10,11... | collective-permute-start | bytes 294920 | tf_op jit(solution)/shard_map/ppermute | solution.py:25
  287.4 18.9 %collective-permute-start.59 = (f32[1,256]{1,0:T(1,128)S(1)}, f32[1,256]{1,0:T(1,128)S(1)}, u32[]{:S(2)}, u32[]{:S(2)}) collective-permute-start(f32[1,256]{1,0:T(1,128)S(1)} %copy-done.71), channel_id=1, source_target_pairs={{0,1},{1,0},{2,3},{3,2},{4,5},{5,4},{6,7},{7,6},{8,9},{9,8},{10,11... | collective-permute-start | bytes 3080 | tf_op jit(solution)/shard_map/ppermute | solution.py:25
  310.3 19.3 %collective-permute-start.61 = (bf16[4,32,2816]{2,1,0:T(8,128)(2,1)}, bf16[4,32,2816]{2,1,0:T(8,128)(2,1)}, u32[]{:S(2)}, u32[]{:S(2)}) collective-permute-start(bf16[4,32,2816]{2,1,0:T(8,128)(2,1)} %add_convert_fusion.4), channel_id=1, source_target_pairs={{0,4},{1,3},{2,6},{3,1},{4,0},{5,7},{6,2},{7,5},{8,12},{9,11},{10,... | collective-permute-start | bytes 2162696 | tf_op jit(solution)/shard_map/ppermute | solution.py:47
  311.0 21.2 %collective-permute-start.60 = (bf16[8,32,2048]{2,1,0:T(8,128)(2,1)}, bf16[8,32,2048]{2,1,0:T(8,128)(2,1)S(1)}, u32[]{:S(2)}, u32[]{:S(2)}) collective-permute-start(bf16[8,32,2048]{2,1,0:T(8,128)(2,1)} %get-tuple-element.231), channel_id=1, source_target_pairs={{0,2},{1,5},{2,0},{3,7},{4,6},{5,1},{6,4},{7,3},{8,10},{9,13},{10,... | collective-permute-start | bytes 3145736 | tf_op jit(solution)/shard_map/ppermute | solution.py:47
  332.2 26.9 %collective-permute-start.62 = (bf16[8,32,3200]{2,1,0:T(8,128)(2,1)}, bf16[8,32,3200]{2,1,0:T(8,128)(2,1)S(1)}, u32[]{:S(2)}, u32[]{:S(2)}) collective-permute-start(bf16[8,32,3200]{2,1,0:T(8,128)(2,1)} %get-tuple-element.236), channel_id=1, source_target_pairs={{0,2},{1,5},{2,0},{3,7},{4,6},{5,1},{6,4},{7,3},{8,10},{9,13},{10,... | collective-permute-start | bytes 4915208 | tf_op jit(solution)/shard_map/ppermute | solution.py:47
  334.9 15.0 %collective-permute-start.63 = (bf16[4,32,2048]{2,1,0:T(8,128)(2,1)S(1)}, bf16[4,32,2048]{2,1,0:T(8,128)(2,1)}, u32[]{:S(2)}, u32[]{:S(2)}) collective-permute-start(bf16[4,32,2048]{2,1,0:T(8,128)(2,1)S(1)} %add_convert_fusion.7), channel_id=1, source_target_pairs={{0,4},{1,3},{2,6},{3,1},{4,0},{5,7},{6,2},{7,5},{8,12},{9,11},{10,... | collective-permute-start | bytes 1572872 | tf_op jit(solution)/shard_map/ppermute | solution.py:47
  360.3 16.5 %collective-permute-start.64 = (bf16[4,32,3200]{2,1,0:T(8,128)(2,1)}, bf16[4,32,3200]{2,1,0:T(8,128)(2,1)}, u32[]{:S(2)}, u32[]{:S(2)}) collective-permute-start(bf16[4,32,3200]{2,1,0:T(8,128)(2,1)} %add_convert_fusion.1), channel_id=1, source_target_pairs={{0,4},{1,3},{2,6},{3,1},{4,0},{5,7},{6,2},{7,5},{8,12},{9,11},{10,... | collective-permute-start | bytes 2457608 | tf_op jit(solution)/shard_map/ppermute | solution.py:47
  363.3 11.4 %collective-permute-start.71 = (bf16[2,176,512]{2,1,0:T(8,128)(2,1)S(1)}, bf16[2,176,512]{2,1,0:T(8,128)(2,1)S(1)}, u32[]{:S(2)}, u32[]{:S(2)}) collective-permute-start(bf16[2,176,512]{2,1,0:T(8,128)(2,1)S(1)} %bitcast.116), channel_id=1, source_target_pairs={{0,2},{1,5},{2,0},{3,7},{4,6},{5,1},{6,4},{7,3},{8,10},{9,13},{10,... | collective-permute-start | bytes 1081352 | tf_op jit(solution)/shard_map/ppermute | solution.py:47
  365.4 19.1 %collective-permute-start.68 = (bf16[32,2048]{1,0:T(8,128)(2,1)}, bf16[32,2048]{1,0:T(8,128)(2,1)}, u32[]{:S(2)}, u32[]{:S(2)}) collective-permute-start(bf16[32,2048]{1,0:T(8,128)(2,1)} %get-tuple-element.282), channel_id=1, source_target_pairs={{0,8},{8,16},{16,24},{24,0},{1,9},{9,17},{17,25},{25,1},{2,10},{10... | collective-permute-start | bytes 393224 | tf_op jit(solution)/shard_map/ppermute | solution.py:25
  365.4 22.1 %collective-permute-start.69 = (bf16[32,2048]{1,0:T(8,128)(2,1)}, bf16[32,2048]{1,0:T(8,128)(2,1)}, u32[]{:S(2)}, u32[]{:S(2)}) collective-permute-start(bf16[32,2048]{1,0:T(8,128)(2,1)} %get-tuple-element.281), channel_id=1, source_target_pairs={{0,16},{8,24},{16,0},{24,8},{1,17},{9,25},{17,1},{25,9},{2,18},{10... | collective-permute-start | bytes 393224 | tf_op jit(solution)/shard_map/ppermute | solution.py:25
  365.4 22.6 %collective-permute-start.70 = (bf16[32,2048]{1,0:T(8,128)(2,1)}, bf16[32,2048]{1,0:T(8,128)(2,1)}, u32[]{:S(2)}, u32[]{:S(2)}) collective-permute-start(bf16[32,2048]{1,0:T(8,128)(2,1)} %get-tuple-element.280), channel_id=1, source_target_pairs={{0,24},{8,0},{16,8},{24,16},{1,25},{9,1},{17,9},{25,17},{2,26},{10... | collective-permute-start | bytes 393224 | tf_op jit(solution)/shard_map/ppermute | solution.py:25
  383.2 14.3 %collective-permute-start.66 = (bf16[32,3200]{1,0:T(8,128)(2,1)S(1)}, bf16[32,3200]{1,0:T(8,128)(2,1)S(1)}, u32[]{:S(2)}, u32[]{:S(2)}) collective-permute-start(bf16[32,3200]{1,0:T(8,128)(2,1)S(1)} %get-tuple-element.267), channel_id=1, source_target_pairs={{0,16},{8,24},{16,0},{24,8},{1,17},{9,25},{17,1},{25,9},{2,18},{10... | collective-permute-start | bytes 614408 | tf_op jit(solution)/shard_map/ppermute | solution.py:25
  384.4 13.3 %collective-permute-start.67 = (bf16[32,3200]{1,0:T(8,128)(2,1)S(1)}, bf16[32,3200]{1,0:T(8,128)(2,1)S(1)}, u32[]{:S(2)}, u32[]{:S(2)}) collective-permute-start(bf16[32,3200]{1,0:T(8,128)(2,1)S(1)} %get-tuple-element.266), channel_id=1, source_target_pairs={{0,24},{8,0},{16,8},{24,16},{1,25},{9,1},{17,9},{25,17},{2,26},{10... | collective-permute-start | bytes 614408 | tf_op jit(solution)/shard_map/ppermute | solution.py:25
  387.5 13.4 %collective-permute-start.73 = (f32[88,512]{1,0:T(8,128)S(1)}, f32[88,512]{1,0:T(8,128)S(1)}, u32[]{:S(2)}, u32[]{:S(2)}) collective-permute-start(f32[88,512]{1,0:T(8,128)S(1)} %get-tuple-element.285), channel_id=1, source_target_pairs={{0,1},{1,0},{2,3},{3,2},{4,5},{5,4},{6,7},{7,6},{8,9},{9,8},{10,11... | collective-permute-start | bytes 540680 | tf_op jit(solution)/shard_map/ppermute | solution.py:25
  (103 other events, 977.0 us)
Sparse Core Ops, SparseCore 0:
  58.6 98.6 all-gather.1
  283.3 53.3 reduce-scatter.4
  339.0 34.1 reduce-scatter.2
